TPU v7x, 32 devices: a whole 2x2x4 slice. The times are simulated.
32 devices in a mesh: group: 2 (over y), row: 4 (over z), col: 4 (over x, core).
Axes of the slice: x: 2, y: 2, z: 4, core: 2. Of those that a mesh axis runs over, the one named last changes fastest.
Arguments:
- pair: bfloat16 [1024, 512, 128], P(('group', 'row'), 'col'), parts along dimension 0, may hold values from -6 to 6
- chain: int32 [8], P('group'), parts along dimension 0, may hold values from 0 to 2
- block_mask: int32 [8, 4], P('group'), parts along dimension 0, may hold values 0 or 1
- w_in: bfloat16 [2, 128, 256], replicated, may hold values from -0.5 to 0.5
- w_gate: bfloat16 [2, 128, 128], replicated, may hold values from -0.5 to 0.5
- w_out: bfloat16 [2, 64, 128], replicated, may hold values from -0.75 to 0.75
- gain_in: float32 [2, 128], replicated, may hold values from 0.1 to 1.9
- gain_out: float32 [2, 64], replicated, may hold values from 0.1 to 1.9
Outputs:
- updated: bfloat16 [1024, 512, 128], P(('group', 'row'), 'col'), parts along dimension 0
There are 2 independent parts, one for each index of `group`. A program takes and returns all parts, laid end to end along the dimension named above; an argument that names none is the same for every part. Nothing has to cross between parts.
All inputs are finite; a program needn't handle non-finite values.
Results may differ from a plain program's by a relative error of at most 0.014.
Values may be sent and summed in bfloat16 or wider, within the bound.
No kernel may reach another device: no remote copies, remote signals or barrier semaphores. Data moves between devices by JAX's collectives and lax.ppermute only.
A program may use at most 128 MiB of HBM per device.

v0:
```python
import jax
import jax.numpy as jnp
from jax import lax
from jax.sharding import PartitionSpec as P

BLOCK = 128


def broadcast(block, axis, owner):
    block = jnp.where(lax.axis_index(axis) == owner, block, jnp.zeros_like(block))
    return lax.psum(block, axis)


def layer_norm(values, gain):
    mean = jnp.mean(values, -1, keepdims=True)
    centred = values - mean
    spread = jnp.mean(centred * centred, -1, keepdims=True)
    return centred * lax.rsqrt(spread + 1e-05) * gain


def project(pair, tile_mask, w_in, w_gate, gain_in):
    normed = layer_norm(pair.astype(jnp.float32), gain_in).astype(jnp.bfloat16)
    hidden = jnp.dot(normed, w_in, preferred_element_type=jnp.float32)
    width = w_in.shape[1] // 4
    masked = tile_mask[..., None]
    left = (masked * jax.nn.sigmoid(hidden[..., width : 2 * width]) * hidden[..., :width]).astype(
        jnp.bfloat16
    )
    right = (
        masked * jax.nn.sigmoid(hidden[..., 3 * width :]) * hidden[..., 2 * width : 3 * width]
    ).astype(jnp.bfloat16)
    gate = jax.nn.sigmoid(jnp.dot(normed, w_gate, preferred_element_type=jnp.float32))
    return (left, right, gate)


def finish(pair, product, gate, w_out, gain_out):
    update = layer_norm(product, gain_out).astype(jnp.bfloat16)
    return (
        pair.astype(jnp.float32) + gate * jnp.dot(update, w_out, preferred_element_type=jnp.float32)
    ).astype(jnp.bfloat16)


def per_device(pair, chain, block_mask, w_in, w_gate, w_out, gain_in, gain_out):
    tile_rows = pair.shape[0]
    tile_cols = pair.shape[1]
    block_count = chain.shape[0]
    ratio = lax.axis_size("row") // lax.axis_size("col")
    row_index = lax.axis_index("row")
    col_index = lax.axis_index("col")
    same = chain[:, None] == chain[None, :]
    blocks = jnp.where(same | (block_mask == 1), 1.0, 0.0).astype(jnp.float32)
    labels = jnp.arange(block_count, dtype=jnp.int32)
    row_blocks = (row_index * tile_rows + jnp.arange(tile_rows, dtype=jnp.int32)) // BLOCK
    col_blocks = (col_index * tile_cols + jnp.arange(tile_cols, dtype=jnp.int32)) // BLOCK
    row_onehot = jnp.where(row_blocks[:, None] == labels[None, :], 1.0, 0.0).astype(jnp.float32)
    col_onehot = jnp.where(col_blocks[:, None] == labels[None, :], 1.0, 0.0).astype(jnp.float32)
    tile_mask = jnp.dot(jnp.dot(row_onehot, blocks), col_onehot.T)
    left, right, gate = project(pair, tile_mask, w_in[0], w_gate[0], gain_in[0])
    partial_terms = jnp.einsum(
        "ikc,jkc->ijc",
        left,
        lax.all_gather(right, "row", axis=0, tiled=True),
        preferred_element_type=jnp.float32,
    )
    product = lax.psum_scatter(
        partial_terms.astype(jnp.bfloat16), "col", scatter_dimension=1, tiled=True
    ).astype(jnp.float32)
    middle = finish(pair, product, gate, w_out[0], gain_out[0])
    left, right, gate = project(middle, tile_mask, w_in[1], w_gate[1], gain_in[1])
    left_cols = lax.all_gather(left, "row", axis=0, tiled=True)
    start_col = row_index % ratio * tile_rows
    left_slice = lax.dynamic_slice_in_dim(left_cols, start_col, tile_rows, 1)
    left_mine = broadcast(left_slice, "col", row_index // ratio)
    product = jnp.einsum(
        "kic,kjc->ijc",
        left_mine,
        lax.all_gather(right, "row", axis=0, tiled=True),
        preferred_element_type=jnp.float32,
    )
    return finish(middle, product, gate, w_out[1], gain_out[1])


def solution(mesh):
    return jax.shard_map(
        per_device,
        mesh=mesh,
        in_specs=(
            P(("group", "row"), "col", None),
            P("group"),
            P("group", None),
            P(),
            P(),
            P(),
            P(),
            P(),
        ),
        out_specs=P(("group", "row"), "col", None),
        check_vma=False,
    )
```

profile of v0, /device:TPU:16, one launch (start us, length us, event | category | flops | bytes accessed | tf_op | source)
XLA Modules:
  0.0 809.6 jit_solution(14772030526765191017)
XLA Ops:
  6.5 6.4 copy.76
  12.9 3.6 convert_reduce_fusion.1
  18.3 10.4 %fusion.47 = f32[128,128,256]{1,2,0:T(8,128)} fusion(bf16[128,128,128]{1,2,0:T(8,128)(2,1)} %copy.76, f32[128]{0:T(128)S(1)} %get-tuple-element.12, f32[128,128]{1,0:T(8,128)S(1)} %add_rsqrt_fusion.3, f32[128,128]{1,0:T(8,128)S(1)} %broadcast_multiply_fusion.3, bf16[2,128,256]{2,1,0:T(8,128)(2,1)S(1)} %copy-done.3), kind=kOutput, calls=%fused_computation.66 | convolution fusion | flops 1084227584 | bytes 21168640 | tf_op jit(solution)/shard_map/dot_general | solution.py:23
  29.2 8.5 %fusion.33 = (bf16[128,128,64]{1,2,0:T(8,128)(2,1)S(1)}, bf16[128,128,64]{1,2,0:T(8,128)(2,1)}) fusion(f32[128,128,256]{1,2,0:T(8,128)} %fusion.47, f32[128,128]{1,0:T(8,128)S(1)} %fusion.44), kind=kLoop, calls=%fused_computation.46 | loop fusion | flops 12582912 | bytes 21037056 | tf_op jit(solution)/shard_map/convert_element_type | solution.py:26
  38.0 148.8 %all-gather.4.cloned.1.call-done = bf16[512,128,64]{1,2,0:T(8,128)(2,1)} async-done(((bf16[128,128,64]{1,2,0:T(8,128)(2,1)}), bf16[512,128,64]{1,2,0:T(8,128)(2,1)}) %all-gather.4.cloned.1.call-update) | async-done | bytes 8388624 | tf_op jit(solution)/shard_map/all_gather | solution.py:62
  186.8 15.6 %convert_bitcast_fusion = bf16[128,512,64]{0,1,2:T(8,128)(2,1)} fusion(bf16[512,128,64]{1,2,0:T(8,128)(2,1)} %all-gather.4.cloned.1.call-done, bf16[128,128,64]{1,2,0:T(8,128)(2,1)S(1)} %get-tuple-element.7), kind=kOutput, calls=%fused_computation.23 | convolution fusion | flops 1077936128 | bytes 18874368 | tf_op jit(solution)/shard_map/ikc,jkc->ijc/dot_general | solution.py:59
  203.2 7.7 fusion.49
  210.9 63.3 %reduce-scatter.2.cloned.1.call-done = bf16[128,128,64]{0,1,2:T(8,128)(2,1)} async-done(((bf16[128,512,64]{0,1,2:T(8,128)(2,1)}), bf16[128,128,64]{0,1,2:T(8,128)(2,1)}) %reduce-scatter.2.cloned.1.call-update) | async-done | bytes 2097168 | tf_op jit(solution)/shard_map/reduce_scatter | solution.py:65
  276.5 2.2 fusion.20
  281.0 3.3 copy.90
  284.3 6.4 convert_reduce_fusion
  292.7 2.5 fusion.51
  295.2 3.8 fusion.28
  299.8 147.2 %all-gather.8.cloned.1.call-done = bf16[512,128,64]{1,2,0:T(8,128)(2,1)} async-done(((bf16[128,128,64]{1,2,0:T(8,128)(2,1)}), bf16[512,128,64]{1,2,0:T(8,128)(2,1)}) %all-gather.8.cloned.1.call-update) | async-done | bytes 8388624 | tf_op jit(solution)/shard_map/all_gather | solution.py:70
  447.0 23.6 %copy_select_fusion = bf16[512,128,64]{1,0,2:T(8,128)(2,1)} fusion(bf16[512,128,64]{1,2,0:T(8,128)(2,1)} %all-gather.8.cloned.1.call-done, pred[]{:T(512)S(6)} %eq.57), kind=kLoop, calls=%fused_computation.20 | loop fusion | flops 4194304 | bytes 16777216 | tf_op jit(solution)/shard_map/jit(_where)/select_n | solution.py:10
  470.6 6.9 fusion.53
  477.5 118.9 %all-gather.6.cloned.1.call-done = bf16[512,128,64]{1,2,0:T(8,128)(2,1)} async-done(((bf16[128,128,64]{1,2,0:T(8,128)(2,1)}), bf16[512,128,64]{1,2,0:T(8,128)(2,1)}) %all-gather.6.cloned.1.call-update) | async-done | bytes 8388624 | tf_op jit(solution)/shard_map/all_gather | solution.py:77
  596.4 155.3 %all-reduce.2.cloned.1.call-done = bf16[512,128,64]{1,0,2:T(8,128)(2,1)} async-done(((bf16[512,128,64]{1,0,2:T(8,128)(2,1)}), bf16[512,128,64]{1,0,2:T(8,128)(2,1)}) %all-reduce.2.cloned.1.call-update) | async-done | bytes 8388624 | tf_op jit(solution)/shard_map/psum | solution.py:11
  751.8 25.6 %bitcast_reduce_fusion = (f32[128,128]{0,1:T(8,128)S(1)}, f32[64,128,128]{2,1,0:T(8,128)}) fusion(bf16[512,128,64]{1,0,2:T(8,128)(2,1)} %all-reduce.2.cloned.1.call-done, bf16[512,128,64]{1,2,0:T(8,128)(2,1)} %all-gather.6.cloned.1.call-done), kind=kOutput, calls=%fused_computation.60 | convolution fusion | flops 1074774016 | bytes 21037056 | tf_op jit(solution)/shard_map/kic,kjc->ijc/dot_general | solution.py:74
  777.6 2.6 multiply_reduce_fusion
  780.5 2.8 multiply_convert_fusion
  783.3 3.0 copy.104
  786.2 10.3 %fusion.11 = bf16[128,128,128]{1,2,0:T(8,128)(2,1)} fusion(bf16[128,128,128]{1,2,0:T(8,128)(2,1)} %copy-done.1, f32[128,128,128]{1,2,0:T(8,128)} %fusion.53, bf16[128,128,64]{1,2,0:T(8,128)(2,1)} %copy.104, bf16[2,64,128]{2,1,0:T(8,128)(2,1)S(1)} %copy-done.7), kind=kOutput, calls=%fused_computation.17 | convolution fusion | flops 283115520 | bytes 18890752 | tf_op jit(solution)/shard_map/dot_general | solution.py:39
  796.5 6.4 copy.106
  (54 shorter events, 11.1 us)
Async XLA Ops:
  6.5 180.2 %all-gather.4.cloned.1.call-start = ((), (), s32[]{:S(2)}) async-start(), calls=%async_computation.1 | async-start | bytes 10485760 | tf_op jit(solution)/shard_map/all_gather | solution.py:62
  12.9 3.6 copy-start
  12.9 5.4 copy-start.5
  12.9 5.4 copy-start.3
  18.3 10.4 %copy-start.8 = (s32[4,4]{1,0:T(4,128)S(1)}, s32[4,4]{1,0:T(4,128)}, u32[]{:S(2)}) copy-start(s32[4,4]{1,0:T(4,128)} %param.10) | copy-start | bytes 196
  18.3 10.4 %copy-start.9 = (s32[4]{0:T(128)S(1)}, s32[4]{0:T(128)}, u32[]{:S(2)}) copy-start(s32[4]{0:T(128)} %param.9) | copy-start | bytes 52
  37.7 236.6 %reduce-scatter.2.cloned.1.call-start = ((), (), s32[]{:S(2)}) async-start(), calls=%async_computation.2 | async-start | bytes 10485760 | tf_op jit(solution)/shard_map/reduce_scatter | solution.py:65
  202.4 0.7 copy-start.6
  202.4 0.9 copy-start.4
  202.4 244.6 %all-gather.8.cloned.1.call-start = ((), (), s32[]{:S(2)}) async-start(), calls=%async_computation.4 | async-start | bytes 10485760 | tf_op jit(solution)/shard_map/all_gather | solution.py:70
  274.2 4.6 copy-start.2
  278.9 5.4 copy-start.7
  290.7 4.4 copy-start.1
  299.0 297.4 %all-gather.6.cloned.1.call-start = ((), (), s32[]{:S(2)}) async-start(), calls=%async_computation.3 | async-start | bytes 10485760 | tf_op jit(solution)/shard_map/all_gather | solution.py:77
  299.6 452.2 %all-reduce.2.cloned.1.call-start = ((), (), s32[]{:S(2)}) async-start(), calls=%async_computation.5 | async-start | bytes 16777216 | tf_op jit(solution)/shard_map/psum | solution.py:11
Sparse Core Ops, SparseCore 0:
  37.8 148.9 all-gather.3
  202.5 71.6 reduce-scatter.1
  299.1 147.8 all-gather.7
  448.5 147.8 all-gather.5
  598.9 152.8 all-reduce.1
where the time goes:
time: 817 us; the launch traced here: 810 us
  waiting for transfers between devices  634 us (78%)
  matrix products  85.8 us (11%)
  other arithmetic  54.9 us (7%)
  local copies, waits for them, and re-layouts  19.9 us (2%)
  between operations  13.6 us (2%)
    all_gather x2, waiting for transfers between devices, per_device(): lax.all_gather(right, 'row', axis=0, tiled=True)  268 us
    psum x1, waiting for transfers between devices, broadcast(): return lax.psum(block, axis)  155 us
    all_gather x1, waiting for transfers between devices, per_device(): left_cols = lax.all_gather(left, 'row', axis=0, tiled=True)  147 us
    reduce_scatter x1, waiting for transfers between devices, per_device(): lax.psum_scatter(partial_terms.astype(jnp.bfloat16), 'col', scatter_dimen...  63.3 us
    dot_general x1, matrix products, per_device(): jnp.einsum('kic,kjc->ijc', left_mine, lax.all_gather(right, 'row', axis=0...  25.6 us
    select_n x1, other arithmetic, broadcast(): jnp.where(lax.axis_index(axis) == owner, block, jnp.zeros_like(block))  23.6 us
    dot_general x2, matrix products, finish(): jnp.dot(update, w_out, preferred_element_type=jnp.float32)  16.7 us
  transfers between devices with their start and end apart: 5, of which 5 were waited for; matrix products, arithmetic and copies ran while one was open for 5% of the time, Pallas kernels for 0%

commit v1 on v0

--- a/solution.py
+++ b/solution.py
@@ -1,9 +1,17 @@
+import functools
+
 import jax
 import jax.numpy as jnp
 from jax import lax
+from jax.experimental import pallas as pl
+from jax.experimental.pallas import tpu as pltpu
 from jax.sharding import PartitionSpec as P
 
 BLOCK = 128
+EPS = 1e-05
+CHUNKS = 4
+STEP = 16
+VMEM = 48 * 1024 * 1024
 
 
 def broadcast(block, axis, owner):
@@ -15,7 +23,7 @@
     mean = jnp.mean(values, -1, keepdims=True)
     centred = values - mean
     spread = jnp.mean(centred * centred, -1, keepdims=True)
-    return centred * lax.rsqrt(spread + 1e-05) * gain
+    return centred * lax.rsqrt(spread + EPS) * gain
 
 
 def project(pair, tile_mask, w_in, w_gate, gain_in):
@@ -40,7 +48,7 @@
     ).astype(jnp.bfloat16)
 
 
-def per_device(pair, chain, block_mask, w_in, w_gate, w_out, gain_in, gain_out):
+def any_mesh(pair, chain, block_mask, w_in, w_gate, w_out, gain_in, gain_out):
     tile_rows = pair.shape[0]
     tile_cols = pair.shape[1]
     block_count = chain.shape[0]
@@ -80,9 +88,303 @@
     return finish(middle, product, gate, w_out[1], gain_out[1])
 
 
+NT = (((1,), (1,)), ((), ()))
+TN = (((0,), (0,)), ((), ()))
+SMEM_SPEC = pl.BlockSpec(memory_space=pltpu.SMEM)
+
+
+def dot(a, b, dims=(((1,), (0,)), ((), ()))):
+    return lax.dot_general(a, b, dims, preferred_element_type=jnp.float32)
+
+
+def norm_rows(rows, gain, mean_of):
+    values = rows.astype(jnp.float32)
+    centred = values - dot(rows, mean_of)
+    square = centred * centred
+    high = square.astype(jnp.bfloat16)
+    low = (square - high.astype(jnp.float32)).astype(jnp.bfloat16)
+    spread = dot(high, mean_of) + dot(low, mean_of)
+    return (centred * lax.rsqrt(spread + EPS) * gain).astype(jnp.bfloat16)
+
+
+def logistic(values):
+    return 0.5 * jnp.tanh(0.5 * values) + 0.5
+
+
+def project_rows(normed, mask, w_t, scratch, left_refs, right_refs, half):
+    hidden = dot(w_t, normed, NT)
+    width = w_t.shape[0] // 4
+    cols = normed.shape[0] // STEP
+    chunks = len(left_refs)
+    for side, refs in enumerate((left_refs, right_refs)):
+        values = hidden[2 * side * width : (2 * side + 1) * width]
+        gates = hidden[(2 * side + 1) * width : (2 * side + 2) * width]
+        kept = mask * logistic(gates) * values
+        for row in range(STEP):
+            scratch[side, pl.ds(row, width, stride=STEP), :] = kept[:, row * cols : (row + 1) * cols]
+        span = width // chunks
+        for n, ref in enumerate(refs):
+            block = scratch[side, n * span * STEP : (n + 1) * span * STEP, :]
+            ref[...] = block.astype(jnp.bfloat16).reshape(ref.shape)
+
+
+def project_kernel(chunks, mask_ref, pair_ref, w_t_ref, gain_ref, mean_ref, *rest):
+    left_refs, right_refs, scratch = rest[:chunks], rest[chunks : 2 * chunks], rest[2 * chunks]
+    rows = pair_ref[...].reshape(-1, pair_ref.shape[-1])
+    normed = norm_rows(rows, gain_ref[...], mean_ref[...])
+    project_rows(normed, mask_ref[0], w_t_ref[...], scratch, left_refs, right_refs, None)
+
+
+def gate_kernel(pair_ref, w_ref, gain_ref, mean_ref, out_ref):
+    rows = pair_ref[...].reshape(-1, pair_ref.shape[-1])
+    normed = norm_rows(rows, gain_ref[...], mean_ref[...])
+    gate = logistic(dot(normed, w_ref[...]))
+    out_ref[...] = gate.astype(out_ref.dtype).reshape(out_ref.shape)
+
+
+def finish_rows(pair_ref, gate_ref, product_refs, w_out_ref, gain_ref, scratch, out_ref):
+    width = w_out_ref.shape[0]
+    cols = pair_ref.shape[1]
+    parts = [ref[...].reshape(-1, STEP, cols) for ref in product_refs]
+    product = jnp.concatenate(parts, 0).astype(jnp.float32)
+    mean = jnp.sum(product, 0, keepdims=True) * (1.0 / width)
+    centred = product - mean
+    spread = jnp.sum(centred * centred, 0, keepdims=True) * (1.0 / width)
+    update = centred * lax.rsqrt(spread + EPS) * gain_ref[...]
+    scratch[...] = update.reshape(width * STEP, cols)
+    w_out = w_out_ref[...]
+    for row in range(STEP):
+        mine = scratch[pl.ds(row, width, stride=STEP), :].astype(jnp.bfloat16)
+        change = dot(mine, w_out, TN)
+        gate = gate_ref[row].astype(jnp.float32)
+        out_ref[row] = (pair_ref[row].astype(jnp.float32) + gate * change).astype(jnp.bfloat16)
+
+
+def finish_kernel(chunks, pair_ref, gate_ref, w_out_ref, gain_ref, *rest):
+    product_refs, out_ref, scratch = rest[:chunks], rest[chunks], rest[chunks + 1]
+    finish_rows(pair_ref, gate_ref, product_refs, w_out_ref, gain_ref, scratch, out_ref)
+
+
+def middle_kernel(
+    chunks, mask_ref, pair_ref, gate_ref, w_out_ref, gain_out_ref, w_t_ref, gain_in_ref, mean_ref, *rest
+):
+    product_refs, rest = rest[:chunks], rest[chunks:]
+    out_ref, rest = rest[0], rest[1:]
+    left_refs, right_refs = rest[:chunks], rest[chunks : 2 * chunks]
+    update_scratch, scratch = rest[2 * chunks :]
+    finish_rows(pair_ref, gate_ref, product_refs, w_out_ref, gain_out_ref, update_scratch, out_ref)
+    rows = out_ref[...].reshape(-1, out_ref.shape[-1])
+    normed = norm_rows(rows, gain_in_ref[...], mean_ref[...])
+    project_rows(normed, mask_ref[0], w_t_ref[...], scratch, left_refs, right_refs, None)
+
+
+def outgoing_kernel(row_ref, left, right, left_pair, right_pair, right_far, right_near, own_ref, pair_ref):
+    def wide(ref):
+        return jnp.concatenate([ref[k, 0] for k in range(ref.shape[0])], 1)
+
+    size = left.shape[-1]
+    lefts = jnp.concatenate([wide(left), wide(left_pair)], 0)
+    for step, ref in ((0, right), (1, right_pair), (3, right_near), (2, right_far)):
+        terms = dot(lefts, wide(ref), NT).astype(jnp.bfloat16)
+        place = row_ref[0] ^ step
+        own_ref[place, 0] = terms[:size]
+        pair_ref[place, 0] = terms[size:]
+
+
+def incoming_kernel(row_ref, left, right, left_pair, right_pair, *outs):
+    def wide(ref):
+        return jnp.concatenate([ref[j, 0] for j in range(ref.shape[0])], 1)
+
+    size = left.shape[-1]
+    rights = jnp.concatenate([wide(right), wide(right_pair)], 0)
+    for step, out in enumerate(outs):
+        place = row_ref[0] ^ step
+        lefts = jnp.concatenate([left[place, 0], left_pair[place, 0]], 0)
+        terms = dot(lefts, rights, TN).astype(jnp.bfloat16)
+        for j in range(out.shape[0]):
+            out[j, 0] = terms[:, j * size : (j + 1) * size]
+
+
+def params():
+    return pltpu.CompilerParams(vmem_limit_bytes=VMEM, dimension_semantics=("arbitrary",))
+
+
+def whole(array):
+    return pl.BlockSpec(array.shape, lambda *_: (0,) * array.ndim)
+
+
+def tile_spec(tile):
+    return pl.BlockSpec((STEP,) + tile.shape[1:], lambda r: (r, 0, 0))
+
+
+def chunk_spec(shape):
+    return pl.BlockSpec(shape[:2] + (STEP, shape[3]), lambda r: (0, 0, r, 0))
+
+
+def cost(flops, nbytes, special=0):
+    return pl.CostEstimate(flops=int(flops), bytes_accessed=int(nbytes), transcendentals=int(special))
+
+
+def project_call(pair, mask, w_t, gain, mean_of, chunk):
+    rows, cols, _ = pair.shape
+    width = w_t.shape[0] // 4
+    outs = [jax.ShapeDtypeStruct(chunk, jnp.bfloat16)] * (2 * CHUNKS)
+    result = pl.pallas_call(
+        functools.partial(project_kernel, CHUNKS),
+        grid=(rows // STEP,),
+        in_specs=[SMEM_SPEC, tile_spec(pair), whole(w_t), whole(gain), whole(mean_of)],
+        out_specs=[chunk_spec(chunk)] * (2 * CHUNKS),
+        out_shape=outs,
+        scratch_shapes=[pltpu.VMEM((2, width * STEP, cols), jnp.float32)],
+        compiler_params=params(),
+        cost_estimate=cost(2e9, 8 << 20, 4 << 20),
+        name="project",
+    )(mask, pair, w_t, gain, mean_of)
+    return result[:CHUNKS], result[CHUNKS:]
+
+
+def gate_call(pair, w, gain, mean_of):
+    return pl.pallas_call(
+        gate_kernel,
+        grid=(pair.shape[0] // STEP,),
+        in_specs=[tile_spec(pair), whole(w), whole(gain), whole(mean_of)],
+        out_specs=tile_spec(pair),
+        out_shape=jax.ShapeDtypeStruct(pair.shape, jnp.bfloat16),
+        compiler_params=params(),
+        cost_estimate=cost(2e9, 8 << 20, 4 << 20),
+        name="gate",
+    )(pair, w, gain, mean_of)
+
+
+def finish_call(pair, gate, products, w_out, gain):
+    rows, cols, _ = pair.shape
+    width = w_out.shape[0]
+    return pl.pallas_call(
+        functools.partial(finish_kernel, CHUNKS),
+        grid=(rows // STEP,),
+        in_specs=[tile_spec(pair), tile_spec(gate), whole(w_out), whole(gain)]
+        + [chunk_spec(p.shape) for p in products],
+        out_specs=tile_spec(pair),
+        out_shape=jax.ShapeDtypeStruct(pair.shape, pair.dtype),
+        scratch_shapes=[pltpu.VMEM((width * STEP, cols), jnp.float32)],
+        compiler_params=params(),
+        cost_estimate=cost(1e9, 14 << 20, 4 << 20),
+        name="finish",
+    )(pair, gate, w_out, gain, *products)
+
+
+def middle_call(mask, pair, gate, products, w_out, gain_out, w_t, gain_in, mean_of, chunk):
+    rows, cols, _ = pair.shape
+    width = w_out.shape[0]
+    outs = [jax.ShapeDtypeStruct(chunk, jnp.bfloat16)] * (2 * CHUNKS)
+    result = pl.pallas_call(
+        functools.partial(middle_kernel, CHUNKS),
+        grid=(rows // STEP,),
+        in_specs=[SMEM_SPEC, tile_spec(pair), tile_spec(gate), whole(w_out), whole(gain_out)]
+        + [whole(w_t), whole(gain_in), whole(mean_of)]
+        + [chunk_spec(p.shape) for p in products],
+        out_specs=[tile_spec(pair)] + [chunk_spec(chunk)] * (2 * CHUNKS),
+        out_shape=[jax.ShapeDtypeStruct(pair.shape, pair.dtype)] + outs,
+        scratch_shapes=[
+            pltpu.VMEM((width * STEP, cols), jnp.float32),
+            pltpu.VMEM((2, width * STEP, cols), jnp.float32),
+        ],
+        compiler_params=params(),
+        cost_estimate=cost(3e9, 18 << 20, 8 << 20),
+        name="middle",
+    )(mask, pair, gate, w_out, gain_out, w_t, gain_in, mean_of, *products)
+    return result[0], result[1 : 1 + CHUNKS], result[1 + CHUNKS :]
+
+
+def product_call(kernel, row, operands, count, name):
+    blocks, channels, size, _ = operands[0].shape
+    spec = pl.BlockSpec((blocks, 1, size, size), lambda c: (0, c, 0, 0))
+    return pl.pallas_call(
+        kernel,
+        grid=(channels,),
+        in_specs=[SMEM_SPEC] + [spec] * len(operands),
+        out_specs=[spec] * count,
+        out_shape=[jax.ShapeDtypeStruct(operands[0].shape, jnp.bfloat16)] * count,
+        compiler_params=params(),
+        cost_estimate=cost(
+            channels * 2 * 2 * (4 * size) ** 2 * size, operands[0].size * 2 * (len(operands) + count)
+        ),
+        name=name,
+    )(row, *operands)
+
+
+def hop(array, pairs, groups):
+    return lax.ppermute(array, "row", pairs)
+
+
+INWARD = [(0, 1), (3, 2)]
+OUTWARD = [(1, 0), (2, 3)]
+ACROSS = [(1, 2), (2, 1)]
+
+
+def exchange(array):
+    return lax.all_to_all(array, "col", 0, 0, tiled=True)
+
+
+def four_by_four(pair, chain, block_mask, w_in, w_gate, w_out, gain_in, gain_out):
+    size = pair.shape[0]
+    channels = pair.shape[2]
+    width = w_out.shape[1]
+    row = lax.axis_index("row")
+    col = lax.axis_index("col")
+    same = chain[row] == chain[col]
+    mask = jnp.where(same | (block_mask[row, col] == 1), 1.0, 0.0).astype(jnp.float32)[None]
+    row_arg = row.astype(jnp.int32)[None]
+    inner = (row == 1) | (row == 2)
+    w_t = jnp.swapaxes(w_in, 1, 2)
+    mean_of = jnp.full((channels, channels), 1.0 / channels, jnp.bfloat16)
+    gain_wide = jnp.broadcast_to(gain_out[:, :, None, None], gain_out.shape + (1, pair.shape[1]))
+    chunk = (4, width // (4 * CHUNKS), size, size)
+
+    def select(own, moved):
+        return jnp.where(inner, own, moved)
+
+    lefts, rights = project_call(pair, mask, w_t[0], gain_in[0][None], mean_of, chunk)
+    gate = gate_call(pair, w_gate[0], gain_in[0][None], mean_of)
+    products = []
+    for left, right in zip(lefts, rights):
+        right = exchange(right)
+        left = exchange(left)
+        right_pair = hop(right, INWARD, None)
+        right_near = hop(right, ACROSS, None)
+        left_pair = hop(left, INWARD, None)
+        right_far = hop(right_pair, ACROSS, None)
+        own, other = product_call(
+            outgoing_kernel,
+            row_arg,
+            (left, right, left_pair, right_pair, right_far, right_near),
+            2,
+            "outgoing",
+        )
+        products.append(exchange(select(own, hop(other, OUTWARD, None))))
+    middle, lefts, rights = middle_call(
+        mask, pair, gate, products, w_out[0], gain_wide[0], w_t[1], gain_in[1][None], mean_of, chunk
+    )
+    gate = gate_call(middle, w_gate[1], gain_in[1][None], mean_of)
+    products = []
+    for left, right in zip(lefts, rights):
+        right = exchange(right)
+        left = exchange(left)
+        right_pair = hop(right, INWARD, None)
+        left_pair = hop(left, INWARD, None)
+        own, other, far, near = product_call(
+            incoming_kernel, row_arg, (left, right, left_pair, right_pair), 4, "incoming"
+        )
+        other = other + hop(far, ACROSS, None)
+        own = own + hop(near, ACROSS, None)
+        products.append(exchange(select(own, hop(other, OUTWARD, None))))
+    return finish_call(middle, gate, products, w_out[1], gain_wide[1])
+
+
 def solution(mesh):
+    four = mesh.shape["row"] == 4 and mesh.shape["col"] == 4
     return jax.shard_map(
-        per_device,
+        four_by_four if four else any_mesh,
         mesh=mesh,
         in_specs=(
             P(("group", "row"), "col", None),

time: 817 us -> 487 us (0.60)
  waiting for transfers between devices: 634 us -> 120 us
  starting transfers between devices: 1.15 us -> 136 us
  blocking collectives: 0 us -> 103 us
  Pallas kernels: 0 us -> 90.4 us
  matrix products: 85.8 us -> 0 us
  other arithmetic: 54.9 us -> 16.3 us
  between operations: 13.6 us -> 2.81 us
    all_gather x3 -> x0, waiting for transfers between devices: 415 us -> none  [the longest x2 268 us: per_device(): lax.all_gather(right, 'row', axis=0, tiled=True)]
    psum x1 -> x0, waiting for transfers between devices: 155 us -> none  [broadcast(): return lax.psum(block, axis)]
    all_to_all x0 -> x9, blocking collectives: none -> 103 us  [exchange(): return lax.all_to_all(array, 'col', 0, 0, tiled=True)]
    pallas_call x0 -> x13, Pallas kernels: none -> 90.4 us  [the longest x8 33.7 us: product_call(): pl.pallas_call(kernel, grid=(channels,), in_specs=[SMEM_SPEC] + [spec] *...]
    dot_general x9 -> x0, matrix products: 85.8 us -> none  [the longest x1 25.6 us: per_device(): jnp.einsum('kic,kjc->ijc', left_mine, lax.all_gather(right, 'row', axis=0...]
    ppermute x0 -> x40, starting transfers between devices: none -> 82.8 us  [hop(): return lax.ppermute(array, 'row', pairs)]
    ppermute x0 -> x40, waiting for transfers between devices: none -> 82.7 us  [hop(): return lax.ppermute(array, 'row', pairs)]
    reduce_scatter x1 -> x0, waiting for transfers between devices: 63.3 us -> none  [per_device(): lax.psum_scatter(partial_terms.astype(jnp.bfloat16), 'col', scatter_dimen...]
  transfers between devices with their start and end apart: 5 -> 55, of which waited for: 5 -> 28; matrix products, arithmetic and copies ran while one was open for 5% -> 3% of each run, Pallas kernels for 0% -> 11%
where the time goes in v1:
time: 487 us; the launch traced here: 483 us
  starting transfers between devices  136 us (28%)
  waiting for transfers between devices  120 us (25%)
  blocking collectives  103 us (21%)
  Pallas kernels  90.4 us (19%)
  other arithmetic  16.3 us (3%)
  local copies, waits for them, and re-layouts  15 us (3%)
    all_to_all x9, blocking collectives, exchange(): return lax.all_to_all(array, 'col', 0, 0, tiled=True)  103 us
    ppermute x40, starting transfers between devices, hop(): return lax.ppermute(array, 'row', pairs)  82.8 us
    ppermute x40, waiting for transfers between devices, hop(): return lax.ppermute(array, 'row', pairs)  82.7 us
    all_to_all x15, starting transfers between devices, exchange(): return lax.all_to_all(array, 'col', 0, 0, tiled=True)  52.7 us
    all_to_all x15, waiting for transfers between devices, exchange(): return lax.all_to_all(array, 'col', 0, 0, tiled=True)  37.2 us
    pallas_call x8, Pallas kernels, product_call(): pl.pallas_call(kernel, grid=(channels,), in_specs=[SMEM_SPEC] + [spec] *...  33.7 us
    pallas_call x2, Pallas kernels, gate_call(): pl.pallas_call(gate_kernel, grid=(pair.shape[0] // STEP,), in_specs=[tile...  18.2 us
    pallas_call x1, Pallas kernels, middle_call(): pl.pallas_call(functools.partial(middle_kernel, CHUNKS), grid=(rows // ST...  16.3 us
  transfers between devices with their start and end apart: 55, of which 28 were waited for; matrix products, arithmetic and copies ran while one was open for 3% of the time, Pallas kernels for 11%

profile of v1, /device:TPU:16, one launch (start us, length us, event | category | flops | bytes accessed | tf_op | source)
XLA Modules:
  0.0 482.5 jit_solution(8666086427779980427)
XLA Ops:
  6.6 12.7 %project.1 = (bf16[4,4,128,128]{3,2,1,0:T(8,128)(2,1)S(1)}, bf16[4,4,128,128]{3,2,1,0:T(8,128)(2,1)S(1)}, bf16[4,4,128,128]{3,2,1,0:T(8,128)(2,1)S(1)}, bf16[4,4...) custom-call(f32[1]{0:T(128)} %bitcast.2.mask_ref, ...), custom_call_target="tpu_custom_call" | custom-call | flops 2000000000 | bytes 8388608 | tf_op jit(solution)/shard_map/project/pallas_call | solution.py:232
  19.3 11.4 %all_to_all.120.right = bf16[4,4,128,128]{3,2,1,0:T(8,128)(2,1)S(1)} all-to-all(bf16[4,4,128,128]{3,2,1,0:T(8,128)(2,1)S(1)} %get-tuple-element.59), channel_id=1, replica_groups=mesh['group'=2,'row'=4,'col'=4] {'col'}, dimensions={0} | all-to-all | bytes 1048576 | tf_op jit(solution)/shard_map/all_to_all | solution.py:326
  30.7 11.2 %all_to_all.121.left = bf16[4,4,128,128]{3,2,1,0:T(8,128)(2,1)S(1)} all-to-all(bf16[4,4,128,128]{3,2,1,0:T(8,128)(2,1)S(1)} %get-tuple-element.58), channel_id=1, replica_groups=mesh['group'=2,'row'=4,'col'=4] {'col'}, dimensions={0} | all-to-all | bytes 1048576 | tf_op jit(solution)/shard_map/all_to_all | solution.py:326
  41.9 11.2 %all_to_all.122.right = bf16[4,4,128,128]{3,2,1,0:T(8,128)(2,1)S(1)} all-to-all(bf16[4,4,128,128]{3,2,1,0:T(8,128)(2,1)S(1)} %get-tuple-element.55), channel_id=1, replica_groups=mesh['group'=2,'row'=4,'col'=4] {'col'}, dimensions={0} | all-to-all | bytes 1048576 | tf_op jit(solution)/shard_map/all_to_all | solution.py:326
  53.2 11.2 %all_to_all.123.left = bf16[4,4,128,128]{3,2,1,0:T(8,128)(2,1)S(1)} all-to-all(bf16[4,4,128,128]{3,2,1,0:T(8,128)(2,1)S(1)} %get-tuple-element.54), channel_id=1, replica_groups=mesh['group'=2,'row'=4,'col'=4] {'col'}, dimensions={0} | all-to-all | bytes 1048576 | tf_op jit(solution)/shard_map/all_to_all | solution.py:326
  88.7 7.2 %collective-permute-done.15.left_pair = bf16[4,4,128,128]{3,2,1,0:T(8,128)(2,1)} collective-permute-done((bf16[4,4,128,128]{3,2,1,0:T(8,128)(2,1)S(1)}, bf16[4,4,128,128]{3,2,1,0:T(8,128)(2,1)}, u32[]{:S(2)}, u32[]{:S(2)}) %collective-permute-start.15) | collective-permute-done | bytes 524320 | tf_op jit(solution)/shard_map/ppermute | solution.py:317
  100.6 6.4 %collective-permute-done.11.right_pair = bf16[4,4,128,128]{3,2,1,0:T(8,128)(2,1)} collective-permute-done((bf16[4,4,128,128]{3,2,1,0:T(8,128)(2,1)S(1)}, bf16[4,4,128,128]{3,2,1,0:T(8,128)(2,1)}, u32[]{:S(2)}, u32[]{:S(2)}) %collective-permute-start.11) | collective-permute-done | bytes 524320 | tf_op jit(solution)/shard_map/ppermute | solution.py:317
  110.7 7.6 %collective-permute-done.10.left_pair = bf16[4,4,128,128]{3,2,1,0:T(8,128)(2,1)} collective-permute-done((bf16[4,4,128,128]{3,2,1,0:T(8,128)(2,1)S(1)}, bf16[4,4,128,128]{3,2,1,0:T(8,128)(2,1)}, u32[]{:S(2)}, u32[]{:S(2)}) %collective-permute-start.10) | collective-permute-done | bytes 524320 | tf_op jit(solution)/shard_map/ppermute | solution.py:317
  145.8 5.7 %collective-permute-done.1.right_pair = bf16[4,4,128,128]{3,2,1,0:T(8,128)(2,1)} collective-permute-done((bf16[4,4,128,128]{3,2,1,0:T(8,128)(2,1)S(1)}, bf16[4,4,128,128]{3,2,1,0:T(8,128)(2,1)}, u32[]{:S(2)}, u32[]{:S(2)}) %collective-permute-start.1) | collective-permute-done | bytes 524320 | tf_op jit(solution)/shard_map/ppermute | solution.py:317
  191.2 6.4 %all-to-all-done.8.rest_2_ = bf16[4,4,128,128]{3,2,1,0:T(8,128)(2,1)S(1)} async-done(((bf16[4,4,128,128]{3,2,1,0:T(8,128)(2,1)}), bf16[4,4,128,128]{3,2,1,0:T(8,128)(2,1)S(1)}, u32[]{:S(2)}, u32[]{:S(2)}) %all-to-all-start.8) | async-done | bytes 524320 | tf_op jit(solution)/shard_map/all_to_all | solution.py:326
  202.2 7.7 %all-to-all-done.5.rest_1_ = bf16[4,4,128,128]{3,2,1,0:T(8,128)(2,1)S(1)} async-done(((bf16[4,4,128,128]{3,2,1,0:T(8,128)(2,1)}), bf16[4,4,128,128]{3,2,1,0:T(8,128)(2,1)S(1)}, u32[]{:S(2)}, u32[]{:S(2)}) %all-to-all-start.5) | async-done | bytes 524320 | tf_op jit(solution)/shard_map/all_to_all | solution.py:326
  213.3 9.1 %gate.2.gate_ref = bf16[128,128,128]{2,1,0:T(8,128)(2,1)S(1)} custom-call(bf16[128,128,128]{2,1,0:T(8,128)(2,1)} %pair_ref.5, bf16[128,128]{1,0:T(8,128)(2,1)S(1)} %get-tuple-element.90.w_ref, f32[1,128]{1,0:T(1,128)S(1)} %get-tuple-element.96.gain_ref, bf16[128,128]{1,0:T(8,128)(2,1)S(1)} %broadcast_in_dim.22.mean_ref), custom_call_target="tpu_custom_call" | custom-call | flops 2000000000 | bytes 8388608 | tf_op jit(solution)/shard_map/gate/pallas_call | solution.py:247
  224.6 16.3 %middle.1 = (bf16[128,128,128]{2,1,0:T(8,128)(2,1)}, bf16[4,4,128,128]{3,2,1,0:T(8,128)(2,1)S(1)}, bf16[4,4,128,128]{3,2,1,0:T(8,128)(2,1)S(1)}, bf16[4,4,128,12...) custom-call(f32[1]{0:T(128)} %bitcast.2.mask_ref, ...), custom_call_target="tpu_custom_call" | custom-call | flops 3000000000 | bytes 18874368 | tf_op jit(solution)/shard_map/middle/pallas_call | solution.py:280
  240.9 11.9 %all_to_all.124.left = bf16[4,4,128,128]{3,2,1,0:T(8,128)(2,1)S(1)} all-to-all(bf16[4,4,128,128]{3,2,1,0:T(8,128)(2,1)S(1)} %get-tuple-element.81), channel_id=1, replica_groups=mesh['group'=2,'row'=4,'col'=4] {'col'}, dimensions={0} | all-to-all | bytes 1048576 | tf_op jit(solution)/shard_map/all_to_all | solution.py:326
  252.8 11.9 %all_to_all.125.right = bf16[4,4,128,128]{3,2,1,0:T(8,128)(2,1)} all-to-all(bf16[4,4,128,128]{3,2,1,0:T(8,128)(2,1)S(1)} %get-tuple-element.82), channel_id=1, replica_groups=mesh['group'=2,'row'=4,'col'=4] {'col'}, dimensions={0} | all-to-all | bytes 1048576 | tf_op jit(solution)/shard_map/all_to_all | solution.py:326
  264.7 11.2 %all_to_all.126.left = bf16[4,4,128,128]{3,2,1,0:T(8,128)(2,1)S(1)} all-to-all(bf16[4,4,128,128]{3,2,1,0:T(8,128)(2,1)S(1)} %get-tuple-element.75), channel_id=1, replica_groups=mesh['group'=2,'row'=4,'col'=4] {'col'}, dimensions={0} | all-to-all | bytes 1048576 | tf_op jit(solution)/shard_map/all_to_all | solution.py:326
  276.0 11.2 %all_to_all.127.right = bf16[4,4,128,128]{3,2,1,0:T(8,128)(2,1)S(1)} all-to-all(bf16[4,4,128,128]{3,2,1,0:T(8,128)(2,1)S(1)} %get-tuple-element.76), channel_id=1, replica_groups=mesh['group'=2,'row'=4,'col'=4] {'col'}, dimensions={0} | all-to-all | bytes 1048576 | tf_op jit(solution)/shard_map/all_to_all | solution.py:326
  287.2 11.2 %all_to_all.128.left = bf16[4,4,128,128]{3,2,1,0:T(8,128)(2,1)S(1)} all-to-all(bf16[4,4,128,128]{3,2,1,0:T(8,128)(2,1)S(1)} %get-tuple-element.69), channel_id=1, replica_groups=mesh['group'=2,'row'=4,'col'=4] {'col'}, dimensions={0} | all-to-all | bytes 1048576 | tf_op jit(solution)/shard_map/all_to_all | solution.py:326
  342.4 9.9 %collective-permute-done.31.right_pair = bf16[4,4,128,128]{3,2,1,0:T(8,128)(2,1)} collective-permute-done((bf16[4,4,128,128]{3,2,1,0:T(8,128)(2,1)S(1)}, bf16[4,4,128,128]{3,2,1,0:T(8,128)(2,1)}, u32[]{:S(2)}, u32[]{:S(2)}) %collective-permute-start.31) | collective-permute-done | bytes 524320 | tf_op jit(solution)/shard_map/ppermute | solution.py:317
  357.7 5.9 %collective-permute-done.25.left_pair = bf16[4,4,128,128]{3,2,1,0:T(8,128)(2,1)} collective-permute-done((bf16[4,4,128,128]{3,2,1,0:T(8,128)(2,1)S(1)}, bf16[4,4,128,128]{3,2,1,0:T(8,128)(2,1)}, u32[]{:S(2)}, u32[]{:S(2)}) %collective-permute-start.25) | collective-permute-done | bytes 524320 | tf_op jit(solution)/shard_map/ppermute | solution.py:317
  366.2 8.6 %collective-permute-done.26.right_pair = bf16[4,4,128,128]{3,2,1,0:T(8,128)(2,1)} collective-permute-done((bf16[4,4,128,128]{3,2,1,0:T(8,128)(2,1)S(1)}, bf16[4,4,128,128]{3,2,1,0:T(8,128)(2,1)}, u32[]{:S(2)}, u32[]{:S(2)}) %collective-permute-start.26) | collective-permute-done | bytes 524320 | tf_op jit(solution)/shard_map/ppermute | solution.py:317
  387.4 9.3 %collective-permute-done.21.right_pair = bf16[4,4,128,128]{3,2,1,0:T(8,128)(2,1)S(1)} collective-permute-done((bf16[4,4,128,128]{3,2,1,0:T(8,128)(2,1)S(1)}, bf16[4,4,128,128]{3,2,1,0:T(8,128)(2,1)S(1)}, u32[]{:S(2)}, u32[]{:S(2)}) %collective-permute-start.21) | collective-permute-done | bytes 524320 | tf_op jit(solution)/shard_map/ppermute | solution.py:317
  461.9 9.1 %gate.3.gate_ref = bf16[128,128,128]{2,1,0:T(8,128)(2,1)S(1)} custom-call(bf16[128,128,128]{2,1,0:T(8,128)(2,1)} %get-tuple-element.62.pair_ref, bf16[128,128]{1,0:T(8,128)(2,1)S(1)} %get-tuple-element.89.w_ref, f32[1,128]{1,0:T(1,128)S(1)} %get-tuple-element.95.gain_in_ref.gain_ref, bf16[128,128]{1,0:T(8,128)(2,1)S(1)} %broadcast_in_dim.22.mean_ref), custom_call_target="tpu_custom_call" | custom-call | flops 2000000000 | bytes 8388608 | tf_op jit(solution)/shard_map/gate/pallas_call | solution.py:247
  473.1 9.4 %finish.1 = bf16[128,128,128]{2,1,0:T(8,128)(2,1)} custom-call(bf16[128,128,128]{2,1,0:T(8,128)(2,1)} %get-tuple-element.62.pair_ref, bf16[128,128,128]{2,1,0:T(8,128)(2,1)} %copy-done, bf16[64,128]{1,0:T(8,128)(2,1)S(1)} %get-tuple-element.91.w_out_ref, f32[64,1,128]{2,1,0:T(1,128)S(1)} %broadcast_in_dim.27.gain_ref, ...), custom_call_target="tpu_custom_call" | custom-call | flops 1000000000 | bytes 14680064 | tf_op jit(solution)/shard_map/finish/pallas_call | solution.py:262
  (187 shorter events, 245.8 us)
Async XLA Ops:
  81.5 28.0 %collective-permute-start.13 = (bf16[4,4,128,128]{3,2,1,0:T(8,128)(2,1)S(1)}, bf16[4,4,128,128]{3,2,1,0:T(8,128)(2,1)}, u32[]{:S(2)}, u32[]{:S(2)}) collective-permute-start(bf16[4,4,128,128]{3,2,1,0:T(8,128)(2,1)S(1)} %all_to_all.122.right), channel_id=1, source_target_pairs={{4,8},{8,4},{5,9},{9,5},{6,10},{10,6},{7,11},{11,7},{20,24},{24,20... | collective-permute-start | bytes 1572872 | tf_op jit(solution)/shard_map/ppermute | solution.py:317
  84.6 33.7 %collective-permute-start.10 = (bf16[4,4,128,128]{3,2,1,0:T(8,128)(2,1)S(1)}, bf16[4,4,128,128]{3,2,1,0:T(8,128)(2,1)}, u32[]{:S(2)}, u32[]{:S(2)}) collective-permute-start(bf16[4,4,128,128]{3,2,1,0:T(8,128)(2,1)S(1)} %all_to_all.123.left), channel_id=1, source_target_pairs={{0,4},{12,8},{1,5},{13,9},{2,6},{14,10},{3,7},{15,11},{16,20},{28,... | collective-permute-start | bytes 1572872 | tf_op jit(solution)/shard_map/ppermute | solution.py:317
  85.9 33.7 %collective-permute-start.17 = (bf16[4,4,128,128]{3,2,1,0:T(8,128)(2,1)}, bf16[4,4,128,128]{3,2,1,0:T(8,128)(2,1)}, u32[]{:S(2)}, u32[]{:S(2)}) collective-permute-start(bf16[4,4,128,128]{3,2,1,0:T(8,128)(2,1)} %collective-permute-done.16.right_pair), channel_id=1, source_target_pairs={{4,8},{8,4},{5,9},{9,5},{6,10},{10,6},{7,11},{11,7},{20,24},{24,20... | collective-permute-start | bytes 1572872 | tf_op jit(solution)/shard_map/ppermute | solution.py:317
  95.8 33.7 %collective-permute-start.6 = (bf16[4,4,128,128]{3,2,1,0:T(8,128)(2,1)S(1)}, bf16[4,4,128,128]{3,2,1,0:T(8,128)(2,1)}, u32[]{:S(2)}, u32[]{:S(2)}) collective-permute-start(bf16[4,4,128,128]{3,2,1,0:T(8,128)(2,1)S(1)} %all-to-all-done.4.right), channel_id=1, source_target_pairs={{0,4},{12,8},{1,5},{13,9},{2,6},{14,10},{3,7},{15,11},{16,20},{28,... | collective-permute-start | bytes 1572872 | tf_op jit(solution)/shard_map/ppermute | solution.py:317
  107.1 30.0 %collective-permute-start.8 = (bf16[4,4,128,128]{3,2,1,0:T(8,128)(2,1)S(1)}, bf16[4,4,128,128]{3,2,1,0:T(8,128)(2,1)}, u32[]{:S(2)}, u32[]{:S(2)}) collective-permute-start(bf16[4,4,128,128]{3,2,1,0:T(8,128)(2,1)S(1)} %all-to-all-done.4.right), channel_id=1, source_target_pairs={{4,8},{8,4},{5,9},{9,5},{6,10},{10,6},{7,11},{11,7},{20,24},{24,20... | collective-permute-start | bytes 1572872 | tf_op jit(solution)/shard_map/ppermute | solution.py:317
  109.4 31.3 %collective-permute-start.5 = (bf16[4,4,128,128]{3,2,1,0:T(8,128)(2,1)S(1)}, bf16[4,4,128,128]{3,2,1,0:T(8,128)(2,1)}, u32[]{:S(2)}, u32[]{:S(2)}) collective-permute-start(bf16[4,4,128,128]{3,2,1,0:T(8,128)(2,1)S(1)} %all-to-all-done.3.left), channel_id=1, source_target_pairs={{0,4},{12,8},{1,5},{13,9},{2,6},{14,10},{3,7},{15,11},{16,20},{28,... | collective-permute-start | bytes 1572872 | tf_op jit(solution)/shard_map/ppermute | solution.py:317
  118.3 33.3 %collective-permute-start.1 = (bf16[4,4,128,128]{3,2,1,0:T(8,128)(2,1)S(1)}, bf16[4,4,128,128]{3,2,1,0:T(8,128)(2,1)}, u32[]{:S(2)}, u32[]{:S(2)}) collective-permute-start(bf16[4,4,128,128]{3,2,1,0:T(8,128)(2,1)S(1)} %all-to-all-done.1.right), channel_id=1, source_target_pairs={{0,4},{12,8},{1,5},{13,9},{2,6},{14,10},{3,7},{15,11},{16,20},{28,... | collective-permute-start | bytes 1572872 | tf_op jit(solution)/shard_map/ppermute | solution.py:317
  119.6 33.3 %collective-permute-start.12 = (bf16[4,4,128,128]{3,2,1,0:T(8,128)(2,1)}, bf16[4,4,128,128]{3,2,1,0:T(8,128)(2,1)}, u32[]{:S(2)}, u32[]{:S(2)}) collective-permute-start(bf16[4,4,128,128]{3,2,1,0:T(8,128)(2,1)} %collective-permute-done.11.right_pair), channel_id=1, source_target_pairs={{4,8},{8,4},{5,9},{9,5},{6,10},{10,6},{7,11},{11,7},{20,24},{24,20... | collective-permute-start | bytes 1572872 | tf_op jit(solution)/shard_map/ppermute | solution.py:317
  129.6 31.0 %collective-permute-start.19 = (bf16[4,4,128,128]{3,2,1,0:T(8,128)(2,1)}, bf16[4,4,128,128]{3,2,1,0:T(8,128)(2,1)}, u32[]{:S(2)}, u32[]{:S(2)}) collective-permute-start(bf16[4,4,128,128]{3,2,1,0:T(8,128)(2,1)} %get-tuple-element.61), channel_id=1, source_target_pairs={{4,0},{8,12},{5,1},{9,13},{6,2},{10,14},{7,3},{11,15},{20,16},{24,... | collective-permute-start | bytes 1572872 | tf_op jit(solution)/shard_map/ppermute | solution.py:317
  137.0 34.8 %collective-permute-start.7 = (bf16[4,4,128,128]{3,2,1,0:T(8,128)(2,1)}, bf16[4,4,128,128]{3,2,1,0:T(8,128)(2,1)}, u32[]{:S(2)}, u32[]{:S(2)}) collective-permute-start(bf16[4,4,128,128]{3,2,1,0:T(8,128)(2,1)} %collective-permute-done.6.right_pair), channel_id=1, source_target_pairs={{4,8},{8,4},{5,9},{9,5},{6,10},{10,6},{7,11},{11,7},{20,24},{24,20... | collective-permute-start | bytes 1572872 | tf_op jit(solution)/shard_map/ppermute | solution.py:317
  140.8 37.8 %collective-permute-start.3 = (bf16[4,4,128,128]{3,2,1,0:T(8,128)(2,1)S(1)}, bf16[4,4,128,128]{3,2,1,0:T(8,128)(2,1)}, u32[]{:S(2)}, u32[]{:S(2)}) collective-permute-start(bf16[4,4,128,128]{3,2,1,0:T(8,128)(2,1)S(1)} %all-to-all-done.1.right), channel_id=1, source_target_pairs={{4,8},{8,4},{5,9},{9,5},{6,10},{10,6},{7,11},{11,7},{20,24},{24,20... | collective-permute-start | bytes 1572872 | tf_op jit(solution)/shard_map/ppermute | solution.py:317
  304.5 36.6 %collective-permute-start.30 = (bf16[4,4,128,128]{3,2,1,0:T(8,128)(2,1)S(1)}, bf16[4,4,128,128]{3,2,1,0:T(8,128)(2,1)}, u32[]{:S(2)}, u32[]{:S(2)}) collective-permute-start(bf16[4,4,128,128]{3,2,1,0:T(8,128)(2,1)S(1)} %all_to_all.126.left), channel_id=1, source_target_pairs={{0,4},{12,8},{1,5},{13,9},{2,6},{14,10},{3,7},{15,11},{16,20},{28,... | collective-permute-start | bytes 1572872 | tf_op jit(solution)/shard_map/ppermute | solution.py:317
  314.2 38.1 %collective-permute-start.31 = (bf16[4,4,128,128]{3,2,1,0:T(8,128)(2,1)S(1)}, bf16[4,4,128,128]{3,2,1,0:T(8,128)(2,1)}, u32[]{:S(2)}, u32[]{:S(2)}) collective-permute-start(bf16[4,4,128,128]{3,2,1,0:T(8,128)(2,1)S(1)} %all_to_all.127.right), channel_id=1, source_target_pairs={{0,4},{12,8},{1,5},{13,9},{2,6},{14,10},{3,7},{15,11},{16,20},{28,... | collective-permute-start | bytes 1572872 | tf_op jit(solution)/shard_map/ppermute | solution.py:317
  315.5 48.1 %collective-permute-start.25 = (bf16[4,4,128,128]{3,2,1,0:T(8,128)(2,1)S(1)}, bf16[4,4,128,128]{3,2,1,0:T(8,128)(2,1)}, u32[]{:S(2)}, u32[]{:S(2)}) collective-permute-start(bf16[4,4,128,128]{3,2,1,0:T(8,128)(2,1)S(1)} %all_to_all.128.left), channel_id=1, source_target_pairs={{0,4},{12,8},{1,5},{13,9},{2,6},{14,10},{3,7},{15,11},{16,20},{28,... | collective-permute-start | bytes 1572872 | tf_op jit(solution)/shard_map/ppermute | solution.py:317
  318.6 56.2 %collective-permute-start.26 = (bf16[4,4,128,128]{3,2,1,0:T(8,128)(2,1)S(1)}, bf16[4,4,128,128]{3,2,1,0:T(8,128)(2,1)}, u32[]{:S(2)}, u32[]{:S(2)}) collective-permute-start(bf16[4,4,128,128]{3,2,1,0:T(8,128)(2,1)S(1)} %all-to-all-done.16.right), channel_id=1, source_target_pairs={{0,4},{12,8},{1,5},{13,9},{2,6},{14,10},{3,7},{15,11},{16,20},{28,... | collective-permute-start | bytes 1572872 | tf_op jit(solution)/shard_map/ppermute | solution.py:317
  337.4 43.7 %collective-permute-start.38 = (bf16[4,4,128,128]{3,2,1,0:T(8,128)(2,1)}, bf16[4,4,128,128]{3,2,1,0:T(8,128)(2,1)}, u32[]{:S(2)}, u32[]{:S(2)}) collective-permute-start(bf16[4,4,128,128]{3,2,1,0:T(8,128)(2,1)} %get-tuple-element.86), channel_id=1, source_target_pairs={{4,8},{8,4},{5,9},{9,5},{6,10},{10,6},{7,11},{11,7},{20,24},{24,20... | collective-permute-start | bytes 1572872 | tf_op jit(solution)/shard_map/ppermute | solution.py:317
  341.1 44.9 %collective-permute-start.20 = (bf16[4,4,128,128]{3,2,1,0:T(8,128)(2,1)S(1)}, bf16[4,4,128,128]{3,2,1,0:T(8,128)(2,1)}, u32[]{:S(2)}, u32[]{:S(2)}) collective-permute-start(bf16[4,4,128,128]{3,2,1,0:T(8,128)(2,1)S(1)} %all-to-all-done.12.left), channel_id=1, source_target_pairs={{0,4},{12,8},{1,5},{13,9},{2,6},{14,10},{3,7},{15,11},{16,20},{28,... | collective-permute-start | bytes 1572872 | tf_op jit(solution)/shard_map/ppermute | solution.py:317
  352.3 44.4 %collective-permute-start.21 = (bf16[4,4,128,128]{3,2,1,0:T(8,128)(2,1)S(1)}, bf16[4,4,128,128]{3,2,1,0:T(8,128)(2,1)S(1)}, u32[]{:S(2)}, u32[]{:S(2)}) collective-permute-start(bf16[4,4,128,128]{3,2,1,0:T(8,128)(2,1)S(1)} %all-to-all-done.13.right), channel_id=1, source_target_pairs={{0,4},{12,8},{1,5},{13,9},{2,6},{14,10},{3,7},{15,11},{16,20},{28,... | collective-permute-start | bytes 1572872 | tf_op jit(solution)/shard_map/ppermute | solution.py:317
  363.6 40.3 %collective-permute-start.33 = (bf16[4,4,128,128]{3,2,1,0:T(8,128)(2,1)S(1)}, bf16[4,4,128,128]{3,2,1,0:T(8,128)(2,1)S(1)}, u32[]{:S(2)}, u32[]{:S(2)}) collective-permute-start(bf16[4,4,128,128]{3,2,1,0:T(8,128)(2,1)S(1)} %get-tuple-element.80), channel_id=1, source_target_pairs={{4,8},{8,4},{5,9},{9,5},{6,10},{10,6},{7,11},{11,7},{20,24},{24,20... | collective-permute-start | bytes 1572872 | tf_op jit(solution)/shard_map/ppermute | solution.py:317
  378.8 29.5 %collective-permute-start.28 = (bf16[4,4,128,128]{3,2,1,0:T(8,128)(2,1)S(1)}, bf16[4,4,128,128]{3,2,1,0:T(8,128)(2,1)S(1)}, u32[]{:S(2)}, u32[]{:S(2)}) collective-permute-start(bf16[4,4,128,128]{3,2,1,0:T(8,128)(2,1)S(1)} %get-tuple-element.74), channel_id=1, source_target_pairs={{4,8},{8,4},{5,9},{9,5},{6,10},{10,6},{7,11},{11,7},{20,24},{24,20... | collective-permute-start | bytes 1572872 | tf_op jit(solution)/shard_map/ppermute | solution.py:317
  381.2 30.2 %collective-permute-start.37 = (bf16[4,4,128,128]{3,2,1,0:T(8,128)(2,1)S(1)}, bf16[4,4,128,128]{3,2,1,0:T(8,128)(2,1)S(1)}, u32[]{:S(2)}, u32[]{:S(2)}) collective-permute-start(bf16[4,4,128,128]{3,2,1,0:T(8,128)(2,1)S(1)} %copy-done.24), channel_id=1, source_target_pairs={{4,8},{8,4},{5,9},{9,5},{6,10},{10,6},{7,11},{11,7},{20,24},{24,20... | collective-permute-start | bytes 1572872 | tf_op jit(solution)/shard_map/ppermute | solution.py:317
  386.1 27.7 %collective-permute-start.39 = (bf16[4,4,128,128]{3,2,1,0:T(8,128)(2,1)S(1)}, bf16[4,4,128,128]{3,2,1,0:T(8,128)(2,1)S(1)}, u32[]{:S(2)}, u32[]{:S(2)}) collective-permute-start(bf16[4,4,128,128]{3,2,1,0:T(8,128)(2,1)S(1)} %add.41), channel_id=1, source_target_pairs={{4,0},{8,12},{5,1},{9,13},{6,2},{10,14},{7,3},{11,15},{20,16},{24,... | collective-permute-start | bytes 1572872 | tf_op jit(solution)/shard_map/ppermute | solution.py:317
  411.4 29.6 %collective-permute-start.27 = (bf16[4,4,128,128]{3,2,1,0:T(8,128)(2,1)}, bf16[4,4,128,128]{3,2,1,0:T(8,128)(2,1)}, u32[]{:S(2)}, u32[]{:S(2)}) collective-permute-start(bf16[4,4,128,128]{3,2,1,0:T(8,128)(2,1)} %get-tuple-element.72), channel_id=1, source_target_pairs={{4,8},{8,4},{5,9},{9,5},{6,10},{10,6},{7,11},{11,7},{20,24},{24,20... | collective-permute-start | bytes 1572872 | tf_op jit(solution)/shard_map/ppermute | solution.py:317
  420.3 30.7 %collective-permute-start.22 = (bf16[4,4,128,128]{3,2,1,0:T(8,128)(2,1)S(1)}, bf16[4,4,128,128]{3,2,1,0:T(8,128)(2,1)}, u32[]{:S(2)}, u32[]{:S(2)}) collective-permute-start(bf16[4,4,128,128]{3,2,1,0:T(8,128)(2,1)S(1)} %copy-done.22), channel_id=1, source_target_pairs={{4,8},{8,4},{5,9},{9,5},{6,10},{10,6},{7,11},{11,7},{20,24},{24,20... | collective-permute-start | bytes 1572872 | tf_op jit(solution)/shard_map/ppermute | solution.py:317
  (59 other events, 1252.3 us)

commit v2 on v0

--- a/solution.py
+++ b/solution.py
@@ -1,9 +1,17 @@
+import functools
+
 import jax
 import jax.numpy as jnp
 from jax import lax
+from jax.experimental import pallas as pl
+from jax.experimental.pallas import tpu as pltpu
 from jax.sharding import PartitionSpec as P
 
 BLOCK = 128
+EPS = 1e-05
+SIZES = (12, 12, 8)
+STEP = 16
+VMEM = 48 * 1024 * 1024
 
 
 def broadcast(block, axis, owner):
@@ -15,7 +23,7 @@
     mean = jnp.mean(values, -1, keepdims=True)
     centred = values - mean
     spread = jnp.mean(centred * centred, -1, keepdims=True)
-    return centred * lax.rsqrt(spread + 1e-05) * gain
+    return centred * lax.rsqrt(spread + EPS) * gain
 
 
 def project(pair, tile_mask, w_in, w_gate, gain_in):
@@ -40,7 +48,7 @@
     ).astype(jnp.bfloat16)
 
 
-def per_device(pair, chain, block_mask, w_in, w_gate, w_out, gain_in, gain_out):
+def any_mesh(pair, chain, block_mask, w_in, w_gate, w_out, gain_in, gain_out):
     tile_rows = pair.shape[0]
     tile_cols = pair.shape[1]
     block_count = chain.shape[0]
@@ -80,9 +88,368 @@
     return finish(middle, product, gate, w_out[1], gain_out[1])
 
 
+NN = (((1,), (0,)), ((), ()))
+NT = (((1,), (1,)), ((), ()))
+TN = (((0,), (0,)), ((), ()))
+SMEM_SPEC = pl.BlockSpec(memory_space=pltpu.SMEM)
+COUNT = len(SIZES)
+
+
+def dot(a, b, dims=NN):
+    return lax.dot_general(a, b, dims, preferred_element_type=jnp.float32)
+
+
+def norm_rows(rows, gain):
+    channels = rows.shape[-1]
+    mean_of = jnp.full((channels, channels), 1.0 / channels, jnp.bfloat16)
+    values = rows.astype(jnp.float32)
+    centred = values - dot(rows, mean_of)
+    square = centred * centred
+    high = square.astype(jnp.bfloat16)
+    low = (square - high.astype(jnp.float32)).astype(jnp.bfloat16)
+    spread = dot(high, mean_of) + dot(low, mean_of)
+    return (centred * lax.rsqrt(spread + EPS) * gain).astype(jnp.bfloat16)
+
+
+def logistic(values):
+    return 0.5 * jnp.tanh(0.5 * values) + 0.5
+
+
+def tile_mask(chain_ref, block_mask_ref):
+    row, col = lax.axis_index("row"), lax.axis_index("col")
+    seen = (chain_ref[row] == chain_ref[col]) | (block_mask_ref[row, col] == 1)
+    return jnp.where(seen, 1.0, 0.0).astype(jnp.float32)
+
+
+def turn_weights(w_ref, w_t):
+    @pl.when(pl.program_id(0) == 0)
+    def _():
+        w_t[...] = w_ref[0].T
+
+
+def project_rows(normed, mask, w_t, scratch, outs):
+    hidden = dot(w_t[...], normed, NT)
+    width = w_t.shape[0] // 4
+    half = width // 2
+    cols = normed.shape[0] // STEP
+    x = lax.axis_index("col") // 2
+    for side in range(2):
+        values = hidden[2 * side * width : (2 * side + 1) * width]
+        gates = hidden[(2 * side + 1) * width : (2 * side + 2) * width]
+        kept = mask * logistic(gates) * values
+        for row in range(STEP):
+            scratch[side, pl.ds(row, width, stride=STEP), :] = kept[:, row * cols : (row + 1) * cols]
+        for other in range(2):
+            start = (x if other == 0 else 1 - x) * half
+            for n, size in enumerate(SIZES):
+                first = pl.multiple_of((start + sum(SIZES[:n])) * STEP, 8)
+                block = scratch[side, pl.ds(first, size * STEP), :]
+                ref = outs[(2 * side + other) * COUNT + n]
+                ref[...] = block.astype(jnp.bfloat16).reshape(ref.shape)
+
+
+def project_kernel(chain_ref, block_mask_ref, pair_ref, w_ref, gain_ref, *rest):
+    outs, (w_t, scratch) = rest[: 4 * COUNT], rest[4 * COUNT :]
+    turn_weights(w_ref, w_t)
+    rows = pair_ref[...].reshape(-1, pair_ref.shape[-1])
+    normed = norm_rows(rows, gain_ref[...])
+    project_rows(normed, tile_mask(chain_ref, block_mask_ref), w_t, scratch, outs)
+
+
+def gate_kernel(pair_ref, w_ref, gain_ref, out_ref):
+    rows = pair_ref[...].reshape(-1, pair_ref.shape[-1])
+    normed = norm_rows(rows, gain_ref[...])
+    gate = logistic(dot(normed, w_ref[0]))
+    out_ref[...] = gate.astype(out_ref.dtype).reshape(out_ref.shape)
+
+
+def finish_rows(pair_ref, gate_ref, product_refs, w_out_ref, gain_ref, scratch, out_ref):
+    width = w_out_ref.shape[1]
+    half = width // 2
+    cols = pair_ref.shape[1]
+    x = lax.axis_index("col") // 2
+    mine, others = pl.multiple_of(x * half, half), pl.multiple_of((1 - x) * half, half)
+    w_out = jnp.concatenate([w_out_ref[0, pl.ds(mine, half)], w_out_ref[0, pl.ds(others, half)]], 0)
+    gain = jnp.concatenate([gain_ref[pl.ds(mine, half)], gain_ref[pl.ds(others, half)]], 0)
+    product = jnp.concatenate([ref[...] for ref in product_refs], 0).astype(jnp.float32)
+    mean = jnp.sum(product, 0, keepdims=True) * (1.0 / width)
+    centred = product - mean
+    spread = jnp.sum(centred * centred, 0, keepdims=True) * (1.0 / width)
+    update = centred * lax.rsqrt(spread + EPS) * gain
+    scratch[...] = update.reshape(width * STEP, cols)
+    for row in range(STEP):
+        change = dot(scratch[pl.ds(row, width, stride=STEP), :].astype(jnp.bfloat16), w_out, TN)
+        gate = gate_ref[row].astype(jnp.float32)
+        out_ref[row] = (pair_ref[row].astype(jnp.float32) + gate * change).astype(jnp.bfloat16)
+
+
+def finish_kernel(pair_ref, gate_ref, w_out_ref, gain_ref, *rest):
+    product_refs, (out_ref, scratch) = rest[: 2 * COUNT], rest[2 * COUNT :]
+    finish_rows(pair_ref, gate_ref, product_refs, w_out_ref, gain_ref, scratch, out_ref)
+
+
+def middle_kernel(
+    chain_ref, block_mask_ref, pair_ref, gate_ref, w_out_ref, gain_out_ref, w_ref, gain_in_ref, *rest
+):
+    product_refs, rest = rest[: 2 * COUNT], rest[2 * COUNT :]
+    out_ref, outs, (update, w_t, scratch) = rest[0], rest[1 : 1 + 4 * COUNT], rest[1 + 4 * COUNT :]
+    turn_weights(w_ref, w_t)
+    finish_rows(pair_ref, gate_ref, product_refs, w_out_ref, gain_out_ref, update, out_ref)
+    rows = out_ref[...].reshape(-1, out_ref.shape[-1])
+    normed = norm_rows(rows, gain_in_ref[...])
+    project_rows(normed, tile_mask(chain_ref, block_mask_ref), w_t, scratch, outs)
+
+
+def outgoing_kernel(
+    l_own, l_x, l_pair, l_pair_x, r_own, r_x, r_pair, r_pair_x, r_far, r_far_x, r_near, r_near_x, *rest
+):
+    own, pair, sent, rights = rest
+    size = l_own.shape[-1]
+    rights[0] = jnp.concatenate([r_own[0], r_x[0]], 1)
+    rights[1] = jnp.concatenate([r_pair[0], r_pair_x[0]], 1)
+    rights[2] = jnp.concatenate([r_far[0], r_far_x[0]], 1)
+    rights[3] = jnp.concatenate([r_near[0], r_near_x[0]], 1)
+    lefts = jnp.concatenate(
+        [jnp.concatenate([l_own[0], l_x[0]], 1), jnp.concatenate([l_pair[0], l_pair_x[0]], 1)], 0
+    )
+    here = lax.axis_index("row") ^ lax.axis_index("col")
+    for place in range(4):
+        terms = dot(lefts, rights[here ^ place], NT).astype(jnp.bfloat16)
+        if place % 2:
+            sent[0, place // 2, 0] = terms[:size]
+            sent[1, place // 2, 0] = terms[size:]
+        else:
+            own[place // 2, 0] = terms[:size]
+            pair[place // 2, 0] = terms[size:]
+
+
+def incoming_kernel(
+    l_own, l_x, l_core, l_core_x, l_pair, l_pair_x, l_pair_core, l_pair_core_x, r_own, r_x, r_pair, r_pair_x, *rest
+):
+    *outs, lefts = rest
+    size = l_own.shape[-1]
+    lefts[0] = jnp.concatenate([l_own[0], l_pair[0]], 0)
+    lefts[1] = jnp.concatenate([l_core[0], l_pair_core[0]], 0)
+    lefts[2] = jnp.concatenate([l_x[0], l_pair_x[0]], 0)
+    lefts[3] = jnp.concatenate([l_core_x[0], l_pair_core_x[0]], 0)
+    rights = jnp.concatenate(
+        [jnp.concatenate([r_own[0], r_x[0]], 1), jnp.concatenate([r_pair[0], r_pair_x[0]], 1)], 0
+    )
+    here = lax.axis_index("row") ^ lax.axis_index("col")
+    for place, out in enumerate(outs):
+        terms = dot(lefts[here ^ place], rights, TN).astype(jnp.bfloat16)
+        out[0, 0] = terms[:, :size]
+        out[1, 0] = terms[:, size:]
+
+
+def params():
+    return pltpu.CompilerParams(vmem_limit_bytes=VMEM, dimension_semantics=("arbitrary",))
+
+
+def part(array, index):
+    return pl.BlockSpec((1,) + array.shape[1:], lambda *_: (index,) + (0,) * (array.ndim - 1))
+
+
+def whole(array):
+    return pl.BlockSpec(array.shape, lambda *_: (0,) * array.ndim)
+
+
+def tile_spec(tile):
+    return pl.BlockSpec((STEP,) + tile.shape[1:], lambda r: (r, 0, 0))
+
+
+def chunk_spec(shape):
+    return pl.BlockSpec((shape[0], STEP, shape[2]), lambda r: (0, r, 0))
+
+
+def cost(flops, nbytes, special=0):
+    return pl.CostEstimate(flops=int(flops), bytes_accessed=int(nbytes), transcendentals=int(special))
+
+
+def chunk_shapes(pair):
+    shapes = [(size,) + pair.shape[:2] for size in SIZES] * 4
+    return [jax.ShapeDtypeStruct(shape, jnp.bfloat16) for shape in shapes]
+
+
+def split(arrays):
+    return [arrays[k * COUNT : (k + 1) * COUNT] for k in range(4)]
+
+
+def project_call(chain, block_mask, pair, w_in, gain_in):
+    rows, cols, _ = pair.shape
+    width = w_in.shape[2] // 4
+    outs = chunk_shapes(pair)
+    result = pl.pallas_call(
+        project_kernel,
+        grid=(rows // STEP,),
+        in_specs=[SMEM_SPEC, SMEM_SPEC, tile_spec(pair), part(w_in, 0), whole(gain_in[:1])],
+        out_specs=[chunk_spec(out.shape) for out in outs],
+        out_shape=outs,
+        scratch_shapes=[
+            pltpu.VMEM((w_in.shape[2], w_in.shape[1]), jnp.bfloat16),
+            pltpu.VMEM((2, width * STEP, cols), jnp.float32),
+        ],
+        compiler_params=params(),
+        cost_estimate=cost(2e9, 8 << 20, 4 << 20),
+        name="project",
+    )(chain, block_mask, pair, w_in, gain_in[:1])
+    return split(result)
+
+
+def gate_call(pair, w_gate, gain_in, index):
+    gain = gain_in[index : index + 1]
+    return pl.pallas_call(
+        gate_kernel,
+        grid=(pair.shape[0] // STEP,),
+        in_specs=[tile_spec(pair), part(w_gate, index), whole(gain)],
+        out_specs=tile_spec(pair),
+        out_shape=jax.ShapeDtypeStruct(pair.shape, jnp.bfloat16),
+        compiler_params=params(),
+        cost_estimate=cost(2e9, 8 << 20, 4 << 20),
+        name="gate",
+    )(pair, w_gate, gain)
+
+
+def finish_call(pair, gate, products, w_out, gain_wide):
+    rows, cols, _ = pair.shape
+    width = w_out.shape[1]
+    return pl.pallas_call(
+        finish_kernel,
+        grid=(rows // STEP,),
+        in_specs=[tile_spec(pair), tile_spec(gate), part(w_out, 1), whole(gain_wide)]
+        + [chunk_spec(p.shape) for p in products],
+        out_specs=tile_spec(pair),
+        out_shape=jax.ShapeDtypeStruct(pair.shape, pair.dtype),
+        scratch_shapes=[pltpu.VMEM((width * STEP, cols), jnp.float32)],
+        compiler_params=params(),
+        cost_estimate=cost(1e9, 14 << 20, 4 << 20),
+        name="finish",
+    )(pair, gate, w_out, gain_wide, *products)
+
+
+def middle_call(chain, block_mask, pair, gate, products, w_out, gain_wide, w_in, gain_in):
+    rows, cols, _ = pair.shape
+    width = w_out.shape[1]
+    outs = chunk_shapes(pair)
+    result = pl.pallas_call(
+        middle_kernel,
+        grid=(rows // STEP,),
+        in_specs=[SMEM_SPEC, SMEM_SPEC, tile_spec(pair), tile_spec(gate), part(w_out, 0)]
+        + [whole(gain_wide), part(w_in, 1), whole(gain_in[1:])]
+        + [chunk_spec(p.shape) for p in products],
+        out_specs=[tile_spec(pair)] + [chunk_spec(out.shape) for out in outs],
+        out_shape=[jax.ShapeDtypeStruct(pair.shape, pair.dtype)] + outs,
+        scratch_shapes=[
+            pltpu.VMEM((width * STEP, cols), jnp.float32),
+            pltpu.VMEM((w_in.shape[2], w_in.shape[1]), jnp.bfloat16),
+            pltpu.VMEM((2, width * STEP, cols), jnp.float32),
+        ],
+        compiler_params=params(),
+        cost_estimate=cost(3e9, 18 << 20, 8 << 20),
+        name="middle",
+    )(chain, block_mask, pair, gate, w_out, gain_wide, w_in, gain_in[1:], *products)
+    return result[0], split(result[1:])
+
+
+def product_call(kernel, operands, leads, scratch, name):
+    channels, size, _ = operands[0].shape
+    spec = pl.BlockSpec((1, size, size), lambda c: (c, 0, 0))
+
+    def out_spec(lead):
+        return pl.BlockSpec(lead + (1, size, size), lambda c: (0,) * len(lead) + (c, 0, 0))
+
+    return pl.pallas_call(
+        kernel,
+        grid=(channels,),
+        in_specs=[spec] * len(operands),
+        out_specs=[out_spec(lead) for lead in leads],
+        out_shape=[jax.ShapeDtypeStruct(lead + operands[0].shape, jnp.bfloat16) for lead in leads],
+        scratch_shapes=[pltpu.VMEM(scratch, jnp.bfloat16)],
+        compiler_params=params(),
+        cost_estimate=cost(channels * 2 * (4 * size) ** 2 * size, operands[0].size * 2 * 20),
+        name=name,
+    )(*operands)
+
+
+def inward(array):
+    return lax.ppermute(array, "row", [(0, 1), (3, 2)])
+
+
+def outward(array):
+    return lax.ppermute(array, "row", [(1, 0), (2, 3)])
+
+
+def across(array):
+    return lax.ppermute(array, "row", [(1, 2), (2, 1)])
+
+
+def other_core(array):
+    return lax.ppermute(array, "col", [(c, c ^ 1) for c in range(4)])
+
+
+def other_x(array):
+    return lax.ppermute(array, "col", [(c, c ^ 2) for c in range(4)])
+
+
+def share(own, pair):
+    row = lax.axis_index("row")
+    ready = jnp.where((row == 1) | (row == 2), own, outward(pair))
+    return ready[0], other_x(ready[1])
+
+
+def four_by_four(pair, chain, block_mask, w_in, w_gate, w_out, gain_in, gain_out):
+    size = pair.shape[0]
+    gain_wide = jnp.broadcast_to(gain_out[:, :, None, None], gain_out.shape + (1, pair.shape[1]))
+
+    parts = project_call(chain, block_mask, pair, w_in, gain_in)
+    gate = gate_call(pair, w_gate, gain_in, 0)
+    products = []
+    for l_own, l_send, r_own, r_send in zip(*parts):
+        r_x = other_x(r_send)
+        l_x = other_x(l_send)
+        r_pair, r_near, l_pair = inward(r_own), across(r_own), inward(l_own)
+        r_far = across(r_pair)
+        r_pair_x, r_near_x, l_pair_x = inward(r_x), across(r_x), inward(l_x)
+        r_far_x = across(r_pair_x)
+        own, other, sent = product_call(
+            outgoing_kernel,
+            (l_own, l_x, l_pair, l_pair_x, r_own, r_x, r_pair, r_pair_x, r_far, r_far_x, r_near, r_near_x),
+            ((2,), (2,), (2, 2)),
+            (4, size, 2 * size),
+            "outgoing",
+        )
+        come = other_core(sent)
+        products.append(share(own + come[0], other + come[1]))
+    products = [p[0] for p in products] + [p[1] for p in products]
+    middle, parts = middle_call(
+        chain, block_mask, pair, gate, products, w_out, gain_wide[0], w_in, gain_in
+    )
+    gate = gate_call(middle, w_gate, gain_in, 1)
+    products = []
+    for l_own, l_send, r_own, r_send in zip(*parts):
+        l_x = other_x(l_send)
+        r_x = other_x(r_send)
+        l_pair, r_pair = inward(l_own), inward(r_own)
+        l_pair_x, r_pair_x = inward(l_x), inward(r_x)
+        own, other, far, near = product_call(
+            incoming_kernel,
+            (l_own, l_x, other_core(l_own), other_core(l_x))
+            + (l_pair, l_pair_x, other_core(l_pair), other_core(l_pair_x))
+            + (r_own, r_x, r_pair, r_pair_x),
+            ((2,), (2,), (2,), (2,)),
+            (4, 2 * size, size),
+            "incoming",
+        )
+        other = other + across(far)
+        products.append(share(own + across(near), other))
+    products = [p[0] for p in products] + [p[1] for p in products]
+    return finish_call(middle, gate, products, w_out, gain_wide[1])
+
+
 def solution(mesh):
+    four = mesh.shape["row"] == 4 and mesh.shape["col"] == 4
     return jax.shard_map(
-        per_device,
+        four_by_four if four else any_mesh,
         mesh=mesh,
         in_specs=(
             P(("group", "row"), "col", None),

time: 817 us -> 440 us (0.54)
  waiting for transfers between devices: 634 us -> 225 us
  starting transfers between devices: 1.15 us -> 109 us
  Pallas kernels: 0 us -> 90.5 us
  matrix products: 85.8 us -> 0 us
  other arithmetic: 54.9 us -> 4.48 us
  between operations: 13.6 us -> 0.83 us
  local copies, waits for them, and re-layouts: 19.9 us -> 8.31 us
    all_gather x3 -> x0, waiting for transfers between devices: 415 us -> none  [the longest x2 268 us: per_device(): lax.all_gather(right, 'row', axis=0, tiled=True)]
    ppermute x0 -> x81, waiting for transfers between devices: none -> 225 us  [the longest x18 77.7 us: across(): return lax.ppermute(array, 'row', [(1, 2), (2, 1)])]
    psum x1 -> x0, waiting for transfers between devices: 155 us -> none  [broadcast(): return lax.psum(block, axis)]
    ppermute x0 -> x81, starting transfers between devices: none -> 109 us  [the longest x18 44.6 us: across(): return lax.ppermute(array, 'row', [(1, 2), (2, 1)])]
    pallas_call x0 -> x11, Pallas kernels: none -> 90.5 us  [the longest x6 31.3 us: product_call(): pl.pallas_call(kernel, grid=(channels,), in_specs=[spec] * len(operands),...]
    dot_general x9 -> x0, matrix products: 85.8 us -> none  [the longest x1 25.6 us: per_device(): jnp.einsum('kic,kjc->ijc', left_mine, lax.all_gather(right, 'row', axis=0...]
    reduce_scatter x1 -> x0, waiting for transfers between devices: 63.3 us -> none  [per_device(): lax.psum_scatter(partial_terms.astype(jnp.bfloat16), 'col', scatter_dimen...]
    select_n x2 -> x5, other arithmetic: 23.6 us -> 0.87 us  [share(): ready = jnp.where((row == 1) | (row == 2), own, outward(pair))]
  transfers between devices with their start and end apart: 5 -> 81, of which waited for: 5 -> 43; matrix products, arithmetic and copies ran while one was open for 5% -> 1% of each run, Pallas kernels for 0% -> 11%
where the time goes in v2:
time: 440 us; the launch traced here: 438 us
  waiting for transfers between devices  225 us (51%)
  starting transfers between devices  109 us (25%)
  Pallas kernels  90.5 us (21%)
  local copies, waits for them, and re-layouts  8.31 us (2%)
  other arithmetic  4.48 us (1%)
    ppermute x18, waiting for transfers between devices, across(): return lax.ppermute(array, 'row', [(1, 2), (2, 1)])  77.7 us
    ppermute x24, waiting for transfers between devices, inward(): return lax.ppermute(array, 'row', [(0, 1), (3, 2)])  65.6 us
    ppermute x18, starting transfers between devices, across(): return lax.ppermute(array, 'row', [(1, 2), (2, 1)])  44.6 us
    ppermute x18, waiting for transfers between devices, other_x(): return lax.ppermute(array, 'col', [(c, c ^ 2) for c in range(4)])  43 us
    ppermute x6, waiting for transfers between devices, outward(): return lax.ppermute(array, 'row', [(1, 0), (2, 3)])  37.6 us
    pallas_call x6, Pallas kernels, product_call(): pl.pallas_call(kernel, grid=(channels,), in_specs=[spec] * len(operands),...  31.3 us
    ppermute x24, starting transfers between devices, inward(): return lax.ppermute(array, 'row', [(0, 1), (3, 2)])  31 us
    ppermute x18, starting transfers between devices, other_x(): return lax.ppermute(array, 'col', [(c, c ^ 2) for c in range(4)])  20.4 us
  transfers between devices with their start and end apart: 81, of which 43 were waited for; matrix products, arithmetic and copies ran while one was open for 1% of the time, Pallas kernels for 11%

profile of v2, /device:TPU:16, one launch (start us, length us, event | category | flops | bytes accessed | tf_op | source)
XLA Modules:
  0.0 438.1 jit_solution(15223418059048891809)
XLA Ops:
  3.0 13.5 %project.1 = (bf16[12,128,128]{2,1,0:T(8,128)(2,1)S(1)}, bf16[12,128,128]{2,1,0:T(8,128)(2,1)S(1)}, bf16[8,128,128]{2,1,0:T(8,128)(2,1)S(1)}, bf16[12,128,128]{2...) custom-call(s32[4]{0:T(128)S(1)} %copy-done.8, ...), custom_call_target="tpu_custom_call" | custom-call | flops 2000000000 | bytes 8388608 | tf_op jit(solution)/shard_map/project/pallas_call | solution.py:282
  69.8 12.8 %collective-permute-done.29.r_pair_x = bf16[8,128,128]{2,1,0:T(8,128)(2,1)S(1)} collective-permute-done((bf16[8,128,128]{2,1,0:T(8,128)(2,1)S(1)}, bf16[8,128,128]{2,1,0:T(8,128)(2,1)S(1)}, u32[]{:S(2)}, u32[]{:S(2)}) %collective-permute-start.29) | collective-permute-done | bytes 262176 | tf_op jit(solution)/shard_map/ppermute | solution.py:375
  98.7 6.3 %collective-permute-done.9.r_near_x = bf16[12,128,128]{2,1,0:T(8,128)(2,1)S(1)} collective-permute-done((bf16[12,128,128]{2,1,0:T(8,128)(2,1)S(1)}, bf16[12,128,128]{2,1,0:T(8,128)(2,1)S(1)}, u32[]{:S(2)}, u32[]{:S(2)}) %collective-permute-start.9) | collective-permute-done | bytes 393248 | tf_op jit(solution)/shard_map/ppermute | solution.py:383
  115.5 6.5 %outgoing.3 = (bf16[2,12,128,128]{3,2,1,0:T(8,128)(2,1)S(1)}, bf16[2,12,128,128]{3,2,1,0:T(8,128)(2,1)}, bf16[2,2,12,128,128]{4,3,2,1,0:T(8,128)(2,1)}) custom-call(bf16[12,128,128]{2,1,0:T(8,128)(2,1)S(1)} %get-tuple-element.51.l_own, bf16[12,128,128]{2,1,0:T(8,128)(2,1)S(1)} %collective-permute-done.l_x, ...), custom_call_target="tpu_custom_call" | custom-call | flops 805306368 | bytes 7864320 | tf_op jit(solution)/shard_map/outgoing/pallas_call | solution.py:361
  127.4 8.4 %collective-permute-done.21.r_near_x = bf16[12,128,128]{2,1,0:T(8,128)(2,1)S(1)} collective-permute-done((bf16[12,128,128]{2,1,0:T(8,128)(2,1)S(1)}, bf16[12,128,128]{2,1,0:T(8,128)(2,1)S(1)}, u32[]{:S(2)}, u32[]{:S(2)}) %collective-permute-start.21) | collective-permute-done | bytes 393248 | tf_op jit(solution)/shard_map/ppermute | solution.py:383
  140.4 6.4 %outgoing.4 = (bf16[2,12,128,128]{3,2,1,0:T(8,128)(2,1)S(1)}, bf16[2,12,128,128]{3,2,1,0:T(8,128)(2,1)}, bf16[2,2,12,128,128]{4,3,2,1,0:T(8,128)(2,1)}) custom-call(bf16[12,128,128]{2,1,0:T(8,128)(2,1)S(1)} %get-tuple-element.58.l_own, bf16[12,128,128]{2,1,0:T(8,128)(2,1)S(1)} %collective-permute-done.12.l_x, ...), custom_call_target="tpu_custom_call" | custom-call | flops 805306368 | bytes 7864320 | tf_op jit(solution)/shard_map/outgoing/pallas_call | solution.py:361
  162.9 15.7 %collective-permute-done.11 = bf16[2,12,128,128]{3,2,1,0:T(8,128)(2,1)} collective-permute-done((bf16[2,12,128,128]{3,2,1,0:T(8,128)(2,1)}, bf16[2,12,128,128]{3,2,1,0:T(8,128)(2,1)}, u32[]{:S(2)}, u32[]{:S(2)}) %collective-permute-start.11) | collective-permute-done | bytes 786464 | tf_op jit(solution)/shard_map/ppermute | solution.py:379
  178.6 16.7 %collective-permute-done.23 = bf16[2,12,128,128]{3,2,1,0:T(8,128)(2,1)} collective-permute-done((bf16[2,12,128,128]{3,2,1,0:T(8,128)(2,1)}, bf16[2,12,128,128]{3,2,1,0:T(8,128)(2,1)}, u32[]{:S(2)}, u32[]{:S(2)}) %collective-permute-start.23) | collective-permute-done | bytes 786464 | tf_op jit(solution)/shard_map/ppermute | solution.py:379
  198.0 9.1 %gate.2.gate_ref = bf16[128,128,128]{2,1,0:T(8,128)(2,1)S(1)} custom-call(bf16[128,128,128]{2,1,0:T(8,128)(2,1)} %pair_ref.5, bf16[2,128,128]{2,1,0:T(8,128)(2,1)S(1)} %copy-done.2, f32[1,128]{1,0:T(1,128)S(1)} %get-tuple-element.112.gain_ref), custom_call_target="tpu_custom_call" | custom-call | flops 2000000000 | bytes 8388608 | tf_op jit(solution)/shard_map/gate/pallas_call | solution.py:301
  209.2 6.0 %collective-permute-done.37.rest_4_ = bf16[12,128,128]{2,1,0:T(8,128)(2,1)S(1)} collective-permute-done((bf16[12,128,128]{2,1,0:T(8,128)(2,1)S(1)}, bf16[12,128,128]{2,1,0:T(8,128)(2,1)S(1)}, u32[]{:S(2)}, u32[]{:S(2)}) %collective-permute-start.37) | collective-permute-done | bytes 393248 | tf_op jit(solution)/shard_map/ppermute | solution.py:391
  216.0 18.1 %middle.1 = (bf16[128,128,128]{2,1,0:T(8,128)(2,1)}, bf16[12,128,128]{2,1,0:T(8,128)(2,1)S(1)}, bf16[12,128,128]{2,1,0:T(8,128)(2,1)S(1)}, bf16[8,128,128]{2,1,0...) custom-call(s32[4]{0:T(128)S(1)} %copy-done.9, ...), custom_call_target="tpu_custom_call" | custom-call | flops 3000000000 | bytes 18874368 | tf_op jit(solution)/shard_map/middle/pallas_call | solution.py:334
  246.7 8.7 %collective-permute-done.72.r_x = bf16[8,128,128]{2,1,0:T(8,128)(2,1)S(1)} collective-permute-done((bf16[8,128,128]{2,1,0:T(8,128)(2,1)S(1)}, bf16[8,128,128]{2,1,0:T(8,128)(2,1)S(1)}, u32[]{:S(2)}, u32[]{:S(2)}) %collective-permute-start.72) | collective-permute-done | bytes 262176 | tf_op jit(solution)/shard_map/ppermute | solution.py:391
  260.8 6.7 %collective-permute-done.59.r_x = bf16[12,128,128]{2,1,0:T(8,128)(2,1)S(1)} collective-permute-done((bf16[12,128,128]{2,1,0:T(8,128)(2,1)S(1)}, bf16[12,128,128]{2,1,0:T(8,128)(2,1)S(1)}, u32[]{:S(2)}, u32[]{:S(2)}) %collective-permute-start.59) | collective-permute-done | bytes 393248 | tf_op jit(solution)/shard_map/ppermute | solution.py:391
  281.9 6.4 %collective-permute-done.47.r_pair = bf16[12,128,128]{2,1,0:T(8,128)(2,1)S(1)} collective-permute-done((bf16[12,128,128]{2,1,0:T(8,128)(2,1)S(1)}, bf16[12,128,128]{2,1,0:T(8,128)(2,1)S(1)}, u32[]{:S(2)}, u32[]{:S(2)}) %collective-permute-start.47) | collective-permute-done | bytes 393248 | tf_op jit(solution)/shard_map/ppermute | solution.py:375
  289.6 12.8 %collective-permute-done.69.l_pair_x = bf16[8,128,128]{2,1,0:T(8,128)(2,1)S(1)} collective-permute-done((bf16[8,128,128]{2,1,0:T(8,128)(2,1)S(1)}, bf16[8,128,128]{2,1,0:T(8,128)(2,1)S(1)}, u32[]{:S(2)}, u32[]{:S(2)}) %collective-permute-start.69) | collective-permute-done | bytes 262176 | tf_op jit(solution)/shard_map/ppermute | solution.py:375
  311.3 6.4 %incoming.4 = (bf16[2,12,128,128]{3,2,1,0:T(8,128)(2,1)S(1)}, bf16[2,12,128,128]{3,2,1,0:T(8,128)(2,1)}, bf16[2,12,128,128]{3,2,1,0:T(8,128)(2,1)}, bf16[2,12,128,128]{3,2,1,0:T(8,128)(2,1)}) custom-call(bf16[12,128,128]{2,1,0:T(8,128)(2,1)S(1)} %get-tuple-element.81.l_own, bf16[12,128,128]{2,1,0:T(8,128)(2,1)S(1)} %collective-permute-done.52.l_x, ...), custom_call_target="tpu_custom_call" | custom-call | flops 805306368 | bytes 7864320 | tf_op jit(solution)/shard_map/incoming/pallas_call | solution.py:361
  331.6 6.5 %collective-permute-done.48.r_pair_x = bf16[12,128,128]{2,1,0:T(8,128)(2,1)S(1)} collective-permute-done((bf16[12,128,128]{2,1,0:T(8,128)(2,1)S(1)}, bf16[12,128,128]{2,1,0:T(8,128)(2,1)S(1)}, u32[]{:S(2)}, u32[]{:S(2)}) %collective-permute-start.48) | collective-permute-done | bytes 393248 | tf_op jit(solution)/shard_map/ppermute | solution.py:375
  338.1 6.3 %incoming.3 = (bf16[2,12,128,128]{3,2,1,0:T(8,128)(2,1)S(1)}, bf16[2,12,128,128]{3,2,1,0:T(8,128)(2,1)}, bf16[2,12,128,128]{3,2,1,0:T(8,128)(2,1)}, bf16[2,12,128,128]{3,2,1,0:T(8,128)(2,1)}) custom-call(bf16[12,128,128]{2,1,0:T(8,128)(2,1)S(1)} %get-tuple-element.73.l_own, bf16[12,128,128]{2,1,0:T(8,128)(2,1)S(1)} %collective-permute-done.39.l_x, ...), custom_call_target="tpu_custom_call" | custom-call | flops 805306368 | bytes 7864320 | tf_op jit(solution)/shard_map/incoming/pallas_call | solution.py:361
  356.9 11.4 %collective-permute-done.50 = bf16[2,12,128,128]{3,2,1,0:T(8,128)(2,1)S(1)} collective-permute-done((bf16[2,12,128,128]{3,2,1,0:T(8,128)(2,1)}, bf16[2,12,128,128]{3,2,1,0:T(8,128)(2,1)S(1)}, u32[]{:S(2)}, u32[]{:S(2)}) %collective-permute-start.50) | collective-permute-done | bytes 786464 | tf_op jit(solution)/shard_map/ppermute | solution.py:383
  370.7 8.8 %collective-permute-done.75 = bf16[2,8,128,128]{3,2,1,0:T(8,128)(2,1)S(1)} collective-permute-done((bf16[2,8,128,128]{3,2,1,0:T(8,128)(2,1)S(1)}, bf16[2,8,128,128]{3,2,1,0:T(8,128)(2,1)S(1)}, u32[]{:S(2)}, u32[]{:S(2)}) %collective-permute-start.75) | collective-permute-done | bytes 524320 | tf_op jit(solution)/shard_map/ppermute | solution.py:383
  381.0 15.4 %collective-permute-done.62 = bf16[2,12,128,128]{3,2,1,0:T(8,128)(2,1)S(1)} collective-permute-done((bf16[2,12,128,128]{3,2,1,0:T(8,128)(2,1)S(1)}, bf16[2,12,128,128]{3,2,1,0:T(8,128)(2,1)S(1)}, u32[]{:S(2)}, u32[]{:S(2)}) %collective-permute-start.62) | collective-permute-done | bytes 786464 | tf_op jit(solution)/shard_map/ppermute | solution.py:383
  397.7 14.6 %collective-permute-done.49 = bf16[2,12,128,128]{3,2,1,0:T(8,128)(2,1)S(1)} collective-permute-done((bf16[2,12,128,128]{3,2,1,0:T(8,128)(2,1)S(1)}, bf16[2,12,128,128]{3,2,1,0:T(8,128)(2,1)S(1)}, u32[]{:S(2)}, u32[]{:S(2)}) %collective-permute-start.49) | collective-permute-done | bytes 786464 | tf_op jit(solution)/shard_map/ppermute | solution.py:383
  414.7 9.1 %gate.3.gate_ref = bf16[128,128,128]{2,1,0:T(8,128)(2,1)S(1)} custom-call(bf16[128,128,128]{2,1,0:T(8,128)(2,1)} %get-tuple-element.72.pair_ref, bf16[2,128,128]{2,1,0:T(8,128)(2,1)S(1)} %copy-done.2, f32[1,128]{1,0:T(1,128)S(1)} %get-tuple-element.111.gain_in_ref.gain_ref), custom_call_target="tpu_custom_call" | custom-call | flops 2000000000 | bytes 8388608 | tf_op jit(solution)/shard_map/gate/pallas_call | solution.py:301
  428.5 9.5 %finish.1 = bf16[128,128,128]{2,1,0:T(8,128)(2,1)} custom-call(bf16[128,128,128]{2,1,0:T(8,128)(2,1)} %get-tuple-element.72.pair_ref, bf16[128,128,128]{2,1,0:T(8,128)(2,1)} %copy-done, bf16[2,64,128]{2,1,0:T(8,128)(2,1)S(1)} %copy-done.3, f32[64,1,128]{2,1,0:T(1,128)S(1)} %broadcast_in_dim.15.gain_ref, ...), custom_call_target="tpu_custom_call" | custom-call | flops 1000000000 | bytes 14680064 | tf_op jit(solution)/shard_map/finish/pallas_call | solution.py:316
  (214 shorter events, 195.4 us)
Async XLA Ops:
  56.5 34.6 %collective-permute-start.5 = (bf16[12,128,128]{2,1,0:T(8,128)(2,1)S(1)}, bf16[12,128,128]{2,1,0:T(8,128)(2,1)S(1)}, u32[]{:S(2)}, u32[]{:S(2)}) collective-permute-start(bf16[12,128,128]{2,1,0:T(8,128)(2,1)S(1)} %collective-permute-done.3.r_x), channel_id=1, source_target_pairs={{0,4},{12,8},{1,5},{13,9},{2,6},{14,10},{3,7},{15,11},{16,20},{28,... | collective-permute-start | bytes 1179656 | tf_op jit(solution)/shard_map/ppermute | solution.py:375
  60.1 22.5 %collective-permute-start.29 = (bf16[8,128,128]{2,1,0:T(8,128)(2,1)S(1)}, bf16[8,128,128]{2,1,0:T(8,128)(2,1)S(1)}, u32[]{:S(2)}, u32[]{:S(2)}) collective-permute-start(bf16[8,128,128]{2,1,0:T(8,128)(2,1)S(1)} %collective-permute-done.27.r_x), channel_id=1, source_target_pairs={{0,4},{12,8},{1,5},{13,9},{2,6},{14,10},{3,7},{15,11},{16,20},{28,... | collective-permute-start | bytes 786440 | tf_op jit(solution)/shard_map/ppermute | solution.py:375
  61.4 23.3 %collective-permute-start.30 = (bf16[8,128,128]{2,1,0:T(8,128)(2,1)S(1)}, bf16[8,128,128]{2,1,0:T(8,128)(2,1)S(1)}, u32[]{:S(2)}, u32[]{:S(2)}) collective-permute-start(bf16[8,128,128]{2,1,0:T(8,128)(2,1)S(1)} %collective-permute-done.28.r_pair), channel_id=1, source_target_pairs={{4,8},{8,4},{5,9},{9,5},{6,10},{10,6},{7,11},{11,7},{20,24},{24,20... | collective-permute-start | bytes 786440 | tf_op jit(solution)/shard_map/ppermute | solution.py:383
  64.0 24.5 %collective-permute-start.33 = (bf16[8,128,128]{2,1,0:T(8,128)(2,1)S(1)}, bf16[8,128,128]{2,1,0:T(8,128)(2,1)S(1)}, u32[]{:S(2)}, u32[]{:S(2)}) collective-permute-start(bf16[8,128,128]{2,1,0:T(8,128)(2,1)S(1)} %collective-permute-done.27.r_x), channel_id=1, source_target_pairs={{4,8},{8,4},{5,9},{9,5},{6,10},{10,6},{7,11},{11,7},{20,24},{24,20... | collective-permute-start | bytes 786440 | tf_op jit(solution)/shard_map/ppermute | solution.py:383
  96.5 25.5 %collective-permute-start.31 = (bf16[8,128,128]{2,1,0:T(8,128)(2,1)S(1)}, bf16[8,128,128]{2,1,0:T(8,128)(2,1)S(1)}, u32[]{:S(2)}, u32[]{:S(2)}) collective-permute-start(bf16[8,128,128]{2,1,0:T(8,128)(2,1)S(1)} %collective-permute-done.29.r_pair_x), channel_id=1, source_target_pairs={{4,8},{8,4},{5,9},{9,5},{6,10},{10,6},{7,11},{11,7},{20,24},{24,20... | collective-permute-start | bytes 786440 | tf_op jit(solution)/shard_map/ppermute | solution.py:383
  107.1 28.8 %collective-permute-start.21 = (bf16[12,128,128]{2,1,0:T(8,128)(2,1)S(1)}, bf16[12,128,128]{2,1,0:T(8,128)(2,1)S(1)}, u32[]{:S(2)}, u32[]{:S(2)}) collective-permute-start(bf16[12,128,128]{2,1,0:T(8,128)(2,1)S(1)} %collective-permute-done.15.r_x), channel_id=1, source_target_pairs={{4,8},{8,4},{5,9},{9,5},{6,10},{10,6},{7,11},{11,7},{20,24},{24,20... | collective-permute-start | bytes 1179656 | tf_op jit(solution)/shard_map/ppermute | solution.py:383
  110.8 25.0 %collective-permute-start.14 = (bf16[12,128,128]{2,1,0:T(8,128)(2,1)S(1)}, bf16[12,128,128]{2,1,0:T(8,128)(2,1)S(1)}, u32[]{:S(2)}, u32[]{:S(2)}) collective-permute-start(bf16[12,128,128]{2,1,0:T(8,128)(2,1)S(1)} %collective-permute-done.12.l_x), channel_id=1, source_target_pairs={{0,4},{12,8},{1,5},{13,9},{2,6},{14,10},{3,7},{15,11},{16,20},{28,... | collective-permute-start | bytes 1179656 | tf_op jit(solution)/shard_map/ppermute | solution.py:375
  113.4 27.0 %collective-permute-start.19 = (bf16[12,128,128]{2,1,0:T(8,128)(2,1)S(1)}, bf16[12,128,128]{2,1,0:T(8,128)(2,1)S(1)}, u32[]{:S(2)}, u32[]{:S(2)}) collective-permute-start(bf16[12,128,128]{2,1,0:T(8,128)(2,1)S(1)} %collective-permute-done.17.r_pair_x), channel_id=1, source_target_pairs={{4,8},{8,4},{5,9},{9,5},{6,10},{10,6},{7,11},{11,7},{20,24},{24,20... | collective-permute-start | bytes 1179656 | tf_op jit(solution)/shard_map/ppermute | solution.py:383
  122.0 27.9 %collective-permute-start.10 = (bf16[2,2,12,128,128]{4,3,2,1,0:T(8,128)(2,1)}, bf16[2,2,12,128,128]{4,3,2,1,0:T(8,128)(2,1)S(1)}, u32[]{:S(2)}, u32[]{:S(2)}) collective-permute-start(bf16[2,2,12,128,128]{4,3,2,1,0:T(8,128)(2,1)} %get-tuple-element.56), channel_id=1, source_target_pairs={{0,1},{1,0},{2,3},{3,2},{4,5},{5,4},{6,7},{7,6},{8,9},{9,8},{10,11... | collective-permute-start | bytes 4718600 | tf_op jit(solution)/shard_map/ppermute | solution.py:387
  151.0 27.6 %collective-permute-start.11 = (bf16[2,12,128,128]{3,2,1,0:T(8,128)(2,1)}, bf16[2,12,128,128]{3,2,1,0:T(8,128)(2,1)}, u32[]{:S(2)}, u32[]{:S(2)}) collective-permute-start(bf16[2,12,128,128]{3,2,1,0:T(8,128)(2,1)} %fusion.3), channel_id=1, source_target_pairs={{4,0},{8,12},{5,1},{9,13},{6,2},{10,14},{7,3},{11,15},{20,16},{24,... | collective-permute-start | bytes 2359304 | tf_op jit(solution)/shard_map/ppermute | solution.py:379
  154.2 41.0 %collective-permute-start.23 = (bf16[2,12,128,128]{3,2,1,0:T(8,128)(2,1)}, bf16[2,12,128,128]{3,2,1,0:T(8,128)(2,1)}, u32[]{:S(2)}, u32[]{:S(2)}) collective-permute-start(bf16[2,12,128,128]{3,2,1,0:T(8,128)(2,1)} %fusion), channel_id=1, source_target_pairs={{4,0},{8,12},{5,1},{9,13},{6,2},{10,14},{7,3},{11,15},{20,16},{24,... | collective-permute-start | bytes 2359304 | tf_op jit(solution)/shard_map/ppermute | solution.py:379
  161.9 47.2 %collective-permute-start.38 = (bf16[8,128,128]{2,1,0:T(8,128)(2,1)S(1)}, bf16[8,128,128]{2,1,0:T(8,128)(2,1)S(1)}, u32[]{:S(2)}, u32[]{:S(2)}) collective-permute-start(bf16[8,128,128]{2,1,0:T(8,128)(2,1)S(1)} %get-tuple-element.107), channel_id=1, source_target_pairs={{0,2},{1,3},{2,0},{3,1},{4,6},{5,7},{6,4},{7,5},{8,10},{9,11},{10,... | collective-permute-start | bytes 786440 | tf_op jit(solution)/shard_map/ppermute | solution.py:391
  275.9 26.5 %collective-permute-start.56 = (bf16[12,128,128]{2,1,0:T(8,128)(2,1)S(1)}, bf16[12,128,128]{2,1,0:T(8,128)(2,1)S(1)}, u32[]{:S(2)}, u32[]{:S(2)}) collective-permute-start(bf16[12,128,128]{2,1,0:T(8,128)(2,1)S(1)} %collective-permute-done.52.l_x), channel_id=1, source_target_pairs={{0,4},{12,8},{1,5},{13,9},{2,6},{14,10},{3,7},{15,11},{16,20},{28,... | collective-permute-start | bytes 1179656 | tf_op jit(solution)/shard_map/ppermute | solution.py:375
  281.4 23.9 %collective-permute-start.54 = (bf16[12,128,128]{2,1,0:T(8,128)(2,1)S(1)}, bf16[12,128,128]{2,1,0:T(8,128)(2,1)S(1)}, u32[]{:S(2)}, u32[]{:S(2)}) collective-permute-start(bf16[12,128,128]{2,1,0:T(8,128)(2,1)S(1)} %collective-permute-done.52.l_x), channel_id=1, source_target_pairs={{0,1},{1,0},{2,3},{3,2},{4,5},{5,4},{6,7},{7,6},{8,9},{9,8},{10,11... | collective-permute-start | bytes 1179656 | tf_op jit(solution)/shard_map/ppermute | solution.py:387
  281.4 24.1 %collective-permute-start.57 = (bf16[12,128,128]{2,1,0:T(8,128)(2,1)S(1)}, bf16[12,128,128]{2,1,0:T(8,128)(2,1)S(1)}, u32[]{:S(2)}, u32[]{:S(2)}) collective-permute-start(bf16[12,128,128]{2,1,0:T(8,128)(2,1)S(1)} %collective-permute-done.55.l_pair), channel_id=1, source_target_pairs={{0,1},{1,0},{2,3},{3,2},{4,5},{5,4},{6,7},{7,6},{8,9},{9,8},{10,11... | collective-permute-start | bytes 1179656 | tf_op jit(solution)/shard_map/ppermute | solution.py:387
  317.7 37.6 %collective-permute-start.63 = (bf16[2,12,128,128]{3,2,1,0:T(8,128)(2,1)}, bf16[2,12,128,128]{3,2,1,0:T(8,128)(2,1)S(1)}, u32[]{:S(2)}, u32[]{:S(2)}) collective-permute-start(bf16[2,12,128,128]{3,2,1,0:T(8,128)(2,1)} %get-tuple-element.88), channel_id=1, source_target_pairs={{4,8},{8,4},{5,9},{9,5},{6,10},{10,6},{7,11},{11,7},{20,24},{24,20... | collective-permute-start | bytes 2359304 | tf_op jit(solution)/shard_map/ppermute | solution.py:383
  344.3 23.9 %collective-permute-start.50 = (bf16[2,12,128,128]{3,2,1,0:T(8,128)(2,1)}, bf16[2,12,128,128]{3,2,1,0:T(8,128)(2,1)S(1)}, u32[]{:S(2)}, u32[]{:S(2)}) collective-permute-start(bf16[2,12,128,128]{3,2,1,0:T(8,128)(2,1)} %get-tuple-element.80), channel_id=1, source_target_pairs={{4,8},{8,4},{5,9},{9,5},{6,10},{10,6},{7,11},{11,7},{20,24},{24,20... | collective-permute-start | bytes 2359304 | tf_op jit(solution)/shard_map/ppermute | solution.py:383
  346.7 32.8 %collective-permute-start.75 = (bf16[2,8,128,128]{3,2,1,0:T(8,128)(2,1)S(1)}, bf16[2,8,128,128]{3,2,1,0:T(8,128)(2,1)S(1)}, u32[]{:S(2)}, u32[]{:S(2)}) collective-permute-start(bf16[2,8,128,128]{3,2,1,0:T(8,128)(2,1)S(1)} %get-tuple-element.94), channel_id=1, source_target_pairs={{4,8},{8,4},{5,9},{9,5},{6,10},{10,6},{7,11},{11,7},{20,24},{24,20... | collective-permute-start | bytes 1572872 | tf_op jit(solution)/shard_map/ppermute | solution.py:383
  351.6 29.3 %collective-permute-start.77 = (bf16[2,8,128,128]{3,2,1,0:T(8,128)(2,1)S(1)}, bf16[2,8,128,128]{3,2,1,0:T(8,128)(2,1)S(1)}, u32[]{:S(2)}, u32[]{:S(2)}) collective-permute-start(bf16[2,8,128,128]{3,2,1,0:T(8,128)(2,1)S(1)} %add.47), channel_id=1, source_target_pairs={{4,0},{8,12},{5,1},{9,13},{6,2},{10,14},{7,3},{11,15},{20,16},{24,... | collective-permute-start | bytes 1572872 | tf_op jit(solution)/shard_map/ppermute | solution.py:379
  353.1 43.3 %collective-permute-start.62 = (bf16[2,12,128,128]{3,2,1,0:T(8,128)(2,1)S(1)}, bf16[2,12,128,128]{3,2,1,0:T(8,128)(2,1)S(1)}, u32[]{:S(2)}, u32[]{:S(2)}) collective-permute-start(bf16[2,12,128,128]{3,2,1,0:T(8,128)(2,1)S(1)} %copy-done.19), channel_id=1, source_target_pairs={{4,8},{8,4},{5,9},{9,5},{6,10},{10,6},{7,11},{11,7},{20,24},{24,20... | collective-permute-start | bytes 2359304 | tf_op jit(solution)/shard_map/ppermute | solution.py:383
  355.5 40.8 %collective-permute-start.64 = (bf16[2,12,128,128]{3,2,1,0:T(8,128)(2,1)S(1)}, bf16[2,12,128,128]{3,2,1,0:T(8,128)(2,1)S(1)}, u32[]{:S(2)}, u32[]{:S(2)}) collective-permute-start(bf16[2,12,128,128]{3,2,1,0:T(8,128)(2,1)S(1)} %add.45), channel_id=1, source_target_pairs={{4,0},{8,12},{5,1},{9,13},{6,2},{10,14},{7,3},{11,15},{20,16},{24,... | collective-permute-start | bytes 2359304 | tf_op jit(solution)/shard_map/ppermute | solution.py:379
  368.3 44.0 %collective-permute-start.49 = (bf16[2,12,128,128]{3,2,1,0:T(8,128)(2,1)S(1)}, bf16[2,12,128,128]{3,2,1,0:T(8,128)(2,1)S(1)}, u32[]{:S(2)}, u32[]{:S(2)}) collective-permute-start(bf16[2,12,128,128]{3,2,1,0:T(8,128)(2,1)S(1)} %copy-done.20), channel_id=1, source_target_pairs={{4,8},{8,4},{5,9},{9,5},{6,10},{10,6},{7,11},{11,7},{20,24},{24,20... | collective-permute-start | bytes 2359304 | tf_op jit(solution)/shard_map/ppermute | solution.py:383
  379.5 32.8 %collective-permute-start.51 = (bf16[2,12,128,128]{3,2,1,0:T(8,128)(2,1)S(1)}, bf16[2,12,128,128]{3,2,1,0:T(8,128)(2,1)S(1)}, u32[]{:S(2)}, u32[]{:S(2)}) collective-permute-start(bf16[2,12,128,128]{3,2,1,0:T(8,128)(2,1)S(1)} %add.43), channel_id=1, source_target_pairs={{4,0},{8,12},{5,1},{9,13},{6,2},{10,14},{7,3},{11,15},{20,16},{24,... | collective-permute-start | bytes 2359304 | tf_op jit(solution)/shard_map/ppermute | solution.py:379
  396.6 31.8 %collective-permute-start.79 = (bf16[12,128,128]{2,1,0:T(8,128)(2,1)S(1)}, bf16[12,128,128]{2,1,0:T(8,128)(2,1)S(1)}, u32[]{:S(2)}, u32[]{:S(2)}) collective-permute-start(bf16[12,128,128]{2,1,0:T(8,128)(2,1)S(1)} %get-tuple-element.97), channel_id=1, source_target_pairs={{0,2},{1,3},{2,0},{3,1},{4,6},{5,7},{6,4},{7,5},{8,10},{9,11},{10,... | collective-permute-start | bytes 1179656 | tf_op jit(solution)/shard_map/ppermute | solution.py:391
  (79 other events, 1111.6 us)

commit v3 on v2

--- a/solution.py
+++ b/solution.py
@@ -9,8 +9,11 @@
 
 BLOCK = 128
 EPS = 1e-05
-SIZES = (12, 12, 8)
+OUT_SIZES = (12, 12, 8)
+IN_SIZES = (6, 10, 10, 6)
 STEP = 16
+WINDOW = 5
+TOLD = 0.05
 VMEM = 48 * 1024 * 1024
 
 
@@ -92,7 +95,6 @@
 NT = (((1,), (1,)), ((), ()))
 TN = (((0,), (0,)), ((), ()))
 SMEM_SPEC = pl.BlockSpec(memory_space=pltpu.SMEM)
-COUNT = len(SIZES)
 
 
 def dot(a, b, dims=NN):
@@ -127,7 +129,7 @@
         w_t[...] = w_ref[0].T
 
 
-def project_rows(normed, mask, w_t, scratch, outs):
+def project_rows(normed, mask, w_t, scratch, outs, sizes):
     hidden = dot(w_t[...], normed, NT)
     width = w_t.shape[0] // 4
     half = width // 2
@@ -139,21 +141,31 @@
         kept = mask * logistic(gates) * values
         for row in range(STEP):
             scratch[side, pl.ds(row, width, stride=STEP), :] = kept[:, row * cols : (row + 1) * cols]
-        for other in range(2):
-            start = (x if other == 0 else 1 - x) * half
-            for n, size in enumerate(SIZES):
-                first = pl.multiple_of((start + sum(SIZES[:n])) * STEP, 8)
-                block = scratch[side, pl.ds(first, size * STEP), :]
-                ref = outs[(2 * side + other) * COUNT + n]
-                ref[...] = block.astype(jnp.bfloat16).reshape(ref.shape)
+    outs = list(outs)
+    for n, size in enumerate(sizes):
+        right, left, *send = [outs.pop(0) for _ in range(4 if n == 0 else 3)]
+
+        def block(side, start):
+            first = pl.multiple_of((start * half + sum(sizes[:n])) * STEP, 8)
+            rows = scratch[side, pl.ds(first, size * STEP), :]
+            return rows.astype(jnp.bfloat16).reshape(right.shape)
+
+        right[...] = block(1, x)
+        left[...] = block(0, x)
+        if n == 0:
+            send[0][...] = block(1, 1 - x)
+            send[1][...] = block(0, 1 - x)
+        else:
+            send[0][0] = block(1, 1 - x)
+            send[0][1] = block(0, 1 - x)
 
 
 def project_kernel(chain_ref, block_mask_ref, pair_ref, w_ref, gain_ref, *rest):
-    outs, (w_t, scratch) = rest[: 4 * COUNT], rest[4 * COUNT :]
+    outs, (w_t, scratch) = rest[:-2], rest[-2:]
     turn_weights(w_ref, w_t)
     rows = pair_ref[...].reshape(-1, pair_ref.shape[-1])
     normed = norm_rows(rows, gain_ref[...])
-    project_rows(normed, tile_mask(chain_ref, block_mask_ref), w_t, scratch, outs)
+    project_rows(normed, tile_mask(chain_ref, block_mask_ref), w_t, scratch, outs, OUT_SIZES)
 
 
 def gate_kernel(pair_ref, w_ref, gain_ref, out_ref):
@@ -184,34 +196,28 @@
 
 
 def finish_kernel(pair_ref, gate_ref, w_out_ref, gain_ref, *rest):
-    product_refs, (out_ref, scratch) = rest[: 2 * COUNT], rest[2 * COUNT :]
+    *product_refs, out_ref, scratch = rest
     finish_rows(pair_ref, gate_ref, product_refs, w_out_ref, gain_ref, scratch, out_ref)
 
 
 def middle_kernel(
     chain_ref, block_mask_ref, pair_ref, gate_ref, w_out_ref, gain_out_ref, w_ref, gain_in_ref, *rest
 ):
-    product_refs, rest = rest[: 2 * COUNT], rest[2 * COUNT :]
-    out_ref, outs, (update, w_t, scratch) = rest[0], rest[1 : 1 + 4 * COUNT], rest[1 + 4 * COUNT :]
+    product_refs, rest = rest[: 2 * len(OUT_SIZES)], rest[2 * len(OUT_SIZES) :]
+    out_ref, outs, (update, w_t, scratch) = rest[0], rest[1:-3], rest[-3:]
     turn_weights(w_ref, w_t)
     finish_rows(pair_ref, gate_ref, product_refs, w_out_ref, gain_out_ref, update, out_ref)
     rows = out_ref[...].reshape(-1, out_ref.shape[-1])
     normed = norm_rows(rows, gain_in_ref[...])
-    project_rows(normed, tile_mask(chain_ref, block_mask_ref), w_t, scratch, outs)
-
-
-def outgoing_kernel(
-    l_own, l_x, l_pair, l_pair_x, r_own, r_x, r_pair, r_pair_x, r_far, r_far_x, r_near, r_near_x, *rest
-):
-    own, pair, sent, rights = rest
-    size = l_own.shape[-1]
-    rights[0] = jnp.concatenate([r_own[0], r_x[0]], 1)
-    rights[1] = jnp.concatenate([r_pair[0], r_pair_x[0]], 1)
-    rights[2] = jnp.concatenate([r_far[0], r_far_x[0]], 1)
-    rights[3] = jnp.concatenate([r_near[0], r_near_x[0]], 1)
-    lefts = jnp.concatenate(
-        [jnp.concatenate([l_own[0], l_x[0]], 1), jnp.concatenate([l_pair[0], l_pair_x[0]], 1)], 0
-    )
+    project_rows(normed, tile_mask(chain_ref, block_mask_ref), w_t, scratch, outs, IN_SIZES)
+
+
+def outgoing_kernel(left, left_pair, right, right_pair, right_far, right_near, outs, rights):
+    *kept, pair, sent = outs
+    for k, blocks in enumerate((right, right_pair, right_far, right_near)):
+        rights[k] = jnp.concatenate(blocks, 1)
+    lefts = jnp.concatenate([jnp.concatenate(left, 1), jnp.concatenate(left_pair, 1)], 0)
+    size = lefts.shape[0] // 2
     here = lax.axis_index("row") ^ lax.axis_index("col")
     for place in range(4):
         terms = dot(lefts, rights[here ^ place], NT).astype(jnp.bfloat16)
@@ -219,27 +225,37 @@
             sent[0, place // 2, 0] = terms[:size]
             sent[1, place // 2, 0] = terms[size:]
         else:
-            own[place // 2, 0] = terms[:size]
+            kept[place // 2][0] = terms[:size]
             pair[place // 2, 0] = terms[size:]
 
 
-def incoming_kernel(
-    l_own, l_x, l_core, l_core_x, l_pair, l_pair_x, l_pair_core, l_pair_core_x, r_own, r_x, r_pair, r_pair_x, *rest
-):
-    *outs, lefts = rest
-    size = l_own.shape[-1]
-    lefts[0] = jnp.concatenate([l_own[0], l_pair[0]], 0)
-    lefts[1] = jnp.concatenate([l_core[0], l_pair_core[0]], 0)
-    lefts[2] = jnp.concatenate([l_x[0], l_pair_x[0]], 0)
-    lefts[3] = jnp.concatenate([l_core_x[0], l_pair_core_x[0]], 0)
-    rights = jnp.concatenate(
-        [jnp.concatenate([r_own[0], r_x[0]], 1), jnp.concatenate([r_pair[0], r_pair_x[0]], 1)], 0
-    )
+def incoming_kernel(left, left_core, left_pair, left_pair_core, right, right_pair, outs, lefts):
+    *kept, pair, far, near = outs
+    for k in range(2):
+        lefts[2 * k] = jnp.concatenate([left[k], left_pair[k]], 0)
+        lefts[2 * k + 1] = jnp.concatenate([left_core[k], left_pair_core[k]], 0)
+    rights = jnp.concatenate([jnp.concatenate(right, 1), jnp.concatenate(right_pair, 1)], 0)
+    size = rights.shape[1] // 2
     here = lax.axis_index("row") ^ lax.axis_index("col")
-    for place, out in enumerate(outs):
+    for place in range(4):
         terms = dot(lefts[here ^ place], rights, TN).astype(jnp.bfloat16)
-        out[0, 0] = terms[:, :size]
-        out[1, 0] = terms[:, size:]
+        for k in range(2):
+            block = terms[:, k * size : (k + 1) * size]
+            if place == 0:
+                kept[k][0] = block
+            else:
+                (pair, far, near)[place - 1][k, 0] = block
+
+
+def pieces_kernel(kernel, counts, *refs):
+    operands, position = [], 0
+    for count in counts:
+        if count == 1:
+            operands.append([refs[position][0, 0], refs[position][1, 0]])
+        else:
+            operands.append([refs[position][0], refs[position + 1][0]])
+        position += count
+    kernel(*operands, refs[position:-1], refs[-1])
 
 
 def params():
@@ -259,26 +275,32 @@
 
 
 def chunk_spec(shape):
-    return pl.BlockSpec((shape[0], STEP, shape[2]), lambda r: (0, r, 0))
+    lead = shape[:-2]
+    return pl.BlockSpec(lead + (STEP, shape[-1]), lambda r: (0,) * len(lead) + (r, 0))
 
 
 def cost(flops, nbytes, special=0):
-    return pl.CostEstimate(flops=int(flops), bytes_accessed=int(nbytes), transcendentals=int(special))
-
-
-def chunk_shapes(pair):
-    shapes = [(size,) + pair.shape[:2] for size in SIZES] * 4
+    return pl.CostEstimate(
+        flops=int(flops * TOLD), bytes_accessed=int(nbytes * TOLD), transcendentals=int(special * TOLD)
+    )
+
+
+def chunk_shapes(pair, sizes):
+    shapes = []
+    for n, size in enumerate(sizes):
+        shape = (size,) + pair.shape[:2]
+        shapes += [shape] * 4 if n == 0 else [shape, shape, (2,) + shape]
     return [jax.ShapeDtypeStruct(shape, jnp.bfloat16) for shape in shapes]
 
 
-def split(arrays):
-    return [arrays[k * COUNT : (k + 1) * COUNT] for k in range(4)]
+def split(arrays, sizes):
+    return [arrays[:4]] + [arrays[3 * n + 1 : 3 * n + 4] for n in range(1, len(sizes))]
 
 
 def project_call(chain, block_mask, pair, w_in, gain_in):
     rows, cols, _ = pair.shape
     width = w_in.shape[2] // 4
-    outs = chunk_shapes(pair)
+    outs = chunk_shapes(pair, OUT_SIZES)
     result = pl.pallas_call(
         project_kernel,
         grid=(rows // STEP,),
@@ -293,7 +315,7 @@
         cost_estimate=cost(2e9, 8 << 20, 4 << 20),
         name="project",
     )(chain, block_mask, pair, w_in, gain_in[:1])
-    return split(result)
+    return split(result, OUT_SIZES)
 
 
 def gate_call(pair, w_gate, gain_in, index):
@@ -330,7 +352,7 @@
 def middle_call(chain, block_mask, pair, gate, products, w_out, gain_wide, w_in, gain_in):
     rows, cols, _ = pair.shape
     width = w_out.shape[1]
-    outs = chunk_shapes(pair)
+    outs = chunk_shapes(pair, IN_SIZES)
     result = pl.pallas_call(
         middle_kernel,
         grid=(rows // STEP,),
@@ -348,101 +370,196 @@
         cost_estimate=cost(3e9, 18 << 20, 8 << 20),
         name="middle",
     )(chain, block_mask, pair, gate, w_out, gain_wide, w_in, gain_in[1:], *products)
-    return result[0], split(result[1:])
+    return result[0], split(result[1:], IN_SIZES)
 
 
 def product_call(kernel, operands, leads, scratch, name):
-    channels, size, _ = operands[0].shape
-    spec = pl.BlockSpec((1, size, size), lambda c: (c, 0, 0))
-
-    def out_spec(lead):
+    counts = [len(operand) if isinstance(operand, tuple) else 1 for operand in operands]
+    arrays = []
+    for operand in operands:
+        arrays += operand if isinstance(operand, tuple) else [operand]
+    channels, size, _ = shape = arrays[0].shape[-3:]
+
+    def spec(lead):
         return pl.BlockSpec(lead + (1, size, size), lambda c: (0,) * len(lead) + (c, 0, 0))
 
     return pl.pallas_call(
-        kernel,
+        functools.partial(pieces_kernel, kernel, counts),
         grid=(channels,),
-        in_specs=[spec] * len(operands),
-        out_specs=[out_spec(lead) for lead in leads],
-        out_shape=[jax.ShapeDtypeStruct(lead + operands[0].shape, jnp.bfloat16) for lead in leads],
+        in_specs=[spec(array.shape[:-3]) for array in arrays],
+        out_specs=[spec(lead) for lead in leads],
+        out_shape=[jax.ShapeDtypeStruct(lead + shape, jnp.bfloat16) for lead in leads],
         scratch_shapes=[pltpu.VMEM(scratch, jnp.bfloat16)],
         compiler_params=params(),
-        cost_estimate=cost(channels * 2 * (4 * size) ** 2 * size, operands[0].size * 2 * 20),
+        cost_estimate=cost(channels * 2 * (4 * size) ** 2 * size, channels * size * size * 2 * 20),
         name=name,
-    )(*operands)
-
-
-def inward(array):
-    return lax.ppermute(array, "row", [(0, 1), (3, 2)])
-
-
-def outward(array):
-    return lax.ppermute(array, "row", [(1, 0), (2, 3)])
-
-
-def across(array):
-    return lax.ppermute(array, "row", [(1, 2), (2, 1)])
-
-
-def other_core(array):
-    return lax.ppermute(array, "col", [(c, c ^ 1) for c in range(4)])
-
-
-def other_x(array):
-    return lax.ppermute(array, "col", [(c, c ^ 2) for c in range(4)])
-
-
-def share(own, pair):
+    )(*arrays)
+
+
+def after(array, *others):
+    return lax.optimization_barrier((array,) + others)[0]
+
+
+class Line:
+    PAIRS = {
+        "inward": ("row", [(0, 1), (3, 2)], 2),
+        "across": ("row", [(1, 2), (2, 1)], 2),
+        "outward": ("row", [(1, 0), (2, 3)], 2),
+        "x": ("col", [(c, c ^ 2) for c in range(4)], 1),
+        "core": ("col", [(c, c ^ 1) for c in range(4)], 0),
+    }
+
+    def __init__(self):
+        self.sent = []
+        self.kinds = {kind: [] for kind in self.PAIRS}
+
+    def __call__(self, kind, array, *others):
+        axis, pairs, depth = self.PAIRS[kind]
+        earlier = self.kinds[kind]
+        waits = list(others)
+        if depth:
+            waits += self.sent[-WINDOW:][:1] if len(self.sent) >= WINDOW else []
+            waits += [earlier[-depth]] if len(earlier) >= depth else []
+        if waits:
+            array = after(array, *waits)
+        result = lax.ppermute(array, axis, pairs)
+        earlier.append(result)
+        if depth:
+            self.sent.append(result)
+        return result
+
+
+def join(first, second):
+    return jnp.stack([first, second])
+
+
+def is_inner():
     row = lax.axis_index("row")
-    ready = jnp.where((row == 1) | (row == 2), own, outward(pair))
-    return ready[0], other_x(ready[1])
+    return (row == 1) | (row == 2)
+
+
+def outgoing(parts, gate):
+    send, inner = Line(), is_inner()
+    count = len(parts)
+    kept, come, returned = [], [], []
+
+    def tail(operands):
+        size = operands[1][0].shape[-1]
+        mine, mine_x, other, sent = product_call(
+            outgoing_kernel, operands, ((), (), (2,), (2, 2)), (4, size, 2 * size), "outgoing"
+        )
+        core = send("core", sent)
+        yield
+        moved = send("outward", other + core[1])
+        returned.append(moved)
+        yield
+        kept.append(jnp.where(inner, mine + core[0, 0], moved[0]))
+        come.append(send("x", jnp.where(inner, mine_x + core[0, 1], moved[1])))
+        yield
+
+    r_own, l_own, r_send, l_send = parts[0]
+    r_x = send("x", r_send)
+    r_pair = send("inward", r_own)
+    r_near = send("across", r_own)
+    l_pair = send("inward", l_own)
+    l_x = send("x", l_send, r_pair, r_near)
+    r_far = send("across", r_pair)
+    r_pair_x = send("inward", r_x, gate)
+    r_near_x = send("across", r_x)
+    x_next = send("x", parts[1][2], l_pair)
+    l_pair_x = send("inward", l_x)
+    r_far_x = send("across", r_pair_x)
+    chunk = [(l_own, l_x), (l_pair, l_pair_x), (r_own, r_x), (r_pair, r_pair_x), (r_far, r_far_x), (r_near, r_near_x)]
+    tails = []
+    for n in range(1, count):
+        r_own, l_own, _ = parts[n]
+        right, left = join(r_own, x_next[0]), join(l_own, x_next[1])
+        r_pair = send("inward", right)
+        r_near = send("across", right)
+        if n + 1 < count:
+            x_next = send("x", parts[n + 1][2])
+        if n > 1:
+            next(tails[n - 2])
+        l_pair = send("inward", left)
+        r_far = send("across", r_pair)
+        if n > 1:
+            next(tails[n - 2])
+        chunk[1] = tuple(after(piece, r_near) for piece in chunk[1]) if n == 1 else after(chunk[1], r_near)
+        tails.append(tail(chunk))
+        next(tails[n - 1])
+        chunk = [left, l_pair, right, r_pair, r_far, r_near]
+    if returned:
+        chunk[0] = after(chunk[0], returned[-1])
+    tails.append(tail(chunk))
+    next(tails[-2])
+    next(tails[-1])
+    next(tails[-2])
+    next(tails[-1])
+    next(tails[-1])
+    return kept + come
+
+
+def incoming(parts, gate):
+    send, inner = Line(), is_inner()
+    count = len(parts)
+    kept, come = [], []
+
+    def tail(operands):
+        size = operands[1].shape[-1]
+        mine, mine_x, other, far, near = product_call(
+            incoming_kernel, operands, ((), (), (2,), (2,), (2,)), (4, 2 * size, size), "incoming"
+        )
+        far = send("across", far)
+        near = send("across", near)
+        yield
+        moved = send("outward", other + far)
+        yield
+        kept.append(jnp.where(inner, mine + near[0], moved[0]))
+        come.append(send("x", jnp.where(inner, mine_x + near[1], moved[1])))
+        yield
+
+    r_own, l_own, r_send, l_send = parts[0]
+    l_x = send("x", l_send)
+    l_pair = send("inward", l_own)
+    r_pair = send("inward", r_own)
+    r_x = send("x", r_send, l_pair)
+    x_next = send("x", parts[1][2], r_pair)
+    l_pair_x = send("inward", l_x)
+    r_pair_x = send("inward", r_x)
+    left, left_pair = join(l_own, l_x), join(l_pair, l_pair_x)
+    chunk = [left, send("core", left), left_pair, send("core", left_pair), (r_own, r_x), (r_pair, r_pair_x)]
+    tails = []
+    for n in range(1, count):
+        r_own, l_own, _ = parts[n]
+        right, left = join(r_own, x_next[0]), join(l_own, x_next[1])
+        left_pair = send("inward", left, *((gate,) if n == 1 else ()))
+        tails.append(tail(chunk))
+        next(tails[n - 1])
+        if n + 1 < count:
+            x_next = send("x", parts[n + 1][2])
+        right_pair = send("inward", right)
+        if n > 1:
+            next(tails[n - 2])
+        next(tails[n - 1])
+        chunk = [left, send("core", left), left_pair, send("core", left_pair), right, right_pair]
+    tails.append(tail(chunk))
+    next(tails[-1])
+    next(tails[-2])
+    next(tails[-1])
+    next(tails[-1])
+    return kept + come
 
 
 def four_by_four(pair, chain, block_mask, w_in, w_gate, w_out, gain_in, gain_out):
-    size = pair.shape[0]
     gain_wide = jnp.broadcast_to(gain_out[:, :, None, None], gain_out.shape + (1, pair.shape[1]))
-
     parts = project_call(chain, block_mask, pair, w_in, gain_in)
     gate = gate_call(pair, w_gate, gain_in, 0)
-    products = []
-    for l_own, l_send, r_own, r_send in zip(*parts):
-        r_x = other_x(r_send)
-        l_x = other_x(l_send)
-        r_pair, r_near, l_pair = inward(r_own), across(r_own), inward(l_own)
-        r_far = across(r_pair)
-        r_pair_x, r_near_x, l_pair_x = inward(r_x), across(r_x), inward(l_x)
-        r_far_x = across(r_pair_x)
-        own, other, sent = product_call(
-            outgoing_kernel,
-            (l_own, l_x, l_pair, l_pair_x, r_own, r_x, r_pair, r_pair_x, r_far, r_far_x, r_near, r_near_x),
-            ((2,), (2,), (2, 2)),
-            (4, size, 2 * size),
-            "outgoing",
-        )
-        come = other_core(sent)
-        products.append(share(own + come[0], other + come[1]))
-    products = [p[0] for p in products] + [p[1] for p in products]
+    products = outgoing(parts, gate)
     middle, parts = middle_call(
         chain, block_mask, pair, gate, products, w_out, gain_wide[0], w_in, gain_in
     )
     gate = gate_call(middle, w_gate, gain_in, 1)
-    products = []
-    for l_own, l_send, r_own, r_send in zip(*parts):
-        l_x = other_x(l_send)
-        r_x = other_x(r_send)
-        l_pair, r_pair = inward(l_own), inward(r_own)
-        l_pair_x, r_pair_x = inward(l_x), inward(r_x)
-        own, other, far, near = product_call(
-            incoming_kernel,
-            (l_own, l_x, other_core(l_own), other_core(l_x))
-            + (l_pair, l_pair_x, other_core(l_pair), other_core(l_pair_x))
-            + (r_own, r_x, r_pair, r_pair_x),
-            ((2,), (2,), (2,), (2,)),
-            (4, 2 * size, size),
-            "incoming",
-        )
-        other = other + across(far)
-        products.append(share(own + across(near), other))
-    products = [p[0] for p in products] + [p[1] for p in products]
+    products = incoming(parts, gate)
     return finish_call(middle, gate, products, w_out, gain_wide[1])
 
 

time: 440 us -> 427 us (0.970)
  waiting for transfers between devices: 225 us -> 205 us
  Pallas kernels: 90.5 us -> 95.8 us
    ppermute x81 -> x68, waiting for transfers between devices: 225 us -> 205 us  [__call__(): result = lax.ppermute(array, axis, pairs)]
    pallas_call x6 -> x7, Pallas kernels: 31.3 us -> 37.7 us  [product_call(): pl.pallas_call(functools.partial(pieces_kernel, kernel, counts), grid=(ch...]
    ppermute x81 -> x68, starting transfers between devices: 109 us -> 106 us  [__call__(): result = lax.ppermute(array, axis, pairs)]
  transfers between devices with their start and end apart: 81 -> 68, of which waited for: 43 -> 32; matrix products, arithmetic and copies ran while one was open for 1% -> 2% of each run, Pallas kernels for 11% -> 13%
where the time goes in v3:
time: 427 us; the launch traced here: 423 us
  waiting for transfers between devices  205 us (48%)
  starting transfers between devices  106 us (25%)
  Pallas kernels  95.8 us (22%)
  local copies, waits for them, and re-layouts  9.44 us (2%)
  other arithmetic  6.86 us (2%)
    ppermute x68, waiting for transfers between devices, __call__(): result = lax.ppermute(array, axis, pairs)  205 us
    ppermute x68, starting transfers between devices, __call__(): result = lax.ppermute(array, axis, pairs)  106 us
    pallas_call x7, Pallas kernels, product_call(): pl.pallas_call(functools.partial(pieces_kernel, kernel, counts), grid=(ch...  37.7 us
    pallas_call x2, Pallas kernels, gate_call(): pl.pallas_call(gate_kernel, grid=(pair.shape[0] // STEP,), in_specs=[tile...  18.2 us
    pallas_call x1, Pallas kernels, middle_call(): pl.pallas_call(middle_kernel, grid=(rows // STEP,), in_specs=[SMEM_SPEC,...  17.8 us
    pallas_call x1, Pallas kernels, project_call(): pl.pallas_call(project_kernel, grid=(rows // STEP,), in_specs=[SMEM_SPEC,...  12.7 us
    pallas_call x1, Pallas kernels, finish_call(): pl.pallas_call(finish_kernel, grid=(rows // STEP,), in_specs=[tile_spec(p...  9.49 us
  transfers between devices with their start and end apart: 68, of which 32 were waited for; matrix products, arithmetic and copies ran while one was open for 2% of the time, Pallas kernels for 13%

profile of v3, /device:TPU:16, one launch (start us, length us, event | category | flops | bytes accessed | tf_op | source)
XLA Modules:
  0.0 423.5 jit_solution(1373171611767437196)
XLA Ops:
  3.0 12.7 %project.1 = (bf16[12,128,128]{2,1,0:T(8,128)(2,1)S(1)}, bf16[12,128,128]{2,1,0:T(8,128)(2,1)S(1)}, bf16[12,128,128]{2,1,0:T(8,128)(2,1)S(1)}, bf16[12,128,128]{...) custom-call(s32[4]{0:T(128)S(1)} %copy-done.8, ...), custom_call_target="tpu_custom_call" | custom-call | flops 100000000 | bytes 419430 | tf_op jit(solution)/shard_map/project/pallas_call | solution.py:304
  22.2 7.4 %collective-permute-done.refs_6_ = bf16[12,128,128]{2,1,0:T(8,128)(2,1)S(1)} collective-permute-done((bf16[12,128,128]{2,1,0:T(8,128)(2,1)S(1)}, bf16[12,128,128]{2,1,0:T(8,128)(2,1)S(1)}, u32[]{:S(2)}, u32[]{:S(2)}) %collective-permute-start) | collective-permute-done | bytes 393248 | tf_op jit(solution)/shard_map/ppermute | solution.py:425
  44.6 9.1 %gate.2.gate_ref = bf16[128,128,128]{2,1,0:T(8,128)(2,1)S(1)} custom-call(bf16[128,128,128]{2,1,0:T(8,128)(2,1)} %pair_ref.5, bf16[2,128,128]{2,1,0:T(8,128)(2,1)S(1)} %copy-done.4, f32[1,128]{1,0:T(1,128)S(1)} %get-tuple-element.252.gain_ref), custom_call_target="tpu_custom_call" | custom-call | flops 100000000 | bytes 419430 | tf_op jit(solution)/shard_map/gate/pallas_call | solution.py:323
  67.4 16.8 %collective-permute-done.10.refs_8_ = bf16[12,128,128]{2,1,0:T(8,128)(2,1)S(1)} collective-permute-done((bf16[12,128,128]{2,1,0:T(8,128)(2,1)S(1)}, bf16[12,128,128]{2,1,0:T(8,128)(2,1)S(1)}, u32[]{:S(2)}, u32[]{:S(2)}) %collective-permute-start.10) | collective-permute-done | bytes 393248 | tf_op jit(solution)/shard_map/ppermute | solution.py:425
  93.8 6.4 %outgoing.3 = (bf16[12,128,128]{2,1,0:T(8,128)(2,1)S(1)}, bf16[12,128,128]{2,1,0:T(8,128)(2,1)S(1)}, bf16[2,12,128,128]{3,2,1,0:T(8,128)(2,1)}, bf16[2,2,12,128,128]{4,3,2,1,0:T(8,128)(2,1)}) custom-call(bf16[12,128,128]{2,1,0:T(8,128)(2,1)S(1)} %get-tuple-element.115.refs_0_, bf16[12,128,128]{2,1,0:T(8,128)(2,1)S(1)} %collective-permute-done.3.refs_1_, ...), custom_call_target="tpu_custom_call" | custom-call | flops 40265320 | bytes 393216 | tf_op jit(solution)/shard_map/outgoing/pallas_call | solution.py:386
  107.3 7.3 %collective-permute-done.13 = bf16[2,8,128,128]{3,2,1,0:T(8,128)(2,1)S(1)} collective-permute-done((bf16[2,8,128,128]{3,2,1,0:T(8,128)(2,1)S(1)}, bf16[2,8,128,128]{3,2,1,0:T(8,128)(2,1)S(1)}, u32[]{:S(2)}, u32[]{:S(2)}) %collective-permute-start.13) | collective-permute-done | bytes 524320 | tf_op jit(solution)/shard_map/ppermute | solution.py:425
  123.7 11.8 %collective-permute-done.16.refs_5_ = bf16[2,8,128,128]{3,2,1,0:T(8,128)(2,1)S(1)} collective-permute-done((bf16[2,8,128,128]{3,2,1,0:T(8,128)(2,1)S(1)}, bf16[2,8,128,128]{3,2,1,0:T(8,128)(2,1)S(1)}, u32[]{:S(2)}, u32[]{:S(2)}) %collective-permute-start.16) | collective-permute-done | bytes 524320 | tf_op jit(solution)/shard_map/ppermute | solution.py:425
  135.5 8.8 %outgoing.4 = (bf16[12,128,128]{2,1,0:T(8,128)(2,1)S(1)}, bf16[12,128,128]{2,1,0:T(8,128)(2,1)S(1)}, bf16[2,12,128,128]{3,2,1,0:T(8,128)(2,1)S(1)}, bf16[2,2,12,128,128]{4,3,2,1,0:T(8,128)(2,1)}) custom-call(bf16[2,12,128,128]{3,2,1,0:T(8,128)(2,1)S(1)} %pad_maximum_fusion.1.refs_0_, bf16[2,12,128,128]{3,2,1,0:T(8,128)(2,1)S(1)} %collective-permute-done.15.refs_1_, ...), custom_call_target="tpu_custom_call" | custom-call | flops 40265320 | bytes 393216 | tf_op jit(solution)/shard_map/outgoing/pallas_call | solution.py:386
  150.5 13.0 %collective-permute-done.14 = bf16[2,12,128,128]{3,2,1,0:T(8,128)(2,1)S(1)} collective-permute-done((bf16[2,12,128,128]{3,2,1,0:T(8,128)(2,1)S(1)}, bf16[2,12,128,128]{3,2,1,0:T(8,128)(2,1)S(1)}, u32[]{:S(2)}, u32[]{:S(2)}) %collective-permute-start.14) | collective-permute-done | bytes 786464 | tf_op jit(solution)/shard_map/ppermute | solution.py:425
  179.6 11.9 %collective-permute-done.20 = bf16[2,12,128,128]{3,2,1,0:T(8,128)(2,1)} collective-permute-done((bf16[2,12,128,128]{3,2,1,0:T(8,128)(2,1)S(1)}, bf16[2,12,128,128]{3,2,1,0:T(8,128)(2,1)}, u32[]{:S(2)}, u32[]{:S(2)}) %collective-permute-start.20) | collective-permute-done | bytes 786464 | tf_op jit(solution)/shard_map/ppermute | solution.py:425
  193.8 8.5 %collective-permute-done.25 = bf16[2,8,128,128]{3,2,1,0:T(8,128)(2,1)S(1)} collective-permute-done((bf16[2,8,128,128]{3,2,1,0:T(8,128)(2,1)S(1)}, bf16[2,8,128,128]{3,2,1,0:T(8,128)(2,1)S(1)}, u32[]{:S(2)}, u32[]{:S(2)}) %collective-permute-start.25) | collective-permute-done | bytes 524320 | tf_op jit(solution)/shard_map/ppermute | solution.py:425
  204.5 7.0 %collective-permute-done.28.rest_5_ = bf16[8,128,128]{2,1,0:T(8,128)(2,1)S(1)} collective-permute-done((bf16[8,128,128]{2,1,0:T(8,128)(2,1)S(1)}, bf16[8,128,128]{2,1,0:T(8,128)(2,1)S(1)}, u32[]{:S(2)}, u32[]{:S(2)}) %collective-permute-start.28) | collective-permute-done | bytes 262176 | tf_op jit(solution)/shard_map/ppermute | solution.py:425
  211.7 17.8 %middle.1 = (bf16[128,128,128]{2,1,0:T(8,128)(2,1)}, bf16[6,128,128]{2,1,0:T(8,128)(2,1)S(1)}, bf16[6,128,128]{2,1,0:T(8,128)(2,1)S(1)}, bf16[6,128,128]{2,1,0:T...) custom-call(s32[4]{0:T(128)S(1)} %copy-done.9, ...), custom_call_target="tpu_custom_call" | custom-call | flops 150000000 | bytes 943718 | tf_op jit(solution)/shard_map/middle/pallas_call | solution.py:356
  249.9 9.1 %gate.3.gate_ref = bf16[128,128,128]{2,1,0:T(8,128)(2,1)S(1)} custom-call(bf16[128,128,128]{2,1,0:T(8,128)(2,1)} %get-tuple-element.163.pair_ref, bf16[2,128,128]{2,1,0:T(8,128)(2,1)S(1)} %copy-done.4, f32[1,128]{1,0:T(1,128)S(1)} %get-tuple-element.251.gain_in_ref.gain_ref), custom_call_target="tpu_custom_call" | custom-call | flops 100000000 | bytes 419430 | tf_op jit(solution)/shard_map/gate/pallas_call | solution.py:323
  265.7 12.3 %collective-permute-done.36.refs_7_ = bf16[6,128,128]{2,1,0:T(8,128)(2,1)S(1)} collective-permute-done((bf16[6,128,128]{2,1,0:T(8,128)(2,1)S(1)}, bf16[6,128,128]{2,1,0:T(8,128)(2,1)S(1)}, u32[]{:S(2)}, u32[]{:S(2)}) %collective-permute-start.36) | collective-permute-done | bytes 196640 | tf_op jit(solution)/shard_map/ppermute | solution.py:425
  285.9 9.4 %collective-permute-done.39 = bf16[2,6,128,128]{3,2,1,0:T(8,128)(2,1)S(1)} collective-permute-done((bf16[2,6,128,128]{3,2,1,0:T(8,128)(2,1)S(1)}, bf16[2,6,128,128]{3,2,1,0:T(8,128)(2,1)S(1)}, u32[]{:S(2)}, u32[]{:S(2)}) %collective-permute-start.39) | collective-permute-done | bytes 393248 | tf_op jit(solution)/shard_map/ppermute | solution.py:425
  303.1 6.6 %incoming.5 = (bf16[10,128,128]{2,1,0:T(8,128)(2,1)S(1)}, bf16[10,128,128]{2,1,0:T(8,128)(2,1)S(1)}, bf16[2,10,128,128]{3,2,1,0:T(8,128)(2,1)S(1)}, bf16[2,10,12...) custom-call(bf16[2,10,128,128]{3,2,1,0:T(8,128)(2,1)S(1)} %pad_maximum_fusion.2.refs_0_, ...), custom_call_target="tpu_custom_call" | custom-call | flops 33554432 | bytes 327680 | tf_op jit(solution)/shard_map/incoming/pallas_call | solution.py:386
  317.1 12.0 %collective-permute-done.47 = bf16[2,10,128,128]{3,2,1,0:T(8,128)(2,1)S(1)} collective-permute-done((bf16[2,10,128,128]{3,2,1,0:T(8,128)(2,1)S(1)}, bf16[2,10,128,128]{3,2,1,0:T(8,128)(2,1)S(1)}, u32[]{:S(2)}, u32[]{:S(2)}) %collective-permute-start.47) | collective-permute-done | bytes 655392 | tf_op jit(solution)/shard_map/ppermute | solution.py:425
  330.7 12.1 %collective-permute-done.46 = bf16[2,10,128,128]{3,2,1,0:T(8,128)(2,1)S(1)} collective-permute-done((bf16[2,10,128,128]{3,2,1,0:T(8,128)(2,1)S(1)}, bf16[2,10,128,128]{3,2,1,0:T(8,128)(2,1)S(1)}, u32[]{:S(2)}, u32[]{:S(2)}) %collective-permute-start.46) | collective-permute-done | bytes 655392 | tf_op jit(solution)/shard_map/ppermute | solution.py:425
  344.9 6.6 %incoming.6 = (bf16[10,128,128]{2,1,0:T(8,128)(2,1)S(1)}, bf16[10,128,128]{2,1,0:T(8,128)(2,1)S(1)}, bf16[2,10,128,128]{3,2,1,0:T(8,128)(2,1)S(1)}, bf16[2,10,12...) custom-call(bf16[2,10,128,128]{3,2,1,0:T(8,128)(2,1)S(1)} %pad_maximum_fusion.4.refs_0_, ...), custom_call_target="tpu_custom_call" | custom-call | flops 33554432 | bytes 327680 | tf_op jit(solution)/shard_map/incoming/pallas_call | solution.py:386
  362.1 7.6 %collective-permute-done.55 = bf16[2,10,128,128]{3,2,1,0:T(8,128)(2,1)S(1)} collective-permute-done((bf16[2,10,128,128]{3,2,1,0:T(8,128)(2,1)S(1)}, bf16[2,10,128,128]{3,2,1,0:T(8,128)(2,1)S(1)}, u32[]{:S(2)}, u32[]{:S(2)}) %collective-permute-start.55) | collective-permute-done | bytes 655392 | tf_op jit(solution)/shard_map/ppermute | solution.py:425
  380.8 8.5 %collective-permute-done.53 = bf16[2,10,128,128]{3,2,1,0:T(8,128)(2,1)S(1)} collective-permute-done((bf16[2,10,128,128]{3,2,1,0:T(8,128)(2,1)S(1)}, bf16[2,10,128,128]{3,2,1,0:T(8,128)(2,1)S(1)}, u32[]{:S(2)}, u32[]{:S(2)}) %collective-permute-start.53) | collective-permute-done | bytes 655392 | tf_op jit(solution)/shard_map/ppermute | solution.py:425
  392.0 5.7 %collective-permute-done.63 = bf16[2,6,128,128]{3,2,1,0:T(8,128)(2,1)S(1)} collective-permute-done((bf16[2,6,128,128]{3,2,1,0:T(8,128)(2,1)S(1)}, bf16[2,6,128,128]{3,2,1,0:T(8,128)(2,1)S(1)}, u32[]{:S(2)}, u32[]{:S(2)}) %collective-permute-start.63) | collective-permute-done | bytes 393248 | tf_op jit(solution)/shard_map/ppermute | solution.py:425
  414.0 9.5 %finish.1 = bf16[128,128,128]{2,1,0:T(8,128)(2,1)} custom-call(bf16[128,128,128]{2,1,0:T(8,128)(2,1)} %get-tuple-element.163.pair_ref, bf16[128,128,128]{2,1,0:T(8,128)(2,1)} %copy-done, bf16[2,64,128]{2,1,0:T(8,128)(2,1)S(1)} %copy-done.5, f32[64,1,128]{2,1,0:T(1,128)S(1)} %broadcast_in_dim.15.gain_ref, ...), custom_call_target="tpu_custom_call" | custom-call | flops 50000000 | bytes 734003 | tf_op jit(solution)/shard_map/finish/pallas_call | solution.py:338
  (201 shorter events, 184.7 us)
Async XLA Ops:
  57.2 31.2 %collective-permute-start.7 = (bf16[2,12,128,128]{3,2,1,0:T(8,128)(2,1)S(1)}, bf16[2,12,128,128]{3,2,1,0:T(8,128)(2,1)S(1)}, u32[]{:S(2)}, u32[]{:S(2)}) collective-permute-start(bf16[2,12,128,128]{3,2,1,0:T(8,128)(2,1)S(1)} %pad_maximum_fusion.refs_2_), channel_id=1, source_target_pairs={{4,8},{8,4},{5,9},{9,5},{6,10},{10,6},{7,11},{11,7},{20,24},{24,20... | collective-permute-start | bytes 2359304 | tf_op jit(solution)/shard_map/ppermute | solution.py:425
  60.5 23.7 %collective-permute-start.10 = (bf16[12,128,128]{2,1,0:T(8,128)(2,1)S(1)}, bf16[12,128,128]{2,1,0:T(8,128)(2,1)S(1)}, u32[]{:S(2)}, u32[]{:S(2)}) collective-permute-start(bf16[12,128,128]{2,1,0:T(8,128)(2,1)S(1)} %collective-permute-done.refs_6_), channel_id=1, source_target_pairs={{4,8},{8,4},{5,9},{9,5},{6,10},{10,6},{7,11},{11,7},{20,24},{24,20... | collective-permute-start | bytes 1179656 | tf_op jit(solution)/shard_map/ppermute | solution.py:425
  63.1 25.3 %collective-permute-start.8 = (bf16[12,128,128]{2,1,0:T(8,128)(2,1)S(1)}, bf16[12,128,128]{2,1,0:T(8,128)(2,1)S(1)}, u32[]{:S(2)}, u32[]{:S(2)}) collective-permute-start(bf16[12,128,128]{2,1,0:T(8,128)(2,1)S(1)} %collective-permute-done.3.refs_1_), channel_id=1, source_target_pairs={{0,4},{12,8},{1,5},{13,9},{2,6},{14,10},{3,7},{15,11},{16,20},{28,... | collective-permute-start | bytes 1179656 | tf_op jit(solution)/shard_map/ppermute | solution.py:425
  100.2 44.1 %collective-permute-start.12 = (bf16[2,2,12,128,128]{4,3,2,1,0:T(8,128)(2,1)}, bf16[2,2,12,128,128]{4,3,2,1,0:T(8,128)(2,1)S(1)}, u32[]{:S(2)}, u32[]{:S(2)}) collective-permute-start(bf16[2,2,12,128,128]{4,3,2,1,0:T(8,128)(2,1)} %get-tuple-element.132), channel_id=1, source_target_pairs={{0,1},{1,0},{2,3},{3,2},{4,5},{5,4},{6,7},{7,6},{8,9},{9,8},{10,11... | collective-permute-start | bytes 4718600 | tf_op jit(solution)/shard_map/ppermute | solution.py:425
  101.5 22.3 %collective-permute-start.15 = (bf16[2,12,128,128]{3,2,1,0:T(8,128)(2,1)S(1)}, bf16[2,12,128,128]{3,2,1,0:T(8,128)(2,1)S(1)}, u32[]{:S(2)}, u32[]{:S(2)}) collective-permute-start(bf16[2,12,128,128]{3,2,1,0:T(8,128)(2,1)S(1)} %pad_maximum_fusion.1.refs_0_), channel_id=1, source_target_pairs={{0,4},{12,8},{1,5},{13,9},{2,6},{14,10},{3,7},{15,11},{16,20},{28,... | collective-permute-start | bytes 2359304 | tf_op jit(solution)/shard_map/ppermute | solution.py:425
  104.0 31.6 %collective-permute-start.18 = (bf16[2,12,128,128]{3,2,1,0:T(8,128)(2,1)S(1)}, bf16[2,12,128,128]{3,2,1,0:T(8,128)(2,1)S(1)}, u32[]{:S(2)}, u32[]{:S(2)}) collective-permute-start(bf16[2,12,128,128]{3,2,1,0:T(8,128)(2,1)S(1)} %collective-permute-done.17.refs_3_), channel_id=1, source_target_pairs={{4,8},{8,4},{5,9},{9,5},{6,10},{10,6},{7,11},{11,7},{20,24},{24,20... | collective-permute-start | bytes 2359304 | tf_op jit(solution)/shard_map/ppermute | solution.py:425
  114.7 20.8 %collective-permute-start.16 = (bf16[2,8,128,128]{3,2,1,0:T(8,128)(2,1)S(1)}, bf16[2,8,128,128]{3,2,1,0:T(8,128)(2,1)S(1)}, u32[]{:S(2)}, u32[]{:S(2)}) collective-permute-start(bf16[2,8,128,128]{3,2,1,0:T(8,128)(2,1)S(1)} %pad_maximum_fusion.6.refs_2_), channel_id=1, source_target_pairs={{4,8},{8,4},{5,9},{9,5},{6,10},{10,6},{7,11},{11,7},{20,24},{24,20... | collective-permute-start | bytes 1572872 | tf_op jit(solution)/shard_map/ppermute | solution.py:425
  117.7 29.4 %collective-permute-start.22 = (bf16[2,8,128,128]{3,2,1,0:T(8,128)(2,1)S(1)}, bf16[2,8,128,128]{3,2,1,0:T(8,128)(2,1)S(1)}, u32[]{:S(2)}, u32[]{:S(2)}) collective-permute-start(bf16[2,8,128,128]{3,2,1,0:T(8,128)(2,1)S(1)} %pad_maximum_fusion.6.refs_2_), channel_id=1, source_target_pairs={{0,4},{12,8},{1,5},{13,9},{2,6},{14,10},{3,7},{15,11},{16,20},{28,... | collective-permute-start | bytes 1572872 | tf_op jit(solution)/shard_map/ppermute | solution.py:425
  144.3 23.8 %collective-permute-start.19 = (bf16[2,2,12,128,128]{4,3,2,1,0:T(8,128)(2,1)}, bf16[2,2,12,128,128]{4,3,2,1,0:T(8,128)(2,1)S(1)}, u32[]{:S(2)}, u32[]{:S(2)}) collective-permute-start(bf16[2,2,12,128,128]{4,3,2,1,0:T(8,128)(2,1)} %get-tuple-element.145), channel_id=1, source_target_pairs={{0,1},{1,0},{2,3},{3,2},{4,5},{5,4},{6,7},{7,6},{8,9},{9,8},{10,11... | collective-permute-start | bytes 4718600 | tf_op jit(solution)/shard_map/ppermute | solution.py:425
  169.3 22.2 %collective-permute-start.20 = (bf16[2,12,128,128]{3,2,1,0:T(8,128)(2,1)S(1)}, bf16[2,12,128,128]{3,2,1,0:T(8,128)(2,1)}, u32[]{:S(2)}, u32[]{:S(2)}) collective-permute-start(bf16[2,12,128,128]{3,2,1,0:T(8,128)(2,1)S(1)} %fusion), channel_id=1, source_target_pairs={{4,0},{8,12},{5,1},{9,13},{6,2},{10,14},{7,3},{11,15},{20,16},{24,... | collective-permute-start | bytes 2359304 | tf_op jit(solution)/shard_map/ppermute | solution.py:425
  175.8 26.5 %collective-permute-start.25 = (bf16[2,8,128,128]{3,2,1,0:T(8,128)(2,1)S(1)}, bf16[2,8,128,128]{3,2,1,0:T(8,128)(2,1)S(1)}, u32[]{:S(2)}, u32[]{:S(2)}) collective-permute-start(bf16[2,8,128,128]{3,2,1,0:T(8,128)(2,1)S(1)} %fusion.2), channel_id=1, source_target_pairs={{4,0},{8,12},{5,1},{9,13},{6,2},{10,14},{7,3},{11,15},{20,16},{24,... | collective-permute-start | bytes 1572872 | tf_op jit(solution)/shard_map/ppermute | solution.py:425
  261.2 24.3 %collective-permute-start.40 = (bf16[2,10,128,128]{3,2,1,0:T(8,128)(2,1)S(1)}, bf16[2,10,128,128]{3,2,1,0:T(8,128)(2,1)S(1)}, u32[]{:S(2)}, u32[]{:S(2)}) collective-permute-start(bf16[2,10,128,128]{3,2,1,0:T(8,128)(2,1)S(1)} %pad_maximum_fusion.2.refs_0_), channel_id=1, source_target_pairs={{0,4},{12,8},{1,5},{13,9},{2,6},{14,10},{3,7},{15,11},{16,20},{28,... | collective-permute-start | bytes 1966088 | tf_op jit(solution)/shard_map/ppermute | solution.py:425
  262.6 23.1 %collective-permute-start.45 = (bf16[2,10,128,128]{3,2,1,0:T(8,128)(2,1)S(1)}, bf16[2,10,128,128]{3,2,1,0:T(8,128)(2,1)S(1)}, u32[]{:S(2)}, u32[]{:S(2)}) collective-permute-start(bf16[2,10,128,128]{3,2,1,0:T(8,128)(2,1)S(1)} %copy-done.20), channel_id=1, source_target_pairs={{0,2},{1,3},{2,0},{3,1},{4,6},{5,7},{6,4},{7,5},{8,10},{9,11},{10,... | collective-permute-start | bytes 1966088 | tf_op jit(solution)/shard_map/ppermute | solution.py:425
  278.0 22.3 %collective-permute-start.44 = (bf16[2,10,128,128]{3,2,1,0:T(8,128)(2,1)S(1)}, bf16[2,10,128,128]{3,2,1,0:T(8,128)(2,1)S(1)}, u32[]{:S(2)}, u32[]{:S(2)}) collective-permute-start(bf16[2,10,128,128]{3,2,1,0:T(8,128)(2,1)S(1)} %pad_maximum_fusion.3.refs_4_), channel_id=1, source_target_pairs={{0,4},{12,8},{1,5},{13,9},{2,6},{14,10},{3,7},{15,11},{16,20},{28,... | collective-permute-start | bytes 1966088 | tf_op jit(solution)/shard_map/ppermute | solution.py:425
  281.8 20.2 %collective-permute-start.42 = (bf16[2,10,128,128]{3,2,1,0:T(8,128)(2,1)S(1)}, bf16[2,10,128,128]{3,2,1,0:T(8,128)(2,1)S(1)}, u32[]{:S(2)}, u32[]{:S(2)}) collective-permute-start(bf16[2,10,128,128]{3,2,1,0:T(8,128)(2,1)S(1)} %pad_maximum_fusion.2.refs_0_), channel_id=1, source_target_pairs={{0,1},{1,0},{2,3},{3,2},{4,5},{5,4},{6,7},{7,6},{8,9},{9,8},{10,11... | collective-permute-start | bytes 1966088 | tf_op jit(solution)/shard_map/ppermute | solution.py:425
  295.3 21.6 %collective-permute-start.50 = (bf16[2,10,128,128]{3,2,1,0:T(8,128)(2,1)S(1)}, bf16[2,10,128,128]{3,2,1,0:T(8,128)(2,1)S(1)}, u32[]{:S(2)}, u32[]{:S(2)}) collective-permute-start(bf16[2,10,128,128]{3,2,1,0:T(8,128)(2,1)S(1)} %pad_maximum_fusion.4.refs_0_), channel_id=1, source_target_pairs={{0,4},{12,8},{1,5},{13,9},{2,6},{14,10},{3,7},{15,11},{16,20},{28,... | collective-permute-start | bytes 1966088 | tf_op jit(solution)/shard_map/ppermute | solution.py:425
  303.1 41.0 %collective-permute-start.49 = (bf16[2,10,128,128]{3,2,1,0:T(8,128)(2,1)S(1)}, bf16[2,10,128,128]{3,2,1,0:T(8,128)(2,1)S(1)}, u32[]{:S(2)}, u32[]{:S(2)}) collective-permute-start(bf16[2,10,128,128]{3,2,1,0:T(8,128)(2,1)S(1)} %pad_maximum_fusion.4.refs_0_), channel_id=1, source_target_pairs={{0,1},{1,0},{2,3},{3,2},{4,5},{5,4},{6,7},{7,6},{8,9},{9,8},{10,11... | collective-permute-start | bytes 1966088 | tf_op jit(solution)/shard_map/ppermute | solution.py:425
  312.9 29.9 %collective-permute-start.46 = (bf16[2,10,128,128]{3,2,1,0:T(8,128)(2,1)S(1)}, bf16[2,10,128,128]{3,2,1,0:T(8,128)(2,1)S(1)}, u32[]{:S(2)}, u32[]{:S(2)}) collective-permute-start(bf16[2,10,128,128]{3,2,1,0:T(8,128)(2,1)S(1)} %get-tuple-element.188), channel_id=1, source_target_pairs={{4,8},{8,4},{5,9},{9,5},{6,10},{10,6},{7,11},{11,7},{20,24},{24,20... | collective-permute-start | bytes 1966088 | tf_op jit(solution)/shard_map/ppermute | solution.py:425
  315.7 28.4 %collective-permute-start.52 = (bf16[2,10,128,128]{3,2,1,0:T(8,128)(2,1)S(1)}, bf16[2,10,128,128]{3,2,1,0:T(8,128)(2,1)S(1)}, u32[]{:S(2)}, u32[]{:S(2)}) collective-permute-start(bf16[2,10,128,128]{3,2,1,0:T(8,128)(2,1)S(1)} %pad_maximum_fusion.5.refs_4_), channel_id=1, source_target_pairs={{0,4},{12,8},{1,5},{13,9},{2,6},{14,10},{3,7},{15,11},{16,20},{28,... | collective-permute-start | bytes 1966088 | tf_op jit(solution)/shard_map/ppermute | solution.py:425
  317.0 27.1 %collective-permute-start.51 = (bf16[2,10,128,128]{3,2,1,0:T(8,128)(2,1)S(1)}, bf16[2,10,128,128]{3,2,1,0:T(8,128)(2,1)S(1)}, u32[]{:S(2)}, u32[]{:S(2)}) collective-permute-start(bf16[2,10,128,128]{3,2,1,0:T(8,128)(2,1)S(1)} %collective-permute-done.50.refs_2_), channel_id=1, source_target_pairs={{0,1},{1,0},{2,3},{3,2},{4,5},{5,4},{6,7},{7,6},{8,9},{9,8},{10,11... | collective-permute-start | bytes 1966088 | tf_op jit(solution)/shard_map/ppermute | solution.py:425
  329.3 50.2 %collective-permute-start.48 = (bf16[2,10,128,128]{3,2,1,0:T(8,128)(2,1)S(1)}, bf16[2,10,128,128]{3,2,1,0:T(8,128)(2,1)S(1)}, u32[]{:S(2)}, u32[]{:S(2)}) collective-permute-start(bf16[2,10,128,128]{3,2,1,0:T(8,128)(2,1)S(1)} %add.75), channel_id=1, source_target_pairs={{4,0},{8,12},{5,1},{9,13},{6,2},{10,14},{7,3},{11,15},{20,16},{24,... | collective-permute-start | bytes 1966088 | tf_op jit(solution)/shard_map/ppermute | solution.py:425
  369.7 19.6 %collective-permute-start.53 = (bf16[2,10,128,128]{3,2,1,0:T(8,128)(2,1)S(1)}, bf16[2,10,128,128]{3,2,1,0:T(8,128)(2,1)S(1)}, u32[]{:S(2)}, u32[]{:S(2)}) collective-permute-start(bf16[2,10,128,128]{3,2,1,0:T(8,128)(2,1)S(1)} %get-tuple-element.199), channel_id=1, source_target_pairs={{4,8},{8,4},{5,9},{9,5},{6,10},{10,6},{7,11},{11,7},{20,24},{24,20... | collective-permute-start | bytes 1966088 | tf_op jit(solution)/shard_map/ppermute | solution.py:425
  372.7 26.5 %collective-permute-start.57 = (bf16[2,10,128,128]{3,2,1,0:T(8,128)(2,1)S(1)}, bf16[2,10,128,128]{3,2,1,0:T(8,128)(2,1)S(1)}, u32[]{:S(2)}, u32[]{:S(2)}) collective-permute-start(bf16[2,10,128,128]{3,2,1,0:T(8,128)(2,1)S(1)} %add.77), channel_id=1, source_target_pairs={{4,0},{8,12},{5,1},{9,13},{6,2},{10,14},{7,3},{11,15},{20,16},{24,... | collective-permute-start | bytes 1966088 | tf_op jit(solution)/shard_map/ppermute | solution.py:425
  376.4 21.3 %collective-permute-start.63 = (bf16[2,6,128,128]{3,2,1,0:T(8,128)(2,1)S(1)}, bf16[2,6,128,128]{3,2,1,0:T(8,128)(2,1)S(1)}, u32[]{:S(2)}, u32[]{:S(2)}) collective-permute-start(bf16[2,6,128,128]{3,2,1,0:T(8,128)(2,1)S(1)} %get-tuple-element.217), channel_id=1, source_target_pairs={{4,8},{8,4},{5,9},{9,5},{6,10},{10,6},{7,11},{11,7},{20,24},{24,20... | collective-permute-start | bytes 1179656 | tf_op jit(solution)/shard_map/ppermute | solution.py:425
  (65 other events, 780.2 us)

commit v4 on v0

--- a/solution.py
+++ b/solution.py
@@ -1,9 +1,21 @@
+import functools
+
 import jax
 import jax.numpy as jnp
 from jax import lax
+from jax.experimental import pallas as pl
+from jax.experimental.pallas import tpu as pltpu
 from jax.sharding import PartitionSpec as P
 
 BLOCK = 128
+EPS = 1e-05
+OUT_SIZES = (12, 10, 6, 4)
+IN_SIZES = (8, 12, 8, 4)
+OUT_ORDER = {'l0': ('r0',), 'r0x': ('l0', 'second'), 'l0x': ('r0x', 'gate'), 'r1': ('l0x',), 'l1': ('r1',), 'r2': ('l1',), 'l2': ('r2',), 'r3': ('l2',), 'l3': ('r3',), 'f0': ('n0',), 'n0x': ('f0',), 'f0x': ('n0x',), 'n1': ('f0x',), 'f1': ('n1',), 'n2': ('f1',), 'f2': ('n2',), 'n3': ('f2',), 'f3': ('n3',), 'xl0': ('xr0',), 'x1': ('xl0',), 'x2': ('x1',), 'x3': ('x2',)}
+IN_ORDER = {'r0': ('l0',), 'l0x': ('r0', 'second'), 'r0x': ('l0x', 'gate'), 'l1': ('r0x',), 'r1': ('l1',), 'l2': ('r1',), 'r2': ('l2',), 'l3': ('r2',), 'r3': ('l3',), 'n0': ('f0',), 'f1': ('n0',), 'n1': ('f1',), 'f2': ('n1',), 'n2': ('f2',), 'f3': ('n2',), 'n3': ('f3',), 'xr0': ('xl0',), 'x1': ('xr0',), 'x2': ('x1',), 'x3': ('x2',)}
+STEP = 16
+TOLD = 0.05
+VMEM = 48 * 1024 * 1024
 
 
 def broadcast(block, axis, owner):
@@ -15,7 +27,7 @@
     mean = jnp.mean(values, -1, keepdims=True)
     centred = values - mean
     spread = jnp.mean(centred * centred, -1, keepdims=True)
-    return centred * lax.rsqrt(spread + 1e-05) * gain
+    return centred * lax.rsqrt(spread + EPS) * gain
 
 
 def project(pair, tile_mask, w_in, w_gate, gain_in):
@@ -40,7 +52,7 @@
     ).astype(jnp.bfloat16)
 
 
-def per_device(pair, chain, block_mask, w_in, w_gate, w_out, gain_in, gain_out):
+def any_mesh(pair, chain, block_mask, w_in, w_gate, w_out, gain_in, gain_out):
     tile_rows = pair.shape[0]
     tile_cols = pair.shape[1]
     block_count = chain.shape[0]
@@ -80,9 +92,552 @@
     return finish(middle, product, gate, w_out[1], gain_out[1])
 
 
+NN = (((1,), (0,)), ((), ()))
+NT = (((1,), (1,)), ((), ()))
+TN = (((0,), (0,)), ((), ()))
+SMEM_SPEC = pl.BlockSpec(memory_space=pltpu.SMEM)
+
+
+def dot(a, b, dims=NN):
+    return lax.dot_general(a, b, dims, preferred_element_type=jnp.float32)
+
+
+def norm_rows(rows, gain):
+    channels = rows.shape[-1]
+    place = lax.broadcasted_iota(jnp.int32, (channels, channels), 0)
+    same = place == lax.broadcasted_iota(jnp.int32, (channels, channels), 1)
+    centre = jnp.where(same, 1.0 - 1.0 / channels, -1.0 / channels).astype(jnp.bfloat16)
+    mean_of = jnp.full((2 * channels, channels), 1.0 / channels, jnp.bfloat16)
+    centred = dot(rows, centre)
+    square = centred * centred
+    high = square.astype(jnp.bfloat16)
+    low = (square - high.astype(jnp.float32)).astype(jnp.bfloat16)
+    spread = dot(jnp.concatenate([high, low], 1), mean_of)
+    return (centred * lax.rsqrt(spread + EPS) * gain).astype(jnp.bfloat16)
+
+
+def logistic(values):
+    return 0.5 * jnp.tanh(0.5 * values) + 0.5
+
+
+def tile_mask(chain_ref, block_mask_ref):
+    row, col = lax.axis_index("row"), lax.axis_index("col")
+    seen = (chain_ref[row] == chain_ref[col]) | (block_mask_ref[row, col] == 1)
+    return jnp.where(seen, 1.0, 0.0).astype(jnp.float32)
+
+
+def turn_weights(w_ref, w_t):
+    @pl.when(pl.program_id(0) == 0)
+    def _():
+        w_t[...] = w_ref[0].T
+
+
+def project_side(normed, mask, w_t, scratch, outs):
+    hidden = dot(w_t[...], normed, NT)
+    width = w_t.shape[0] // 2
+    half = width // 2
+    cols = normed.shape[0] // STEP
+    x = lax.axis_index("col") // 2
+    kept = mask * logistic(hidden[width:]) * hidden[:width]
+    for row in range(STEP):
+        scratch[pl.ds(row, width, stride=STEP), :] = kept[:, row * cols : (row + 1) * cols]
+    count = len(outs) // 2
+    for start, refs in ((x, outs[:count]), (1 - x, outs[count:])):
+        done = 0
+        for ref in refs:
+            size = ref.shape[-3]
+            rows = scratch[pl.ds(pl.multiple_of((start * half + done) * STEP, 8), size * STEP), :]
+            ref[...] = rows.astype(jnp.bfloat16).reshape(ref.shape)
+            done += size
+
+
+def first_kernel(chain_ref, block_mask_ref, pair_ref, w_ref, gain_ref, normed_ref, *rest):
+    *outs, w_t, scratch = rest
+    turn_weights(w_ref, w_t)
+    rows = pair_ref[...].reshape(-1, pair_ref.shape[-1])
+    normed = norm_rows(rows, gain_ref[0:1])
+    normed_ref[...] = normed.reshape(normed_ref.shape)
+    project_side(normed, tile_mask(chain_ref, block_mask_ref), w_t, scratch, outs)
+
+
+def second_kernel(count, chain_ref, block_mask_ref, normed_ref, w_ref, *rest):
+    *outs, w_t, scratch = rest[count:]
+    turn_weights(w_ref, w_t)
+    normed = normed_ref[...].reshape(-1, normed_ref.shape[-1])
+    project_side(normed, tile_mask(chain_ref, block_mask_ref), w_t, scratch, outs)
+
+
+def gate_kernel(normed_ref, w_ref, out_ref):
+    rows = normed_ref[...].reshape(-1, normed_ref.shape[-1])
+    out_ref[...] = logistic(dot(rows, w_ref[0])).astype(out_ref.dtype).reshape(out_ref.shape)
+
+
+def finish_rows(pair_ref, gate_ref, product_refs, w_out_ref, gain_ref, scratch, twice, out_ref):
+    width = w_out_ref.shape[1]
+    half = width // 2
+    cols = pair_ref.shape[1]
+    x = lax.axis_index("col") // 2
+    mine, others = pl.multiple_of(x * half, half), pl.multiple_of((1 - x) * half, half)
+
+    @pl.when(pl.program_id(0) == 0)
+    def _():
+        w_out = jnp.concatenate([w_out_ref[0, pl.ds(mine, half)], w_out_ref[0, pl.ds(others, half)]], 0)
+        none = jnp.zeros_like(w_out)
+        twice[...] = jnp.concatenate(
+            [jnp.concatenate([w_out, none], 1), jnp.concatenate([none, w_out], 1)], 0
+        )
+
+    gain = jnp.concatenate([gain_ref[pl.ds(mine, half)], gain_ref[pl.ds(others, half)]], 0)
+    product = jnp.concatenate([ref[...] for ref in product_refs], 0).astype(jnp.float32)
+    mean = jnp.sum(product, 0, keepdims=True) * (1.0 / width)
+    centred = product - mean
+    spread = jnp.sum(centred * centred, 0, keepdims=True) * (1.0 / width)
+    update = centred * lax.rsqrt(spread + EPS) * gain
+    scratch[...] = update.reshape(width * STEP, cols)
+    for row in range(0, STEP, 2):
+        two = jnp.concatenate(
+            [scratch[pl.ds(row, width, stride=STEP), :], scratch[pl.ds(row + 1, width, stride=STEP), :]], 0
+        )
+        changes = dot(two.astype(jnp.bfloat16), twice[...], TN)
+        for k in range(2):
+            change = changes[:, k * pair_ref.shape[2] : (k + 1) * pair_ref.shape[2]]
+            gate = gate_ref[row + k].astype(jnp.float32)
+            old = pair_ref[row + k].astype(jnp.float32)
+            out_ref[row + k] = (old + gate * change).astype(jnp.bfloat16)
+
+
+def finish_kernel(pair_ref, gate_ref, w_out_ref, gain_ref, *rest):
+    *product_refs, out_ref, scratch, twice = rest
+    finish_rows(pair_ref, gate_ref, product_refs, w_out_ref, gain_ref, scratch, twice, out_ref)
+
+
+def middle_kernel(
+    count, chain_ref, block_mask_ref, pair_ref, gate_ref, w_out_ref, gain_out_ref, w_ref, gain_in_ref, *rest
+):
+    product_refs, (out_ref, normed_ref, *outs, update, twice, w_t, scratch) = rest[:count], rest[count:]
+    turn_weights(w_ref, w_t)
+    finish_rows(pair_ref, gate_ref, product_refs, w_out_ref, gain_out_ref, update, twice, out_ref)
+    rows = out_ref[...].reshape(-1, out_ref.shape[-1])
+    normed = norm_rows(rows, gain_in_ref[1:2])
+    normed_ref[...] = normed.reshape(normed_ref.shape)
+    project_side(normed, tile_mask(chain_ref, block_mask_ref), w_t, scratch, outs)
+
+
+def outgoing_kernel(left, left_pair, right, right_pair, right_far, right_near, outs, rights):
+    *kept, pair, sent = outs
+    for k, blocks in enumerate((right, right_pair, right_far, right_near)):
+        rights[k] = jnp.concatenate(blocks, 1)
+    lefts = jnp.concatenate([jnp.concatenate(left, 1), jnp.concatenate(left_pair, 1)], 0)
+    size = lefts.shape[0] // 2
+    here = lax.axis_index("row") ^ lax.axis_index("col")
+    for place in range(4):
+        terms = dot(lefts, rights[here ^ place], NT).astype(jnp.bfloat16)
+        if place % 2:
+            sent[0, place // 2, 0] = terms[:size]
+            sent[1, place // 2, 0] = terms[size:]
+        else:
+            kept[place // 2][0] = terms[:size]
+            pair[place // 2, 0] = terms[size:]
+
+
+def incoming_kernel(left, left_core, left_pair, left_pair_core, right, right_pair, outs, lefts):
+    *kept, pair, far, near = outs
+    for k in range(2):
+        lefts[2 * k] = jnp.concatenate([left[k], left_pair[k]], 0)
+        lefts[2 * k + 1] = jnp.concatenate([left_core[k], left_pair_core[k]], 0)
+    rights = jnp.concatenate([jnp.concatenate(right, 1), jnp.concatenate(right_pair, 1)], 0)
+    size = rights.shape[1] // 2
+    here = lax.axis_index("row") ^ lax.axis_index("col")
+    for place in range(4):
+        terms = dot(lefts[here ^ place], rights, TN).astype(jnp.bfloat16)
+        for k in range(2):
+            block = terms[:, k * size : (k + 1) * size]
+            if place == 0:
+                kept[k][0] = block
+            else:
+                (pair, far, near)[place - 1][k, 0] = block
+
+
+def pieces_kernel(kernel, counts, *refs):
+    operands, position = [], 0
+    for count in counts:
+        if count == 1:
+            operands.append([refs[position][0, 0], refs[position][1, 0]])
+        else:
+            operands.append([refs[position][0], refs[position + 1][0]])
+        position += count
+    kernel(*operands, refs[position:-1], refs[-1])
+
+
+def params():
+    return pltpu.CompilerParams(vmem_limit_bytes=VMEM, dimension_semantics=("arbitrary",))
+
+
+def part(array, index):
+    return pl.BlockSpec((1,) + array.shape[1:], lambda *_: (index,) + (0,) * (array.ndim - 1))
+
+
+def whole(array):
+    return pl.BlockSpec(array.shape, lambda *_: (0,) * array.ndim)
+
+
+def tile_spec(tile):
+    return pl.BlockSpec((STEP,) + tile.shape[1:], lambda r: (r, 0, 0))
+
+
+def chunk_spec(shape):
+    lead = shape[:-2]
+    return pl.BlockSpec(lead + (STEP, shape[-1]), lambda r: (0,) * len(lead) + (r, 0))
+
+
+def cost(flops, nbytes, special=0):
+    return pl.CostEstimate(
+        flops=int(flops * TOLD), bytes_accessed=int(nbytes * TOLD), transcendentals=int(special * TOLD)
+    )
+
+
+LEFT, RIGHT = 0, 1
+
+
+def side_outs(pair, sizes, slot):
+    tile = pair.shape[:2]
+    shapes = [(size,) + tile for size in sizes + sizes[:1]] + [(2, size) + tile for size in sizes[1:]]
+
+    def spec(shape):
+        if len(shape) == 3:
+            return chunk_spec(shape)
+        return pl.BlockSpec((1, shape[1], STEP, shape[3]), lambda r: (slot, 0, r, 0))
+
+    return [jax.ShapeDtypeStruct(shape, jnp.bfloat16) for shape in shapes], [spec(shape) for shape in shapes]
+
+
+def side_weights(w_in, index, side):
+    return pl.BlockSpec((1, w_in.shape[1], w_in.shape[2] // 2), lambda *_: (index, 0, side))
+
+
+def side_scratch(pair, w_in):
+    width = w_in.shape[2] // 4
+    return [
+        pltpu.VMEM((w_in.shape[2] // 2, w_in.shape[1]), jnp.bfloat16),
+        pltpu.VMEM((width * STEP, pair.shape[1]), jnp.float32),
+    ]
+
+
+def finish_scratch(pair, w_out):
+    return [
+        pltpu.VMEM((w_out.shape[1] * STEP, pair.shape[1]), jnp.float32),
+        pltpu.VMEM((2 * w_out.shape[1], 2 * w_out.shape[2]), jnp.bfloat16),
+    ]
+
+
+def first_call(chain, block_mask, pair, w_in, gain_in):
+    outs, specs = side_outs(pair, OUT_SIZES, 0)
+    normed, *result = pl.pallas_call(
+        first_kernel,
+        grid=(pair.shape[0] // STEP,),
+        in_specs=[SMEM_SPEC, SMEM_SPEC, tile_spec(pair), side_weights(w_in, 0, RIGHT), whole(gain_in)],
+        out_specs=[tile_spec(pair)] + specs,
+        out_shape=[jax.ShapeDtypeStruct(pair.shape, pair.dtype)] + outs,
+        scratch_shapes=side_scratch(pair, w_in),
+        compiler_params=params(),
+        cost_estimate=cost(2e9, 8 << 20, 4 << 20),
+        name="project",
+    )(chain, block_mask, pair, w_in, gain_in)
+    return normed, result
+
+
+def second_call(chain, block_mask, normed, w_in, index, side, sizes, shared):
+    outs, specs = side_outs(normed, sizes, 1)
+    count = len(shared)
+    return pl.pallas_call(
+        functools.partial(second_kernel, count),
+        grid=(normed.shape[0] // STEP,),
+        in_specs=[SMEM_SPEC, SMEM_SPEC, tile_spec(normed), side_weights(w_in, index, side)]
+        + [pl.BlockSpec(memory_space=pl.ANY)] * count,
+        out_specs=specs,
+        out_shape=outs,
+        input_output_aliases={4 + k: len(outs) - count + k for k in range(count)},
+        scratch_shapes=side_scratch(normed, w_in),
+        compiler_params=params(),
+        cost_estimate=cost(1e9, 8 << 20, 2 << 20),
+        name="second",
+    )(chain, block_mask, normed, w_in, *shared)
+
+
+def gate_call(normed, w_gate, index):
+    return pl.pallas_call(
+        gate_kernel,
+        grid=(normed.shape[0] // STEP,),
+        in_specs=[tile_spec(normed), part(w_gate, index)],
+        out_specs=tile_spec(normed),
+        out_shape=jax.ShapeDtypeStruct(normed.shape, jnp.bfloat16),
+        compiler_params=params(),
+        cost_estimate=cost(1e9, 8 << 20, 2 << 20),
+        name="gate",
+    )(normed, w_gate)
+
+
+def finish_call(pair, gate, products, w_out, gain_wide):
+    return pl.pallas_call(
+        finish_kernel,
+        grid=(pair.shape[0] // STEP,),
+        in_specs=[tile_spec(pair), tile_spec(gate), part(w_out, 1), whole(gain_wide)]
+        + [chunk_spec(p.shape) for p in products],
+        out_specs=tile_spec(pair),
+        out_shape=jax.ShapeDtypeStruct(pair.shape, pair.dtype),
+        scratch_shapes=finish_scratch(pair, w_out),
+        compiler_params=params(),
+        cost_estimate=cost(1e9, 14 << 20, 4 << 20),
+        name="finish",
+    )(pair, gate, w_out, gain_wide, *products)
+
+
+def middle_call(chain, block_mask, pair, gate, products, w_out, gain_wide, w_in, gain_in):
+    outs, specs = side_outs(pair, IN_SIZES, 0)
+    middle, normed, *result = pl.pallas_call(
+        functools.partial(middle_kernel, len(products)),
+        grid=(pair.shape[0] // STEP,),
+        in_specs=[SMEM_SPEC, SMEM_SPEC, tile_spec(pair), tile_spec(gate), part(w_out, 0)]
+        + [whole(gain_wide), side_weights(w_in, 1, LEFT), whole(gain_in)]
+        + [chunk_spec(p.shape) for p in products],
+        out_specs=[tile_spec(pair)] * 2 + specs,
+        out_shape=[jax.ShapeDtypeStruct(pair.shape, pair.dtype)] * 2 + outs,
+        scratch_shapes=finish_scratch(pair, w_out) + side_scratch(pair, w_in),
+        compiler_params=params(),
+        cost_estimate=cost(3e9, 18 << 20, 8 << 20),
+        name="middle",
+    )(chain, block_mask, pair, gate, w_out, gain_wide, w_in, gain_in, *products)
+    return middle, normed, result
+
+
+def product_call(kernel, operands, leads, scratch, name):
+    counts = [len(operand) if isinstance(operand, tuple) else 1 for operand in operands]
+    arrays = []
+    for operand in operands:
+        arrays += operand if isinstance(operand, tuple) else [operand]
+    channels, size, _ = shape = arrays[0].shape[-3:]
+
+    def spec(lead):
+        return pl.BlockSpec(lead + (1, size, size), lambda c: (0,) * len(lead) + (c, 0, 0))
+
+    return pl.pallas_call(
+        functools.partial(pieces_kernel, kernel, counts),
+        grid=(channels,),
+        in_specs=[spec(array.shape[:-3]) for array in arrays],
+        out_specs=[spec(lead) for lead in leads],
+        out_shape=[jax.ShapeDtypeStruct(lead + shape, jnp.bfloat16) for lead in leads],
+        scratch_shapes=[pltpu.VMEM(scratch, jnp.bfloat16)],
+        compiler_params=params(),
+        cost_estimate=cost(channels * 2 * (4 * size) ** 2 * size, channels * size * size * 2 * 20),
+        name=name,
+    )(*arrays)
+
+
+WAYS = {
+    "in": ("row", [(0, 1), (3, 2)]),
+    "across": ("row", [(1, 2), (2, 1)]),
+    "out": ("row", [(1, 0), (2, 3)]),
+    "x": ("col", [(c, c ^ 2) for c in range(4)]),
+    "core": ("col", [(c, c ^ 1) for c in range(4)]),
+}
+
+
+class Graph:
+    def __init__(self, order, first, count):
+        self.order, self.first, self.count = order, first, count
+        self.steps, self.made = {}, {}
+
+    def add(self, name, operand, step):
+        self.steps[name] = (operand, step)
+
+    def send(self, name, way, operand):
+        axis, pairs = WAYS[way]
+        self.add(name, operand, lambda array: lax.ppermute(array, axis, pairs))
+
+    def get(self, name):
+        if name not in self.made:
+            operand, step = self.steps[name]
+            waits = [self.get(other) for other in self.order.get(name, ())]
+            array = operand()
+            if waits:
+                array = lax.optimization_barrier((array, *waits))[0]
+            self.made[name] = step(array)
+        return self.made[name]
+
+
+def join(first, second):
+    return jnp.stack([first, second])
+
+
+def is_inner():
+    row = lax.axis_index("row")
+    return (row == 1) | (row == 2)
+
+
+def shared_steps(graph, n, mine, other):
+    inner = is_inner()
+    get = graph.get
+
+    def ready(k):
+        return jnp.where(inner, mine(k), get(f"o{n}")[k])
+
+    graph.send(f"o{n}", "out", other)
+    graph.send(f"b{n}", "x", lambda: ready(1))
+    graph.add(f"k{n}", lambda: ready(0), lambda array: array)
+
+
+def finished(graph, count):
+    return graph.get("gate"), [graph.get(kind + str(n)) for kind in ("k", "b") for n in range(count)]
+
+
+def outgoing(first, normed, second, gate):
+    count = len(OUT_SIZES)
+    graph = Graph(OUT_ORDER, first, count)
+    get, send = graph.get, graph.send
+    graph.add("second", lambda: normed, second)
+    graph.add("gate", lambda: normed, gate)
+    send("xr0", "x", lambda: first[count])
+    send("xl0", "x", lambda: get("second")[count])
+    for end, right, left in (
+        ("", lambda: first[0], lambda: get("second")[0]),
+        ("x", lambda: get("xr0"), lambda: get("xl0")),
+    ):
+        send("r0" + end, "in", right)
+        send("n0" + end, "across", right)
+        send("l0" + end, "in", left)
+        send("f0" + end, "across", lambda end=end: get("r0" + end))
+    product_steps(
+        graph,
+        0,
+        lambda: [(get("second")[0], get("xl0")), (get("l0"), get("l0x")), (first[0], get("xr0"))]
+        + [(get(name), get(name + "x")) for name in ("r0", "f0", "n0")],
+    )
+    for n in range(1, count):
+        later_steps(graph, n)
+    return finished(graph, count)
+
+
+def later_steps(graph, n):
+    get, send = graph.get, graph.send
+    first, count = graph.first, graph.count
+    send(f"x{n}", "x", lambda: get("second")[count + n])
+    graph.add(f"jr{n}", lambda: first[n], lambda own: join(own, get(f"x{n}")[0]))
+    graph.add(f"jl{n}", lambda: get("second")[n], lambda own: join(own, get(f"x{n}")[1]))
+    send(f"r{n}", "in", lambda: get(f"jr{n}"))
+    send(f"n{n}", "across", lambda: get(f"jr{n}"))
+    send(f"l{n}", "in", lambda: get(f"jl{n}"))
+    send(f"f{n}", "across", lambda: get(f"r{n}"))
+    product_steps(graph, n, lambda: [get(name + str(n)) for name in ("jl", "l", "jr", "r", "f", "n")])
+
+
+def product_steps(graph, n, operands):
+    get, send = graph.get, graph.send
+
+    def first():
+        head = operands()[0]
+        return head[0] if isinstance(head, tuple) else head
+
+    def product(head):
+        head_of, *others = operands()
+        head = (head, head_of[1]) if isinstance(head_of, tuple) else head
+        size = head_of[0].shape[-1]
+        return product_call(
+            outgoing_kernel, [head, *others], ((), (), (2,), (2, 2)), (4, size, 2 * size), "outgoing"
+        )
+
+    graph.add(f"p{n}", first, product)
+    send(f"c{n}", "core", lambda: get(f"p{n}")[3])
+    shared_steps(
+        graph,
+        n,
+        lambda k: get(f"p{n}")[k] + get(f"c{n}")[0, k],
+        lambda: get(f"p{n}")[2] + get(f"c{n}")[1],
+    )
+
+
+def incoming(first, normed, second, gate):
+    count = len(IN_SIZES)
+    graph = Graph(IN_ORDER, first, count)
+    get, send = graph.get, graph.send
+    graph.add("second", lambda: normed, second)
+    graph.add("gate", lambda: normed, gate)
+    send("xl0", "x", lambda: first[count])
+    send("xr0", "x", lambda: get("second")[count])
+    send("l0", "in", lambda: first[0])
+    send("r0", "in", lambda: get("second")[0])
+    send("l0x", "in", lambda: get("xl0"))
+    send("r0x", "in", lambda: get("xr0"))
+    graph.add("jl0", lambda: first[0], lambda own: join(own, get("xl0")))
+    graph.add("jp0", lambda: get("l0"), lambda own: join(own, get("l0x")))
+    send("cl0", "core", lambda: get("jl0"))
+    send("cp0", "core", lambda: get("jp0"))
+    incoming_product(
+        graph, 0, lambda: [get("jp0"), get("cp0"), (get("second")[0], get("xr0")), (get("r0"), get("r0x"))]
+    )
+    for n in range(1, count):
+        incoming_later(graph, n)
+    return finished(graph, count)
+
+
+def incoming_later(graph, n):
+    get, send = graph.get, graph.send
+    first, count = graph.first, graph.count
+    send(f"x{n}", "x", lambda: get("second")[count + n])
+    graph.add(f"jl{n}", lambda: first[n], lambda own: join(own, get(f"x{n}")[0]))
+    graph.add(f"jr{n}", lambda: get("second")[n], lambda own: join(own, get(f"x{n}")[1]))
+    send(f"l{n}", "in", lambda: get(f"jl{n}"))
+    send(f"r{n}", "in", lambda: get(f"jr{n}"))
+    send(f"cl{n}", "core", lambda: get(f"jl{n}"))
+    send(f"cp{n}", "core", lambda: get(f"l{n}"))
+    incoming_product(graph, n, lambda: [get(name + str(n)) for name in ("l", "cp", "jr", "r")])
+
+
+def incoming_product(graph, n, others):
+    get, send = graph.get, graph.send
+
+    def product(left):
+        size = left.shape[-1]
+        return product_call(
+            incoming_kernel,
+            [left, get(f"cl{n}"), *others()],
+            ((), (), (2,), (2,), (2,)),
+            (4, 2 * size, size),
+            "incoming",
+        )
+
+    graph.add(f"p{n}", lambda: get(f"jl{n}"), product)
+    send(f"f{n}", "across", lambda: get(f"p{n}")[3])
+    send(f"n{n}", "across", lambda: get(f"p{n}")[4])
+    shared_steps(
+        graph,
+        n,
+        lambda k: get(f"p{n}")[k] + get(f"n{n}")[k],
+        lambda: get(f"p{n}")[2] + get(f"f{n}"),
+    )
+
+
+def four_by_four(pair, chain, block_mask, w_in, w_gate, w_out, gain_in, gain_out):
+    gain_wide = jnp.broadcast_to(gain_out[:, :, None, None], gain_out.shape + (1, pair.shape[1]))
+
+    def rest_of(index, side, sizes, first):
+        def second(normed):
+            return second_call(chain, block_mask, normed, w_in, index, side, sizes, first[len(sizes) + 1 :])
+
+        return second, lambda normed: gate_call(normed, w_gate, index)
+
+    normed, first = first_call(chain, block_mask, pair, w_in, gain_in)
+    gate, products = outgoing(first, normed, *rest_of(0, LEFT, OUT_SIZES, first))
+    middle, normed, first = middle_call(
+        chain, block_mask, pair, gate, products, w_out, gain_wide[0], w_in, gain_in
+    )
+    gate, products = incoming(first, normed, *rest_of(1, RIGHT, IN_SIZES, first))
+    return finish_call(middle, gate, products, w_out, gain_wide[1])
+
+
 def solution(mesh):
+    four = mesh.shape["row"] == 4 and mesh.shape["col"] == 4
     return jax.shard_map(
-        per_device,
+        four_by_four if four else any_mesh,
         mesh=mesh,
         in_specs=(
             P(("group", "row"), "col", None),

time: 817 us -> 400 us (0.49)
  waiting for transfers between devices: 634 us -> 160 us
  starting transfers between devices: 1.15 us -> 120 us
  Pallas kernels: 0 us -> 94.7 us
  matrix products: 85.8 us -> 0 us
  other arithmetic: 54.9 us -> 9.67 us
  between operations: 13.6 us -> 1.07 us
  local copies, waits for them, and re-layouts: 19.9 us -> 8.33 us
    all_gather x3 -> x0, waiting for transfers between devices: 415 us -> none  [the longest x2 268 us: per_device(): lax.all_gather(right, 'row', axis=0, tiled=True)]
    ppermute x0 -> x76, waiting for transfers between devices: none -> 160 us  [send(): self.add(name, operand, lambda array: lax.ppermute(array, axis, pairs))]
    psum x1 -> x0, waiting for transfers between devices: 155 us -> none  [broadcast(): return lax.psum(block, axis)]
    ppermute x0 -> x76, starting transfers between devices: none -> 120 us  [send(): self.add(name, operand, lambda array: lax.ppermute(array, axis, pairs))]
    pallas_call x0 -> x15, Pallas kernels: none -> 94.7 us  [the longest x8 33.5 us: product_call(): pl.pallas_call(functools.partial(pieces_kernel, kernel, counts), grid=(ch...]
    dot_general x9 -> x0, matrix products: 85.8 us -> none  [the longest x1 25.6 us: per_device(): jnp.einsum('kic,kjc->ijc', left_mine, lax.all_gather(right, 'row', axis=0...]
    reduce_scatter x1 -> x0, waiting for transfers between devices: 63.3 us -> none  [per_device(): lax.psum_scatter(partial_terms.astype(jnp.bfloat16), 'col', scatter_dimen...]
    select_n x2 -> x8, other arithmetic: 23.6 us -> 3.91 us  [ready(): return jnp.where(inner, mine(k), get(f'o{n}')[k])]
  transfers between devices with their start and end apart: 5 -> 76, of which waited for: 5 -> 37; matrix products, arithmetic and copies ran while one was open for 5% -> 3% of each run, Pallas kernels for 0% -> 15%
where the time goes in v4:
time: 400 us; the launch traced here: 394 us
  waiting for transfers between devices  160 us (40%)
  starting transfers between devices  120 us (30%)
  Pallas kernels  94.7 us (24%)
  other arithmetic  9.67 us (2%)
  local copies, waits for them, and re-layouts  8.33 us (2%)
    ppermute x76, waiting for transfers between devices, send(): self.add(name, operand, lambda array: lax.ppermute(array, axis, pairs))  160 us
    ppermute x76, starting transfers between devices, send(): self.add(name, operand, lambda array: lax.ppermute(array, axis, pairs))  120 us
    pallas_call x8, Pallas kernels, product_call(): pl.pallas_call(functools.partial(pieces_kernel, kernel, counts), grid=(ch...  33.5 us
    pallas_call x1, Pallas kernels, middle_call(): pl.pallas_call(functools.partial(middle_kernel, len(products)), grid=(pai...  15.3 us
    pallas_call x2, Pallas kernels, second_call(): pl.pallas_call(functools.partial(second_kernel, count), grid=(normed.shap...  13.7 us
    pallas_call x2, Pallas kernels, gate_call(): pl.pallas_call(gate_kernel, grid=(normed.shape[0] // STEP,), in_specs=[ti...  11.8 us
    pallas_call x1, Pallas kernels, first_call(): pl.pallas_call(first_kernel, grid=(pair.shape[0] // STEP,), in_specs=[SME...  11 us
    pallas_call x1, Pallas kernels, finish_call(): pl.pallas_call(finish_kernel, grid=(pair.shape[0] // STEP,), in_specs=[ti...  9.51 us
  transfers between devices with their start and end apart: 76, of which 37 were waited for; matrix products, arithmetic and copies ran while one was open for 3% of the time, Pallas kernels for 15%

profile of v4, /device:TPU:16, one launch (start us, length us, event | category | flops | bytes accessed | tf_op | source)
XLA Modules:
  0.0 393.9 jit_solution(18011490610026212692)
XLA Ops:
  2.9 11.0 %project.1 = (bf16[128,128,128]{2,1,0:T(8,128)(2,1)}, bf16[12,128,128]{2,1,0:T(8,128)(2,1)S(1)}, bf16[10,128,128]{2,1,0:T(8,128)(2,1)S(1)}, bf16[6,128,128]{2,1,...) custom-call(s32[4]{0:T(128)S(1)} %copy-done.11, ...), custom_call_target="tpu_custom_call" | custom-call | flops 100000000 | bytes 419430 | tf_op jit(solution)/shard_map/project/pallas_call | solution.py:335
  19.1 6.9 %second.2 = (bf16[12,128,128]{2,1,0:T(8,128)(2,1)S(1)}, bf16[10,128,128]{2,1,0:T(8,128)(2,1)S(1)}, bf16[6,128,128]{2,1,0:T(8,128)(2,1)S(1)}, bf16[4,128,128]{2,1...) custom-call(s32[4]{0:T(128)S(1)} %copy-done.12, ...), custom_call_target="tpu_custom_call", output_to_operand_aliasing={{5}: (4, {}), {6}: (5, {}), {7}: (6, {})} | custom-call | flops 50000000 | bytes 419430 | tf_op jit(solution)/shard_map/second/pallas_call | solution.py:352
  32.0 5.0 %collective-permute-done.1.refs_1_ = bf16[12,128,128]{2,1,0:T(8,128)(2,1)S(1)} collective-permute-done((bf16[12,128,128]{2,1,0:T(8,128)(2,1)S(1)}, bf16[12,128,128]{2,1,0:T(8,128)(2,1)S(1)}, u32[]{:S(2)}, u32[]{:S(2)}) %collective-permute-start.1) | collective-permute-done | bytes 393248 | tf_op jit(solution)/shard_map/ppermute | solution.py:455
  43.9 5.9 %gate.2.gate_ref = bf16[128,128,128]{2,1,0:T(8,128)(2,1)S(1)} custom-call(bf16[128,128,128]{2,1,0:T(8,128)(2,1)} %get-tuple-element.118.normed_ref, bf16[2,128,128]{2,1,0:T(8,128)(2,1)S(1)} %copy-done.4), custom_call_target="tpu_custom_call" | custom-call | flops 50000000 | bytes 419430 | tf_op jit(solution)/shard_map/gate/pallas_call | solution.py:368
  55.9 6.6 %collective-permute-done.5.refs_3_ = bf16[12,128,128]{2,1,0:T(8,128)(2,1)S(1)} collective-permute-done((bf16[12,128,128]{2,1,0:T(8,128)(2,1)S(1)}, bf16[12,128,128]{2,1,0:T(8,128)(2,1)S(1)}, u32[]{:S(2)}, u32[]{:S(2)}) %collective-permute-start.5) | collective-permute-done | bytes 393248 | tf_op jit(solution)/shard_map/ppermute | solution.py:455
  66.1 6.5 %outgoing.4 = (bf16[12,128,128]{2,1,0:T(8,128)(2,1)S(1)}, bf16[12,128,128]{2,1,0:T(8,128)(2,1)S(1)}, bf16[2,12,128,128]{3,2,1,0:T(8,128)(2,1)}, bf16[2,2,12,128,128]{4,3,2,1,0:T(8,128)(2,1)}) custom-call(bf16[12,128,128]{2,1,0:T(8,128)(2,1)S(1)} %get-tuple-element.127.refs_0_, bf16[12,128,128]{2,1,0:T(8,128)(2,1)S(1)} %collective-permute-done.1.refs_1_, ...), custom_call_target="tpu_custom_call" | custom-call | flops 40265320 | bytes 393216 | tf_op jit(solution)/shard_map/outgoing/pallas_call | solution.py:423
  72.7 5.1 %collective-permute-done.13.refs_3_ = bf16[2,10,128,128]{3,2,1,0:T(8,128)(2,1)S(1)} collective-permute-done((bf16[2,10,128,128]{3,2,1,0:T(8,128)(2,1)S(1)}, bf16[2,10,128,128]{3,2,1,0:T(8,128)(2,1)S(1)}, u32[]{:S(2)}, u32[]{:S(2)}) %collective-permute-start.13) | collective-permute-done | bytes 655392 | tf_op jit(solution)/shard_map/ppermute | solution.py:455
  83.1 6.1 %collective-permute-done.19 = bf16[2,6,128,128]{3,2,1,0:T(8,128)(2,1)S(1)} collective-permute-done((bf16[2,6,128,128]{3,2,1,0:T(8,128)(2,1)S(1)}, bf16[2,6,128,128]{3,2,1,0:T(8,128)(2,1)S(1)}, u32[]{:S(2)}, u32[]{:S(2)}) %collective-permute-start.19) | collective-permute-done | bytes 393248 | tf_op jit(solution)/shard_map/ppermute | solution.py:455
  93.6 5.8 %outgoing.5 = (bf16[10,128,128]{2,1,0:T(8,128)(2,1)S(1)}, bf16[10,128,128]{2,1,0:T(8,128)(2,1)S(1)}, bf16[2,10,128,128]{3,2,1,0:T(8,128)(2,1)S(1)}, bf16[2,2,10,128,128]{4,3,2,1,0:T(8,128)(2,1)}) custom-call(bf16[2,10,128,128]{3,2,1,0:T(8,128)(2,1)S(1)} %pad_maximum_fusion.2.refs_0_, bf16[2,10,128,128]{3,2,1,0:T(8,128)(2,1)S(1)} %collective-permute-done.14.refs_1_, ...), custom_call_target="tpu_custom_call" | custom-call | flops 33554432 | bytes 327680 | tf_op jit(solution)/shard_map/outgoing/pallas_call | solution.py:423
  105.4 7.4 %collective-permute-done.20.refs_3_ = bf16[2,6,128,128]{3,2,1,0:T(8,128)(2,1)S(1)} collective-permute-done((bf16[2,6,128,128]{3,2,1,0:T(8,128)(2,1)S(1)}, bf16[2,6,128,128]{3,2,1,0:T(8,128)(2,1)S(1)}, u32[]{:S(2)}, u32[]{:S(2)}) %collective-permute-start.20) | collective-permute-done | bytes 393248 | tf_op jit(solution)/shard_map/ppermute | solution.py:455
  160.6 5.6 %collective-permute-done.25 = bf16[2,6,128,128]{3,2,1,0:T(8,128)(2,1)S(1)} collective-permute-done((bf16[2,6,128,128]{3,2,1,0:T(8,128)(2,1)S(1)}, bf16[2,6,128,128]{3,2,1,0:T(8,128)(2,1)S(1)}, u32[]{:S(2)}, u32[]{:S(2)}) %collective-permute-start.25) | collective-permute-done | bytes 393248 | tf_op jit(solution)/shard_map/ppermute | solution.py:455
  176.4 15.3 %middle.1 = (bf16[128,128,128]{2,1,0:T(8,128)(2,1)}, bf16[128,128,128]{2,1,0:T(8,128)(2,1)}, bf16[8,128,128]{2,1,0:T(8,128)(2,1)S(1)}, bf16[12,128,128]{2,1,0:T(...) custom-call(s32[4]{0:T(128)S(1)} %copy-done.12, ...), custom_call_target="tpu_custom_call" | custom-call | flops 150000000 | bytes 943718 | tf_op jit(solution)/shard_map/middle/pallas_call | solution.py:397
  193.2 6.8 %second.3 = (bf16[8,128,128]{2,1,0:T(8,128)(2,1)S(1)}, bf16[12,128,128]{2,1,0:T(8,128)(2,1)S(1)}, bf16[8,128,128]{2,1,0:T(8,128)(2,1)S(1)}, bf16[4,128,128]{2,1,...) custom-call(s32[4]{0:T(128)S(1)} %copy-done.12, ...), custom_call_target="tpu_custom_call", output_to_operand_aliasing={{5}: (4, {}), {6}: (5, {}), {7}: (6, {})} | custom-call | flops 50000000 | bytes 419430 | tf_op jit(solution)/shard_map/second/pallas_call | solution.py:352
  201.9 5.1 %collective-permute-done.43.refs_5_ = bf16[8,128,128]{2,1,0:T(8,128)(2,1)S(1)} collective-permute-done((bf16[8,128,128]{2,1,0:T(8,128)(2,1)S(1)}, bf16[8,128,128]{2,1,0:T(8,128)(2,1)S(1)}, u32[]{:S(2)}, u32[]{:S(2)}) %collective-permute-start.43) | collective-permute-done | bytes 262176 | tf_op jit(solution)/shard_map/ppermute | solution.py:455
  210.2 7.0 %collective-permute-done.40.refs_6_ = bf16[8,128,128]{2,1,0:T(8,128)(2,1)S(1)} collective-permute-done((bf16[8,128,128]{2,1,0:T(8,128)(2,1)S(1)}, bf16[8,128,128]{2,1,0:T(8,128)(2,1)S(1)}, u32[]{:S(2)}, u32[]{:S(2)}) %collective-permute-start.40) | collective-permute-done | bytes 262176 | tf_op jit(solution)/shard_map/ppermute | solution.py:455
  218.4 5.9 %gate.3.gate_ref = bf16[128,128,128]{2,1,0:T(8,128)(2,1)S(1)} custom-call(bf16[128,128,128]{2,1,0:T(8,128)(2,1)} %get-tuple-element.174.normed_ref, bf16[2,128,128]{2,1,0:T(8,128)(2,1)S(1)} %copy-done.4), custom_call_target="tpu_custom_call" | custom-call | flops 50000000 | bytes 419430 | tf_op jit(solution)/shard_map/gate/pallas_call | solution.py:368
  226.9 8.5 %collective-permute-done.44.refs_7_ = bf16[8,128,128]{2,1,0:T(8,128)(2,1)S(1)} collective-permute-done((bf16[8,128,128]{2,1,0:T(8,128)(2,1)S(1)}, bf16[8,128,128]{2,1,0:T(8,128)(2,1)S(1)}, u32[]{:S(2)}, u32[]{:S(2)}) %collective-permute-start.44) | collective-permute-done | bytes 262176 | tf_op jit(solution)/shard_map/ppermute | solution.py:455
  245.0 10.7 %collective-permute-done.50.refs_2_ = bf16[2,12,128,128]{3,2,1,0:T(8,128)(2,1)S(1)} collective-permute-done((bf16[2,12,128,128]{3,2,1,0:T(8,128)(2,1)S(1)}, bf16[2,12,128,128]{3,2,1,0:T(8,128)(2,1)S(1)}, u32[]{:S(2)}, u32[]{:S(2)}) %collective-permute-start.50) | collective-permute-done | bytes 786464 | tf_op jit(solution)/shard_map/ppermute | solution.py:455
  262.3 15.2 %collective-permute-done.52.refs_5_ = bf16[2,12,128,128]{3,2,1,0:T(8,128)(2,1)S(1)} collective-permute-done((bf16[2,12,128,128]{3,2,1,0:T(8,128)(2,1)S(1)}, bf16[2,12,128,128]{3,2,1,0:T(8,128)(2,1)S(1)}, u32[]{:S(2)}, u32[]{:S(2)}) %collective-permute-start.52) | collective-permute-done | bytes 786464 | tf_op jit(solution)/shard_map/ppermute | solution.py:455
  278.4 8.2 %incoming.5 = (bf16[12,128,128]{2,1,0:T(8,128)(2,1)S(1)}, bf16[12,128,128]{2,1,0:T(8,128)(2,1)S(1)}, bf16[2,12,128,128]{3,2,1,0:T(8,128)(2,1)S(1)}, bf16[2,12,12...) custom-call(bf16[2,12,128,128]{3,2,1,0:T(8,128)(2,1)S(1)} %pad_maximum_fusion.refs_0_, ...), custom_call_target="tpu_custom_call" | custom-call | flops 40265320 | bytes 393216 | tf_op jit(solution)/shard_map/incoming/pallas_call | solution.py:423
  290.9 16.8 %collective-permute-done.53 = bf16[2,12,128,128]{3,2,1,0:T(8,128)(2,1)S(1)} collective-permute-done((bf16[2,12,128,128]{3,2,1,0:T(8,128)(2,1)S(1)}, bf16[2,12,128,128]{3,2,1,0:T(8,128)(2,1)S(1)}, u32[]{:S(2)}, u32[]{:S(2)}) %collective-permute-start.53) | collective-permute-done | bytes 786464 | tf_op jit(solution)/shard_map/ppermute | solution.py:455
  314.1 12.9 %collective-permute-done.60.refs_5_ = bf16[2,8,128,128]{3,2,1,0:T(8,128)(2,1)S(1)} collective-permute-done((bf16[2,8,128,128]{3,2,1,0:T(8,128)(2,1)S(1)}, bf16[2,8,128,128]{3,2,1,0:T(8,128)(2,1)S(1)}, u32[]{:S(2)}, u32[]{:S(2)}) %collective-permute-start.60) | collective-permute-done | bytes 524320 | tf_op jit(solution)/shard_map/ppermute | solution.py:455
  337.7 7.4 %collective-permute-done.61 = bf16[2,8,128,128]{3,2,1,0:T(8,128)(2,1)S(1)} collective-permute-done((bf16[2,8,128,128]{3,2,1,0:T(8,128)(2,1)S(1)}, bf16[2,8,128,128]{3,2,1,0:T(8,128)(2,1)S(1)}, u32[]{:S(2)}, u32[]{:S(2)}) %collective-permute-start.61) | collective-permute-done | bytes 524320 | tf_op jit(solution)/shard_map/ppermute | solution.py:455
  384.4 9.5 %finish.1 = bf16[128,128,128]{2,1,0:T(8,128)(2,1)} custom-call(bf16[128,128,128]{2,1,0:T(8,128)(2,1)} %get-tuple-element.173.pair_ref, bf16[128,128,128]{2,1,0:T(8,128)(2,1)} %copy-done, bf16[2,64,128]{2,1,0:T(8,128)(2,1)S(1)} %copy-done.7, f32[64,1,128]{2,1,0:T(1,128)S(1)} %broadcast_in_dim.15.gain_ref, ...), custom_call_target="tpu_custom_call" | custom-call | flops 50000000 | bytes 734003 | tf_op jit(solution)/shard_map/finish/pallas_call | solution.py:381
  (226 shorter events, 191.9 us)
Async XLA Ops:
  36.9 18.8 %collective-permute-start.12 = (bf16[2,10,128,128]{3,2,1,0:T(8,128)(2,1)S(1)}, bf16[2,10,128,128]{3,2,1,0:T(8,128)(2,1)S(1)}, u32[]{:S(2)}, u32[]{:S(2)}) collective-permute-start(bf16[2,10,128,128]{3,2,1,0:T(8,128)(2,1)S(1)} %get-tuple-element.142), channel_id=1, source_target_pairs={{0,2},{1,3},{2,0},{3,1},{4,6},{5,7},{6,4},{7,5},{8,10},{9,11},{10,... | collective-permute-start | bytes 1966088 | tf_op jit(solution)/shard_map/ppermute | solution.py:455
  72.6 44.5 %collective-permute-start.10 = (bf16[2,2,12,128,128]{4,3,2,1,0:T(8,128)(2,1)}, bf16[2,2,12,128,128]{4,3,2,1,0:T(8,128)(2,1)S(1)}, u32[]{:S(2)}, u32[]{:S(2)}) collective-permute-start(bf16[2,2,12,128,128]{4,3,2,1,0:T(8,128)(2,1)} %get-tuple-element.140), channel_id=1, source_target_pairs={{0,1},{1,0},{2,3},{3,2},{4,5},{5,4},{6,7},{7,6},{8,9},{9,8},{10,11... | collective-permute-start | bytes 4718600 | tf_op jit(solution)/shard_map/ppermute | solution.py:455
  99.4 39.7 %collective-permute-start.17 = (bf16[2,2,10,128,128]{4,3,2,1,0:T(8,128)(2,1)}, bf16[2,2,10,128,128]{4,3,2,1,0:T(8,128)(2,1)}, u32[]{:S(2)}, u32[]{:S(2)}) collective-permute-start(bf16[2,2,10,128,128]{4,3,2,1,0:T(8,128)(2,1)} %get-tuple-element.149), channel_id=1, source_target_pairs={{0,1},{1,0},{2,3},{3,2},{4,5},{5,4},{6,7},{7,6},{8,9},{9,8},{10,11... | collective-permute-start | bytes 3932168 | tf_op jit(solution)/shard_map/ppermute | solution.py:455
  103.8 17.6 %collective-permute-start.26 = (bf16[2,4,128,128]{3,2,1,0:T(8,128)(2,1)S(1)}, bf16[2,4,128,128]{3,2,1,0:T(8,128)(2,1)S(1)}, u32[]{:S(2)}, u32[]{:S(2)}) collective-permute-start(bf16[2,4,128,128]{3,2,1,0:T(8,128)(2,1)S(1)} %get-tuple-element.160), channel_id=1, source_target_pairs={{0,2},{1,3},{2,0},{3,1},{4,6},{5,7},{6,4},{7,5},{8,10},{9,11},{10,... | collective-permute-start | bytes 786440 | tf_op jit(solution)/shard_map/ppermute | solution.py:455
  118.2 30.3 %collective-permute-start.11 = (bf16[2,12,128,128]{3,2,1,0:T(8,128)(2,1)}, bf16[2,12,128,128]{3,2,1,0:T(8,128)(2,1)}, u32[]{:S(2)}, u32[]{:S(2)}) collective-permute-start(bf16[2,12,128,128]{3,2,1,0:T(8,128)(2,1)} %fusion), channel_id=1, source_target_pairs={{4,0},{8,12},{5,1},{9,13},{6,2},{10,14},{7,3},{11,15},{20,16},{24,... | collective-permute-start | bytes 2359304 | tf_op jit(solution)/shard_map/ppermute | solution.py:455
  133.9 17.5 %collective-permute-start.24 = (bf16[2,2,6,128,128]{4,3,2,1,0:T(8,128)(2,1)}, bf16[2,2,6,128,128]{4,3,2,1,0:T(8,128)(2,1)}, u32[]{:S(2)}, u32[]{:S(2)}) collective-permute-start(bf16[2,2,6,128,128]{4,3,2,1,0:T(8,128)(2,1)} %get-tuple-element.158), channel_id=1, source_target_pairs={{0,1},{1,0},{2,3},{3,2},{4,5},{5,4},{6,7},{7,6},{8,9},{9,8},{10,11... | collective-permute-start | bytes 2359304 | tf_op jit(solution)/shard_map/ppermute | solution.py:455
  140.4 17.4 %collective-permute-start.18 = (bf16[2,10,128,128]{3,2,1,0:T(8,128)(2,1)S(1)}, bf16[2,10,128,128]{3,2,1,0:T(8,128)(2,1)S(1)}, u32[]{:S(2)}, u32[]{:S(2)}) collective-permute-start(bf16[2,10,128,128]{3,2,1,0:T(8,128)(2,1)S(1)} %fusion.1), channel_id=1, source_target_pairs={{4,0},{8,12},{5,1},{9,13},{6,2},{10,14},{7,3},{11,15},{20,16},{24,... | collective-permute-start | bytes 1966088 | tf_op jit(solution)/shard_map/ppermute | solution.py:455
  149.9 23.0 %collective-permute-start.33 = (bf16[12,128,128]{2,1,0:T(8,128)(2,1)S(1)}, bf16[12,128,128]{2,1,0:T(8,128)(2,1)S(1)}, u32[]{:S(2)}, u32[]{:S(2)}) collective-permute-start(bf16[12,128,128]{2,1,0:T(8,128)(2,1)S(1)} %get-tuple-element.231), channel_id=1, source_target_pairs={{0,2},{1,3},{2,0},{3,1},{4,6},{5,7},{6,4},{7,5},{8,10},{9,11},{10,... | collective-permute-start | bytes 1179656 | tf_op jit(solution)/shard_map/ppermute | solution.py:455
  153.8 17.3 %collective-permute-start.32 = (bf16[2,4,128,128]{3,2,1,0:T(8,128)(2,1)S(1)}, bf16[2,4,128,128]{3,2,1,0:T(8,128)(2,1)S(1)}, u32[]{:S(2)}, u32[]{:S(2)}) collective-permute-start(bf16[2,4,128,128]{3,2,1,0:T(8,128)(2,1)S(1)} %fusion.23), channel_id=1, source_target_pairs={{4,0},{8,12},{5,1},{9,13},{6,2},{10,14},{7,3},{11,15},{20,16},{24,... | collective-permute-start | bytes 786440 | tf_op jit(solution)/shard_map/ppermute | solution.py:455
  159.1 17.2 %collective-permute-start.34 = (bf16[10,128,128]{2,1,0:T(8,128)(2,1)S(1)}, bf16[10,128,128]{2,1,0:T(8,128)(2,1)S(1)}, u32[]{:S(2)}, u32[]{:S(2)}) collective-permute-start(bf16[10,128,128]{2,1,0:T(8,128)(2,1)S(1)} %get-tuple-element.233), channel_id=1, source_target_pairs={{0,2},{1,3},{2,0},{3,1},{4,6},{5,7},{6,4},{7,5},{8,10},{9,11},{10,... | collective-permute-start | bytes 983048 | tf_op jit(solution)/shard_map/ppermute | solution.py:455
  207.0 19.7 %collective-permute-start.48 = (bf16[2,12,128,128]{3,2,1,0:T(8,128)(2,1)S(1)}, bf16[2,12,128,128]{3,2,1,0:T(8,128)(2,1)S(1)}, u32[]{:S(2)}, u32[]{:S(2)}) collective-permute-start(bf16[2,12,128,128]{3,2,1,0:T(8,128)(2,1)S(1)} %get-tuple-element.198), channel_id=1, source_target_pairs={{0,2},{1,3},{2,0},{3,1},{4,6},{5,7},{6,4},{7,5},{8,10},{9,11},{10,... | collective-permute-start | bytes 2359304 | tf_op jit(solution)/shard_map/ppermute | solution.py:455
  235.4 20.3 %collective-permute-start.50 = (bf16[2,12,128,128]{3,2,1,0:T(8,128)(2,1)S(1)}, bf16[2,12,128,128]{3,2,1,0:T(8,128)(2,1)S(1)}, u32[]{:S(2)}, u32[]{:S(2)}) collective-permute-start(bf16[2,12,128,128]{3,2,1,0:T(8,128)(2,1)S(1)} %pad_maximum_fusion.refs_0_), channel_id=1, source_target_pairs={{0,4},{12,8},{1,5},{13,9},{2,6},{14,10},{3,7},{15,11},{16,20},{28,... | collective-permute-start | bytes 2359304 | tf_op jit(solution)/shard_map/ppermute | solution.py:455
  244.8 17.4 %collective-permute-start.49 = (bf16[2,12,128,128]{3,2,1,0:T(8,128)(2,1)S(1)}, bf16[2,12,128,128]{3,2,1,0:T(8,128)(2,1)S(1)}, u32[]{:S(2)}, u32[]{:S(2)}) collective-permute-start(bf16[2,12,128,128]{3,2,1,0:T(8,128)(2,1)S(1)} %pad_maximum_fusion.refs_0_), channel_id=1, source_target_pairs={{0,1},{1,0},{2,3},{3,2},{4,5},{5,4},{6,7},{7,6},{8,9},{9,8},{10,11... | collective-permute-start | bytes 2359304 | tf_op jit(solution)/shard_map/ppermute | solution.py:455
  255.7 21.8 %collective-permute-start.52 = (bf16[2,12,128,128]{3,2,1,0:T(8,128)(2,1)S(1)}, bf16[2,12,128,128]{3,2,1,0:T(8,128)(2,1)S(1)}, u32[]{:S(2)}, u32[]{:S(2)}) collective-permute-start(bf16[2,12,128,128]{3,2,1,0:T(8,128)(2,1)S(1)} %pad_maximum_fusion.1.refs_4_), channel_id=1, source_target_pairs={{0,4},{12,8},{1,5},{13,9},{2,6},{14,10},{3,7},{15,11},{16,20},{28,... | collective-permute-start | bytes 2359304 | tf_op jit(solution)/shard_map/ppermute | solution.py:455
  257.8 28.8 %collective-permute-start.46 = (bf16[2,8,128,128]{3,2,1,0:T(8,128)(2,1)S(1)}, bf16[2,8,128,128]{3,2,1,0:T(8,128)(2,1)S(1)}, u32[]{:S(2)}, u32[]{:S(2)}) collective-permute-start(bf16[2,8,128,128]{3,2,1,0:T(8,128)(2,1)S(1)} %get-tuple-element.195), channel_id=1, source_target_pairs={{4,8},{8,4},{5,9},{9,5},{6,10},{10,6},{7,11},{11,7},{20,24},{24,20... | collective-permute-start | bytes 1572872 | tf_op jit(solution)/shard_map/ppermute | solution.py:455
  260.7 28.8 %collective-permute-start.56 = (bf16[2,8,128,128]{3,2,1,0:T(8,128)(2,1)S(1)}, bf16[2,8,128,128]{3,2,1,0:T(8,128)(2,1)S(1)}, u32[]{:S(2)}, u32[]{:S(2)}) collective-permute-start(bf16[2,8,128,128]{3,2,1,0:T(8,128)(2,1)S(1)} %get-tuple-element.208), channel_id=1, source_target_pairs={{0,2},{1,3},{2,0},{3,1},{4,6},{5,7},{6,4},{7,5},{8,10},{9,11},{10,... | collective-permute-start | bytes 1572872 | tf_op jit(solution)/shard_map/ppermute | solution.py:455
  286.6 21.1 %collective-permute-start.53 = (bf16[2,12,128,128]{3,2,1,0:T(8,128)(2,1)S(1)}, bf16[2,12,128,128]{3,2,1,0:T(8,128)(2,1)S(1)}, u32[]{:S(2)}, u32[]{:S(2)}) collective-permute-start(bf16[2,12,128,128]{3,2,1,0:T(8,128)(2,1)S(1)} %get-tuple-element.204), channel_id=1, source_target_pairs={{4,8},{8,4},{5,9},{9,5},{6,10},{10,6},{7,11},{11,7},{20,24},{24,20... | collective-permute-start | bytes 2359304 | tf_op jit(solution)/shard_map/ppermute | solution.py:455
  289.6 21.1 %collective-permute-start.58 = (bf16[2,8,128,128]{3,2,1,0:T(8,128)(2,1)S(1)}, bf16[2,8,128,128]{3,2,1,0:T(8,128)(2,1)S(1)}, u32[]{:S(2)}, u32[]{:S(2)}) collective-permute-start(bf16[2,8,128,128]{3,2,1,0:T(8,128)(2,1)S(1)} %pad_maximum_fusion.6.refs_0_), channel_id=1, source_target_pairs={{0,4},{12,8},{1,5},{13,9},{2,6},{14,10},{3,7},{15,11},{16,20},{28,... | collective-permute-start | bytes 1572872 | tf_op jit(solution)/shard_map/ppermute | solution.py:455
  307.7 22.4 %collective-permute-start.54 = (bf16[2,12,128,128]{3,2,1,0:T(8,128)(2,1)S(1)}, bf16[2,12,128,128]{3,2,1,0:T(8,128)(2,1)S(1)}, u32[]{:S(2)}, u32[]{:S(2)}) collective-permute-start(bf16[2,12,128,128]{3,2,1,0:T(8,128)(2,1)S(1)} %get-tuple-element.205), channel_id=1, source_target_pairs={{4,8},{8,4},{5,9},{9,5},{6,10},{10,6},{7,11},{11,7},{20,24},{24,20... | collective-permute-start | bytes 2359304 | tf_op jit(solution)/shard_map/ppermute | solution.py:455
  312.6 23.7 %collective-permute-start.64 = (bf16[2,4,128,128]{3,2,1,0:T(8,128)(2,1)S(1)}, bf16[2,4,128,128]{3,2,1,0:T(8,128)(2,1)S(1)}, u32[]{:S(2)}, u32[]{:S(2)}) collective-permute-start(bf16[2,4,128,128]{3,2,1,0:T(8,128)(2,1)S(1)} %get-tuple-element.218), channel_id=1, source_target_pairs={{0,2},{1,3},{2,0},{3,1},{4,6},{5,7},{6,4},{7,5},{8,10},{9,11},{10,... | collective-permute-start | bytes 786440 | tf_op jit(solution)/shard_map/ppermute | solution.py:455
  334.9 28.9 %collective-permute-start.55 = (bf16[2,12,128,128]{3,2,1,0:T(8,128)(2,1)S(1)}, bf16[2,12,128,128]{3,2,1,0:T(8,128)(2,1)S(1)}, u32[]{:S(2)}, u32[]{:S(2)}) collective-permute-start(bf16[2,12,128,128]{3,2,1,0:T(8,128)(2,1)S(1)} %add.87), channel_id=1, source_target_pairs={{4,0},{8,12},{5,1},{9,13},{6,2},{10,14},{7,3},{11,15},{20,16},{24,... | collective-permute-start | bytes 2359304 | tf_op jit(solution)/shard_map/ppermute | solution.py:455
  349.6 25.4 %collective-permute-start.63 = (bf16[2,8,128,128]{3,2,1,0:T(8,128)(2,1)S(1)}, bf16[2,8,128,128]{3,2,1,0:T(8,128)(2,1)S(1)}, u32[]{:S(2)}, u32[]{:S(2)}) collective-permute-start(bf16[2,8,128,128]{3,2,1,0:T(8,128)(2,1)S(1)} %add.89), channel_id=1, source_target_pairs={{4,0},{8,12},{5,1},{9,13},{6,2},{10,14},{7,3},{11,15},{20,16},{24,... | collective-permute-start | bytes 1572872 | tf_op jit(solution)/shard_map/ppermute | solution.py:455
  354.3 26.1 %collective-permute-start.72 = (bf16[8,128,128]{2,1,0:T(8,128)(2,1)S(1)}, bf16[8,128,128]{2,1,0:T(8,128)(2,1)S(1)}, u32[]{:S(2)}, u32[]{:S(2)}) collective-permute-start(bf16[8,128,128]{2,1,0:T(8,128)(2,1)S(1)} %get-tuple-element.241), channel_id=1, source_target_pairs={{0,2},{1,3},{2,0},{3,1},{4,6},{5,7},{6,4},{7,5},{8,10},{9,11},{10,... | collective-permute-start | bytes 786440 | tf_op jit(solution)/shard_map/ppermute | solution.py:455
  363.9 16.5 %collective-permute-start.73 = (bf16[12,128,128]{2,1,0:T(8,128)(2,1)S(1)}, bf16[12,128,128]{2,1,0:T(8,128)(2,1)S(1)}, u32[]{:S(2)}, u32[]{:S(2)}) collective-permute-start(bf16[12,128,128]{2,1,0:T(8,128)(2,1)S(1)} %get-tuple-element.235), channel_id=1, source_target_pairs={{0,2},{1,3},{2,0},{3,1},{4,6},{5,7},{6,4},{7,5},{8,10},{9,11},{10,... | collective-permute-start | bytes 1179656 | tf_op jit(solution)/shard_map/ppermute | solution.py:455
  (74 other events, 765.1 us)

commit v5 on v0

--- a/solution.py
+++ b/solution.py
@@ -1,9 +1,21 @@
+import functools
+
 import jax
 import jax.numpy as jnp
 from jax import lax
+from jax.experimental import pallas as pl
+from jax.experimental.pallas import tpu as pltpu
 from jax.sharding import PartitionSpec as P
 
 BLOCK = 128
+EPS = 1e-05
+OUT_SIZES = (8, 10, 8, 6)
+IN_SIZES = (8, 10, 8, 6)
+OUT_ORDER = {'i1': ('i0',), 'i2': ('i1',), 'i3': ('i2',), 'i4': ('i3',), 'i5': ('i4',), 'a1': ('a0',), 'a2': ('a1',), 'a3': ('a2',), 'a4': ('a3',), 'a5': ('a4',), 'x1': ('x0', 'a0'), 'x2': ('x1',), 'x3': ('x2',), 'p3': ('o1',)}
+IN_ORDER = {'i0x': ('i0',), 'i1': ('i0x',), 'i2': ('i1',), 'i3': ('i2',), 'a1': ('a0',), 'a2': ('a1',), 'a3': ('a2',), 'x1': ('x0', 'i0'), 'x2': ('x1',), 'x3': ('x2',)}
+STEP = 32
+TOLD = 0.05
+VMEM = 48 * 1024 * 1024
 
 
 def broadcast(block, axis, owner):
@@ -15,7 +27,7 @@
     mean = jnp.mean(values, -1, keepdims=True)
     centred = values - mean
     spread = jnp.mean(centred * centred, -1, keepdims=True)
-    return centred * lax.rsqrt(spread + 1e-05) * gain
+    return centred * lax.rsqrt(spread + EPS) * gain
 
 
 def project(pair, tile_mask, w_in, w_gate, gain_in):
@@ -40,7 +52,7 @@
     ).astype(jnp.bfloat16)
 
 
-def per_device(pair, chain, block_mask, w_in, w_gate, w_out, gain_in, gain_out):
+def any_mesh(pair, chain, block_mask, w_in, w_gate, w_out, gain_in, gain_out):
     tile_rows = pair.shape[0]
     tile_cols = pair.shape[1]
     block_count = chain.shape[0]
@@ -80,9 +92,517 @@
     return finish(middle, product, gate, w_out[1], gain_out[1])
 
 
+NN = (((1,), (0,)), ((), ()))
+NT = (((1,), (1,)), ((), ()))
+TN = (((0,), (0,)), ((), ()))
+SMEM_SPEC = pl.BlockSpec(memory_space=pltpu.SMEM)
+
+
+def dot(a, b, dims=NN):
+    return lax.dot_general(a, b, dims, preferred_element_type=jnp.float32)
+
+
+def norm_rows(rows, gain):
+    channels = rows.shape[-1]
+    place = lax.broadcasted_iota(jnp.int32, (channels, channels), 0)
+    same = place == lax.broadcasted_iota(jnp.int32, (channels, channels), 1)
+    centre = jnp.where(same, 1.0 - 1.0 / channels, -1.0 / channels).astype(jnp.bfloat16)
+    mean_of = jnp.full((2 * channels, channels), 1.0 / channels, jnp.bfloat16)
+    centred = dot(rows, centre)
+    square = centred * centred
+    high = square.astype(jnp.bfloat16)
+    low = (square - high.astype(jnp.float32)).astype(jnp.bfloat16)
+    spread = dot(jnp.concatenate([high, low], 1), mean_of)
+    return (centred * lax.rsqrt(spread + EPS) * gain).astype(jnp.bfloat16)
+
+
+def logistic(values):
+    return 0.5 * jnp.tanh(0.5 * values) + 0.5
+
+
+def tile_mask(chain_ref, block_mask_ref):
+    row, col = lax.axis_index("row"), lax.axis_index("col")
+    seen = (chain_ref[row] == chain_ref[col]) | (block_mask_ref[row, col] == 1)
+    return jnp.where(seen, 1.0, 0.0).astype(jnp.float32)
+
+
+def pick_weights(w_ref, turned, picked):
+    @pl.when(pl.program_id(0) == 0)
+    def _():
+        turned[...] = w_ref[0].astype(jnp.float32).T
+        half = turned.shape[0] // 8
+        x = lax.axis_index("col") // 2
+        rows = []
+        for kind in range(4):
+            for other in (x, 1 - x):
+                rows.append(turned[pl.ds(pl.multiple_of((2 * kind + other) * half, 8), half), :])
+        picked[...] = jnp.concatenate(rows, 0).astype(jnp.bfloat16)
+
+
+def project_part(normed, mask, picked, scratch, sides, sizes):
+    hidden = dot(picked[...], normed, NT)
+    width = picked.shape[0] // 4
+    cols = normed.shape[0] // STEP
+    for side, refs in enumerate(sides):
+        values = hidden[2 * side * width : (2 * side + 1) * width]
+        gates = hidden[(2 * side + 1) * width : (2 * side + 2) * width]
+        kept = mask * logistic(gates) * values
+        for row in range(STEP):
+            scratch[side, pl.ds(row, width, stride=STEP), :] = kept[:, row * cols : (row + 1) * cols]
+        done = 0
+        for ref, size in zip(refs, sizes * 2):
+            rows = scratch[side, done * STEP : (done + size) * STEP, :]
+            ref[...] = rows.astype(jnp.bfloat16).reshape(ref.shape)
+            done += size
+
+
+def split_sides(outs, count, apart):
+    lefts, rights = [], []
+    for n in range(count):
+        if apart:
+            rights.append(outs[2 * n])
+            lefts.append(outs[2 * n + 1])
+        else:
+            lefts.append(outs[n].at[0])
+            rights.append(outs[n].at[1])
+    for ref in outs[-count:]:
+        lefts.append(ref.at[1 if apart else 0])
+        rights.append(ref.at[0 if apart else 1])
+    return lefts, rights
+
+
+def project_all(rows, gain, mask, w_gate_ref, gate_ref, picked, scratch, outs, sizes, apart):
+    normed = norm_rows(rows, gain)
+    project_part(normed, mask, picked, scratch, split_sides(outs, len(sizes), apart), sizes)
+    gate = logistic(dot(normed, w_gate_ref[0]))
+    gate_ref[...] = gate.astype(gate_ref.dtype).reshape(gate_ref.shape)
+
+
+def first_kernel(sizes, chain_ref, block_mask_ref, pair_ref, w_ref, w_gate_ref, gain_ref, gate_ref, *rest):
+    *outs, turned, picked, scratch = rest
+    pick_weights(w_ref, turned, picked)
+    rows = pair_ref[...].reshape(-1, pair_ref.shape[-1])
+    mask = tile_mask(chain_ref, block_mask_ref)
+    project_all(rows, gain_ref[0:1], mask, w_gate_ref, gate_ref, picked, scratch, outs, sizes, True)
+
+
+def finish_rows(pair_ref, gate_ref, product_refs, w_out_ref, gain_ref, scratch, twice, out_ref):
+    width = w_out_ref.shape[1]
+    half = width // 2
+    cols = pair_ref.shape[1]
+    x = lax.axis_index("col") // 2
+    mine, others = pl.multiple_of(x * half, half), pl.multiple_of((1 - x) * half, half)
+
+    @pl.when(pl.program_id(0) == 0)
+    def _():
+        w_out = jnp.concatenate([w_out_ref[0, pl.ds(mine, half)], w_out_ref[0, pl.ds(others, half)]], 0)
+        none = jnp.zeros_like(w_out)
+        twice[...] = jnp.concatenate(
+            [jnp.concatenate([w_out, none], 1), jnp.concatenate([none, w_out], 1)], 0
+        )
+
+    gain = jnp.concatenate([gain_ref[pl.ds(mine, half)], gain_ref[pl.ds(others, half)]], 0)
+    product = jnp.concatenate([ref[...] for ref in product_refs], 0).astype(jnp.float32)
+    mean = jnp.sum(product, 0, keepdims=True) * (1.0 / width)
+    centred = product - mean
+    spread = jnp.sum(centred * centred, 0, keepdims=True) * (1.0 / width)
+    update = centred * lax.rsqrt(spread + EPS) * gain
+    scratch[...] = update.reshape(width * STEP, cols)
+    for row in range(0, STEP, 2):
+        two = jnp.concatenate(
+            [scratch[pl.ds(row, width, stride=STEP), :], scratch[pl.ds(row + 1, width, stride=STEP), :]], 0
+        )
+        changes = dot(two.astype(jnp.bfloat16), twice[...], TN)
+        for k in range(2):
+            change = changes[:, k * pair_ref.shape[2] : (k + 1) * pair_ref.shape[2]]
+            gate = gate_ref[row + k].astype(jnp.float32)
+            old = pair_ref[row + k].astype(jnp.float32)
+            out_ref[row + k] = (old + gate * change).astype(jnp.bfloat16)
+
+
+def finish_kernel(pair_ref, gate_ref, w_out_ref, gain_ref, *rest):
+    *product_refs, out_ref, scratch, twice = rest
+    finish_rows(pair_ref, gate_ref, product_refs, w_out_ref, gain_ref, scratch, twice, out_ref)
+
+
+def middle_kernel(
+    sizes,
+    count,
+    chain_ref,
+    block_mask_ref,
+    pair_ref,
+    gate_ref,
+    w_out_ref,
+    gain_out_ref,
+    w_ref,
+    w_gate_ref,
+    gain_in_ref,
+    *rest,
+):
+    product_refs, (out_ref, next_ref, *outs, update, twice, turned, picked, scratch) = rest[:count], rest[count:]
+    pick_weights(w_ref, turned, picked)
+    finish_rows(pair_ref, gate_ref, product_refs, w_out_ref, gain_out_ref, update, twice, out_ref)
+    rows = out_ref[...].reshape(-1, out_ref.shape[-1])
+    mask = tile_mask(chain_ref, block_mask_ref)
+    project_all(rows, gain_in_ref[1:2], mask, w_gate_ref, next_ref, picked, scratch, outs, sizes, False)
+
+
+def outgoing_kernel(left, left_pair, right, right_pair, right_far, right_near, outs, rights):
+    *kept, pair, sent = outs
+    for k, blocks in enumerate((right, right_pair, right_far, right_near)):
+        rights[k] = jnp.concatenate(blocks, 1)
+    lefts = jnp.concatenate([jnp.concatenate(left, 1), jnp.concatenate(left_pair, 1)], 0)
+    size = lefts.shape[0] // 2
+    here = lax.axis_index("row") ^ lax.axis_index("col")
+    for place in range(4):
+        terms = dot(lefts, rights[here ^ place], NT).astype(jnp.bfloat16)
+        if place % 2:
+            sent[0, place // 2, 0] = terms[:size]
+            sent[1, place // 2, 0] = terms[size:]
+        else:
+            kept[place // 2][0] = terms[:size]
+            pair[place // 2, 0] = terms[size:]
+
+
+def incoming_kernel(left, left_core, left_pair, left_pair_core, right, right_pair, outs, lefts):
+    *kept, pair, cross = outs
+    for k in range(2):
+        lefts[2 * k] = jnp.concatenate([left[k], left_pair[k]], 0)
+        lefts[2 * k + 1] = jnp.concatenate([left_core[k], left_pair_core[k]], 0)
+    rights = jnp.concatenate([jnp.concatenate(right, 1), jnp.concatenate(right_pair, 1)], 0)
+    size = rights.shape[1] // 2
+    here = lax.axis_index("row") ^ lax.axis_index("col")
+    for place in range(4):
+        terms = dot(lefts[here ^ place], rights, TN).astype(jnp.bfloat16)
+        for k in range(2):
+            block = terms[:, k * size : (k + 1) * size]
+            if place == 0:
+                kept[k][0] = block
+            else:
+                (pair, cross.at[0], cross.at[1])[place - 1][k, 0] = block
+
+
+def pieces_kernel(kernel, count, *refs):
+    blocks = [ref[(0,) * (len(ref.shape) - 2)] for ref in refs[:count]]
+    kernel(*[blocks[k : k + 2] for k in range(0, count, 2)], refs[count:-1], refs[-1])
+
+
+def params():
+    return pltpu.CompilerParams(vmem_limit_bytes=VMEM, dimension_semantics=("arbitrary",))
+
+
+def part(array, index):
+    return pl.BlockSpec((1,) + array.shape[1:], lambda *_: (index,) + (0,) * (array.ndim - 1))
+
+
+def whole(array):
+    return pl.BlockSpec(array.shape, lambda *_: (0,) * array.ndim)
+
+
+def tile_spec(tile):
+    return pl.BlockSpec((STEP,) + tile.shape[1:], lambda r: (r, 0, 0))
+
+
+def chunk_spec(shape):
+    lead = shape[:-2]
+    return pl.BlockSpec(lead + (STEP, shape[-1]), lambda r: (0,) * len(lead) + (r, 0))
+
+
+def cost(flops, nbytes, special=0):
+    return pl.CostEstimate(
+        flops=int(flops * TOLD), bytes_accessed=int(nbytes * TOLD), transcendentals=int(special * TOLD)
+    )
+
+
+def part_outs(pair, sizes, apart):
+    tile = pair.shape[:2]
+    own = [(size,) + tile for size in sizes]
+    both_sides = [(2,) + shape for shape in own]
+    shapes = ([shape for shape in own for _ in range(2)] if apart else both_sides) + both_sides
+    return [jax.ShapeDtypeStruct(shape, jnp.bfloat16) for shape in shapes], [chunk_spec(shape) for shape in shapes]
+
+
+def part_scratch(pair, w_in, sizes):
+    width = 2 * sum(sizes)
+    return [
+        pltpu.VMEM((w_in.shape[2], w_in.shape[1]), jnp.float32),
+        pltpu.VMEM((4 * width, w_in.shape[1]), jnp.bfloat16),
+        pltpu.VMEM((2, width * STEP, pair.shape[1]), jnp.float32),
+    ]
+
+
+def finish_scratch(pair, w_out):
+    return [
+        pltpu.VMEM((w_out.shape[1] * STEP, pair.shape[1]), jnp.float32),
+        pltpu.VMEM((2 * w_out.shape[1], 2 * w_out.shape[2]), jnp.bfloat16),
+    ]
+
+
+def first_call(chain, block_mask, pair, w_in, w_gate, gain_in):
+    outs, specs = part_outs(pair, OUT_SIZES, True)
+    gate, *result = pl.pallas_call(
+        functools.partial(first_kernel, OUT_SIZES),
+        grid=(pair.shape[0] // STEP,),
+        in_specs=[SMEM_SPEC, SMEM_SPEC, tile_spec(pair), part(w_in, 0), part(w_gate, 0), whole(gain_in)],
+        out_specs=[tile_spec(pair)] + specs,
+        out_shape=[jax.ShapeDtypeStruct(pair.shape, pair.dtype)] + outs,
+        scratch_shapes=part_scratch(pair, w_in, OUT_SIZES),
+        compiler_params=params(),
+        cost_estimate=cost(2e9, 8 << 20, 4 << 20),
+        name="project",
+    )(chain, block_mask, pair, w_in, w_gate, gain_in)
+    return gate, result
+
+
+def finish_call(pair, gate, products, w_out, gain_wide):
+    return pl.pallas_call(
+        finish_kernel,
+        grid=(pair.shape[0] // STEP,),
+        in_specs=[tile_spec(pair), tile_spec(gate), part(w_out, 1), whole(gain_wide)]
+        + [chunk_spec(p.shape) for p in products],
+        out_specs=tile_spec(pair),
+        out_shape=jax.ShapeDtypeStruct(pair.shape, pair.dtype),
+        scratch_shapes=finish_scratch(pair, w_out),
+        compiler_params=params(),
+        cost_estimate=cost(1e9, 14 << 20, 4 << 20),
+        name="finish",
+    )(pair, gate, w_out, gain_wide, *products)
+
+
+def middle_call(chain, block_mask, pair, gate, products, w_out, gain_wide, w_in, w_gate, gain_in):
+    outs, specs = part_outs(pair, IN_SIZES, False)
+    middle, gate, *result = pl.pallas_call(
+        functools.partial(middle_kernel, IN_SIZES, len(products)),
+        grid=(pair.shape[0] // STEP,),
+        in_specs=[SMEM_SPEC, SMEM_SPEC, tile_spec(pair), tile_spec(gate), part(w_out, 0)]
+        + [whole(gain_wide), part(w_in, 1), part(w_gate, 1), whole(gain_in)]
+        + [chunk_spec(p.shape) for p in products],
+        out_specs=[tile_spec(pair)] * 2 + specs,
+        out_shape=[jax.ShapeDtypeStruct(pair.shape, pair.dtype)] * 2 + outs,
+        scratch_shapes=finish_scratch(pair, w_out) + part_scratch(pair, w_in, IN_SIZES),
+        compiler_params=params(),
+        cost_estimate=cost(3e9, 18 << 20, 8 << 20),
+        name="middle",
+    )(chain, block_mask, pair, gate, w_out, gain_wide, w_in, w_gate, gain_in, *products)
+    return middle, gate, result
+
+
+def product_call(kernel, operands, channels, leads, scratch, name):
+    pieces = [piece for operand in operands for piece in operand]
+    size = pieces[0][0].shape[-1]
+
+    def piece_spec(array, lead, first):
+        return pl.BlockSpec((1,) * (len(lead) + 1) + (size, size), lambda c: lead + (first + c, 0, 0))
+
+    def out_spec(lead):
+        return pl.BlockSpec(lead + (1, size, size), lambda c: (0,) * len(lead) + (c, 0, 0))
+
+    return pl.pallas_call(
+        functools.partial(pieces_kernel, kernel, len(pieces)),
+        grid=(channels,),
+        in_specs=[piece_spec(*piece) for piece in pieces],
+        out_specs=[out_spec(lead) for lead in leads],
+        out_shape=[jax.ShapeDtypeStruct(lead + (channels, size, size), jnp.bfloat16) for lead in leads],
+        scratch_shapes=[pltpu.VMEM(scratch, jnp.bfloat16)],
+        compiler_params=params(),
+        cost_estimate=cost(channels * 2 * (4 * size) ** 2 * size, channels * size * size * 2 * 20),
+        name=name,
+    )(*[piece[0] for piece in pieces])
+
+
+WAYS = {
+    "in": ("row", [(0, 1), (3, 2)]),
+    "across": ("row", [(1, 2), (2, 1)]),
+    "out": ("row", [(1, 0), (2, 3)]),
+    "x": ("col", [(c, c ^ 2) for c in range(4)]),
+    "core": ("col", [(c, c ^ 1) for c in range(4)]),
+}
+
+
+class Graph:
+    def __init__(self, order):
+        self.order, self.steps, self.made = order, {}, {}
+
+    def add(self, name, operand, step):
+        self.steps[name] = (operand, step)
+
+    def send(self, name, way, operand):
+        axis, pairs = WAYS[way]
+        self.add(name, operand, lambda array: lax.ppermute(array, axis, pairs))
+
+    def get(self, name):
+        if name not in self.made:
+            operand, step = self.steps[name]
+            waits = [self.get(other) for other in self.order.get(name, ())]
+            array = operand()
+            if waits:
+                array = lax.optimization_barrier((array, *waits))[0]
+            self.made[name] = step(array)
+        return self.made[name]
+
+
+def pack(*columns):
+    return jnp.stack([jnp.concatenate([column[k] for column in columns]) for k in range(2)])
+
+
+def both(array, first=0, lead=()):
+    return [(array, (k,) + lead, first) for k in range(2)]
+
+
+def is_inner():
+    row = lax.axis_index("row")
+    return (row == 1) | (row == 2)
+
+
+def shared_steps(graph, n, mine, other):
+    inner = is_inner()
+    get = graph.get
+
+    def ready(k):
+        return jnp.where(inner, mine(k), get(f"o{n}")[k])
+
+    graph.send(f"o{n}", "out", other)
+    graph.send(f"b{n}", "x", lambda: ready(1))
+    graph.add(f"k{n}", lambda: ready(0), lambda array: array)
+
+
+def finished(graph, count):
+    return [graph.get(kind + str(n)) for kind in ("k", "b") for n in range(count)]
+
+
+def outgoing(parts):
+    count = len(OUT_SIZES)
+    graph = Graph(OUT_ORDER)
+    get, send = graph.get, graph.send
+    for n in range(count):
+        send(f"x{n}", "x", lambda n=n: parts[2 * count + n])
+    later = lambda n, side: parts[2 * n + side]
+    right_of = lambda n: (later(n, 0), get(f"x{n}")[0])
+    left_of = lambda n: (later(n, 1), get(f"x{n}")[1])
+    first = parts
+    zero = OUT_SIZES[0]
+    send("i0", "in", lambda: first[0])
+    send("a0", "across", lambda: first[0])
+    send("i1", "in", lambda: jnp.concatenate([get("x0")[0], first[1]]))
+    send("a1", "across", lambda: jnp.concatenate([get("x0")[0], get("i0")]))
+
+    def come(n):
+        array, skip = get(f"i{n + 1}"), zero // 2 if n == 1 else OUT_SIZES[n - 1]
+        return (array[0, skip:], array[1, skip:])
+
+    def halves(array):
+        return (array[: zero // 2], array[zero // 2 :])
+
+    def inward(n):
+        before = halves(get("x0")[1]) if n == 1 else left_of(n - 1)
+        return pack(before, right_of(n)) if n < count else pack(before)
+
+    def across(n):
+        before = halves(get("i1")[:zero]) if n == 1 else come(n - 1)
+        return pack(before, right_of(n)) if n < count else pack(before)
+
+    for n in range(1, count + 1):
+        send(f"i{n + 1}", "in", lambda n=n: inward(n))
+        send(f"a{n + 1}", "across", lambda n=n: across(n))
+
+    def product(n, left):
+        size = left.shape[-1]
+        if n == 0:
+            x_left = lambda array: array[:, : zero // 2].reshape((zero,) + array.shape[2:])
+            operands = [
+                [(left, (), 0), (get("x0"), (1,), 0)],
+                [(get("i1"), (), zero), (x_left(get("i2")), (), 0)],
+                [(first[0], (), 0), (get("x0"), (0,), 0)],
+                [(get("i0"), (), 0), (get("i1"), (), 0)],
+                [(get("a1"), (), zero), (x_left(get("a2")), (), 0)],
+                [(get("a0"), (), 0), (get("a1"), (), 0)],
+            ]
+        else:
+            skip = zero // 2 if n == 1 else OUT_SIZES[n - 1]
+            operands = [
+                [(left, (), 0), (get(f"x{n}"), (1,), 0)],
+                both(get(f"i{n + 2}")),
+                [(later(n, 0), (), 0), (get(f"x{n}"), (0,), 0)],
+                both(get(f"i{n + 1}"), skip),
+                both(get(f"a{n + 2}")),
+                both(get(f"a{n + 1}"), skip),
+            ]
+        leads = ((), (), (2,), (2, 2))
+        return product_call(outgoing_kernel, operands, left.shape[0], leads, (4, size, 2 * size), "outgoing")
+
+    for n in range(count):
+        graph.add(f"p{n}", lambda n=n: later(n, 1), functools.partial(product, n))
+        send(f"c{n}", "core", lambda n=n: get(f"p{n}")[3])
+        shared_steps(
+            graph,
+            n,
+            lambda k, n=n: get(f"p{n}")[k] + get(f"c{n}")[0, k],
+            lambda n=n: get(f"p{n}")[2] + get(f"c{n}")[1],
+        )
+    return finished(graph, count)
+
+
+def incoming(parts):
+    count = len(IN_SIZES)
+    graph = Graph(IN_ORDER)
+    get, send = graph.get, graph.send
+    for n in range(count):
+        send(f"x{n}", "x", lambda n=n: parts[count + n])
+    send("i0", "in", lambda: parts[0])
+    send("i0x", "in", lambda: get("x0"))
+    send("cl0", "core", lambda: parts[0])
+    send("clx", "core", lambda: get("x0"))
+    send("cp0", "core", lambda: get("i0"))
+    send("cpx", "core", lambda: get("i0x"))
+    for n in range(1, count):
+        graph.add(f"j{n}", lambda n=n: parts[n], lambda own, n=n: jnp.stack([own, get(f"x{n}")], 1))
+        send(f"i{n}", "in", lambda n=n: get(f"j{n}"))
+        send(f"cl{n}", "core", lambda n=n: get(f"j{n}")[0])
+        send(f"cp{n}", "core", lambda n=n: get(f"i{n}")[0])
+
+    def product(n, own):
+        size = own.shape[-1]
+        if n == 0:
+            side = lambda name, name_x, slot: [
+                (own if name is None else get(name), (slot,), 0),
+                (get(name_x), (slot,), 0),
+            ]
+            operands = [side(None, "x0", 0), side("cl0", "clx", 0), side("i0", "i0x", 0), side("cp0", "cpx", 0)]
+            operands += [side(None, "x0", 1), side("i0", "i0x", 1)]
+        else:
+            side = lambda array, slot: [(array, (slot, k), 0) for k in range(2)]
+            operands = [side(own, 0), both(get(f"cl{n}")), side(get(f"i{n}"), 0), both(get(f"cp{n}"))]
+            operands += [side(own, 1), side(get(f"i{n}"), 1)]
+        leads = ((), (), (2,), (2, 2))
+        return product_call(incoming_kernel, operands, IN_SIZES[n], leads, (4, 2 * size, size), "incoming")
+
+    for n in range(count):
+        graph.add(f"p{n}", lambda n=n: get(f"j{n}") if n else parts[0], functools.partial(product, n))
+        send(f"a{n}", "across", lambda n=n: get(f"p{n}")[3])
+        shared_steps(
+            graph,
+            n,
+            lambda k, n=n: get(f"p{n}")[k] + get(f"a{n}")[1, k],
+            lambda n=n: get(f"p{n}")[2] + get(f"a{n}")[0],
+        )
+    return finished(graph, count)
+
+
+def four_by_four(pair, chain, block_mask, w_in, w_gate, w_out, gain_in, gain_out):
+    gain_wide = jnp.broadcast_to(gain_out[:, :, None, None], gain_out.shape + (1, pair.shape[1]))
+    gate, parts = first_call(chain, block_mask, pair, w_in, w_gate, gain_in)
+    products = outgoing(parts)
+    middle, gate, parts = middle_call(
+        chain, block_mask, pair, gate, products, w_out, gain_wide[0], w_in, w_gate, gain_in
+    )
+    products = incoming(parts)
+    return finish_call(middle, gate, products, w_out, gain_wide[1])
+
+
 def solution(mesh):
+    four = mesh.shape["row"] == 4 and mesh.shape["col"] == 4
     return jax.shard_map(
-        per_device,
+        four_by_four if four else any_mesh,
         mesh=mesh,
         in_specs=(
             P(("group", "row"), "col", None),

time: 817 us -> 410 us (0.50)
  waiting for transfers between devices: 634 us -> 225 us
  matrix products: 85.8 us -> 0 us
  Pallas kernels: 0 us -> 83.4 us
  starting transfers between devices: 1.15 us -> 76.2 us
  other arithmetic: 54.9 us -> 10.8 us
  local copies, waits for them, and re-layouts: 19.9 us -> 6.32 us
  between operations: 13.6 us -> 0.97 us
    all_gather x3 -> x0, waiting for transfers between devices: 415 us -> none  [the longest x2 268 us: per_device(): lax.all_gather(right, 'row', axis=0, tiled=True)]
    ppermute x0 -> x59, waiting for transfers between devices: none -> 225 us  [send(): self.add(name, operand, lambda array: lax.ppermute(array, axis, pairs))]
    psum x1 -> x0, waiting for transfers between devices: 155 us -> none  [broadcast(): return lax.psum(block, axis)]
    dot_general x9 -> x0, matrix products: 85.8 us -> none  [the longest x1 25.6 us: per_device(): jnp.einsum('kic,kjc->ijc', left_mine, lax.all_gather(right, 'row', axis=0...]
    pallas_call x0 -> x11, Pallas kernels: none -> 83.4 us  [the longest x8 34.9 us: product_call(): pl.pallas_call(functools.partial(pieces_kernel, kernel, len(pieces)), gri...]
    ppermute x0 -> x59, starting transfers between devices: none -> 76.2 us  [send(): self.add(name, operand, lambda array: lax.ppermute(array, axis, pairs))]
    reduce_scatter x1 -> x0, waiting for transfers between devices: 63.3 us -> none  [per_device(): lax.psum_scatter(partial_terms.astype(jnp.bfloat16), 'col', scatter_dimen...]
    select_n x2 -> x8, other arithmetic: 23.6 us -> 3.7 us  [ready(): return jnp.where(inner, mine(k), get(f'o{n}')[k])]
  transfers between devices with their start and end apart: 5 -> 59, of which waited for: 5 -> 35; matrix products, arithmetic and copies ran while one was open for 5% -> 3% of each run, Pallas kernels for 0% -> 9%
where the time goes in v5:
time: 410 us; the launch traced here: 402 us
  waiting for transfers between devices  225 us (55%)
  Pallas kernels  83.4 us (20%)
  starting transfers between devices  76.2 us (19%)
  other arithmetic  10.8 us (3%)
  local copies, waits for them, and re-layouts  6.32 us (2%)
    ppermute x59, waiting for transfers between devices, send(): self.add(name, operand, lambda array: lax.ppermute(array, axis, pairs))  225 us
    ppermute x59, starting transfers between devices, send(): self.add(name, operand, lambda array: lax.ppermute(array, axis, pairs))  76.2 us
    pallas_call x8, Pallas kernels, product_call(): pl.pallas_call(functools.partial(pieces_kernel, kernel, len(pieces)), gri...  34.9 us
    pallas_call x1, Pallas kernels, middle_call(): pl.pallas_call(functools.partial(middle_kernel, IN_SIZES, len(products)),...  23.1 us
    pallas_call x1, Pallas kernels, first_call(): pl.pallas_call(functools.partial(first_kernel, OUT_SIZES), grid=(pair.sha...  16.3 us
    pallas_call x1, Pallas kernels, finish_call(): pl.pallas_call(finish_kernel, grid=(pair.shape[0] // STEP,), in_specs=[ti...  9.07 us
  transfers between devices with their start and end apart: 59, of which 35 were waited for; matrix products, arithmetic and copies ran while one was open for 3% of the time, Pallas kernels for 9%

profile of v5, /device:TPU:16, one launch (start us, length us, event | category | flops | bytes accessed | tf_op | source)
XLA Modules:
  0.0 402.3 jit_solution(15850670115794106822)
XLA Ops:
  3.8 16.3 %project.1 = (bf16[128,128,128]{2,1,0:T(8,128)(2,1)}, bf16[8,128,128]{2,1,0:T(8,128)(2,1)S(1)}, bf16[8,128,128]{2,1,0:T(8,128)(2,1)S(1)}, bf16[10,128,128]{2,1,0...) custom-call(s32[4]{0:T(128)S(1)} %copy-done.9, ...), custom_call_target="tpu_custom_call" | custom-call | flops 100000000 | bytes 419430 | tf_op jit(solution)/shard_map/project/pallas_call | solution.py:343
  25.2 8.5 %collective-permute-done.refs_1_.refs_5_ = bf16[2,8,128,128]{3,2,1,0:T(8,128)(2,1)S(1)} collective-permute-done((bf16[2,8,128,128]{3,2,1,0:T(8,128)(2,1)S(1)}, bf16[2,8,128,128]{3,2,1,0:T(8,128)(2,1)S(1)}, u32[]{:S(2)}, u32[]{:S(2)}) %collective-permute-start) | collective-permute-done | bytes 524320 | tf_op jit(solution)/shard_map/ppermute | solution.py:431
  36.7 11.8 %collective-permute-done.2.refs_2_.refs_7_ = bf16[16,128,128]{2,1,0:T(8,128)(2,1)S(1)} collective-permute-done((bf16[16,128,128]{2,1,0:T(8,128)(2,1)S(1)}, bf16[16,128,128]{2,1,0:T(8,128)(2,1)S(1)}, u32[]{:S(2)}, u32[]{:S(2)}) %collective-permute-start.2) | collective-permute-done | bytes 524320 | tf_op jit(solution)/shard_map/ppermute | solution.py:431
  56.3 9.8 %collective-permute-done.6.refs_8_.refs_11_ = bf16[16,128,128]{2,1,0:T(8,128)(2,1)S(1)} collective-permute-done((bf16[16,128,128]{2,1,0:T(8,128)(2,1)S(1)}, bf16[16,128,128]{2,1,0:T(8,128)(2,1)S(1)}, u32[]{:S(2)}, u32[]{:S(2)}) %collective-permute-start.6) | collective-permute-done | bytes 524320 | tf_op jit(solution)/shard_map/ppermute | solution.py:431
  76.1 11.4 %collective-permute-done.7.refs_10_.refs_11_ = bf16[2,14,128,128]{3,2,1,0:T(8,128)(2,1)S(1)} collective-permute-done((bf16[2,14,128,128]{3,2,1,0:T(8,128)(2,1)S(1)}, bf16[2,14,128,128]{3,2,1,0:T(8,128)(2,1)S(1)}, u32[]{:S(2)}, u32[]{:S(2)}) %collective-permute-start.7) | collective-permute-done | bytes 917536 | tf_op jit(solution)/shard_map/ppermute | solution.py:431
  94.4 6.2 %collective-permute-done.11.refs_2_.refs_3_.refs_6_.refs_7_ = bf16[2,18,128,128]{3,2,1,0:T(8,128)(2,1)S(1)} collective-permute-done((bf16[2,18,128,128]{3,2,1,0:T(8,128)(2,1)S(1)}, bf16[2,18,128,128]{3,2,1,0:T(8,128)(2,1)S(1)}, u32[]{:S(2)}, u32[]{:S(2)}) %collective-permute-start.11) | collective-permute-done | bytes 1179680 | tf_op jit(solution)/shard_map/ppermute | solution.py:431
  100.6 13.1 %collective-permute-done.12.refs_8_.refs_9_.refs_10_.refs_11_ = bf16[2,18,128,128]{3,2,1,0:T(8,128)(2,1)S(1)} collective-permute-done((bf16[2,18,128,128]{3,2,1,0:T(8,128)(2,1)}, bf16[2,18,128,128]{3,2,1,0:T(8,128)(2,1)S(1)}, u32[]{:S(2)}, u32[]{:S(2)}) %collective-permute-start.12) | collective-permute-done | bytes 1179680 | tf_op jit(solution)/shard_map/ppermute | solution.py:431
  114.6 7.1 %outgoing.5 = (bf16[10,128,128]{2,1,0:T(8,128)(2,1)S(1)}, bf16[10,128,128]{2,1,0:T(8,128)(2,1)S(1)}, bf16[2,10,128,128]{3,2,1,0:T(8,128)(2,1)S(1)}, bf16[2,2,10,128,128]{4,3,2,1,0:T(8,128)(2,1)}) custom-call(bf16[10,128,128]{2,1,0:T(8,128)(2,1)S(1)} %get-tuple-element.98.refs_0_, bf16[2,10,128,128]{3,2,1,0:T(8,128)(2,1)S(1)} %collective-permute-done.4.refs_1_.refs_5_, ...), custom_call_target="tpu_custom_call" | custom-call | flops 33554432 | bytes 327680 | tf_op jit(solution)/shard_map/outgoing/pallas_call | solution.py:400
  129.0 17.7 %collective-permute-done.16.refs_2_.refs_3_.refs_6_.refs_7_ = bf16[2,14,128,128]{3,2,1,0:T(8,128)(2,1)S(1)} collective-permute-done((bf16[2,14,128,128]{3,2,1,0:T(8,128)(2,1)S(1)}, bf16[2,14,128,128]{3,2,1,0:T(8,128)(2,1)S(1)}, u32[]{:S(2)}, u32[]{:S(2)}) %collective-permute-start.16) | collective-permute-done | bytes 917536 | tf_op jit(solution)/shard_map/ppermute | solution.py:431
  148.1 5.9 %outgoing.6 = (bf16[8,128,128]{2,1,0:T(8,128)(2,1)S(1)}, bf16[8,128,128]{2,1,0:T(8,128)(2,1)S(1)}, bf16[2,8,128,128]{3,2,1,0:T(8,128)(2,1)S(1)}, bf16[2,2,8,128,128]{4,3,2,1,0:T(8,128)(2,1)}) custom-call(bf16[8,128,128]{2,1,0:T(8,128)(2,1)S(1)} %get-tuple-element.107.refs_0_, bf16[2,8,128,128]{3,2,1,0:T(8,128)(2,1)S(1)} %collective-permute-done.10.refs_1_.refs_5_, ...), custom_call_target="tpu_custom_call" | custom-call | flops 26843544 | bytes 262144 | tf_op jit(solution)/shard_map/outgoing/pallas_call | solution.py:400
  186.0 8.8 %collective-permute-done.19 = bf16[2,8,128,128]{3,2,1,0:T(8,128)(2,1)S(1)} collective-permute-done((bf16[2,8,128,128]{3,2,1,0:T(8,128)(2,1)S(1)}, bf16[2,8,128,128]{3,2,1,0:T(8,128)(2,1)S(1)}, u32[]{:S(2)}, u32[]{:S(2)}) %collective-permute-start.19) | collective-permute-done | bytes 524320 | tf_op jit(solution)/shard_map/ppermute | solution.py:431
  203.3 4.8 %collective-permute-done.27.rest_7_ = bf16[6,128,128]{2,1,0:T(8,128)(2,1)S(1)} collective-permute-done((bf16[6,128,128]{2,1,0:T(8,128)(2,1)S(1)}, bf16[6,128,128]{2,1,0:T(8,128)(2,1)S(1)}, u32[]{:S(2)}, u32[]{:S(2)}) %collective-permute-start.27) | collective-permute-done | bytes 196640 | tf_op jit(solution)/shard_map/ppermute | solution.py:431
  208.3 23.1 %middle.1 = (bf16[128,128,128]{2,1,0:T(8,128)(2,1)}, bf16[128,128,128]{2,1,0:T(8,128)(2,1)}, bf16[2,8,128,128]{3,2,1,0:T(8,128)(2,1)S(1)}, bf16[2,10,128,128]{3,...) custom-call(s32[4]{0:T(128)S(1)} %copy-done.10, ...), custom_call_target="tpu_custom_call" | custom-call | flops 150000000 | bytes 943718 | tf_op jit(solution)/shard_map/middle/pallas_call | solution.py:374
  233.5 8.8 %collective-permute-done.28.refs_1_.refs_9_ = bf16[2,8,128,128]{3,2,1,0:T(8,128)(2,1)S(1)} collective-permute-done((bf16[2,8,128,128]{3,2,1,0:T(8,128)(2,1)S(1)}, bf16[2,8,128,128]{3,2,1,0:T(8,128)(2,1)S(1)}, u32[]{:S(2)}, u32[]{:S(2)}) %collective-permute-start.28) | collective-permute-done | bytes 524320 | tf_op jit(solution)/shard_map/ppermute | solution.py:431
  247.3 10.3 %collective-permute-done.37 = bf16[2,10,128,128]{3,2,1,0:T(8,128)(2,1)S(1)} collective-permute-done((bf16[2,10,128,128]{3,2,1,0:T(8,128)(2,1)}, bf16[2,10,128,128]{3,2,1,0:T(8,128)(2,1)S(1)}, u32[]{:S(2)}, u32[]{:S(2)}) %collective-permute-start.37) | collective-permute-done | bytes 655392 | tf_op jit(solution)/shard_map/ppermute | solution.py:431
  270.2 15.3 %collective-permute-done.39.refs_4_.refs_5_.refs_10_.refs_11_ = bf16[2,2,10,128,128]{4,3,2,1,0:T(8,128)(2,1)S(1)} collective-permute-done((bf16[2,2,10,128,128]{4,3,2,1,0:T(8,128)(2,1)S(1)}, bf16[2,2,10,128,128]{4,3,2,1,0:T(8,128)(2,1)S(1)}, u32[]{:S(2)}, u32[]{:S(2)}) %collective-permute-start.39) | collective-permute-done | bytes 1310752 | tf_op jit(solution)/shard_map/ppermute | solution.py:431
  287.9 6.3 %incoming.5 = (bf16[10,128,128]{2,1,0:T(8,128)(2,1)S(1)}, bf16[10,128,128]{2,1,0:T(8,128)(2,1)S(1)}, bf16[2,10,128,128]{3,2,1,0:T(8,128)(2,1)S(1)}, bf16[2,2,10,128,128]{4,3,2,1,0:T(8,128)(2,1)S(1)}) custom-call(bf16[2,2,10,128,128]{4,3,2,1,0:T(8,128)(2,1)S(1)} %pad_maximum_fusion.refs_0_.refs_1_.refs_8_.refs_9_, ...), custom_call_target="tpu_custom_call" | custom-call | flops 33554432 | bytes 327680 | tf_op jit(solution)/shard_map/incoming/pallas_call | solution.py:400
  298.8 14.5 %collective-permute-done.45.refs_4_.refs_5_.refs_10_.refs_11_ = bf16[2,2,8,128,128]{4,3,2,1,0:T(8,128)(2,1)S(1)} collective-permute-done((bf16[2,2,8,128,128]{4,3,2,1,0:T(8,128)(2,1)S(1)}, bf16[2,2,8,128,128]{4,3,2,1,0:T(8,128)(2,1)S(1)}, u32[]{:S(2)}, u32[]{:S(2)}) %collective-permute-start.45) | collective-permute-done | bytes 1048608 | tf_op jit(solution)/shard_map/ppermute | solution.py:431
  318.1 8.6 %collective-permute-done.41 = bf16[2,2,10,128,128]{4,3,2,1,0:T(8,128)(2,1)S(1)} collective-permute-done((bf16[2,2,10,128,128]{4,3,2,1,0:T(8,128)(2,1)S(1)}, bf16[2,2,10,128,128]{4,3,2,1,0:T(8,128)(2,1)S(1)}, u32[]{:S(2)}, u32[]{:S(2)}) %collective-permute-start.41) | collective-permute-done | bytes 1310752 | tf_op jit(solution)/shard_map/ppermute | solution.py:431
  329.4 5.9 %collective-permute-done.51.refs_4_.refs_5_.refs_10_.refs_11_ = bf16[2,2,6,128,128]{4,3,2,1,0:T(8,128)(2,1)S(1)} collective-permute-done((bf16[2,2,6,128,128]{4,3,2,1,0:T(8,128)(2,1)S(1)}, bf16[2,2,6,128,128]{4,3,2,1,0:T(8,128)(2,1)S(1)}, u32[]{:S(2)}, u32[]{:S(2)}) %collective-permute-start.51) | collective-permute-done | bytes 786464 | tf_op jit(solution)/shard_map/ppermute | solution.py:431
  339.3 12.9 %collective-permute-done.47 = bf16[2,2,8,128,128]{4,3,2,1,0:T(8,128)(2,1)S(1)} collective-permute-done((bf16[2,2,8,128,128]{4,3,2,1,0:T(8,128)(2,1)S(1)}, bf16[2,2,8,128,128]{4,3,2,1,0:T(8,128)(2,1)S(1)}, u32[]{:S(2)}, u32[]{:S(2)}) %collective-permute-start.47) | collective-permute-done | bytes 1048608 | tf_op jit(solution)/shard_map/ppermute | solution.py:431
  358.7 12.2 %collective-permute-done.53 = bf16[2,2,6,128,128]{4,3,2,1,0:T(8,128)(2,1)S(1)} collective-permute-done((bf16[2,2,6,128,128]{4,3,2,1,0:T(8,128)(2,1)S(1)}, bf16[2,2,6,128,128]{4,3,2,1,0:T(8,128)(2,1)S(1)}, u32[]{:S(2)}, u32[]{:S(2)}) %collective-permute-start.53) | collective-permute-done | bytes 786464 | tf_op jit(solution)/shard_map/ppermute | solution.py:431
  373.6 8.8 %collective-permute-done.48 = bf16[2,8,128,128]{3,2,1,0:T(8,128)(2,1)S(1)} collective-permute-done((bf16[2,8,128,128]{3,2,1,0:T(8,128)(2,1)S(1)}, bf16[2,8,128,128]{3,2,1,0:T(8,128)(2,1)S(1)}, u32[]{:S(2)}, u32[]{:S(2)}) %collective-permute-start.48) | collective-permute-done | bytes 524320 | tf_op jit(solution)/shard_map/ppermute | solution.py:431
  393.3 9.1 %finish.1 = bf16[128,128,128]{2,1,0:T(8,128)(2,1)} custom-call(bf16[128,128,128]{2,1,0:T(8,128)(2,1)} %get-tuple-element.127.pair_ref, bf16[128,128,128]{2,1,0:T(8,128)(2,1)} %get-tuple-element.128.gate_ref, bf16[2,64,128]{2,1,0:T(8,128)(2,1)S(1)} %copy-done.4, f32[64,1,128]{2,1,0:T(1,128)S(1)} %broadcast_in_dim.15.gain_ref, ...), custom_call_target="tpu_custom_call" | custom-call | flops 50000000 | bytes 734003 | tf_op jit(solution)/shard_map/finish/pallas_call | solution.py:358
  (194 shorter events, 144.2 us)
Async XLA Ops:
  51.1 22.2 %collective-permute-start.5 = (bf16[2,14,128,128]{3,2,1,0:T(8,128)(2,1)S(1)}, bf16[2,14,128,128]{3,2,1,0:T(8,128)(2,1)S(1)}, u32[]{:S(2)}, u32[]{:S(2)}) collective-permute-start(bf16[2,14,128,128]{3,2,1,0:T(8,128)(2,1)S(1)} %pad_maximum_fusion.4), channel_id=1, source_target_pairs={{0,4},{12,8},{1,5},{13,9},{2,6},{14,10},{3,7},{15,11},{16,20},{28,... | collective-permute-start | bytes 2752520 | tf_op jit(solution)/shard_map/ppermute | solution.py:431
  66.1 21.3 %collective-permute-start.7 = (bf16[2,14,128,128]{3,2,1,0:T(8,128)(2,1)S(1)}, bf16[2,14,128,128]{3,2,1,0:T(8,128)(2,1)S(1)}, u32[]{:S(2)}, u32[]{:S(2)}) collective-permute-start(bf16[2,14,128,128]{3,2,1,0:T(8,128)(2,1)S(1)} %pad_maximum_fusion.5), channel_id=1, source_target_pairs={{4,8},{8,4},{5,9},{9,5},{6,10},{10,6},{7,11},{11,7},{20,24},{24,20... | collective-permute-start | bytes 2752520 | tf_op jit(solution)/shard_map/ppermute | solution.py:431
  73.7 26.9 %collective-permute-start.11 = (bf16[2,18,128,128]{3,2,1,0:T(8,128)(2,1)S(1)}, bf16[2,18,128,128]{3,2,1,0:T(8,128)(2,1)S(1)}, u32[]{:S(2)}, u32[]{:S(2)}) collective-permute-start(bf16[2,18,128,128]{3,2,1,0:T(8,128)(2,1)S(1)} %pad_maximum_fusion.2), channel_id=1, source_target_pairs={{0,4},{12,8},{1,5},{13,9},{2,6},{14,10},{3,7},{15,11},{16,20},{28,... | collective-permute-start | bytes 3538952 | tf_op jit(solution)/shard_map/ppermute | solution.py:431
  87.4 26.2 %collective-permute-start.12 = (bf16[2,18,128,128]{3,2,1,0:T(8,128)(2,1)}, bf16[2,18,128,128]{3,2,1,0:T(8,128)(2,1)S(1)}, u32[]{:S(2)}, u32[]{:S(2)}) collective-permute-start(bf16[2,18,128,128]{3,2,1,0:T(8,128)(2,1)} %pad_maximum_fusion.3), channel_id=1, source_target_pairs={{4,8},{8,4},{5,9},{9,5},{6,10},{10,6},{7,11},{11,7},{20,24},{24,20... | collective-permute-start | bytes 3538952 | tf_op jit(solution)/shard_map/ppermute | solution.py:431
  89.6 32.1 %collective-permute-start.15 = (bf16[2,6,128,128]{3,2,1,0:T(8,128)(2,1)S(1)}, bf16[2,6,128,128]{3,2,1,0:T(8,128)(2,1)S(1)}, u32[]{:S(2)}, u32[]{:S(2)}) collective-permute-start(bf16[2,6,128,128]{3,2,1,0:T(8,128)(2,1)S(1)} %get-tuple-element.110), channel_id=1, source_target_pairs={{0,2},{1,3},{2,0},{3,1},{4,6},{5,7},{6,4},{7,5},{8,10},{9,11},{10,... | collective-permute-start | bytes 1179656 | tf_op jit(solution)/shard_map/ppermute | solution.py:431
  94.3 63.3 %collective-permute-start.8 = (bf16[2,2,8,128,128]{4,3,2,1,0:T(8,128)(2,1)S(1)}, bf16[2,2,8,128,128]{4,3,2,1,0:T(8,128)(2,1)}, u32[]{:S(2)}, u32[]{:S(2)}) collective-permute-start(bf16[2,2,8,128,128]{4,3,2,1,0:T(8,128)(2,1)S(1)} %get-tuple-element.96), channel_id=1, source_target_pairs={{0,1},{1,0},{2,3},{3,2},{4,5},{5,4},{6,7},{7,6},{8,9},{9,8},{10,11... | collective-permute-start | bytes 3145736 | tf_op jit(solution)/shard_map/ppermute | solution.py:431
  122.1 24.6 %collective-permute-start.16 = (bf16[2,14,128,128]{3,2,1,0:T(8,128)(2,1)S(1)}, bf16[2,14,128,128]{3,2,1,0:T(8,128)(2,1)S(1)}, u32[]{:S(2)}, u32[]{:S(2)}) collective-permute-start(bf16[2,14,128,128]{3,2,1,0:T(8,128)(2,1)S(1)} %pad_maximum_fusion.6), channel_id=1, source_target_pairs={{0,4},{12,8},{1,5},{13,9},{2,6},{14,10},{3,7},{15,11},{16,20},{28,... | collective-permute-start | bytes 2752520 | tf_op jit(solution)/shard_map/ppermute | solution.py:431
  123.5 24.6 %collective-permute-start.17 = (bf16[2,14,128,128]{3,2,1,0:T(8,128)(2,1)S(1)}, bf16[2,14,128,128]{3,2,1,0:T(8,128)(2,1)S(1)}, u32[]{:S(2)}, u32[]{:S(2)}) collective-permute-start(bf16[2,14,128,128]{3,2,1,0:T(8,128)(2,1)S(1)} %pad_maximum_fusion.7), channel_id=1, source_target_pairs={{4,8},{8,4},{5,9},{9,5},{6,10},{10,6},{7,11},{11,7},{20,24},{24,20... | collective-permute-start | bytes 2752520 | tf_op jit(solution)/shard_map/ppermute | solution.py:431
  125.8 36.8 %collective-permute-start.14 = (bf16[2,10,128,128]{3,2,1,0:T(8,128)(2,1)S(1)}, bf16[2,10,128,128]{3,2,1,0:T(8,128)(2,1)S(1)}, u32[]{:S(2)}, u32[]{:S(2)}) collective-permute-start(bf16[2,10,128,128]{3,2,1,0:T(8,128)(2,1)S(1)} %fusion.3), channel_id=1, source_target_pairs={{4,0},{8,12},{5,1},{9,13},{6,2},{10,14},{7,3},{11,15},{20,16},{24,... | collective-permute-start | bytes 1966088 | tf_op jit(solution)/shard_map/ppermute | solution.py:431
  154.1 22.8 %collective-permute-start.18 = (bf16[2,2,8,128,128]{4,3,2,1,0:T(8,128)(2,1)}, bf16[2,2,8,128,128]{4,3,2,1,0:T(8,128)(2,1)}, u32[]{:S(2)}, u32[]{:S(2)}) collective-permute-start(bf16[2,2,8,128,128]{4,3,2,1,0:T(8,128)(2,1)} %get-tuple-element.114), channel_id=1, source_target_pairs={{0,1},{1,0},{2,3},{3,2},{4,5},{5,4},{6,7},{7,6},{8,9},{9,8},{10,11... | collective-permute-start | bytes 3145736 | tf_op jit(solution)/shard_map/ppermute | solution.py:431
  175.6 27.7 %collective-permute-start.24 = (bf16[8,128,128]{2,1,0:T(8,128)(2,1)S(1)}, bf16[8,128,128]{2,1,0:T(8,128)(2,1)S(1)}, u32[]{:S(2)}, u32[]{:S(2)}) collective-permute-start(bf16[8,128,128]{2,1,0:T(8,128)(2,1)S(1)} %get-tuple-element.173), channel_id=1, source_target_pairs={{0,2},{1,3},{2,0},{3,1},{4,6},{5,7},{6,4},{7,5},{8,10},{9,11},{10,... | collective-permute-start | bytes 786440 | tf_op jit(solution)/shard_map/ppermute | solution.py:431
  183.5 17.8 %collective-permute-start.23 = (bf16[2,6,128,128]{3,2,1,0:T(8,128)(2,1)S(1)}, bf16[2,6,128,128]{3,2,1,0:T(8,128)(2,1)S(1)}, u32[]{:S(2)}, u32[]{:S(2)}) collective-permute-start(bf16[2,6,128,128]{3,2,1,0:T(8,128)(2,1)S(1)} %fusion.25), channel_id=1, source_target_pairs={{4,0},{8,12},{5,1},{9,13},{6,2},{10,14},{7,3},{11,15},{20,16},{24,... | collective-permute-start | bytes 1179656 | tf_op jit(solution)/shard_map/ppermute | solution.py:431
  185.1 18.1 %collective-permute-start.25 = (bf16[10,128,128]{2,1,0:T(8,128)(2,1)S(1)}, bf16[10,128,128]{2,1,0:T(8,128)(2,1)S(1)}, u32[]{:S(2)}, u32[]{:S(2)}) collective-permute-start(bf16[10,128,128]{2,1,0:T(8,128)(2,1)S(1)} %get-tuple-element.165), channel_id=1, source_target_pairs={{0,2},{1,3},{2,0},{3,1},{4,6},{5,7},{6,4},{7,5},{8,10},{9,11},{10,... | collective-permute-start | bytes 983048 | tf_op jit(solution)/shard_map/ppermute | solution.py:431
  257.8 27.8 %collective-permute-start.39 = (bf16[2,2,10,128,128]{4,3,2,1,0:T(8,128)(2,1)S(1)}, bf16[2,2,10,128,128]{4,3,2,1,0:T(8,128)(2,1)S(1)}, u32[]{:S(2)}, u32[]{:S(2)}) collective-permute-start(bf16[2,2,10,128,128]{4,3,2,1,0:T(8,128)(2,1)S(1)} %pad_maximum_fusion.refs_0_.refs_1_.refs_8_.refs_9_), channel_id=1, source_target_pairs={{0,4},{12,8},{1,5},{13,9},{2,6},{14,10},{3,7},{15,11},{16,20},{28,... | collective-permute-start | bytes 3932168 | tf_op jit(solution)/shard_map/ppermute | solution.py:431
  261.1 24.6 %collective-permute-start.43 = (bf16[2,8,128,128]{3,2,1,0:T(8,128)(2,1)S(1)}, bf16[2,8,128,128]{3,2,1,0:T(8,128)(2,1)S(1)}, u32[]{:S(2)}, u32[]{:S(2)}) collective-permute-start(bf16[2,8,128,128]{3,2,1,0:T(8,128)(2,1)S(1)} %get-tuple-element.145), channel_id=1, source_target_pairs={{0,2},{1,3},{2,0},{3,1},{4,6},{5,7},{6,4},{7,5},{8,10},{9,11},{10,... | collective-permute-start | bytes 1572872 | tf_op jit(solution)/shard_map/ppermute | solution.py:431
  267.6 27.3 %collective-permute-start.35 = (bf16[2,2,8,128,128]{4,3,2,1,0:T(8,128)(2,1)}, bf16[2,2,8,128,128]{4,3,2,1,0:T(8,128)(2,1)S(1)}, u32[]{:S(2)}, u32[]{:S(2)}) collective-permute-start(bf16[2,2,8,128,128]{4,3,2,1,0:T(8,128)(2,1)} %get-tuple-element.133), channel_id=1, source_target_pairs={{4,8},{8,4},{5,9},{9,5},{6,10},{10,6},{7,11},{11,7},{20,24},{24,20... | collective-permute-start | bytes 3145736 | tf_op jit(solution)/shard_map/ppermute | solution.py:431
  286.6 26.7 %collective-permute-start.45 = (bf16[2,2,8,128,128]{4,3,2,1,0:T(8,128)(2,1)S(1)}, bf16[2,2,8,128,128]{4,3,2,1,0:T(8,128)(2,1)S(1)}, u32[]{:S(2)}, u32[]{:S(2)}) collective-permute-start(bf16[2,2,8,128,128]{4,3,2,1,0:T(8,128)(2,1)S(1)} %pad_maximum_fusion.1.refs_0_.refs_1_.refs_8_.refs_9_), channel_id=1, source_target_pairs={{0,4},{12,8},{1,5},{13,9},{2,6},{14,10},{3,7},{15,11},{16,20},{28,... | collective-permute-start | bytes 3145736 | tf_op jit(solution)/shard_map/ppermute | solution.py:431
  294.9 31.9 %collective-permute-start.41 = (bf16[2,2,10,128,128]{4,3,2,1,0:T(8,128)(2,1)S(1)}, bf16[2,2,10,128,128]{4,3,2,1,0:T(8,128)(2,1)S(1)}, u32[]{:S(2)}, u32[]{:S(2)}) collective-permute-start(bf16[2,2,10,128,128]{4,3,2,1,0:T(8,128)(2,1)S(1)} %get-tuple-element.141), channel_id=1, source_target_pairs={{4,8},{8,4},{5,9},{9,5},{6,10},{10,6},{7,11},{11,7},{20,24},{24,20... | collective-permute-start | bytes 3932168 | tf_op jit(solution)/shard_map/ppermute | solution.py:431
  313.5 21.8 %collective-permute-start.51 = (bf16[2,2,6,128,128]{4,3,2,1,0:T(8,128)(2,1)S(1)}, bf16[2,2,6,128,128]{4,3,2,1,0:T(8,128)(2,1)S(1)}, u32[]{:S(2)}, u32[]{:S(2)}) collective-permute-start(bf16[2,2,6,128,128]{4,3,2,1,0:T(8,128)(2,1)S(1)} %pad_maximum_fusion.8.refs_0_.refs_1_.refs_8_.refs_9_), channel_id=1, source_target_pairs={{0,4},{12,8},{1,5},{13,9},{2,6},{14,10},{3,7},{15,11},{16,20},{28,... | collective-permute-start | bytes 2359304 | tf_op jit(solution)/shard_map/ppermute | solution.py:431
  326.8 25.4 %collective-permute-start.47 = (bf16[2,2,8,128,128]{4,3,2,1,0:T(8,128)(2,1)S(1)}, bf16[2,2,8,128,128]{4,3,2,1,0:T(8,128)(2,1)S(1)}, u32[]{:S(2)}, u32[]{:S(2)}) collective-permute-start(bf16[2,2,8,128,128]{4,3,2,1,0:T(8,128)(2,1)S(1)} %get-tuple-element.149), channel_id=1, source_target_pairs={{4,8},{8,4},{5,9},{9,5},{6,10},{10,6},{7,11},{11,7},{20,24},{24,20... | collective-permute-start | bytes 3145736 | tf_op jit(solution)/shard_map/ppermute | solution.py:431
  335.5 20.6 %collective-permute-start.36 = (bf16[2,8,128,128]{3,2,1,0:T(8,128)(2,1)S(1)}, bf16[2,8,128,128]{3,2,1,0:T(8,128)(2,1)S(1)}, u32[]{:S(2)}, u32[]{:S(2)}) collective-permute-start(bf16[2,8,128,128]{3,2,1,0:T(8,128)(2,1)S(1)} %fusion.11), channel_id=1, source_target_pairs={{4,0},{8,12},{5,1},{9,13},{6,2},{10,14},{7,3},{11,15},{20,16},{24,... | collective-permute-start | bytes 1572872 | tf_op jit(solution)/shard_map/ppermute | solution.py:431
  352.1 18.8 %collective-permute-start.53 = (bf16[2,2,6,128,128]{4,3,2,1,0:T(8,128)(2,1)S(1)}, bf16[2,2,6,128,128]{4,3,2,1,0:T(8,128)(2,1)S(1)}, u32[]{:S(2)}, u32[]{:S(2)}) collective-permute-start(bf16[2,2,6,128,128]{4,3,2,1,0:T(8,128)(2,1)S(1)} %get-tuple-element.157), channel_id=1, source_target_pairs={{4,8},{8,4},{5,9},{9,5},{6,10},{10,6},{7,11},{11,7},{20,24},{24,20... | collective-permute-start | bytes 2359304 | tf_op jit(solution)/shard_map/ppermute | solution.py:431
  356.1 32.4 %collective-permute-start.55 = (bf16[8,128,128]{2,1,0:T(8,128)(2,1)S(1)}, bf16[8,128,128]{2,1,0:T(8,128)(2,1)S(1)}, u32[]{:S(2)}, u32[]{:S(2)}) collective-permute-start(bf16[8,128,128]{2,1,0:T(8,128)(2,1)S(1)} %get-tuple-element.169), channel_id=1, source_target_pairs={{0,2},{1,3},{2,0},{3,1},{4,6},{5,7},{6,4},{7,5},{8,10},{9,11},{10,... | collective-permute-start | bytes 786440 | tf_op jit(solution)/shard_map/ppermute | solution.py:431
  357.4 25.0 %collective-permute-start.48 = (bf16[2,8,128,128]{3,2,1,0:T(8,128)(2,1)S(1)}, bf16[2,8,128,128]{3,2,1,0:T(8,128)(2,1)S(1)}, u32[]{:S(2)}, u32[]{:S(2)}) collective-permute-start(bf16[2,8,128,128]{3,2,1,0:T(8,128)(2,1)S(1)} %fusion.10), channel_id=1, source_target_pairs={{4,0},{8,12},{5,1},{9,13},{6,2},{10,14},{7,3},{11,15},{20,16},{24,... | collective-permute-start | bytes 1572872 | tf_op jit(solution)/shard_map/ppermute | solution.py:431
  (53 other events, 485.7 us)

commit v6 on v5

--- a/solution.py
+++ b/solution.py
@@ -9,11 +9,11 @@
 
 BLOCK = 128
 EPS = 1e-05
-OUT_SIZES = (8, 10, 8, 6)
-IN_SIZES = (8, 10, 8, 6)
-OUT_ORDER = {'i1': ('i0',), 'i2': ('i1',), 'i3': ('i2',), 'i4': ('i3',), 'i5': ('i4',), 'a1': ('a0',), 'a2': ('a1',), 'a3': ('a2',), 'a4': ('a3',), 'a5': ('a4',), 'x1': ('x0', 'a0'), 'x2': ('x1',), 'x3': ('x2',), 'p3': ('o1',)}
-IN_ORDER = {'i0x': ('i0',), 'i1': ('i0x',), 'i2': ('i1',), 'i3': ('i2',), 'a1': ('a0',), 'a2': ('a1',), 'a3': ('a2',), 'x1': ('x0', 'i0'), 'x2': ('x1',), 'x3': ('x2',)}
-STEP = 32
+OUT_SIZES = (8, 8, 8, 4, 4)
+IN_SIZES = (8, 8, 8, 4, 4)
+OUT_ORDER = {'i1': ('i0',), 'i2': ('i1',), 'i3': ('i2',), 'i4': ('i3',), 'i5': ('i4',), 'i6': ('i5',), 'a1': ('a0',), 'a2': ('a1',), 'a3': ('a2',), 'a4': ('a3',), 'a5': ('a4',), 'a6': ('a5',), 'o1': ('o0',), 'o2': ('o1',), 'o3': ('o2',), 'o4': ('o3',), 'x1': ('a0',), 'x2': ('a1',), 'p2': ('o0',), 'p3': ('o1',), 'p4': ('o2',)}
+IN_ORDER = {'i0x': ('i0',), 'i1': ('i0x',), 'i2': ('i1',), 'i3': ('i2',), 'i4': ('i3',), 'a1': ('a0',), 'a2': ('a1',), 'a3': ('a2',), 'a4': ('a3',), 'o1': ('o0',), 'o2': ('o1',), 'o3': ('o2',), 'o4': ('o3',), 'x1': ('i0',), 'x2': ('i0x',), 'b4': ('b3',)}
+STEP = 16
 TOLD = 0.05
 VMEM = 48 * 1024 * 1024
 
@@ -139,20 +139,22 @@
         picked[...] = jnp.concatenate(rows, 0).astype(jnp.bfloat16)
 
 
-def project_part(normed, mask, picked, scratch, sides, sizes):
+def project_row(row, normed, mask, picked, scratch):
     hidden = dot(picked[...], normed, NT)
     width = picked.shape[0] // 4
-    cols = normed.shape[0] // STEP
-    for side, refs in enumerate(sides):
+    for side in range(2):
         values = hidden[2 * side * width : (2 * side + 1) * width]
         gates = hidden[(2 * side + 1) * width : (2 * side + 2) * width]
-        kept = mask * logistic(gates) * values
-        for row in range(STEP):
-            scratch[side, pl.ds(row, width, stride=STEP), :] = kept[:, row * cols : (row + 1) * cols]
+        scratch[side, pl.ds(row, width, stride=STEP), :] = mask * logistic(gates) * values
+
+
+def project_out(scratch, sides, sizes):
+    for side, refs in enumerate(sides):
         done = 0
         for ref, size in zip(refs, sizes * 2):
-            rows = scratch[side, done * STEP : (done + size) * STEP, :]
-            ref[...] = rows.astype(jnp.bfloat16).reshape(ref.shape)
+            for k in range(size):
+                rows = scratch[side, (done + k) * STEP : (done + k + 1) * STEP, :]
+                ref[k] = rows.astype(jnp.bfloat16)
             done += size
 
 
@@ -171,19 +173,24 @@
     return lefts, rights
 
 
-def project_all(rows, gain, mask, w_gate_ref, gate_ref, picked, scratch, outs, sizes, apart):
-    normed = norm_rows(rows, gain)
-    project_part(normed, mask, picked, scratch, split_sides(outs, len(sizes), apart), sizes)
-    gate = logistic(dot(normed, w_gate_ref[0]))
-    gate_ref[...] = gate.astype(gate_ref.dtype).reshape(gate_ref.shape)
+def project_all(rows_ref, gain, mask, w_gate_ref, gate_ref, picked, scratch, outs, sizes, apart):
+    for row in range(STEP):
+        normed = norm_rows(rows_ref[row], gain)
+        project_row(row, normed, mask, picked, scratch)
+        gate_ref[row] = logistic(dot(normed, w_gate_ref[0])).astype(gate_ref.dtype)
+    project_out(scratch, split_sides(outs, len(sizes), apart), sizes)
 
 
 def first_kernel(sizes, chain_ref, block_mask_ref, pair_ref, w_ref, w_gate_ref, gain_ref, gate_ref, *rest):
     *outs, turned, picked, scratch = rest
     pick_weights(w_ref, turned, picked)
-    rows = pair_ref[...].reshape(-1, pair_ref.shape[-1])
     mask = tile_mask(chain_ref, block_mask_ref)
-    project_all(rows, gain_ref[0:1], mask, w_gate_ref, gate_ref, picked, scratch, outs, sizes, True)
+    project_all(pair_ref, gain_ref[0:1], mask, w_gate_ref, gate_ref, picked, scratch, outs, sizes, True)
+
+
+def added(terms):
+    lanes = [functools.reduce(jnp.add, terms[k::4]) for k in range(4)]
+    return (lanes[0] + lanes[1]) + (lanes[2] + lanes[3])
 
 
 def finish_rows(pair_ref, gate_ref, product_refs, w_out_ref, gain_ref, scratch, twice, out_ref):
@@ -201,13 +208,15 @@
             [jnp.concatenate([w_out, none], 1), jnp.concatenate([none, w_out], 1)], 0
         )
 
-    gain = jnp.concatenate([gain_ref[pl.ds(mine, half)], gain_ref[pl.ds(others, half)]], 0)
-    product = jnp.concatenate([ref[...] for ref in product_refs], 0).astype(jnp.float32)
-    mean = jnp.sum(product, 0, keepdims=True) * (1.0 / width)
-    centred = product - mean
-    spread = jnp.sum(centred * centred, 0, keepdims=True) * (1.0 / width)
-    update = centred * lax.rsqrt(spread + EPS) * gain
-    scratch[...] = update.reshape(width * STEP, cols)
+    for start in range(0, STEP, 16):
+        group = [(ref, k, start) for ref in product_refs for k in range(ref.shape[0])]
+        read = lambda at: at[0][at[1], at[2] : at[2] + 16, :].astype(jnp.float32)
+        mean = added([read(at) for at in group]) * (1.0 / width)
+        spread = added([jnp.square(read(at) - mean) for at in group]) * (1.0 / width)
+        scale = lax.rsqrt(spread + EPS)
+        for n, at in enumerate(group):
+            gain = gain_ref[(mine if n < half else others) + n % half]
+            scratch[n * STEP + start : n * STEP + start + 16, :] = (read(at) - mean) * scale * gain
     for row in range(0, STEP, 2):
         two = jnp.concatenate(
             [scratch[pl.ds(row, width, stride=STEP), :], scratch[pl.ds(row + 1, width, stride=STEP), :]], 0
@@ -242,9 +251,8 @@
     product_refs, (out_ref, next_ref, *outs, update, twice, turned, picked, scratch) = rest[:count], rest[count:]
     pick_weights(w_ref, turned, picked)
     finish_rows(pair_ref, gate_ref, product_refs, w_out_ref, gain_out_ref, update, twice, out_ref)
-    rows = out_ref[...].reshape(-1, out_ref.shape[-1])
     mask = tile_mask(chain_ref, block_mask_ref)
-    project_all(rows, gain_in_ref[1:2], mask, w_gate_ref, next_ref, picked, scratch, outs, sizes, False)
+    project_all(out_ref, gain_in_ref[1:2], mask, w_gate_ref, next_ref, picked, scratch, outs, sizes, False)
 
 
 def outgoing_kernel(left, left_pair, right, right_pair, right_far, right_near, outs, rights):

time: 410 us -> 435 us (1.061)
  waiting for transfers between devices: 225 us -> 172 us
  Pallas kernels: 83.4 us -> 128 us
  starting transfers between devices: 76.2 us -> 112 us
    ppermute x59 -> x72, waiting for transfers between devices: 225 us -> 172 us  [send(): self.add(name, operand, lambda array: lax.ppermute(array, axis, pairs))]
    ppermute x59 -> x72, starting transfers between devices: 76.2 us -> 112 us  [send(): self.add(name, operand, lambda array: lax.ppermute(array, axis, pairs))]
    pallas_call x1, Pallas kernels: 16.3 us -> 42.3 us  [first_call(): pl.pallas_call(functools.partial(first_kernel, OUT_SIZES), grid=(pair.sha...]
    pallas_call x1, Pallas kernels: 23.1 us -> 46.5 us  [middle_call(): pl.pallas_call(functools.partial(middle_kernel, IN_SIZES, len(products)),...]
    pallas_call x8 -> x10, Pallas kernels: 34.9 us -> 29.9 us  [product_call(): pl.pallas_call(functools.partial(pieces_kernel, kernel, len(pieces)), gri...]
  transfers between devices with their start and end apart: 59 -> 72, of which waited for: 35 -> 38; matrix products, arithmetic and copies ran while one was open for 3% -> 3% of each run, Pallas kernels for 9% -> 7%
where the time goes in v6:
time: 435 us; the launch traced here: 431 us
  waiting for transfers between devices  172 us (40%)
  Pallas kernels  128 us (29%)
  starting transfers between devices  112 us (26%)
  other arithmetic  11.2 us (3%)
  local copies, waits for them, and re-layouts  6.62 us (2%)
    ppermute x72, waiting for transfers between devices, send(): self.add(name, operand, lambda array: lax.ppermute(array, axis, pairs))  172 us
    ppermute x72, starting transfers between devices, send(): self.add(name, operand, lambda array: lax.ppermute(array, axis, pairs))  112 us
    pallas_call x1, Pallas kernels, middle_call(): pl.pallas_call(functools.partial(middle_kernel, IN_SIZES, len(products)),...  46.5 us
    pallas_call x1, Pallas kernels, first_call(): pl.pallas_call(functools.partial(first_kernel, OUT_SIZES), grid=(pair.sha...  42.3 us
    pallas_call x10, Pallas kernels, product_call(): pl.pallas_call(functools.partial(pieces_kernel, kernel, len(pieces)), gri...  29.9 us
    pallas_call x1, Pallas kernels, finish_call(): pl.pallas_call(finish_kernel, grid=(pair.shape[0] // STEP,), in_specs=[ti...  9.53 us
  transfers between devices with their start and end apart: 72, of which 38 were waited for; matrix products, arithmetic and copies ran while one was open for 3% of the time, Pallas kernels for 7%

profile of v6, /device:TPU:16, one launch (start us, length us, event | category | flops | bytes accessed | tf_op | source)
XLA Modules:
  0.0 431.4 jit_solution(2356787436723962619)
XLA Ops:
  3.8 42.3 %project.1 = (bf16[128,128,128]{2,1,0:T(8,128)(2,1)}, bf16[8,128,128]{2,1,0:T(8,128)(2,1)S(1)}, bf16[8,128,128]{2,1,0:T(8,128)(2,1)S(1)}, bf16[8,128,128]{2,1,0:...) custom-call(s32[4]{0:T(128)S(1)} %copy-done.15, ...), custom_call_target="tpu_custom_call" | custom-call | flops 100000000 | bytes 419430 | tf_op jit(solution)/shard_map/project/pallas_call | solution.py:351
  51.2 6.0 %collective-permute-done.3.refs_10_ = bf16[8,128,128]{2,1,0:T(8,128)(2,1)S(1)} collective-permute-done((bf16[8,128,128]{2,1,0:T(8,128)(2,1)S(1)}, bf16[8,128,128]{2,1,0:T(8,128)(2,1)S(1)}, u32[]{:S(2)}, u32[]{:S(2)}) %collective-permute-start.3) | collective-permute-done | bytes 262176 | tf_op jit(solution)/shard_map/ppermute | solution.py:439
  64.7 6.3 %collective-permute-done.4.refs_1_.refs_5_ = bf16[2,8,128,128]{3,2,1,0:T(8,128)(2,1)S(1)} collective-permute-done((bf16[2,8,128,128]{3,2,1,0:T(8,128)(2,1)S(1)}, bf16[2,8,128,128]{3,2,1,0:T(8,128)(2,1)S(1)}, u32[]{:S(2)}, u32[]{:S(2)}) %collective-permute-start.4) | collective-permute-done | bytes 524320 | tf_op jit(solution)/shard_map/ppermute | solution.py:439
  80.1 6.8 %collective-permute-done.10.refs_1_.refs_5_ = bf16[2,8,128,128]{3,2,1,0:T(8,128)(2,1)S(1)} collective-permute-done((bf16[2,8,128,128]{3,2,1,0:T(8,128)(2,1)S(1)}, bf16[2,8,128,128]{3,2,1,0:T(8,128)(2,1)S(1)}, u32[]{:S(2)}, u32[]{:S(2)}) %collective-permute-start.10) | collective-permute-done | bytes 524320 | tf_op jit(solution)/shard_map/ppermute | solution.py:439
  86.9 6.1 %collective-permute-done.5.refs_6_.refs_7_ = bf16[2,12,128,128]{3,2,1,0:T(8,128)(2,1)S(1)} collective-permute-done((bf16[2,12,128,128]{3,2,1,0:T(8,128)(2,1)S(1)}, bf16[2,12,128,128]{3,2,1,0:T(8,128)(2,1)S(1)}, u32[]{:S(2)}, u32[]{:S(2)}) %collective-permute-start.5) | collective-permute-done | bytes 786464 | tf_op jit(solution)/shard_map/ppermute | solution.py:439
  102.8 14.6 %collective-permute-done.11.refs_2_.refs_3_.refs_6_.refs_7_ = bf16[2,16,128,128]{3,2,1,0:T(8,128)(2,1)S(1)} collective-permute-done((bf16[2,16,128,128]{3,2,1,0:T(8,128)(2,1)}, bf16[2,16,128,128]{3,2,1,0:T(8,128)(2,1)S(1)}, u32[]{:S(2)}, u32[]{:S(2)}) %collective-permute-start.11) | collective-permute-done | bytes 1048608 | tf_op jit(solution)/shard_map/ppermute | solution.py:439
  127.0 5.0 %outgoing.6 = (bf16[8,128,128]{2,1,0:T(8,128)(2,1)S(1)}, bf16[8,128,128]{2,1,0:T(8,128)(2,1)S(1)}, bf16[2,8,128,128]{3,2,1,0:T(8,128)(2,1)S(1)}, bf16[2,2,8,128,128]{4,3,2,1,0:T(8,128)(2,1)S(1)}) custom-call(bf16[8,128,128]{2,1,0:T(8,128)(2,1)S(1)} %get-tuple-element.124.refs_0_, bf16[2,8,128,128]{3,2,1,0:T(8,128)(2,1)S(1)} %collective-permute-done.4.refs_1_.refs_5_, ...), custom_call_target="tpu_custom_call" | custom-call | flops 26843544 | bytes 262144 | tf_op jit(solution)/shard_map/outgoing/pallas_call | solution.py:408
  137.4 5.0 %outgoing.7 = (bf16[8,128,128]{2,1,0:T(8,128)(2,1)S(1)}, bf16[8,128,128]{2,1,0:T(8,128)(2,1)S(1)}, bf16[2,8,128,128]{3,2,1,0:T(8,128)(2,1)S(1)}, bf16[2,2,8,128,128]{4,3,2,1,0:T(8,128)(2,1)S(1)}) custom-call(bf16[8,128,128]{2,1,0:T(8,128)(2,1)S(1)} %get-tuple-element.135.refs_0_, bf16[2,8,128,128]{3,2,1,0:T(8,128)(2,1)S(1)} %collective-permute-done.10.refs_1_.refs_5_, ...), custom_call_target="tpu_custom_call" | custom-call | flops 26843544 | bytes 262144 | tf_op jit(solution)/shard_map/outgoing/pallas_call | solution.py:408
  149.0 7.1 %collective-permute-done.14 = bf16[2,8,128,128]{3,2,1,0:T(8,128)(2,1)S(1)} collective-permute-done((bf16[2,8,128,128]{3,2,1,0:T(8,128)(2,1)S(1)}, bf16[2,8,128,128]{3,2,1,0:T(8,128)(2,1)S(1)}, u32[]{:S(2)}, u32[]{:S(2)}) %collective-permute-start.14) | collective-permute-done | bytes 524320 | tf_op jit(solution)/shard_map/ppermute | solution.py:439
  156.2 5.2 %collective-permute-start.19 = (bf16[2,8,128,128]{3,2,1,0:T(8,128)(2,1)}, bf16[2,8,128,128]{3,2,1,0:T(8,128)(2,1)}, u32[]{:S(2)}, u32[]{:S(2)}) collective-permute-start(bf16[2,8,128,128]{3,2,1,0:T(8,128)(2,1)} %fusion.11), channel_id=1, source_target_pairs={{4,0},{8,12},{5,1},{9,13},{6,2},{10,14},{7,3},{11,15},{20,16},{24,... | collective-permute-start | bytes 1572872 | tf_op jit(solution)/shard_map/ppermute | solution.py:439
  182.6 5.1 %collective-permute-done.24 = bf16[2,4,128,128]{3,2,1,0:T(8,128)(2,1)S(1)} collective-permute-done((bf16[2,4,128,128]{3,2,1,0:T(8,128)(2,1)S(1)}, bf16[2,4,128,128]{3,2,1,0:T(8,128)(2,1)S(1)}, u32[]{:S(2)}, u32[]{:S(2)}) %collective-permute-start.24) | collective-permute-done | bytes 262176 | tf_op jit(solution)/shard_map/ppermute | solution.py:439
  197.9 4.9 %collective-permute-done.31.rest_7_ = bf16[8,128,128]{2,1,0:T(8,128)(2,1)S(1)} collective-permute-done((bf16[8,128,128]{2,1,0:T(8,128)(2,1)S(1)}, bf16[8,128,128]{2,1,0:T(8,128)(2,1)S(1)}, u32[]{:S(2)}, u32[]{:S(2)}) %collective-permute-start.31) | collective-permute-done | bytes 262176 | tf_op jit(solution)/shard_map/ppermute | solution.py:439
  206.7 46.5 %middle.1 = (bf16[128,128,128]{2,1,0:T(8,128)(2,1)}, bf16[128,128,128]{2,1,0:T(8,128)(2,1)}, bf16[2,8,128,128]{3,2,1,0:T(8,128)(2,1)S(1)}, bf16[2,8,128,128]{3,2...) custom-call(s32[4]{0:T(128)S(1)} %copy-done.16, ...), custom_call_target="tpu_custom_call" | custom-call | flops 150000000 | bytes 943718 | tf_op jit(solution)/shard_map/middle/pallas_call | solution.py:382
  255.1 12.0 %collective-permute-done.37.refs_4_.refs_10_ = bf16[2,8,128,128]{3,2,1,0:T(8,128)(2,1)S(1)} collective-permute-done((bf16[2,8,128,128]{3,2,1,0:T(8,128)(2,1)S(1)}, bf16[2,8,128,128]{3,2,1,0:T(8,128)(2,1)S(1)}, u32[]{:S(2)}, u32[]{:S(2)}) %collective-permute-start.37) | collective-permute-done | bytes 524320 | tf_op jit(solution)/shard_map/ppermute | solution.py:439
  269.1 9.2 %collective-permute-done.43 = bf16[2,8,128,128]{3,2,1,0:T(8,128)(2,1)S(1)} collective-permute-done((bf16[2,8,128,128]{3,2,1,0:T(8,128)(2,1)S(1)}, bf16[2,8,128,128]{3,2,1,0:T(8,128)(2,1)S(1)}, u32[]{:S(2)}, u32[]{:S(2)}) %collective-permute-start.43) | collective-permute-done | bytes 524320 | tf_op jit(solution)/shard_map/ppermute | solution.py:439
  297.0 6.8 %collective-permute-done.45.refs_4_.refs_5_.refs_10_.refs_11_ = bf16[2,2,8,128,128]{4,3,2,1,0:T(8,128)(2,1)S(1)} collective-permute-done((bf16[2,2,8,128,128]{4,3,2,1,0:T(8,128)(2,1)S(1)}, bf16[2,2,8,128,128]{4,3,2,1,0:T(8,128)(2,1)S(1)}, u32[]{:S(2)}, u32[]{:S(2)}) %collective-permute-start.45) | collective-permute-done | bytes 1048608 | tf_op jit(solution)/shard_map/ppermute | solution.py:439
  310.0 6.8 %collective-permute-done.41 = bf16[2,2,8,128,128]{4,3,2,1,0:T(8,128)(2,1)S(1)} collective-permute-done((bf16[2,2,8,128,128]{4,3,2,1,0:T(8,128)(2,1)}, bf16[2,2,8,128,128]{4,3,2,1,0:T(8,128)(2,1)S(1)}, u32[]{:S(2)}, u32[]{:S(2)}) %collective-permute-start.41) | collective-permute-done | bytes 1048608 | tf_op jit(solution)/shard_map/ppermute | solution.py:439
  319.7 5.6 %collective-permute-done.51.refs_4_.refs_5_.refs_10_.refs_11_ = bf16[2,2,8,128,128]{4,3,2,1,0:T(8,128)(2,1)S(1)} collective-permute-done((bf16[2,2,8,128,128]{4,3,2,1,0:T(8,128)(2,1)S(1)}, bf16[2,2,8,128,128]{4,3,2,1,0:T(8,128)(2,1)S(1)}, u32[]{:S(2)}, u32[]{:S(2)}) %collective-permute-start.51) | collective-permute-done | bytes 1048608 | tf_op jit(solution)/shard_map/ppermute | solution.py:439
  330.3 12.8 %collective-permute-done.47 = bf16[2,2,8,128,128]{4,3,2,1,0:T(8,128)(2,1)S(1)} collective-permute-done((bf16[2,2,8,128,128]{4,3,2,1,0:T(8,128)(2,1)S(1)}, bf16[2,2,8,128,128]{4,3,2,1,0:T(8,128)(2,1)S(1)}, u32[]{:S(2)}, u32[]{:S(2)}) %collective-permute-start.47) | collective-permute-done | bytes 1048608 | tf_op jit(solution)/shard_map/ppermute | solution.py:439
  348.4 4.6 %collective-permute-start.42 = (bf16[2,8,128,128]{3,2,1,0:T(8,128)(2,1)S(1)}, bf16[2,8,128,128]{3,2,1,0:T(8,128)(2,1)S(1)}, u32[]{:S(2)}, u32[]{:S(2)}) collective-permute-start(bf16[2,8,128,128]{3,2,1,0:T(8,128)(2,1)S(1)} %fusion.10), channel_id=1, source_target_pairs={{4,0},{8,12},{5,1},{9,13},{6,2},{10,14},{7,3},{11,15},{20,16},{24,... | collective-permute-start | bytes 1572872 | tf_op jit(solution)/shard_map/ppermute | solution.py:439
  353.6 6.0 %collective-permute-done.57.refs_4_.refs_5_.refs_10_.refs_11_ = bf16[2,2,4,128,128]{4,3,2,1,0:T(8,128)(2,1)S(1)} collective-permute-done((bf16[2,2,4,128,128]{4,3,2,1,0:T(8,128)(2,1)S(1)}, bf16[2,2,4,128,128]{4,3,2,1,0:T(8,128)(2,1)S(1)}, u32[]{:S(2)}, u32[]{:S(2)}) %collective-permute-start.57) | collective-permute-done | bytes 524320 | tf_op jit(solution)/shard_map/ppermute | solution.py:439
  375.0 5.2 %collective-permute-done.48 = bf16[2,8,128,128]{3,2,1,0:T(8,128)(2,1)S(1)} collective-permute-done((bf16[2,8,128,128]{3,2,1,0:T(8,128)(2,1)S(1)}, bf16[2,8,128,128]{3,2,1,0:T(8,128)(2,1)S(1)}, u32[]{:S(2)}, u32[]{:S(2)}) %collective-permute-start.48) | collective-permute-done | bytes 524320 | tf_op jit(solution)/shard_map/ppermute | solution.py:439
  411.3 5.4 %collective-permute-done.70.rest_8_ = bf16[4,128,128]{2,1,0:T(8,128)(2,1)S(1)} collective-permute-done((bf16[4,128,128]{2,1,0:T(8,128)(2,1)S(1)}, bf16[4,128,128]{2,1,0:T(8,128)(2,1)S(1)}, u32[]{:S(2)}, u32[]{:S(2)}) %collective-permute-start.70) | collective-permute-done | bytes 131104 | tf_op jit(solution)/shard_map/ppermute | solution.py:439
  421.8 9.5 %finish.1 = bf16[128,128,128]{2,1,0:T(8,128)(2,1)} custom-call(bf16[128,128,128]{2,1,0:T(8,128)(2,1)} %get-tuple-element.167.pair_ref, bf16[128,128,128]{2,1,0:T(8,128)(2,1)} %get-tuple-element.168.gate_ref, bf16[2,64,128]{2,1,0:T(8,128)(2,1)S(1)} %copy-done.8, f32[64,1,128]{2,1,0:T(1,128)S(1)} %broadcast_in_dim.15.gain_ref, ...), custom_call_target="tpu_custom_call" | custom-call | flops 50000000 | bytes 734003 | tf_op jit(solution)/shard_map/finish/pallas_call | solution.py:366
  (253 shorter events, 185.1 us)
Async XLA Ops:
  74.8 18.2 %collective-permute-start.5 = (bf16[2,12,128,128]{3,2,1,0:T(8,128)(2,1)S(1)}, bf16[2,12,128,128]{3,2,1,0:T(8,128)(2,1)S(1)}, u32[]{:S(2)}, u32[]{:S(2)}) collective-permute-start(bf16[2,12,128,128]{3,2,1,0:T(8,128)(2,1)S(1)} %pad_maximum_fusion.4), channel_id=1, source_target_pairs={{0,4},{12,8},{1,5},{13,9},{2,6},{14,10},{3,7},{15,11},{16,20},{28,... | collective-permute-start | bytes 2359304 | tf_op jit(solution)/shard_map/ppermute | solution.py:439
  77.7 19.5 %collective-permute-start.7 = (bf16[2,12,128,128]{3,2,1,0:T(8,128)(2,1)S(1)}, bf16[2,12,128,128]{3,2,1,0:T(8,128)(2,1)S(1)}, u32[]{:S(2)}, u32[]{:S(2)}) collective-permute-start(bf16[2,12,128,128]{3,2,1,0:T(8,128)(2,1)S(1)} %pad_maximum_fusion.5), channel_id=1, source_target_pairs={{4,8},{8,4},{5,9},{9,5},{6,10},{10,6},{7,11},{11,7},{20,24},{24,20... | collective-permute-start | bytes 2359304 | tf_op jit(solution)/shard_map/ppermute | solution.py:439
  94.3 23.1 %collective-permute-start.11 = (bf16[2,16,128,128]{3,2,1,0:T(8,128)(2,1)}, bf16[2,16,128,128]{3,2,1,0:T(8,128)(2,1)S(1)}, u32[]{:S(2)}, u32[]{:S(2)}) collective-permute-start(bf16[2,16,128,128]{3,2,1,0:T(8,128)(2,1)} %pad_maximum_fusion.2), channel_id=1, source_target_pairs={{0,4},{12,8},{1,5},{13,9},{2,6},{14,10},{3,7},{15,11},{16,20},{28,... | collective-permute-start | bytes 3145736 | tf_op jit(solution)/shard_map/ppermute | solution.py:439
  97.3 23.6 %collective-permute-start.12 = (bf16[2,16,128,128]{3,2,1,0:T(8,128)(2,1)S(1)}, bf16[2,16,128,128]{3,2,1,0:T(8,128)(2,1)S(1)}, u32[]{:S(2)}, u32[]{:S(2)}) collective-permute-start(bf16[2,16,128,128]{3,2,1,0:T(8,128)(2,1)S(1)} %pad_maximum_fusion.3), channel_id=1, source_target_pairs={{4,8},{8,4},{5,9},{9,5},{6,10},{10,6},{7,11},{11,7},{20,24},{24,20... | collective-permute-start | bytes 3145736 | tf_op jit(solution)/shard_map/ppermute | solution.py:439
  102.7 20.6 %collective-permute-start.8 = (bf16[2,2,8,128,128]{4,3,2,1,0:T(8,128)(2,1)S(1)}, bf16[2,2,8,128,128]{4,3,2,1,0:T(8,128)(2,1)S(1)}, u32[]{:S(2)}, u32[]{:S(2)}) collective-permute-start(bf16[2,2,8,128,128]{4,3,2,1,0:T(8,128)(2,1)S(1)} %get-tuple-element.122), channel_id=1, source_target_pairs={{0,1},{1,0},{2,3},{3,2},{4,5},{5,4},{6,7},{7,6},{8,9},{9,8},{10,11... | collective-permute-start | bytes 3145736 | tf_op jit(solution)/shard_map/ppermute | solution.py:439
  118.6 16.6 %collective-permute-start.16 = (bf16[2,12,128,128]{3,2,1,0:T(8,128)(2,1)}, bf16[2,12,128,128]{3,2,1,0:T(8,128)(2,1)S(1)}, u32[]{:S(2)}, u32[]{:S(2)}) collective-permute-start(bf16[2,12,128,128]{3,2,1,0:T(8,128)(2,1)} %pad_maximum_fusion.6), channel_id=1, source_target_pairs={{0,4},{12,8},{1,5},{13,9},{2,6},{14,10},{3,7},{15,11},{16,20},{28,... | collective-permute-start | bytes 2359304 | tf_op jit(solution)/shard_map/ppermute | solution.py:439
  120.9 16.6 %collective-permute-start.17 = (bf16[2,12,128,128]{3,2,1,0:T(8,128)(2,1)}, bf16[2,12,128,128]{3,2,1,0:T(8,128)(2,1)S(1)}, u32[]{:S(2)}, u32[]{:S(2)}) collective-permute-start(bf16[2,12,128,128]{3,2,1,0:T(8,128)(2,1)} %pad_maximum_fusion.7), channel_id=1, source_target_pairs={{4,8},{8,4},{5,9},{9,5},{6,10},{10,6},{7,11},{11,7},{20,24},{24,20... | collective-permute-start | bytes 2359304 | tf_op jit(solution)/shard_map/ppermute | solution.py:439
  144.2 17.9 %collective-permute-start.21 = (bf16[2,8,128,128]{3,2,1,0:T(8,128)(2,1)S(1)}, bf16[2,8,128,128]{3,2,1,0:T(8,128)(2,1)S(1)}, u32[]{:S(2)}, u32[]{:S(2)}) collective-permute-start(bf16[2,8,128,128]{3,2,1,0:T(8,128)(2,1)S(1)} %pad_maximum_fusion.16), channel_id=1, source_target_pairs={{0,4},{12,8},{1,5},{13,9},{2,6},{14,10},{3,7},{15,11},{16,20},{28,... | collective-permute-start | bytes 1572872 | tf_op jit(solution)/shard_map/ppermute | solution.py:439
  145.6 18.6 %collective-permute-start.22 = (bf16[2,8,128,128]{3,2,1,0:T(8,128)(2,1)S(1)}, bf16[2,8,128,128]{3,2,1,0:T(8,128)(2,1)S(1)}, u32[]{:S(2)}, u32[]{:S(2)}) collective-permute-start(bf16[2,8,128,128]{3,2,1,0:T(8,128)(2,1)S(1)} %pad_maximum_fusion.17), channel_id=1, source_target_pairs={{4,8},{8,4},{5,9},{9,5},{6,10},{10,6},{7,11},{11,7},{20,24},{24,20... | collective-permute-start | bytes 1572872 | tf_op jit(solution)/shard_map/ppermute | solution.py:439
  156.2 15.9 %collective-permute-start.19 = (bf16[2,8,128,128]{3,2,1,0:T(8,128)(2,1)}, bf16[2,8,128,128]{3,2,1,0:T(8,128)(2,1)}, u32[]{:S(2)}, u32[]{:S(2)}) collective-permute-start(bf16[2,8,128,128]{3,2,1,0:T(8,128)(2,1)} %fusion.11), channel_id=1, source_target_pairs={{4,0},{8,12},{5,1},{9,13},{6,2},{10,14},{7,3},{11,15},{20,16},{24,... | collective-permute-start | bytes 1572872 | tf_op jit(solution)/shard_map/ppermute | solution.py:439
  176.9 21.0 %collective-permute-start.29 = (bf16[8,128,128]{2,1,0:T(8,128)(2,1)S(1)}, bf16[8,128,128]{2,1,0:T(8,128)(2,1)S(1)}, u32[]{:S(2)}, u32[]{:S(2)}) collective-permute-start(bf16[8,128,128]{2,1,0:T(8,128)(2,1)S(1)} %get-tuple-element.225), channel_id=1, source_target_pairs={{0,2},{1,3},{2,0},{3,1},{4,6},{5,7},{6,4},{7,5},{8,10},{9,11},{10,... | collective-permute-start | bytes 786440 | tf_op jit(solution)/shard_map/ppermute | solution.py:439
  182.0 15.9 %collective-permute-start.30 = (bf16[8,128,128]{2,1,0:T(8,128)(2,1)S(1)}, bf16[8,128,128]{2,1,0:T(8,128)(2,1)S(1)}, u32[]{:S(2)}, u32[]{:S(2)}) collective-permute-start(bf16[8,128,128]{2,1,0:T(8,128)(2,1)S(1)} %get-tuple-element.223), channel_id=1, source_target_pairs={{0,2},{1,3},{2,0},{3,1},{4,6},{5,7},{6,4},{7,5},{8,10},{9,11},{10,... | collective-permute-start | bytes 786440 | tf_op jit(solution)/shard_map/ppermute | solution.py:439
  280.5 23.3 %collective-permute-start.45 = (bf16[2,2,8,128,128]{4,3,2,1,0:T(8,128)(2,1)S(1)}, bf16[2,2,8,128,128]{4,3,2,1,0:T(8,128)(2,1)S(1)}, u32[]{:S(2)}, u32[]{:S(2)}) collective-permute-start(bf16[2,2,8,128,128]{4,3,2,1,0:T(8,128)(2,1)S(1)} %pad_maximum_fusion.refs_0_.refs_1_.refs_8_.refs_9_), channel_id=1, source_target_pairs={{0,4},{12,8},{1,5},{13,9},{2,6},{14,10},{3,7},{15,11},{16,20},{28,... | collective-permute-start | bytes 3145736 | tf_op jit(solution)/shard_map/ppermute | solution.py:439
  289.5 27.3 %collective-permute-start.41 = (bf16[2,2,8,128,128]{4,3,2,1,0:T(8,128)(2,1)}, bf16[2,2,8,128,128]{4,3,2,1,0:T(8,128)(2,1)S(1)}, u32[]{:S(2)}, u32[]{:S(2)}) collective-permute-start(bf16[2,2,8,128,128]{4,3,2,1,0:T(8,128)(2,1)} %get-tuple-element.173), channel_id=1, source_target_pairs={{4,8},{8,4},{5,9},{9,5},{6,10},{10,6},{7,11},{11,7},{20,24},{24,20... | collective-permute-start | bytes 3145736 | tf_op jit(solution)/shard_map/ppermute | solution.py:439
  303.8 21.5 %collective-permute-start.51 = (bf16[2,2,8,128,128]{4,3,2,1,0:T(8,128)(2,1)S(1)}, bf16[2,2,8,128,128]{4,3,2,1,0:T(8,128)(2,1)S(1)}, u32[]{:S(2)}, u32[]{:S(2)}) collective-permute-start(bf16[2,2,8,128,128]{4,3,2,1,0:T(8,128)(2,1)S(1)} %pad_maximum_fusion.1.refs_0_.refs_1_.refs_8_.refs_9_), channel_id=1, source_target_pairs={{0,4},{12,8},{1,5},{13,9},{2,6},{14,10},{3,7},{15,11},{16,20},{28,... | collective-permute-start | bytes 3145736 | tf_op jit(solution)/shard_map/ppermute | solution.py:439
  316.8 26.2 %collective-permute-start.47 = (bf16[2,2,8,128,128]{4,3,2,1,0:T(8,128)(2,1)S(1)}, bf16[2,2,8,128,128]{4,3,2,1,0:T(8,128)(2,1)S(1)}, u32[]{:S(2)}, u32[]{:S(2)}) collective-permute-start(bf16[2,2,8,128,128]{4,3,2,1,0:T(8,128)(2,1)S(1)} %get-tuple-element.181), channel_id=1, source_target_pairs={{4,8},{8,4},{5,9},{9,5},{6,10},{10,6},{7,11},{11,7},{20,24},{24,20... | collective-permute-start | bytes 3145736 | tf_op jit(solution)/shard_map/ppermute | solution.py:439
  325.4 20.3 %collective-permute-start.55 = (bf16[2,4,128,128]{3,2,1,0:T(8,128)(2,1)S(1)}, bf16[2,4,128,128]{3,2,1,0:T(8,128)(2,1)S(1)}, u32[]{:S(2)}, u32[]{:S(2)}) collective-permute-start(bf16[2,4,128,128]{3,2,1,0:T(8,128)(2,1)S(1)} %get-tuple-element.194), channel_id=1, source_target_pairs={{0,2},{1,3},{2,0},{3,1},{4,6},{5,7},{6,4},{7,5},{8,10},{9,11},{10,... | collective-permute-start | bytes 786440 | tf_op jit(solution)/shard_map/ppermute | solution.py:439
  343.1 27.6 %collective-permute-start.53 = (bf16[2,2,8,128,128]{4,3,2,1,0:T(8,128)(2,1)S(1)}, bf16[2,2,8,128,128]{4,3,2,1,0:T(8,128)(2,1)S(1)}, u32[]{:S(2)}, u32[]{:S(2)}) collective-permute-start(bf16[2,2,8,128,128]{4,3,2,1,0:T(8,128)(2,1)S(1)} %get-tuple-element.190), channel_id=1, source_target_pairs={{4,8},{8,4},{5,9},{9,5},{6,10},{10,6},{7,11},{11,7},{20,24},{24,20... | collective-permute-start | bytes 3145736 | tf_op jit(solution)/shard_map/ppermute | solution.py:439
  348.3 21.0 %collective-permute-start.56 = (bf16[2,4,128,128]{3,2,1,0:T(8,128)(2,1)S(1)}, bf16[2,4,128,128]{3,2,1,0:T(8,128)(2,1)S(1)}, u32[]{:S(2)}, u32[]{:S(2)}) collective-permute-start(bf16[2,4,128,128]{3,2,1,0:T(8,128)(2,1)S(1)} %fusion.29), channel_id=1, source_target_pairs={{0,1},{1,0},{2,3},{3,2},{4,5},{5,4},{6,7},{7,6},{8,9},{9,8},{10,11... | collective-permute-start | bytes 786440 | tf_op jit(solution)/shard_map/ppermute | solution.py:439
  348.4 16.4 %collective-permute-start.42 = (bf16[2,8,128,128]{3,2,1,0:T(8,128)(2,1)S(1)}, bf16[2,8,128,128]{3,2,1,0:T(8,128)(2,1)S(1)}, u32[]{:S(2)}, u32[]{:S(2)}) collective-permute-start(bf16[2,8,128,128]{3,2,1,0:T(8,128)(2,1)S(1)} %fusion.10), channel_id=1, source_target_pairs={{4,0},{8,12},{5,1},{9,13},{6,2},{10,14},{7,3},{11,15},{20,16},{24,... | collective-permute-start | bytes 1572872 | tf_op jit(solution)/shard_map/ppermute | solution.py:439
  364.8 15.4 %collective-permute-start.48 = (bf16[2,8,128,128]{3,2,1,0:T(8,128)(2,1)S(1)}, bf16[2,8,128,128]{3,2,1,0:T(8,128)(2,1)S(1)}, u32[]{:S(2)}, u32[]{:S(2)}) collective-permute-start(bf16[2,8,128,128]{3,2,1,0:T(8,128)(2,1)S(1)} %fusion.9), channel_id=1, source_target_pairs={{4,0},{8,12},{5,1},{9,13},{6,2},{10,14},{7,3},{11,15},{20,16},{24,... | collective-permute-start | bytes 1572872 | tf_op jit(solution)/shard_map/ppermute | solution.py:439
  370.7 15.4 %collective-permute-start.59 = (bf16[2,2,4,128,128]{4,3,2,1,0:T(8,128)(2,1)S(1)}, bf16[2,2,4,128,128]{4,3,2,1,0:T(8,128)(2,1)S(1)}, u32[]{:S(2)}, u32[]{:S(2)}) collective-permute-start(bf16[2,2,4,128,128]{4,3,2,1,0:T(8,128)(2,1)S(1)} %get-tuple-element.198), channel_id=1, source_target_pairs={{4,8},{8,4},{5,9},{9,5},{6,10},{10,6},{7,11},{11,7},{20,24},{24,20... | collective-permute-start | bytes 1572872 | tf_op jit(solution)/shard_map/ppermute | solution.py:439
  389.7 28.0 %collective-permute-start.67 = (bf16[8,128,128]{2,1,0:T(8,128)(2,1)S(1)}, bf16[8,128,128]{2,1,0:T(8,128)(2,1)S(1)}, u32[]{:S(2)}, u32[]{:S(2)}) collective-permute-start(bf16[8,128,128]{2,1,0:T(8,128)(2,1)S(1)} %get-tuple-element.219), channel_id=1, source_target_pairs={{0,2},{1,3},{2,0},{3,1},{4,6},{5,7},{6,4},{7,5},{8,10},{9,11},{10,... | collective-permute-start | bytes 786440 | tf_op jit(solution)/shard_map/ppermute | solution.py:439
  399.2 18.5 %collective-permute-start.68 = (bf16[8,128,128]{2,1,0:T(8,128)(2,1)S(1)}, bf16[8,128,128]{2,1,0:T(8,128)(2,1)S(1)}, u32[]{:S(2)}, u32[]{:S(2)}) collective-permute-start(bf16[8,128,128]{2,1,0:T(8,128)(2,1)S(1)} %get-tuple-element.217), channel_id=1, source_target_pairs={{0,2},{1,3},{2,0},{3,1},{4,6},{5,7},{6,4},{7,5},{8,10},{9,11},{10,... | collective-permute-start | bytes 786440 | tf_op jit(solution)/shard_map/ppermute | solution.py:439
  (75 other events, 864.5 us)

commit v7 on v5

--- a/solution.py
+++ b/solution.py
@@ -9,11 +9,13 @@
 
 BLOCK = 128
 EPS = 1e-05
-OUT_SIZES = (8, 10, 8, 6)
-IN_SIZES = (8, 10, 8, 6)
-OUT_ORDER = {'i1': ('i0',), 'i2': ('i1',), 'i3': ('i2',), 'i4': ('i3',), 'i5': ('i4',), 'a1': ('a0',), 'a2': ('a1',), 'a3': ('a2',), 'a4': ('a3',), 'a5': ('a4',), 'x1': ('x0', 'a0'), 'x2': ('x1',), 'x3': ('x2',), 'p3': ('o1',)}
-IN_ORDER = {'i0x': ('i0',), 'i1': ('i0x',), 'i2': ('i1',), 'i3': ('i2',), 'a1': ('a0',), 'a2': ('a1',), 'a3': ('a2',), 'x1': ('x0', 'i0'), 'x2': ('x1',), 'x3': ('x2',)}
-STEP = 32
+OUT_SIZES = (8, 8, 8, 4, 4)
+IN_SIZES = (8, 8, 8, 4, 4)
+OUT_GROUPS = (1, 1, 1, 1, 1)
+IN_GROUPS = (1, 1, 1, 1, 1)
+OUT_ORDER = {'i1': ('i0',), 'i2': ('i1',), 'i3': ('i2',), 'i4': ('i3',), 'i5': ('i4',), 'i6': ('i5',), 'a1': ('a0',), 'a2': ('a1',), 'a3': ('a2',), 'a4': ('a3',), 'a5': ('a4', 'p1'), 'a6': ('a5',), 'x1': ('x0', 'a0'), 'x2': ('x1', 'a1'), 'x3': ('x2',), 'x4': ('x3',), 'o2': ('o1',), 'p2': ('o0',), 'p3': ('o1',), 'p4': ('o2',)}
+IN_ORDER = {'i0x': ('i0',), 'i2': ('i1',), 'i3': ('i2',), 'i4': ('i3',), 'a1': ('a0',), 'a2': ('a1',), 'a3': ('a2',), 'x1': ('x0', 'i0'), 'o2': ('o1',), 'o3': ('o2',), 'o4': ('o3',), 'x2': ('i0x',), 'b0': ('x3',)}
+STEP = 16
 TOLD = 0.05
 VMEM = 48 * 1024 * 1024
 
@@ -116,17 +118,13 @@
     return (centred * lax.rsqrt(spread + EPS) * gain).astype(jnp.bfloat16)
 
 
-def logistic(values):
-    return 0.5 * jnp.tanh(0.5 * values) + 0.5
-
-
 def tile_mask(chain_ref, block_mask_ref):
     row, col = lax.axis_index("row"), lax.axis_index("col")
     seen = (chain_ref[row] == chain_ref[col]) | (block_mask_ref[row, col] == 1)
     return jnp.where(seen, 1.0, 0.0).astype(jnp.float32)
 
 
-def pick_weights(w_ref, turned, picked):
+def pick_weights(w_ref, w_gate_ref, mask, turned, picked, picked_gate):
     @pl.when(pl.program_id(0) == 0)
     def _():
         turned[...] = w_ref[0].astype(jnp.float32).T
@@ -135,18 +133,20 @@
         rows = []
         for kind in range(4):
             for other in (x, 1 - x):
-                rows.append(turned[pl.ds(pl.multiple_of((2 * kind + other) * half, 8), half), :])
+                some = turned[pl.ds(pl.multiple_of((2 * kind + other) * half, 8), half), :]
+                rows.append(some * (0.5 if kind % 2 else 0.5 * mask))
         picked[...] = jnp.concatenate(rows, 0).astype(jnp.bfloat16)
-
-
-def project_part(normed, mask, picked, scratch, sides, sizes):
+        picked_gate[...] = (w_gate_ref[0].astype(jnp.float32) * 0.5).astype(jnp.bfloat16)
+
+
+def project_part(normed, picked, scratch, sides, sizes):
     hidden = dot(picked[...], normed, NT)
     width = picked.shape[0] // 4
     cols = normed.shape[0] // STEP
     for side, refs in enumerate(sides):
         values = hidden[2 * side * width : (2 * side + 1) * width]
         gates = hidden[(2 * side + 1) * width : (2 * side + 2) * width]
-        kept = mask * logistic(gates) * values
+        kept = (jnp.tanh(gates) + 1.0) * values
         for row in range(STEP):
             scratch[side, pl.ds(row, width, stride=STEP), :] = kept[:, row * cols : (row + 1) * cols]
         done = 0
@@ -171,19 +171,18 @@
     return lefts, rights
 
 
-def project_all(rows, gain, mask, w_gate_ref, gate_ref, picked, scratch, outs, sizes, apart):
+def project_all(rows, gain, gate_ref, picked, picked_gate, scratch, outs, sizes, apart):
     normed = norm_rows(rows, gain)
-    project_part(normed, mask, picked, scratch, split_sides(outs, len(sizes), apart), sizes)
-    gate = logistic(dot(normed, w_gate_ref[0]))
+    project_part(normed, picked, scratch, split_sides(outs, len(sizes), apart), sizes)
+    gate = 0.5 * jnp.tanh(dot(normed, picked_gate[...])) + 0.5
     gate_ref[...] = gate.astype(gate_ref.dtype).reshape(gate_ref.shape)
 
 
 def first_kernel(sizes, chain_ref, block_mask_ref, pair_ref, w_ref, w_gate_ref, gain_ref, gate_ref, *rest):
-    *outs, turned, picked, scratch = rest
-    pick_weights(w_ref, turned, picked)
+    *outs, turned, picked, picked_gate, scratch = rest
+    pick_weights(w_ref, w_gate_ref, tile_mask(chain_ref, block_mask_ref), turned, picked, picked_gate)
     rows = pair_ref[...].reshape(-1, pair_ref.shape[-1])
-    mask = tile_mask(chain_ref, block_mask_ref)
-    project_all(rows, gain_ref[0:1], mask, w_gate_ref, gate_ref, picked, scratch, outs, sizes, True)
+    project_all(rows, gain_ref[0:1], gate_ref, picked, picked_gate, scratch, outs, sizes, True)
 
 
 def finish_rows(pair_ref, gate_ref, product_refs, w_out_ref, gain_ref, scratch, twice, out_ref):
@@ -239,12 +238,12 @@
     gain_in_ref,
     *rest,
 ):
-    product_refs, (out_ref, next_ref, *outs, update, twice, turned, picked, scratch) = rest[:count], rest[count:]
-    pick_weights(w_ref, turned, picked)
+    product_refs, (out_ref, next_ref, *outs) = rest[:count], rest[count:]
+    *outs, update, twice, turned, picked, picked_gate, scratch = outs
+    pick_weights(w_ref, w_gate_ref, tile_mask(chain_ref, block_mask_ref), turned, picked, picked_gate)
     finish_rows(pair_ref, gate_ref, product_refs, w_out_ref, gain_out_ref, update, twice, out_ref)
     rows = out_ref[...].reshape(-1, out_ref.shape[-1])
-    mask = tile_mask(chain_ref, block_mask_ref)
-    project_all(rows, gain_in_ref[1:2], mask, w_gate_ref, next_ref, picked, scratch, outs, sizes, False)
+    project_all(rows, gain_in_ref[1:2], next_ref, picked, picked_gate, scratch, outs, sizes, False)
 
 
 def outgoing_kernel(left, left_pair, right, right_pair, right_far, right_near, outs, rights):
@@ -327,6 +326,7 @@
     return [
         pltpu.VMEM((w_in.shape[2], w_in.shape[1]), jnp.float32),
         pltpu.VMEM((4 * width, w_in.shape[1]), jnp.bfloat16),
+        pltpu.VMEM((w_in.shape[1], w_in.shape[1]), jnp.bfloat16),
         pltpu.VMEM((2, width * STEP, pair.shape[1]), jnp.float32),
     ]
 
@@ -454,20 +454,25 @@
     return (row == 1) | (row == 2)
 
 
-def shared_steps(graph, n, mine, other):
+def shared_steps(graph, groups, mine, other):
     inner = is_inner()
     get = graph.get
-
-    def ready(k):
-        return jnp.where(inner, mine(k), get(f"o{n}")[k])
-
-    graph.send(f"o{n}", "out", other)
-    graph.send(f"b{n}", "x", lambda: ready(1))
-    graph.add(f"k{n}", lambda: ready(0), lambda array: array)
-
-
-def finished(graph, count):
-    return [graph.get(kind + str(n)) for kind in ("k", "b") for n in range(count)]
+    first, names = 0, []
+
+    def joined(arrays, axis):
+        return arrays[0] if len(arrays) == 1 else jnp.concatenate(arrays, axis)
+
+    for g, size in enumerate(groups):
+        chunks = range(first, first + size)
+        first += size
+
+        def ready(k, g=g, chunks=chunks):
+            return jnp.where(inner, joined([mine(n, k) for n in chunks], 0), get(f"o{g}")[k])
+
+        graph.send(f"o{g}", "out", lambda chunks=chunks: joined([other(n) for n in chunks], 1))
+        graph.send(f"b{g}", "x", lambda ready=ready: ready(1))
+        graph.add(f"k{g}", lambda ready=ready: ready(0), lambda array: array)
+    return [get(kind + str(g)) for kind in ("k", "b") for g in range(len(groups))]
 
 
 def outgoing(parts):
@@ -533,13 +538,12 @@
     for n in range(count):
         graph.add(f"p{n}", lambda n=n: later(n, 1), functools.partial(product, n))
         send(f"c{n}", "core", lambda n=n: get(f"p{n}")[3])
-        shared_steps(
-            graph,
-            n,
-            lambda k, n=n: get(f"p{n}")[k] + get(f"c{n}")[0, k],
-            lambda n=n: get(f"p{n}")[2] + get(f"c{n}")[1],
-        )
-    return finished(graph, count)
+    return shared_steps(
+        graph,
+        OUT_GROUPS,
+        lambda n, k: get(f"p{n}")[k] + get(f"c{n}")[0, k],
+        lambda n: get(f"p{n}")[2] + get(f"c{n}")[1],
+    )
 
 
 def incoming(parts):
@@ -579,13 +583,12 @@
     for n in range(count):
         graph.add(f"p{n}", lambda n=n: get(f"j{n}") if n else parts[0], functools.partial(product, n))
         send(f"a{n}", "across", lambda n=n: get(f"p{n}")[3])
-        shared_steps(
-            graph,
-            n,
-            lambda k, n=n: get(f"p{n}")[k] + get(f"a{n}")[1, k],
-            lambda n=n: get(f"p{n}")[2] + get(f"a{n}")[0],
-        )
-    return finished(graph, count)
+    return shared_steps(
+        graph,
+        IN_GROUPS,
+        lambda n, k: get(f"p{n}")[k] + get(f"a{n}")[1, k],
+        lambda n: get(f"p{n}")[2] + get(f"a{n}")[0],
+    )
 
 
 def four_by_four(pair, chain, block_mask, w_in, w_gate, w_out, gain_in, gain_out):

time: 410 us -> 363 us (0.89)
  waiting for transfers between devices: 225 us -> 172 us
  starting transfers between devices: 76.2 us -> 98.2 us
  Pallas kernels: 83.4 us -> 72.9 us
  other arithmetic: 10.8 us -> 6.36 us
    ppermute x59 -> x72, waiting for transfers between devices: 225 us -> 172 us  [send(): self.add(name, operand, lambda array: lax.ppermute(array, axis, pairs))]
    ppermute x59 -> x72, starting transfers between devices: 76.2 us -> 98.2 us  [send(): self.add(name, operand, lambda array: lax.ppermute(array, axis, pairs))]
    pallas_call x8 -> x10, Pallas kernels: 34.9 us -> 30.2 us  [product_call(): pl.pallas_call(functools.partial(pieces_kernel, kernel, len(pieces)), gri...]
  transfers between devices with their start and end apart: 59 -> 72, of which waited for: 35 -> 39; matrix products, arithmetic and copies ran while one was open for 3% -> 2% of each run, Pallas kernels for 9% -> 8%
where the time goes in v7:
time: 363 us; the launch traced here: 359 us
  waiting for transfers between devices  172 us (47%)
  starting transfers between devices  98.2 us (27%)
  Pallas kernels  72.9 us (20%)
  local copies, waits for them, and re-layouts  8.73 us (2%)
  other arithmetic  6.36 us (2%)
    ppermute x72, waiting for transfers between devices, send(): self.add(name, operand, lambda array: lax.ppermute(array, axis, pairs))  172 us
    ppermute x72, starting transfers between devices, send(): self.add(name, operand, lambda array: lax.ppermute(array, axis, pairs))  98.2 us
    pallas_call x10, Pallas kernels, product_call(): pl.pallas_call(functools.partial(pieces_kernel, kernel, len(pieces)), gri...  30.2 us
    pallas_call x1, Pallas kernels, middle_call(): pl.pallas_call(functools.partial(middle_kernel, IN_SIZES, len(products)),...  19.1 us
    pallas_call x1, Pallas kernels, first_call(): pl.pallas_call(functools.partial(first_kernel, OUT_SIZES), grid=(pair.sha...  14 us
    pallas_call x1, Pallas kernels, finish_call(): pl.pallas_call(finish_kernel, grid=(pair.shape[0] // STEP,), in_specs=[ti...  9.53 us
    unnamed x82, local copies, waits for them, and re-layouts  7.34 us
  transfers between devices with their start and end apart: 72, of which 39 were waited for; matrix products, arithmetic and copies ran while one was open for 2% of the time, Pallas kernels for 8%

profile of v7, /device:TPU:16, one launch (start us, length us, event | category | flops | bytes accessed | tf_op | source)
XLA Modules:
  0.0 359.2 jit_solution(5107515585170715147)
XLA Ops:
  3.8 14.0 %project.1 = (bf16[128,128,128]{2,1,0:T(8,128)(2,1)}, bf16[8,128,128]{2,1,0:T(8,128)(2,1)S(1)}, bf16[8,128,128]{2,1,0:T(8,128)(2,1)S(1)}, bf16[8,128,128]{2,1,0:...) custom-call(s32[4]{0:T(128)S(1)} %copy-done.27, ...), custom_call_target="tpu_custom_call" | custom-call | flops 100000000 | bytes 419430 | tf_op jit(solution)/shard_map/project/pallas_call | solution.py:343
  23.0 6.0 %collective-permute-done.3.refs_10_ = bf16[8,128,128]{2,1,0:T(8,128)(2,1)S(1)} collective-permute-done((bf16[8,128,128]{2,1,0:T(8,128)(2,1)S(1)}, bf16[8,128,128]{2,1,0:T(8,128)(2,1)S(1)}, u32[]{:S(2)}, u32[]{:S(2)}) %collective-permute-start.3) | collective-permute-done | bytes 262176 | tf_op jit(solution)/shard_map/ppermute | solution.py:431
  36.8 7.5 %collective-permute-done.4.refs_1_.refs_5_ = bf16[2,8,128,128]{3,2,1,0:T(8,128)(2,1)S(1)} collective-permute-done((bf16[2,8,128,128]{3,2,1,0:T(8,128)(2,1)S(1)}, bf16[2,8,128,128]{3,2,1,0:T(8,128)(2,1)S(1)}, u32[]{:S(2)}, u32[]{:S(2)}) %collective-permute-start.4) | collective-permute-done | bytes 524320 | tf_op jit(solution)/shard_map/ppermute | solution.py:431
  52.1 8.6 %collective-permute-done.10.refs_1_.refs_5_ = bf16[2,8,128,128]{3,2,1,0:T(8,128)(2,1)S(1)} collective-permute-done((bf16[2,8,128,128]{3,2,1,0:T(8,128)(2,1)S(1)}, bf16[2,8,128,128]{3,2,1,0:T(8,128)(2,1)S(1)}, u32[]{:S(2)}, u32[]{:S(2)}) %collective-permute-start.10) | collective-permute-done | bytes 524320 | tf_op jit(solution)/shard_map/ppermute | solution.py:431
  60.8 6.1 %collective-permute-done.5.refs_6_.refs_7_ = bf16[2,12,128,128]{3,2,1,0:T(8,128)(2,1)S(1)} collective-permute-done((bf16[2,12,128,128]{3,2,1,0:T(8,128)(2,1)S(1)}, bf16[2,12,128,128]{3,2,1,0:T(8,128)(2,1)S(1)}, u32[]{:S(2)}, u32[]{:S(2)}) %collective-permute-start.5) | collective-permute-done | bytes 786464 | tf_op jit(solution)/shard_map/ppermute | solution.py:431
  75.8 15.3 %collective-permute-done.11.refs_2_.refs_3_.refs_6_.refs_7_ = bf16[2,16,128,128]{3,2,1,0:T(8,128)(2,1)S(1)} collective-permute-done((bf16[2,16,128,128]{3,2,1,0:T(8,128)(2,1)S(1)}, bf16[2,16,128,128]{3,2,1,0:T(8,128)(2,1)S(1)}, u32[]{:S(2)}, u32[]{:S(2)}) %collective-permute-start.11) | collective-permute-done | bytes 1048608 | tf_op jit(solution)/shard_map/ppermute | solution.py:431
  99.1 5.0 %outgoing.6 = (bf16[8,128,128]{2,1,0:T(8,128)(2,1)S(1)}, bf16[8,128,128]{2,1,0:T(8,128)(2,1)S(1)}, bf16[2,8,128,128]{3,2,1,0:T(8,128)(2,1)S(1)}, bf16[2,2,8,128,128]{4,3,2,1,0:T(8,128)(2,1)S(1)}) custom-call(bf16[8,128,128]{2,1,0:T(8,128)(2,1)S(1)} %get-tuple-element.120.refs_0_, bf16[2,8,128,128]{3,2,1,0:T(8,128)(2,1)S(1)} %collective-permute-done.4.refs_1_.refs_5_, ...), custom_call_target="tpu_custom_call" | custom-call | flops 26843544 | bytes 262144 | tf_op jit(solution)/shard_map/outgoing/pallas_call | solution.py:400
  110.9 5.0 %outgoing.7 = (bf16[8,128,128]{2,1,0:T(8,128)(2,1)S(1)}, bf16[8,128,128]{2,1,0:T(8,128)(2,1)S(1)}, bf16[2,8,128,128]{3,2,1,0:T(8,128)(2,1)S(1)}, bf16[2,2,8,128,128]{4,3,2,1,0:T(8,128)(2,1)S(1)}) custom-call(bf16[8,128,128]{2,1,0:T(8,128)(2,1)S(1)} %get-tuple-element.130.refs_0_, bf16[2,8,128,128]{3,2,1,0:T(8,128)(2,1)S(1)} %collective-permute-done.10.refs_1_.refs_5_, ...), custom_call_target="tpu_custom_call" | custom-call | flops 26843544 | bytes 262144 | tf_op jit(solution)/shard_map/outgoing/pallas_call | solution.py:400
  122.3 7.3 %collective-permute-done.14 = bf16[2,8,128,128]{3,2,1,0:T(8,128)(2,1)S(1)} collective-permute-done((bf16[2,8,128,128]{3,2,1,0:T(8,128)(2,1)S(1)}, bf16[2,8,128,128]{3,2,1,0:T(8,128)(2,1)S(1)}, u32[]{:S(2)}, u32[]{:S(2)}) %collective-permute-start.14) | collective-permute-done | bytes 524320 | tf_op jit(solution)/shard_map/ppermute | solution.py:431
  129.6 5.2 %collective-permute-start.19 = (bf16[2,8,128,128]{3,2,1,0:T(8,128)(2,1)}, bf16[2,8,128,128]{3,2,1,0:T(8,128)(2,1)}, u32[]{:S(2)}, u32[]{:S(2)}) collective-permute-start(bf16[2,8,128,128]{3,2,1,0:T(8,128)(2,1)} %fusion.11), channel_id=1, source_target_pairs={{4,0},{8,12},{5,1},{9,13},{6,2},{10,14},{7,3},{11,15},{20,16},{24,... | collective-permute-start | bytes 1572872 | tf_op jit(solution)/shard_map/ppermute | solution.py:431
  168.1 5.7 %collective-permute-done.32.rest_8_ = bf16[4,128,128]{2,1,0:T(8,128)(2,1)S(1)} collective-permute-done((bf16[4,128,128]{2,1,0:T(8,128)(2,1)S(1)}, bf16[4,128,128]{2,1,0:T(8,128)(2,1)S(1)}, u32[]{:S(2)}, u32[]{:S(2)}) %collective-permute-start.32) | collective-permute-done | bytes 131104 | tf_op jit(solution)/shard_map/ppermute | solution.py:431
  176.4 19.1 %middle.1 = (bf16[128,128,128]{2,1,0:T(8,128)(2,1)}, bf16[128,128,128]{2,1,0:T(8,128)(2,1)}, bf16[2,8,128,128]{3,2,1,0:T(8,128)(2,1)S(1)}, bf16[2,8,128,128]{3,2...) custom-call(s32[4]{0:T(128)S(1)} %copy-done.28, ...), custom_call_target="tpu_custom_call" | custom-call | flops 150000000 | bytes 943718 | tf_op jit(solution)/shard_map/middle/pallas_call | solution.py:374
  198.5 10.6 %collective-permute-done.34.refs_1_.refs_9_ = bf16[2,8,128,128]{3,2,1,0:T(8,128)(2,1)S(1)} collective-permute-done((bf16[2,8,128,128]{3,2,1,0:T(8,128)(2,1)S(1)}, bf16[2,8,128,128]{3,2,1,0:T(8,128)(2,1)S(1)}, u32[]{:S(2)}, u32[]{:S(2)}) %collective-permute-start.34) | collective-permute-done | bytes 524320 | tf_op jit(solution)/shard_map/ppermute | solution.py:431
  214.1 10.3 %collective-permute-done.43 = bf16[2,8,128,128]{3,2,1,0:T(8,128)(2,1)S(1)} collective-permute-done((bf16[2,8,128,128]{3,2,1,0:T(8,128)(2,1)S(1)}, bf16[2,8,128,128]{3,2,1,0:T(8,128)(2,1)S(1)}, u32[]{:S(2)}, u32[]{:S(2)}) %collective-permute-start.43) | collective-permute-done | bytes 524320 | tf_op jit(solution)/shard_map/ppermute | solution.py:431
  236.1 5.6 %collective-permute-done.49 = bf16[2,8,128,128]{3,2,1,0:T(8,128)(2,1)S(1)} collective-permute-done((bf16[2,8,128,128]{3,2,1,0:T(8,128)(2,1)}, bf16[2,8,128,128]{3,2,1,0:T(8,128)(2,1)S(1)}, u32[]{:S(2)}, u32[]{:S(2)}) %collective-permute-start.49) | collective-permute-done | bytes 524320 | tf_op jit(solution)/shard_map/ppermute | solution.py:431
  241.8 7.3 %collective-permute-done.45.refs_4_.refs_5_.refs_10_.refs_11_ = bf16[2,2,8,128,128]{4,3,2,1,0:T(8,128)(2,1)S(1)} collective-permute-done((bf16[2,2,8,128,128]{4,3,2,1,0:T(8,128)(2,1)S(1)}, bf16[2,2,8,128,128]{4,3,2,1,0:T(8,128)(2,1)S(1)}, u32[]{:S(2)}, u32[]{:S(2)}) %collective-permute-start.45) | collective-permute-done | bytes 1048608 | tf_op jit(solution)/shard_map/ppermute | solution.py:431
  255.3 5.6 %collective-permute-done.41 = bf16[2,2,8,128,128]{4,3,2,1,0:T(8,128)(2,1)S(1)} collective-permute-done((bf16[2,2,8,128,128]{4,3,2,1,0:T(8,128)(2,1)}, bf16[2,2,8,128,128]{4,3,2,1,0:T(8,128)(2,1)S(1)}, u32[]{:S(2)}, u32[]{:S(2)}) %collective-permute-start.41) | collective-permute-done | bytes 1048608 | tf_op jit(solution)/shard_map/ppermute | solution.py:431
  265.0 7.7 %collective-permute-done.51.refs_4_.refs_5_.refs_10_.refs_11_ = bf16[2,2,8,128,128]{4,3,2,1,0:T(8,128)(2,1)S(1)} collective-permute-done((bf16[2,2,8,128,128]{4,3,2,1,0:T(8,128)(2,1)S(1)}, bf16[2,2,8,128,128]{4,3,2,1,0:T(8,128)(2,1)S(1)}, u32[]{:S(2)}, u32[]{:S(2)}) %collective-permute-start.51) | collective-permute-done | bytes 1048608 | tf_op jit(solution)/shard_map/ppermute | solution.py:431
  276.6 5.5 %collective-permute-done.61 = bf16[2,4,128,128]{3,2,1,0:T(8,128)(2,1)S(1)} collective-permute-done((bf16[2,4,128,128]{3,2,1,0:T(8,128)(2,1)S(1)}, bf16[2,4,128,128]{3,2,1,0:T(8,128)(2,1)S(1)}, u32[]{:S(2)}, u32[]{:S(2)}) %collective-permute-start.61) | collective-permute-done | bytes 262176 | tf_op jit(solution)/shard_map/ppermute | solution.py:431
  292.6 4.6 %collective-permute-start.48 = (bf16[2,8,128,128]{3,2,1,0:T(8,128)(2,1)S(1)}, bf16[2,8,128,128]{3,2,1,0:T(8,128)(2,1)S(1)}, u32[]{:S(2)}, u32[]{:S(2)}) collective-permute-start(bf16[2,8,128,128]{3,2,1,0:T(8,128)(2,1)S(1)} %fusion.9), channel_id=1, source_target_pairs={{4,0},{8,12},{5,1},{9,13},{6,2},{10,14},{7,3},{11,15},{20,16},{24,... | collective-permute-start | bytes 1572872 | tf_op jit(solution)/shard_map/ppermute | solution.py:431
  299.0 7.2 %collective-permute-done.63.refs_4_.refs_5_.refs_10_.refs_11_ = bf16[2,2,4,128,128]{4,3,2,1,0:T(8,128)(2,1)S(1)} collective-permute-done((bf16[2,2,4,128,128]{4,3,2,1,0:T(8,128)(2,1)S(1)}, bf16[2,2,4,128,128]{4,3,2,1,0:T(8,128)(2,1)S(1)}, u32[]{:S(2)}, u32[]{:S(2)}) %collective-permute-start.63) | collective-permute-done | bytes 524320 | tf_op jit(solution)/shard_map/ppermute | solution.py:431
  306.3 6.3 %collective-permute-done.53 = bf16[2,2,8,128,128]{4,3,2,1,0:T(8,128)(2,1)S(1)} collective-permute-done((bf16[2,2,8,128,128]{4,3,2,1,0:T(8,128)(2,1)S(1)}, bf16[2,2,8,128,128]{4,3,2,1,0:T(8,128)(2,1)S(1)}, u32[]{:S(2)}, u32[]{:S(2)}) %collective-permute-start.53) | collective-permute-done | bytes 1048608 | tf_op jit(solution)/shard_map/ppermute | solution.py:431
  323.2 6.1 %collective-permute-done.59 = bf16[2,2,4,128,128]{4,3,2,1,0:T(8,128)(2,1)S(1)} collective-permute-done((bf16[2,2,4,128,128]{4,3,2,1,0:T(8,128)(2,1)S(1)}, bf16[2,2,4,128,128]{4,3,2,1,0:T(8,128)(2,1)S(1)}, u32[]{:S(2)}, u32[]{:S(2)}) %collective-permute-start.59) | collective-permute-done | bytes 524320 | tf_op jit(solution)/shard_map/ppermute | solution.py:431
  349.6 9.5 %finish.1 = bf16[128,128,128]{2,1,0:T(8,128)(2,1)} custom-call(bf16[128,128,128]{2,1,0:T(8,128)(2,1)} %get-tuple-element.162.pair_ref, bf16[128,128,128]{2,1,0:T(8,128)(2,1)} %get-tuple-element.163.gate_ref, bf16[2,64,128]{2,1,0:T(8,128)(2,1)S(1)} %copy-done.22, f32[64,1,128]{2,1,0:T(1,128)S(1)} %broadcast_in_dim.15.gain_ref, ...), custom_call_target="tpu_custom_call" | custom-call | flops 50000000 | bytes 734003 | tf_op jit(solution)/shard_map/finish/pallas_call | solution.py:358
  (281 shorter events, 166.6 us)
Async XLA Ops:
  47.8 19.1 %collective-permute-start.5 = (bf16[2,12,128,128]{3,2,1,0:T(8,128)(2,1)S(1)}, bf16[2,12,128,128]{3,2,1,0:T(8,128)(2,1)S(1)}, u32[]{:S(2)}, u32[]{:S(2)}) collective-permute-start(bf16[2,12,128,128]{3,2,1,0:T(8,128)(2,1)S(1)} %pad_maximum_fusion.4), channel_id=1, source_target_pairs={{0,4},{12,8},{1,5},{13,9},{2,6},{14,10},{3,7},{15,11},{16,20},{28,... | collective-permute-start | bytes 2359304 | tf_op jit(solution)/shard_map/ppermute | solution.py:431
  49.8 20.4 %collective-permute-start.7 = (bf16[2,12,128,128]{3,2,1,0:T(8,128)(2,1)S(1)}, bf16[2,12,128,128]{3,2,1,0:T(8,128)(2,1)S(1)}, u32[]{:S(2)}, u32[]{:S(2)}) collective-permute-start(bf16[2,12,128,128]{3,2,1,0:T(8,128)(2,1)S(1)} %pad_maximum_fusion.5), channel_id=1, source_target_pairs={{4,8},{8,4},{5,9},{9,5},{6,10},{10,6},{7,11},{11,7},{20,24},{24,20... | collective-permute-start | bytes 2359304 | tf_op jit(solution)/shard_map/ppermute | solution.py:431
  67.2 23.8 %collective-permute-start.11 = (bf16[2,16,128,128]{3,2,1,0:T(8,128)(2,1)S(1)}, bf16[2,16,128,128]{3,2,1,0:T(8,128)(2,1)S(1)}, u32[]{:S(2)}, u32[]{:S(2)}) collective-permute-start(bf16[2,16,128,128]{3,2,1,0:T(8,128)(2,1)S(1)} %pad_maximum_fusion.2), channel_id=1, source_target_pairs={{0,4},{12,8},{1,5},{13,9},{2,6},{14,10},{3,7},{15,11},{16,20},{28,... | collective-permute-start | bytes 3145736 | tf_op jit(solution)/shard_map/ppermute | solution.py:431
  70.2 23.7 %collective-permute-start.12 = (bf16[2,16,128,128]{3,2,1,0:T(8,128)(2,1)}, bf16[2,16,128,128]{3,2,1,0:T(8,128)(2,1)S(1)}, u32[]{:S(2)}, u32[]{:S(2)}) collective-permute-start(bf16[2,16,128,128]{3,2,1,0:T(8,128)(2,1)} %pad_maximum_fusion.3), channel_id=1, source_target_pairs={{4,8},{8,4},{5,9},{9,5},{6,10},{10,6},{7,11},{11,7},{20,24},{24,20... | collective-permute-start | bytes 3145736 | tf_op jit(solution)/shard_map/ppermute | solution.py:431
  75.6 20.6 %collective-permute-start.8 = (bf16[2,2,8,128,128]{4,3,2,1,0:T(8,128)(2,1)S(1)}, bf16[2,2,8,128,128]{4,3,2,1,0:T(8,128)(2,1)S(1)}, u32[]{:S(2)}, u32[]{:S(2)}) collective-permute-start(bf16[2,2,8,128,128]{4,3,2,1,0:T(8,128)(2,1)S(1)} %get-tuple-element.118), channel_id=1, source_target_pairs={{0,1},{1,0},{2,3},{3,2},{4,5},{5,4},{6,7},{7,6},{8,9},{9,8},{10,11... | collective-permute-start | bytes 3145736 | tf_op jit(solution)/shard_map/ppermute | solution.py:431
  91.3 17.3 %collective-permute-start.16 = (bf16[2,12,128,128]{3,2,1,0:T(8,128)(2,1)S(1)}, bf16[2,12,128,128]{3,2,1,0:T(8,128)(2,1)S(1)}, u32[]{:S(2)}, u32[]{:S(2)}) collective-permute-start(bf16[2,12,128,128]{3,2,1,0:T(8,128)(2,1)S(1)} %pad_maximum_fusion.6), channel_id=1, source_target_pairs={{0,4},{12,8},{1,5},{13,9},{2,6},{14,10},{3,7},{15,11},{16,20},{28,... | collective-permute-start | bytes 2359304 | tf_op jit(solution)/shard_map/ppermute | solution.py:431
  93.9 17.0 %collective-permute-start.17 = (bf16[2,12,128,128]{3,2,1,0:T(8,128)(2,1)S(1)}, bf16[2,12,128,128]{3,2,1,0:T(8,128)(2,1)S(1)}, u32[]{:S(2)}, u32[]{:S(2)}) collective-permute-start(bf16[2,12,128,128]{3,2,1,0:T(8,128)(2,1)S(1)} %pad_maximum_fusion.7), channel_id=1, source_target_pairs={{4,8},{8,4},{5,9},{9,5},{6,10},{10,6},{7,11},{11,7},{20,24},{24,20... | collective-permute-start | bytes 2359304 | tf_op jit(solution)/shard_map/ppermute | solution.py:431
  117.7 17.9 %collective-permute-start.21 = (bf16[2,8,128,128]{3,2,1,0:T(8,128)(2,1)S(1)}, bf16[2,8,128,128]{3,2,1,0:T(8,128)(2,1)S(1)}, u32[]{:S(2)}, u32[]{:S(2)}) collective-permute-start(bf16[2,8,128,128]{3,2,1,0:T(8,128)(2,1)S(1)} %pad_maximum_fusion.16), channel_id=1, source_target_pairs={{0,4},{12,8},{1,5},{13,9},{2,6},{14,10},{3,7},{15,11},{16,20},{28,... | collective-permute-start | bytes 1572872 | tf_op jit(solution)/shard_map/ppermute | solution.py:431
  119.1 18.5 %collective-permute-start.22 = (bf16[2,8,128,128]{3,2,1,0:T(8,128)(2,1)S(1)}, bf16[2,8,128,128]{3,2,1,0:T(8,128)(2,1)S(1)}, u32[]{:S(2)}, u32[]{:S(2)}) collective-permute-start(bf16[2,8,128,128]{3,2,1,0:T(8,128)(2,1)S(1)} %pad_maximum_fusion.17), channel_id=1, source_target_pairs={{4,8},{8,4},{5,9},{9,5},{6,10},{10,6},{7,11},{11,7},{20,24},{24,20... | collective-permute-start | bytes 1572872 | tf_op jit(solution)/shard_map/ppermute | solution.py:431
  129.6 15.9 %collective-permute-start.19 = (bf16[2,8,128,128]{3,2,1,0:T(8,128)(2,1)}, bf16[2,8,128,128]{3,2,1,0:T(8,128)(2,1)}, u32[]{:S(2)}, u32[]{:S(2)}) collective-permute-start(bf16[2,8,128,128]{3,2,1,0:T(8,128)(2,1)} %fusion.11), channel_id=1, source_target_pairs={{4,0},{8,12},{5,1},{9,13},{6,2},{10,14},{7,3},{11,15},{20,16},{24,... | collective-permute-start | bytes 1572872 | tf_op jit(solution)/shard_map/ppermute | solution.py:431
  150.6 17.5 %collective-permute-start.29 = (bf16[8,128,128]{2,1,0:T(8,128)(2,1)S(1)}, bf16[8,128,128]{2,1,0:T(8,128)(2,1)S(1)}, u32[]{:S(2)}, u32[]{:S(2)}) collective-permute-start(bf16[8,128,128]{2,1,0:T(8,128)(2,1)S(1)} %get-tuple-element.217), channel_id=1, source_target_pairs={{0,2},{1,3},{2,0},{3,1},{4,6},{5,7},{6,4},{7,5},{8,10},{9,11},{10,... | collective-permute-start | bytes 786440 | tf_op jit(solution)/shard_map/ppermute | solution.py:431
  157.8 16.0 %collective-permute-start.31 = (bf16[8,128,128]{2,1,0:T(8,128)(2,1)S(1)}, bf16[8,128,128]{2,1,0:T(8,128)(2,1)S(1)}, u32[]{:S(2)}, u32[]{:S(2)}) collective-permute-start(bf16[8,128,128]{2,1,0:T(8,128)(2,1)S(1)} %get-tuple-element.213), channel_id=1, source_target_pairs={{0,2},{1,3},{2,0},{3,1},{4,6},{5,7},{6,4},{7,5},{8,10},{9,11},{10,... | collective-permute-start | bytes 786440 | tf_op jit(solution)/shard_map/ppermute | solution.py:431
  224.5 24.6 %collective-permute-start.45 = (bf16[2,2,8,128,128]{4,3,2,1,0:T(8,128)(2,1)S(1)}, bf16[2,2,8,128,128]{4,3,2,1,0:T(8,128)(2,1)S(1)}, u32[]{:S(2)}, u32[]{:S(2)}) collective-permute-start(bf16[2,2,8,128,128]{4,3,2,1,0:T(8,128)(2,1)S(1)} %pad_maximum_fusion.refs_0_.refs_1_.refs_8_.refs_9_), channel_id=1, source_target_pairs={{0,4},{12,8},{1,5},{13,9},{2,6},{14,10},{3,7},{15,11},{16,20},{28,... | collective-permute-start | bytes 3145736 | tf_op jit(solution)/shard_map/ppermute | solution.py:431
  233.6 27.3 %collective-permute-start.41 = (bf16[2,2,8,128,128]{4,3,2,1,0:T(8,128)(2,1)}, bf16[2,2,8,128,128]{4,3,2,1,0:T(8,128)(2,1)S(1)}, u32[]{:S(2)}, u32[]{:S(2)}) collective-permute-start(bf16[2,2,8,128,128]{4,3,2,1,0:T(8,128)(2,1)} %get-tuple-element.168), channel_id=1, source_target_pairs={{4,8},{8,4},{5,9},{9,5},{6,10},{10,6},{7,11},{11,7},{20,24},{24,20... | collective-permute-start | bytes 3145736 | tf_op jit(solution)/shard_map/ppermute | solution.py:431
  249.1 23.6 %collective-permute-start.51 = (bf16[2,2,8,128,128]{4,3,2,1,0:T(8,128)(2,1)S(1)}, bf16[2,2,8,128,128]{4,3,2,1,0:T(8,128)(2,1)S(1)}, u32[]{:S(2)}, u32[]{:S(2)}) collective-permute-start(bf16[2,2,8,128,128]{4,3,2,1,0:T(8,128)(2,1)S(1)} %pad_maximum_fusion.1.refs_0_.refs_1_.refs_8_.refs_9_), channel_id=1, source_target_pairs={{0,4},{12,8},{1,5},{13,9},{2,6},{14,10},{3,7},{15,11},{16,20},{28,... | collective-permute-start | bytes 3145736 | tf_op jit(solution)/shard_map/ppermute | solution.py:431
  260.9 26.2 %collective-permute-start.47 = (bf16[2,2,8,128,128]{4,3,2,1,0:T(8,128)(2,1)S(1)}, bf16[2,2,8,128,128]{4,3,2,1,0:T(8,128)(2,1)S(1)}, u32[]{:S(2)}, u32[]{:S(2)}) collective-permute-start(bf16[2,2,8,128,128]{4,3,2,1,0:T(8,128)(2,1)S(1)} %get-tuple-element.175), channel_id=1, source_target_pairs={{4,8},{8,4},{5,9},{9,5},{6,10},{10,6},{7,11},{11,7},{20,24},{24,20... | collective-permute-start | bytes 3145736 | tf_op jit(solution)/shard_map/ppermute | solution.py:431
  264.9 17.2 %collective-permute-start.50 = (bf16[2,8,128,128]{3,2,1,0:T(8,128)(2,1)S(1)}, bf16[2,8,128,128]{3,2,1,0:T(8,128)(2,1)S(1)}, u32[]{:S(2)}, u32[]{:S(2)}) collective-permute-start(bf16[2,8,128,128]{3,2,1,0:T(8,128)(2,1)S(1)} %fusion.5), channel_id=1, source_target_pairs={{0,1},{1,0},{2,3},{3,2},{4,5},{5,4},{6,7},{7,6},{8,9},{9,8},{10,11... | collective-permute-start | bytes 1572872 | tf_op jit(solution)/shard_map/ppermute | solution.py:431
  287.1 25.4 %collective-permute-start.53 = (bf16[2,2,8,128,128]{4,3,2,1,0:T(8,128)(2,1)S(1)}, bf16[2,2,8,128,128]{4,3,2,1,0:T(8,128)(2,1)S(1)}, u32[]{:S(2)}, u32[]{:S(2)}) collective-permute-start(bf16[2,2,8,128,128]{4,3,2,1,0:T(8,128)(2,1)S(1)} %get-tuple-element.183), channel_id=1, source_target_pairs={{4,8},{8,4},{5,9},{9,5},{6,10},{10,6},{7,11},{11,7},{20,24},{24,20... | collective-permute-start | bytes 3145736 | tf_op jit(solution)/shard_map/ppermute | solution.py:431
  289.6 31.7 %collective-permute-start.42 = (bf16[2,8,128,128]{3,2,1,0:T(8,128)(2,1)S(1)}, bf16[2,8,128,128]{3,2,1,0:T(8,128)(2,1)S(1)}, u32[]{:S(2)}, u32[]{:S(2)}) collective-permute-start(bf16[2,8,128,128]{3,2,1,0:T(8,128)(2,1)S(1)} %fusion.10), channel_id=1, source_target_pairs={{4,0},{8,12},{5,1},{9,13},{6,2},{10,14},{7,3},{11,15},{20,16},{24,... | collective-permute-start | bytes 1572872 | tf_op jit(solution)/shard_map/ppermute | solution.py:431
  292.6 22.5 %collective-permute-start.48 = (bf16[2,8,128,128]{3,2,1,0:T(8,128)(2,1)S(1)}, bf16[2,8,128,128]{3,2,1,0:T(8,128)(2,1)S(1)}, u32[]{:S(2)}, u32[]{:S(2)}) collective-permute-start(bf16[2,8,128,128]{3,2,1,0:T(8,128)(2,1)S(1)} %fusion.9), channel_id=1, source_target_pairs={{4,0},{8,12},{5,1},{9,13},{6,2},{10,14},{7,3},{11,15},{20,16},{24,... | collective-permute-start | bytes 1572872 | tf_op jit(solution)/shard_map/ppermute | solution.py:431
  297.2 19.1 %collective-permute-start.62 = (bf16[2,4,128,128]{3,2,1,0:T(8,128)(2,1)S(1)}, bf16[2,4,128,128]{3,2,1,0:T(8,128)(2,1)S(1)}, u32[]{:S(2)}, u32[]{:S(2)}) collective-permute-start(bf16[2,4,128,128]{3,2,1,0:T(8,128)(2,1)S(1)} %fusion.27), channel_id=1, source_target_pairs={{0,1},{1,0},{2,3},{3,2},{4,5},{5,4},{6,7},{7,6},{8,9},{9,8},{10,11... | collective-permute-start | bytes 786440 | tf_op jit(solution)/shard_map/ppermute | solution.py:431
  312.5 16.7 %collective-permute-start.59 = (bf16[2,2,4,128,128]{4,3,2,1,0:T(8,128)(2,1)S(1)}, bf16[2,2,4,128,128]{4,3,2,1,0:T(8,128)(2,1)S(1)}, u32[]{:S(2)}, u32[]{:S(2)}) collective-permute-start(bf16[2,2,4,128,128]{4,3,2,1,0:T(8,128)(2,1)S(1)} %get-tuple-element.191), channel_id=1, source_target_pairs={{4,8},{8,4},{5,9},{9,5},{6,10},{10,6},{7,11},{11,7},{20,24},{24,20... | collective-permute-start | bytes 1572872 | tf_op jit(solution)/shard_map/ppermute | solution.py:431
  317.9 19.1 %collective-permute-start.65 = (bf16[2,2,4,128,128]{4,3,2,1,0:T(8,128)(2,1)S(1)}, bf16[2,2,4,128,128]{4,3,2,1,0:T(8,128)(2,1)S(1)}, u32[]{:S(2)}, u32[]{:S(2)}) collective-permute-start(bf16[2,2,4,128,128]{4,3,2,1,0:T(8,128)(2,1)S(1)} %get-tuple-element.198), channel_id=1, source_target_pairs={{4,8},{8,4},{5,9},{9,5},{6,10},{10,6},{7,11},{11,7},{20,24},{24,20... | collective-permute-start | bytes 1572872 | tf_op jit(solution)/shard_map/ppermute | solution.py:431
  321.4 23.2 %collective-permute-start.67 = (bf16[8,128,128]{2,1,0:T(8,128)(2,1)S(1)}, bf16[8,128,128]{2,1,0:T(8,128)(2,1)S(1)}, u32[]{:S(2)}, u32[]{:S(2)}) collective-permute-start(bf16[8,128,128]{2,1,0:T(8,128)(2,1)S(1)} %get-tuple-element.202), channel_id=1, source_target_pairs={{0,2},{1,3},{2,0},{3,1},{4,6},{5,7},{6,4},{7,5},{8,10},{9,11},{10,... | collective-permute-start | bytes 786440 | tf_op jit(solution)/shard_map/ppermute | solution.py:431
  (89 other events, 1238.5 us)

commit v8 on v7

--- a/solution.py
+++ b/solution.py
@@ -13,11 +13,12 @@
 IN_SIZES = (8, 8, 8, 4, 4)
 OUT_GROUPS = (1, 1, 1, 1, 1)
 IN_GROUPS = (1, 1, 1, 1, 1)
-OUT_ORDER = {'i1': ('i0',), 'i2': ('i1',), 'i3': ('i2',), 'i4': ('i3',), 'i5': ('i4',), 'i6': ('i5',), 'a1': ('a0',), 'a2': ('a1',), 'a3': ('a2',), 'a4': ('a3',), 'a5': ('a4', 'p1'), 'a6': ('a5',), 'x1': ('x0', 'a0'), 'x2': ('x1', 'a1'), 'x3': ('x2',), 'x4': ('x3',), 'o2': ('o1',), 'p2': ('o0',), 'p3': ('o1',), 'p4': ('o2',)}
-IN_ORDER = {'i0x': ('i0',), 'i2': ('i1',), 'i3': ('i2',), 'i4': ('i3',), 'a1': ('a0',), 'a2': ('a1',), 'a3': ('a2',), 'x1': ('x0', 'i0'), 'o2': ('o1',), 'o3': ('o2',), 'o4': ('o3',), 'x2': ('i0x',), 'b0': ('x3',)}
+OUT_ORDER = {'i1': ('i0',), 'i2': ('i1',), 'i3': ('i2',), 'i4': ('i3',), 'i5': ('i4',), 'i6': ('i5',), 'a1': ('a0',), 'a2': ('a1',), 'a3': ('a2',), 'a4': ('a3',), 'a5': ('a4', 'p1'), 'a6': ('a5',), 'x2': ('x1', 'a1'), 'x3': ('x2',), 'x4': ('x3',), 'o2': ('o1',), 'x1': ('a0',), 'p2': ('o0',), 'p3': ('o1',), 'p4': ('o2',)}
+IN_ORDER = {'i0x': ('i0',), 'i2': ('i1',), 'i3': ('i2',), 'i4': ('i3',), 'a1': ('a0', 'i1'), 'x1': ('x0', 'i0'), 'o2': ('o1',), 'o3': ('o2',), 'o4': ('o3',), 'x2': ('i0x',), 'b0': ('x3',)}
 STEP = 16
 TOLD = 0.05
-VMEM = 48 * 1024 * 1024
+VMEM = 28 * 1024 * 1024
+PRODUCT_VMEM = 10 * 1024 * 1024
 
 
 def broadcast(block, axis, owner):
@@ -286,8 +287,10 @@
     kernel(*[blocks[k : k + 2] for k in range(0, count, 2)], refs[count:-1], refs[-1])
 
 
-def params():
-    return pltpu.CompilerParams(vmem_limit_bytes=VMEM, dimension_semantics=("arbitrary",))
+def params(limit=VMEM):
+    return pltpu.CompilerParams(
+        vmem_limit_bytes=limit, dimension_semantics=("arbitrary",), fuse_transposed_lhs_in_matmul=True
+    )
 
 
 def part(array, index):
@@ -404,7 +407,7 @@
         out_specs=[out_spec(lead) for lead in leads],
         out_shape=[jax.ShapeDtypeStruct(lead + (channels, size, size), jnp.bfloat16) for lead in leads],
         scratch_shapes=[pltpu.VMEM(scratch, jnp.bfloat16)],
-        compiler_params=params(),
+        compiler_params=params(PRODUCT_VMEM),
         cost_estimate=cost(channels * 2 * (4 * size) ** 2 * size, channels * size * size * 2 * 20),
         name=name,
     )(*[piece[0] for piece in pieces])

time: 363 us -> 357 us (0.983)
  Pallas kernels: 72.9 us -> 62.4 us
  waiting for transfers between devices: 172 us -> 179 us
  starting transfers between devices: 98.2 us -> 94 us
  local copies, waits for them, and re-layouts: 8.73 us -> 12.4 us
    ppermute x72, waiting for transfers between devices: 172 us -> 179 us  [send(): self.add(name, operand, lambda array: lax.ppermute(array, axis, pairs))]
    pallas_call x10, Pallas kernels: 30.2 us -> 24.8 us  [product_call(): pl.pallas_call(functools.partial(pieces_kernel, kernel, len(pieces)), gri...]
    ppermute x72, starting transfers between devices: 98.2 us -> 94 us  [send(): self.add(name, operand, lambda array: lax.ppermute(array, axis, pairs))]
    unnamed x82 -> x88, local copies, waits for them, and re-layouts: 7.34 us -> 11 us
  transfers between devices with their start and end apart: 72 -> 72, of which waited for: 39 -> 41; matrix products, arithmetic and copies ran while one was open for 2% -> 2% of each run, Pallas kernels for 8% -> 7%
where the time goes in v8:
time: 357 us; the launch traced here: 355 us
  waiting for transfers between devices  179 us (50%)
  starting transfers between devices  94 us (26%)
  Pallas kernels  62.4 us (17%)
  local copies, waits for them, and re-layouts  12.4 us (3%)
  other arithmetic  5.51 us (2%)
    ppermute x72, waiting for transfers between devices, send(): self.add(name, operand, lambda array: lax.ppermute(array, axis, pairs))  179 us
    ppermute x72, starting transfers between devices, send(): self.add(name, operand, lambda array: lax.ppermute(array, axis, pairs))  94 us
    pallas_call x10, Pallas kernels, product_call(): pl.pallas_call(functools.partial(pieces_kernel, kernel, len(pieces)), gri...  24.8 us
    pallas_call x1, Pallas kernels, middle_call(): pl.pallas_call(functools.partial(middle_kernel, IN_SIZES, len(products)),...  18 us
    pallas_call x1, Pallas kernels, first_call(): pl.pallas_call(functools.partial(first_kernel, OUT_SIZES), grid=(pair.sha...  12.8 us
    unnamed x88, local copies, waits for them, and re-layouts  11 us
  transfers between devices with their start and end apart: 72, of which 41 were waited for; matrix products, arithmetic and copies ran while one was open for 2% of the time, Pallas kernels for 7%

profile of v8, /device:TPU:16, one launch (start us, length us, event | category | flops | bytes accessed | tf_op | source)
XLA Modules:
  0.0 354.8 jit_solution(1442219927781264312)
XLA Ops:
  6.0 12.8 %project.1 = (bf16[128,128,128]{2,1,0:T(8,128)(2,1)S(1)}, bf16[8,128,128]{2,1,0:T(8,128)(2,1)S(1)}, bf16[8,128,128]{2,1,0:T(8,128)(2,1)S(1)}, bf16[8,128,128]{2,...) custom-call(s32[4]{0:T(128)S(1)} %copy-done.31, ...), custom_call_target="tpu_custom_call" | custom-call | flops 100000000 | bytes 419430 | tf_op jit(solution)/shard_map/project/pallas_call | solution.py:346
  24.0 6.0 %collective-permute-done.3.refs_10_ = bf16[8,128,128]{2,1,0:T(8,128)(2,1)S(1)} collective-permute-done((bf16[8,128,128]{2,1,0:T(8,128)(2,1)S(1)}, bf16[8,128,128]{2,1,0:T(8,128)(2,1)S(1)}, u32[]{:S(2)}, u32[]{:S(2)}) %collective-permute-start.3) | collective-permute-done | bytes 262176 | tf_op jit(solution)/shard_map/ppermute | solution.py:434
  37.5 6.3 %collective-permute-done.4.refs_1_.refs_5_ = bf16[2,8,128,128]{3,2,1,0:T(8,128)(2,1)S(1)} collective-permute-done((bf16[2,8,128,128]{3,2,1,0:T(8,128)(2,1)S(1)}, bf16[2,8,128,128]{3,2,1,0:T(8,128)(2,1)S(1)}, u32[]{:S(2)}, u32[]{:S(2)}) %collective-permute-start.4) | collective-permute-done | bytes 524320 | tf_op jit(solution)/shard_map/ppermute | solution.py:434
  52.9 6.8 %collective-permute-done.10.refs_1_.refs_5_ = bf16[2,8,128,128]{3,2,1,0:T(8,128)(2,1)S(1)} collective-permute-done((bf16[2,8,128,128]{3,2,1,0:T(8,128)(2,1)S(1)}, bf16[2,8,128,128]{3,2,1,0:T(8,128)(2,1)S(1)}, u32[]{:S(2)}, u32[]{:S(2)}) %collective-permute-start.10) | collective-permute-done | bytes 524320 | tf_op jit(solution)/shard_map/ppermute | solution.py:434
  59.7 6.1 %collective-permute-done.5.refs_6_.refs_7_ = bf16[2,12,128,128]{3,2,1,0:T(8,128)(2,1)S(1)} collective-permute-done((bf16[2,12,128,128]{3,2,1,0:T(8,128)(2,1)S(1)}, bf16[2,12,128,128]{3,2,1,0:T(8,128)(2,1)S(1)}, u32[]{:S(2)}, u32[]{:S(2)}) %collective-permute-start.5) | collective-permute-done | bytes 786464 | tf_op jit(solution)/shard_map/ppermute | solution.py:434
  75.3 13.9 %collective-permute-done.11.refs_2_.refs_3_.refs_6_.refs_7_ = bf16[2,16,128,128]{3,2,1,0:T(8,128)(2,1)S(1)} collective-permute-done((bf16[2,16,128,128]{3,2,1,0:T(8,128)(2,1)S(1)}, bf16[2,16,128,128]{3,2,1,0:T(8,128)(2,1)S(1)}, u32[]{:S(2)}, u32[]{:S(2)}) %collective-permute-start.11) | collective-permute-done | bytes 1048608 | tf_op jit(solution)/shard_map/ppermute | solution.py:434
  118.2 7.0 %collective-permute-done.14 = bf16[2,8,128,128]{3,2,1,0:T(8,128)(2,1)S(1)} collective-permute-done((bf16[2,8,128,128]{3,2,1,0:T(8,128)(2,1)S(1)}, bf16[2,8,128,128]{3,2,1,0:T(8,128)(2,1)S(1)}, u32[]{:S(2)}, u32[]{:S(2)}) %collective-permute-start.14) | collective-permute-done | bytes 524320 | tf_op jit(solution)/shard_map/ppermute | solution.py:434
  125.3 5.2 %collective-permute-start.19 = (bf16[2,8,128,128]{3,2,1,0:T(8,128)(2,1)}, bf16[2,8,128,128]{3,2,1,0:T(8,128)(2,1)}, u32[]{:S(2)}, u32[]{:S(2)}) collective-permute-start(bf16[2,8,128,128]{3,2,1,0:T(8,128)(2,1)} %fusion.11), channel_id=1, source_target_pairs={{4,0},{8,12},{5,1},{9,13},{6,2},{10,14},{7,3},{11,15},{20,16},{24,... | collective-permute-start | bytes 1572872 | tf_op jit(solution)/shard_map/ppermute | solution.py:434
  158.4 4.0 %collective-permute-done.28 = bf16[2,4,128,128]{3,2,1,0:T(8,128)(2,1)S(1)} collective-permute-done((bf16[2,4,128,128]{3,2,1,0:T(8,128)(2,1)S(1)}, bf16[2,4,128,128]{3,2,1,0:T(8,128)(2,1)S(1)}, u32[]{:S(2)}, u32[]{:S(2)}) %collective-permute-start.28) | collective-permute-done | bytes 262176 | tf_op jit(solution)/shard_map/ppermute | solution.py:434
  162.9 6.6 %collective-permute-done.32.rest_8_ = bf16[4,128,128]{2,1,0:T(8,128)(2,1)S(1)} collective-permute-done((bf16[4,128,128]{2,1,0:T(8,128)(2,1)S(1)}, bf16[4,128,128]{2,1,0:T(8,128)(2,1)S(1)}, u32[]{:S(2)}, u32[]{:S(2)}) %collective-permute-start.32) | collective-permute-done | bytes 131104 | tf_op jit(solution)/shard_map/ppermute | solution.py:434
  172.1 18.0 %middle.1 = (bf16[128,128,128]{2,1,0:T(8,128)(2,1)S(1)}, bf16[128,128,128]{2,1,0:T(8,128)(2,1)S(1)}, bf16[2,8,128,128]{3,2,1,0:T(8,128)(2,1)S(1)}, bf16[2,8,128,...) custom-call(s32[4]{0:T(128)S(1)} %copy-done.32, ...), custom_call_target="tpu_custom_call" | custom-call | flops 150000000 | bytes 943718 | tf_op jit(solution)/shard_map/middle/pallas_call | solution.py:377
  192.2 11.6 %collective-permute-done.34.refs_1_.refs_9_ = bf16[2,8,128,128]{3,2,1,0:T(8,128)(2,1)S(1)} collective-permute-done((bf16[2,8,128,128]{3,2,1,0:T(8,128)(2,1)S(1)}, bf16[2,8,128,128]{3,2,1,0:T(8,128)(2,1)S(1)}, u32[]{:S(2)}, u32[]{:S(2)}) %collective-permute-start.34) | collective-permute-done | bytes 524320 | tf_op jit(solution)/shard_map/ppermute | solution.py:434
  208.8 9.4 %collective-permute-done.43 = bf16[2,8,128,128]{3,2,1,0:T(8,128)(2,1)S(1)} collective-permute-done((bf16[2,8,128,128]{3,2,1,0:T(8,128)(2,1)S(1)}, bf16[2,8,128,128]{3,2,1,0:T(8,128)(2,1)S(1)}, u32[]{:S(2)}, u32[]{:S(2)}) %collective-permute-start.43) | collective-permute-done | bytes 524320 | tf_op jit(solution)/shard_map/ppermute | solution.py:434
  229.0 7.6 %collective-permute-done.49 = bf16[2,8,128,128]{3,2,1,0:T(8,128)(2,1)S(1)} collective-permute-done((bf16[2,8,128,128]{3,2,1,0:T(8,128)(2,1)S(1)}, bf16[2,8,128,128]{3,2,1,0:T(8,128)(2,1)S(1)}, u32[]{:S(2)}, u32[]{:S(2)}) %collective-permute-start.49) | collective-permute-done | bytes 524320 | tf_op jit(solution)/shard_map/ppermute | solution.py:434
  236.7 7.1 %collective-permute-done.45.refs_4_.refs_5_.refs_10_.refs_11_ = bf16[2,2,8,128,128]{4,3,2,1,0:T(8,128)(2,1)S(1)} collective-permute-done((bf16[2,2,8,128,128]{4,3,2,1,0:T(8,128)(2,1)S(1)}, bf16[2,2,8,128,128]{4,3,2,1,0:T(8,128)(2,1)S(1)}, u32[]{:S(2)}, u32[]{:S(2)}) %collective-permute-start.45) | collective-permute-done | bytes 1048608 | tf_op jit(solution)/shard_map/ppermute | solution.py:434
  256.3 12.0 %collective-permute-done.51.refs_4_.refs_5_.refs_10_.refs_11_ = bf16[2,2,8,128,128]{4,3,2,1,0:T(8,128)(2,1)S(1)} collective-permute-done((bf16[2,2,8,128,128]{4,3,2,1,0:T(8,128)(2,1)S(1)}, bf16[2,2,8,128,128]{4,3,2,1,0:T(8,128)(2,1)S(1)}, u32[]{:S(2)}, u32[]{:S(2)}) %collective-permute-start.51) | collective-permute-done | bytes 1048608 | tf_op jit(solution)/shard_map/ppermute | solution.py:434
  270.0 7.2 %collective-permute-done.61 = bf16[2,4,128,128]{3,2,1,0:T(8,128)(2,1)S(1)} collective-permute-done((bf16[2,4,128,128]{3,2,1,0:T(8,128)(2,1)S(1)}, bf16[2,4,128,128]{3,2,1,0:T(8,128)(2,1)S(1)}, u32[]{:S(2)}, u32[]{:S(2)}) %collective-permute-start.61) | collective-permute-done | bytes 262176 | tf_op jit(solution)/shard_map/ppermute | solution.py:434
  286.3 4.6 %collective-permute-start.48 = (bf16[2,8,128,128]{3,2,1,0:T(8,128)(2,1)S(1)}, bf16[2,8,128,128]{3,2,1,0:T(8,128)(2,1)S(1)}, u32[]{:S(2)}, u32[]{:S(2)}) collective-permute-start(bf16[2,8,128,128]{3,2,1,0:T(8,128)(2,1)S(1)} %fusion.9), channel_id=1, source_target_pairs={{4,0},{8,12},{5,1},{9,13},{6,2},{10,14},{7,3},{11,15},{20,16},{24,... | collective-permute-start | bytes 1572872 | tf_op jit(solution)/shard_map/ppermute | solution.py:434
  292.7 7.5 %collective-permute-done.63.refs_4_.refs_5_.refs_10_.refs_11_ = bf16[2,2,4,128,128]{4,3,2,1,0:T(8,128)(2,1)S(1)} collective-permute-done((bf16[2,2,4,128,128]{4,3,2,1,0:T(8,128)(2,1)S(1)}, bf16[2,2,4,128,128]{4,3,2,1,0:T(8,128)(2,1)S(1)}, u32[]{:S(2)}, u32[]{:S(2)}) %collective-permute-start.63) | collective-permute-done | bytes 524320 | tf_op jit(solution)/shard_map/ppermute | solution.py:434
  303.4 4.6 %collective-permute-done.53 = bf16[2,2,8,128,128]{4,3,2,1,0:T(8,128)(2,1)S(1)} collective-permute-done((bf16[2,2,8,128,128]{4,3,2,1,0:T(8,128)(2,1)S(1)}, bf16[2,2,8,128,128]{4,3,2,1,0:T(8,128)(2,1)S(1)}, u32[]{:S(2)}, u32[]{:S(2)}) %collective-permute-start.53) | collective-permute-done | bytes 1048608 | tf_op jit(solution)/shard_map/ppermute | solution.py:434
  322.5 4.4 %collective-permute-start.60 = (bf16[2,4,128,128]{3,2,1,0:T(8,128)(2,1)S(1)}, bf16[2,4,128,128]{3,2,1,0:T(8,128)(2,1)S(1)}, u32[]{:S(2)}, u32[]{:S(2)}) collective-permute-start(bf16[2,4,128,128]{3,2,1,0:T(8,128)(2,1)S(1)} %fusion.37), channel_id=1, source_target_pairs={{4,0},{8,12},{5,1},{9,13},{6,2},{10,14},{7,3},{11,15},{20,16},{24,... | collective-permute-start | bytes 786440 | tf_op jit(solution)/shard_map/ppermute | solution.py:434
  331.7 4.4 %collective-permute-start.66 = (bf16[2,4,128,128]{3,2,1,0:T(8,128)(2,1)S(1)}, bf16[2,4,128,128]{3,2,1,0:T(8,128)(2,1)S(1)}, u32[]{:S(2)}, u32[]{:S(2)}) collective-permute-start(bf16[2,4,128,128]{3,2,1,0:T(8,128)(2,1)S(1)} %fusion.36), channel_id=1, source_target_pairs={{4,0},{8,12},{5,1},{9,13},{6,2},{10,14},{7,3},{11,15},{20,16},{24,... | collective-permute-start | bytes 786440 | tf_op jit(solution)/shard_map/ppermute | solution.py:434
  340.1 5.0 %collective-permute-done.69.rest_7_ = bf16[8,128,128]{2,1,0:T(8,128)(2,1)S(1)} collective-permute-done((bf16[8,128,128]{2,1,0:T(8,128)(2,1)S(1)}, bf16[8,128,128]{2,1,0:T(8,128)(2,1)S(1)}, u32[]{:S(2)}, u32[]{:S(2)}) %collective-permute-start.69) | collective-permute-done | bytes 262176 | tf_op jit(solution)/shard_map/ppermute | solution.py:434
  348.0 6.8 %finish.1 = bf16[128,128,128]{2,1,0:T(8,128)(2,1)} custom-call(bf16[128,128,128]{2,1,0:T(8,128)(2,1)S(1)} %get-tuple-element.160.pair_ref, bf16[128,128,128]{2,1,0:T(8,128)(2,1)S(1)} %get-tuple-element.161.gate_ref, bf16[2,64,128]{2,1,0:T(8,128)(2,1)S(1)} %copy-done.26, f32[64,1,128]{2,1,0:T(1,128)S(1)} %broadcast_in_dim.15.gain_ref, ...), custom_call_target="tpu_custom_call" | custom-call | flops 50000000 | bytes 734003 | tf_op jit(solution)/shard_map/finish/pallas_call | solution.py:361
  (287 shorter events, 168.5 us)
Async XLA Ops:
  47.6 18.2 %collective-permute-start.5 = (bf16[2,12,128,128]{3,2,1,0:T(8,128)(2,1)S(1)}, bf16[2,12,128,128]{3,2,1,0:T(8,128)(2,1)S(1)}, u32[]{:S(2)}, u32[]{:S(2)}) collective-permute-start(bf16[2,12,128,128]{3,2,1,0:T(8,128)(2,1)S(1)} %pad_maximum_fusion.4), channel_id=1, source_target_pairs={{0,4},{12,8},{1,5},{13,9},{2,6},{14,10},{3,7},{15,11},{16,20},{28,... | collective-permute-start | bytes 2359304 | tf_op jit(solution)/shard_map/ppermute | solution.py:434
  50.5 18.6 %collective-permute-start.7 = (bf16[2,12,128,128]{3,2,1,0:T(8,128)(2,1)S(1)}, bf16[2,12,128,128]{3,2,1,0:T(8,128)(2,1)S(1)}, u32[]{:S(2)}, u32[]{:S(2)}) collective-permute-start(bf16[2,12,128,128]{3,2,1,0:T(8,128)(2,1)S(1)} %pad_maximum_fusion.5), channel_id=1, source_target_pairs={{4,8},{8,4},{5,9},{9,5},{6,10},{10,6},{7,11},{11,7},{20,24},{24,20... | collective-permute-start | bytes 2359304 | tf_op jit(solution)/shard_map/ppermute | solution.py:434
  66.1 23.0 %collective-permute-start.11 = (bf16[2,16,128,128]{3,2,1,0:T(8,128)(2,1)S(1)}, bf16[2,16,128,128]{3,2,1,0:T(8,128)(2,1)S(1)}, u32[]{:S(2)}, u32[]{:S(2)}) collective-permute-start(bf16[2,16,128,128]{3,2,1,0:T(8,128)(2,1)S(1)} %pad_maximum_fusion.2), channel_id=1, source_target_pairs={{0,4},{12,8},{1,5},{13,9},{2,6},{14,10},{3,7},{15,11},{16,20},{28,... | collective-permute-start | bytes 3145736 | tf_op jit(solution)/shard_map/ppermute | solution.py:434
  69.1 23.3 %collective-permute-start.12 = (bf16[2,16,128,128]{3,2,1,0:T(8,128)(2,1)S(1)}, bf16[2,16,128,128]{3,2,1,0:T(8,128)(2,1)S(1)}, u32[]{:S(2)}, u32[]{:S(2)}) collective-permute-start(bf16[2,16,128,128]{3,2,1,0:T(8,128)(2,1)S(1)} %pad_maximum_fusion.3), channel_id=1, source_target_pairs={{4,8},{8,4},{5,9},{9,5},{6,10},{10,6},{7,11},{11,7},{20,24},{24,20... | collective-permute-start | bytes 3145736 | tf_op jit(solution)/shard_map/ppermute | solution.py:434
  75.2 19.5 %collective-permute-start.8 = (bf16[2,2,8,128,128]{4,3,2,1,0:T(8,128)(2,1)S(1)}, bf16[2,2,8,128,128]{4,3,2,1,0:T(8,128)(2,1)S(1)}, u32[]{:S(2)}, u32[]{:S(2)}) collective-permute-start(bf16[2,2,8,128,128]{4,3,2,1,0:T(8,128)(2,1)S(1)} %get-tuple-element.116), channel_id=1, source_target_pairs={{0,1},{1,0},{2,3},{3,2},{4,5},{5,4},{6,7},{7,6},{8,9},{9,8},{10,11... | collective-permute-start | bytes 3145736 | tf_op jit(solution)/shard_map/ppermute | solution.py:434
  89.5 16.5 %collective-permute-start.16 = (bf16[2,12,128,128]{3,2,1,0:T(8,128)(2,1)S(1)}, bf16[2,12,128,128]{3,2,1,0:T(8,128)(2,1)S(1)}, u32[]{:S(2)}, u32[]{:S(2)}) collective-permute-start(bf16[2,12,128,128]{3,2,1,0:T(8,128)(2,1)S(1)} %pad_maximum_fusion.6), channel_id=1, source_target_pairs={{0,4},{12,8},{1,5},{13,9},{2,6},{14,10},{3,7},{15,11},{16,20},{28,... | collective-permute-start | bytes 2359304 | tf_op jit(solution)/shard_map/ppermute | solution.py:434
  92.4 16.2 %collective-permute-start.17 = (bf16[2,12,128,128]{3,2,1,0:T(8,128)(2,1)S(1)}, bf16[2,12,128,128]{3,2,1,0:T(8,128)(2,1)S(1)}, u32[]{:S(2)}, u32[]{:S(2)}) collective-permute-start(bf16[2,12,128,128]{3,2,1,0:T(8,128)(2,1)S(1)} %pad_maximum_fusion.7), channel_id=1, source_target_pairs={{4,8},{8,4},{5,9},{9,5},{6,10},{10,6},{7,11},{11,7},{20,24},{24,20... | collective-permute-start | bytes 2359304 | tf_op jit(solution)/shard_map/ppermute | solution.py:434
  113.3 17.9 %collective-permute-start.21 = (bf16[2,8,128,128]{3,2,1,0:T(8,128)(2,1)S(1)}, bf16[2,8,128,128]{3,2,1,0:T(8,128)(2,1)S(1)}, u32[]{:S(2)}, u32[]{:S(2)}) collective-permute-start(bf16[2,8,128,128]{3,2,1,0:T(8,128)(2,1)S(1)} %pad_maximum_fusion.16), channel_id=1, source_target_pairs={{0,4},{12,8},{1,5},{13,9},{2,6},{14,10},{3,7},{15,11},{16,20},{28,... | collective-permute-start | bytes 1572872 | tf_op jit(solution)/shard_map/ppermute | solution.py:434
  114.7 18.6 %collective-permute-start.22 = (bf16[2,8,128,128]{3,2,1,0:T(8,128)(2,1)S(1)}, bf16[2,8,128,128]{3,2,1,0:T(8,128)(2,1)S(1)}, u32[]{:S(2)}, u32[]{:S(2)}) collective-permute-start(bf16[2,8,128,128]{3,2,1,0:T(8,128)(2,1)S(1)} %pad_maximum_fusion.17), channel_id=1, source_target_pairs={{4,8},{8,4},{5,9},{9,5},{6,10},{10,6},{7,11},{11,7},{20,24},{24,20... | collective-permute-start | bytes 1572872 | tf_op jit(solution)/shard_map/ppermute | solution.py:434
  146.3 16.6 %collective-permute-start.29 = (bf16[8,128,128]{2,1,0:T(8,128)(2,1)S(1)}, bf16[8,128,128]{2,1,0:T(8,128)(2,1)S(1)}, u32[]{:S(2)}, u32[]{:S(2)}) collective-permute-start(bf16[8,128,128]{2,1,0:T(8,128)(2,1)S(1)} %get-tuple-element.213), channel_id=1, source_target_pairs={{0,2},{1,3},{2,0},{3,1},{4,6},{5,7},{6,4},{7,5},{8,10},{9,11},{10,... | collective-permute-start | bytes 786440 | tf_op jit(solution)/shard_map/ppermute | solution.py:434
  218.3 25.5 %collective-permute-start.45 = (bf16[2,2,8,128,128]{4,3,2,1,0:T(8,128)(2,1)S(1)}, bf16[2,2,8,128,128]{4,3,2,1,0:T(8,128)(2,1)S(1)}, u32[]{:S(2)}, u32[]{:S(2)}) collective-permute-start(bf16[2,2,8,128,128]{4,3,2,1,0:T(8,128)(2,1)S(1)} %pad_maximum_fusion.refs_0_.refs_1_.refs_8_.refs_9_), channel_id=1, source_target_pairs={{0,4},{12,8},{1,5},{13,9},{2,6},{14,10},{3,7},{15,11},{16,20},{28,... | collective-permute-start | bytes 3145736 | tf_op jit(solution)/shard_map/ppermute | solution.py:434
  227.0 27.1 %collective-permute-start.41 = (bf16[2,2,8,128,128]{4,3,2,1,0:T(8,128)(2,1)S(1)}, bf16[2,2,8,128,128]{4,3,2,1,0:T(8,128)(2,1)S(1)}, u32[]{:S(2)}, u32[]{:S(2)}) collective-permute-start(bf16[2,2,8,128,128]{4,3,2,1,0:T(8,128)(2,1)S(1)} %get-tuple-element.166), channel_id=1, source_target_pairs={{4,8},{8,4},{5,9},{9,5},{6,10},{10,6},{7,11},{11,7},{20,24},{24,20... | collective-permute-start | bytes 3145736 | tf_op jit(solution)/shard_map/ppermute | solution.py:434
  243.8 24.6 %collective-permute-start.51 = (bf16[2,2,8,128,128]{4,3,2,1,0:T(8,128)(2,1)S(1)}, bf16[2,2,8,128,128]{4,3,2,1,0:T(8,128)(2,1)S(1)}, u32[]{:S(2)}, u32[]{:S(2)}) collective-permute-start(bf16[2,2,8,128,128]{4,3,2,1,0:T(8,128)(2,1)S(1)} %pad_maximum_fusion.1.refs_0_.refs_1_.refs_8_.refs_9_), channel_id=1, source_target_pairs={{0,4},{12,8},{1,5},{13,9},{2,6},{14,10},{3,7},{15,11},{16,20},{28,... | collective-permute-start | bytes 3145736 | tf_op jit(solution)/shard_map/ppermute | solution.py:434
  245.8 22.8 %collective-permute-start.55 = (bf16[2,4,128,128]{3,2,1,0:T(8,128)(2,1)S(1)}, bf16[2,4,128,128]{3,2,1,0:T(8,128)(2,1)S(1)}, u32[]{:S(2)}, u32[]{:S(2)}) collective-permute-start(bf16[2,4,128,128]{3,2,1,0:T(8,128)(2,1)S(1)} %get-tuple-element.184), channel_id=1, source_target_pairs={{0,2},{1,3},{2,0},{3,1},{4,6},{5,7},{6,4},{7,5},{8,10},{9,11},{10,... | collective-permute-start | bytes 786440 | tf_op jit(solution)/shard_map/ppermute | solution.py:434
  247.1 30.2 %collective-permute-start.50 = (bf16[2,8,128,128]{3,2,1,0:T(8,128)(2,1)S(1)}, bf16[2,8,128,128]{3,2,1,0:T(8,128)(2,1)S(1)}, u32[]{:S(2)}, u32[]{:S(2)}) collective-permute-start(bf16[2,8,128,128]{3,2,1,0:T(8,128)(2,1)S(1)} %fusion.5), channel_id=1, source_target_pairs={{0,1},{1,0},{2,3},{3,2},{4,5},{5,4},{6,7},{7,6},{8,9},{9,8},{10,11... | collective-permute-start | bytes 1572872 | tf_op jit(solution)/shard_map/ppermute | solution.py:434
  254.1 32.0 %collective-permute-start.47 = (bf16[2,2,8,128,128]{4,3,2,1,0:T(8,128)(2,1)S(1)}, bf16[2,2,8,128,128]{4,3,2,1,0:T(8,128)(2,1)S(1)}, u32[]{:S(2)}, u32[]{:S(2)}) collective-permute-start(bf16[2,2,8,128,128]{4,3,2,1,0:T(8,128)(2,1)S(1)} %get-tuple-element.173), channel_id=1, source_target_pairs={{4,8},{8,4},{5,9},{9,5},{6,10},{10,6},{7,11},{11,7},{20,24},{24,20... | collective-permute-start | bytes 3145736 | tf_op jit(solution)/shard_map/ppermute | solution.py:434
  268.6 16.2 %collective-permute-start.57 = (bf16[2,2,4,128,128]{4,3,2,1,0:T(8,128)(2,1)S(1)}, bf16[2,2,4,128,128]{4,3,2,1,0:T(8,128)(2,1)S(1)}, u32[]{:S(2)}, u32[]{:S(2)}) collective-permute-start(bf16[2,2,4,128,128]{4,3,2,1,0:T(8,128)(2,1)S(1)} %pad_maximum_fusion.14.refs_0_.refs_1_.refs_8_.refs_9_), channel_id=1, source_target_pairs={{0,4},{12,8},{1,5},{13,9},{2,6},{14,10},{3,7},{15,11},{16,20},{28,... | collective-permute-start | bytes 1572872 | tf_op jit(solution)/shard_map/ppermute | solution.py:434
  280.2 27.8 %collective-permute-start.53 = (bf16[2,2,8,128,128]{4,3,2,1,0:T(8,128)(2,1)S(1)}, bf16[2,2,8,128,128]{4,3,2,1,0:T(8,128)(2,1)S(1)}, u32[]{:S(2)}, u32[]{:S(2)}) collective-permute-start(bf16[2,2,8,128,128]{4,3,2,1,0:T(8,128)(2,1)S(1)} %get-tuple-element.180), channel_id=1, source_target_pairs={{4,8},{8,4},{5,9},{9,5},{6,10},{10,6},{7,11},{11,7},{20,24},{24,20... | collective-permute-start | bytes 3145736 | tf_op jit(solution)/shard_map/ppermute | solution.py:434
  282.2 34.2 %collective-permute-start.42 = (bf16[2,8,128,128]{3,2,1,0:T(8,128)(2,1)S(1)}, bf16[2,8,128,128]{3,2,1,0:T(8,128)(2,1)S(1)}, u32[]{:S(2)}, u32[]{:S(2)}) collective-permute-start(bf16[2,8,128,128]{3,2,1,0:T(8,128)(2,1)S(1)} %fusion.10), channel_id=1, source_target_pairs={{4,0},{8,12},{5,1},{9,13},{6,2},{10,14},{7,3},{11,15},{20,16},{24,... | collective-permute-start | bytes 1572872 | tf_op jit(solution)/shard_map/ppermute | solution.py:434
  286.3 21.9 %collective-permute-start.48 = (bf16[2,8,128,128]{3,2,1,0:T(8,128)(2,1)S(1)}, bf16[2,8,128,128]{3,2,1,0:T(8,128)(2,1)S(1)}, u32[]{:S(2)}, u32[]{:S(2)}) collective-permute-start(bf16[2,8,128,128]{3,2,1,0:T(8,128)(2,1)S(1)} %fusion.9), channel_id=1, source_target_pairs={{4,0},{8,12},{5,1},{9,13},{6,2},{10,14},{7,3},{11,15},{20,16},{24,... | collective-permute-start | bytes 1572872 | tf_op jit(solution)/shard_map/ppermute | solution.py:434
  290.9 20.3 %collective-permute-start.62 = (bf16[2,4,128,128]{3,2,1,0:T(8,128)(2,1)S(1)}, bf16[2,4,128,128]{3,2,1,0:T(8,128)(2,1)S(1)}, u32[]{:S(2)}, u32[]{:S(2)}) collective-permute-start(bf16[2,4,128,128]{3,2,1,0:T(8,128)(2,1)S(1)} %fusion.27), channel_id=1, source_target_pairs={{0,1},{1,0},{2,3},{3,2},{4,5},{5,4},{6,7},{7,6},{8,9},{9,8},{10,11... | collective-permute-start | bytes 786440 | tf_op jit(solution)/shard_map/ppermute | solution.py:434
  300.1 19.2 %collective-permute-start.59 = (bf16[2,2,4,128,128]{4,3,2,1,0:T(8,128)(2,1)S(1)}, bf16[2,2,4,128,128]{4,3,2,1,0:T(8,128)(2,1)S(1)}, u32[]{:S(2)}, u32[]{:S(2)}) collective-permute-start(bf16[2,2,4,128,128]{4,3,2,1,0:T(8,128)(2,1)S(1)} %get-tuple-element.187), channel_id=1, source_target_pairs={{4,8},{8,4},{5,9},{9,5},{6,10},{10,6},{7,11},{11,7},{20,24},{24,20... | collective-permute-start | bytes 1572872 | tf_op jit(solution)/shard_map/ppermute | solution.py:434
  312.8 17.4 %collective-permute-start.65 = (bf16[2,2,4,128,128]{4,3,2,1,0:T(8,128)(2,1)S(1)}, bf16[2,2,4,128,128]{4,3,2,1,0:T(8,128)(2,1)S(1)}, u32[]{:S(2)}, u32[]{:S(2)}) collective-permute-start(bf16[2,2,4,128,128]{4,3,2,1,0:T(8,128)(2,1)S(1)} %get-tuple-element.194), channel_id=1, source_target_pairs={{4,8},{8,4},{5,9},{9,5},{6,10},{10,6},{7,11},{11,7},{20,24},{24,20... | collective-permute-start | bytes 1572872 | tf_op jit(solution)/shard_map/ppermute | solution.py:434
  316.5 23.6 %collective-permute-start.67 = (bf16[8,128,128]{2,1,0:T(8,128)(2,1)S(1)}, bf16[8,128,128]{2,1,0:T(8,128)(2,1)S(1)}, u32[]{:S(2)}, u32[]{:S(2)}) collective-permute-start(bf16[8,128,128]{2,1,0:T(8,128)(2,1)S(1)} %get-tuple-element.198), channel_id=1, source_target_pairs={{0,2},{1,3},{2,0},{3,1},{4,6},{5,7},{6,4},{7,5},{8,10},{9,11},{10,... | collective-permute-start | bytes 786440 | tf_op jit(solution)/shard_map/ppermute | solution.py:434
  (92 other events, 1241.6 us)

commit v9 on v8

--- a/solution.py
+++ b/solution.py
@@ -9,14 +9,15 @@
 
 BLOCK = 128
 EPS = 1e-05
-OUT_SIZES = (8, 8, 8, 4, 4)
+OUT_SIZES = (10, 8, 8, 4, 2)
 IN_SIZES = (8, 8, 8, 4, 4)
 OUT_GROUPS = (1, 1, 1, 1, 1)
 IN_GROUPS = (1, 1, 1, 1, 1)
-OUT_ORDER = {'i1': ('i0',), 'i2': ('i1',), 'i3': ('i2',), 'i4': ('i3',), 'i5': ('i4',), 'i6': ('i5',), 'a1': ('a0',), 'a2': ('a1',), 'a3': ('a2',), 'a4': ('a3',), 'a5': ('a4', 'p1'), 'a6': ('a5',), 'x2': ('x1', 'a1'), 'x3': ('x2',), 'x4': ('x3',), 'o2': ('o1',), 'x1': ('a0',), 'p2': ('o0',), 'p3': ('o1',), 'p4': ('o2',)}
-IN_ORDER = {'i0x': ('i0',), 'i2': ('i1',), 'i3': ('i2',), 'i4': ('i3',), 'a1': ('a0', 'i1'), 'x1': ('x0', 'i0'), 'o2': ('o1',), 'o3': ('o2',), 'o4': ('o3',), 'x2': ('i0x',), 'b0': ('x3',)}
+OUT_ORDER = {'i1': ('i0',), 'i2': ('i1',), 'i3': ('i2',), 'i4': ('i3',), 'i5': ('i4',), 'i6': ('i5',), 'a1': ('a0',), 'a2': ('a1',), 'a3': ('a2',), 'a4': ('a3',), 'a5': ('a4',), 'a6': ('a5', 'b0', 'i6'), 'x3': ('x2',), 'x5': ('x4',), 'x1': ('a0',), 'x2': ('a1',), 'p3': ('o1',), 'p4': ('o2',)}
+IN_ORDER = {'i0x': ('i0',), 'i3': ('i2',), 'i4': ('i3',), 'a1': ('a0', 'i1'), 'a3': ('a2',), 'o2': ('o1',), 'o3': ('o2',), 'o4': ('o3',), 'x1': ('i0',), 'x2': ('i0x',), 'c4': ('c3',)}
 STEP = 16
 TOLD = 0.05
+FIRST_VMEM = 48 * 1024 * 1024
 VMEM = 28 * 1024 * 1024
 PRODUCT_VMEM = 10 * 1024 * 1024
 
@@ -157,24 +158,21 @@
             done += size
 
 
-def split_sides(outs, count, apart):
-    lefts, rights = [], []
-    for n in range(count):
-        if apart:
-            rights.append(outs[2 * n])
-            lefts.append(outs[2 * n + 1])
-        else:
-            lefts.append(outs[n].at[0])
-            rights.append(outs[n].at[1])
-    for ref in outs[-count:]:
-        lefts.append(ref.at[1 if apart else 0])
-        rights.append(ref.at[0 if apart else 1])
+def split_sides(outs, sizes, apart):
+    count = len(sizes)
+    if not apart:
+        return [ref.at[0] for ref in outs], [ref.at[1] for ref in outs]
+    rights, lefts, sent = list(outs[: 2 * count : 2]), list(outs[1 : 2 * count : 2]), outs[2 * count :]
+    for n, size in enumerate(sizes):
+        skip = sizes[n - 1] if n else 0
+        rights.append(sent[n].at[skip : skip + size])
+        lefts.append(sent[n + 1].at[0:size])
     return lefts, rights
 
 
 def project_all(rows, gain, gate_ref, picked, picked_gate, scratch, outs, sizes, apart):
     normed = norm_rows(rows, gain)
-    project_part(normed, picked, scratch, split_sides(outs, len(sizes), apart), sizes)
+    project_part(normed, picked, scratch, split_sides(outs, sizes, apart), sizes)
     gate = 0.5 * jnp.tanh(dot(normed, picked_gate[...])) + 0.5
     gate_ref[...] = gate.astype(gate_ref.dtype).reshape(gate_ref.shape)
 
@@ -318,9 +316,11 @@
 
 def part_outs(pair, sizes, apart):
     tile = pair.shape[:2]
-    own = [(size,) + tile for size in sizes]
-    both_sides = [(2,) + shape for shape in own]
-    shapes = ([shape for shape in own for _ in range(2)] if apart else both_sides) + both_sides
+    if apart:
+        staged = zip((0,) + sizes, sizes + (0,))
+        shapes = [(size,) + tile for size in sizes for _ in range(2)] + [(a + b,) + tile for a, b in staged]
+    else:
+        shapes = [(2, size) + tile for size in sizes] * 2
     return [jax.ShapeDtypeStruct(shape, jnp.bfloat16) for shape in shapes], [chunk_spec(shape) for shape in shapes]
 
 
@@ -350,7 +350,7 @@
         out_specs=[tile_spec(pair)] + specs,
         out_shape=[jax.ShapeDtypeStruct(pair.shape, pair.dtype)] + outs,
         scratch_shapes=part_scratch(pair, w_in, OUT_SIZES),
-        compiler_params=params(),
+        compiler_params=params(FIRST_VMEM),
         cost_estimate=cost(2e9, 8 << 20, 4 << 20),
         name="project",
     )(chain, block_mask, pair, w_in, w_gate, gain_in)
@@ -482,17 +482,20 @@
     count = len(OUT_SIZES)
     graph = Graph(OUT_ORDER)
     get, send = graph.get, graph.send
-    for n in range(count):
+    for n in range(count + 1):
         send(f"x{n}", "x", lambda n=n: parts[2 * count + n])
+    before = lambda n: OUT_SIZES[n - 1] if n else 0
+    right_x = lambda n: (get(f"x{n}"), (), before(n))
+    left_x = lambda n: (get(f"x{n + 1}"), (), 0)
     later = lambda n, side: parts[2 * n + side]
-    right_of = lambda n: (later(n, 0), get(f"x{n}")[0])
-    left_of = lambda n: (later(n, 1), get(f"x{n}")[1])
+    right_of = lambda n: (later(n, 0), get(f"x{n}")[before(n) :])
+    left_of = lambda n: (later(n, 1), get(f"x{n + 1}")[: OUT_SIZES[n]])
     first = parts
     zero = OUT_SIZES[0]
     send("i0", "in", lambda: first[0])
     send("a0", "across", lambda: first[0])
-    send("i1", "in", lambda: jnp.concatenate([get("x0")[0], first[1]]))
-    send("a1", "across", lambda: jnp.concatenate([get("x0")[0], get("i0")]))
+    send("i1", "in", lambda: jnp.concatenate([get("x0"), first[1]]))
+    send("a1", "across", lambda: jnp.concatenate([get("x0"), get("i0")]))
 
     def come(n):
         array, skip = get(f"i{n + 1}"), zero // 2 if n == 1 else OUT_SIZES[n - 1]
@@ -502,12 +505,12 @@
         return (array[: zero // 2], array[zero // 2 :])
 
     def inward(n):
-        before = halves(get("x0")[1]) if n == 1 else left_of(n - 1)
-        return pack(before, right_of(n)) if n < count else pack(before)
+        behind = halves(get("x1")[:zero]) if n == 1 else left_of(n - 1)
+        return pack(behind, right_of(n)) if n < count else pack(behind)
 
     def across(n):
-        before = halves(get("i1")[:zero]) if n == 1 else come(n - 1)
-        return pack(before, right_of(n)) if n < count else pack(before)
+        behind = halves(get("i1")[:zero]) if n == 1 else come(n - 1)
+        return pack(behind, right_of(n)) if n < count else pack(behind)
 
     for n in range(1, count + 1):
         send(f"i{n + 1}", "in", lambda n=n: inward(n))
@@ -518,9 +521,9 @@
         if n == 0:
             x_left = lambda array: array[:, : zero // 2].reshape((zero,) + array.shape[2:])
             operands = [
-                [(left, (), 0), (get("x0"), (1,), 0)],
+                [(left, (), 0), left_x(0)],
                 [(get("i1"), (), zero), (x_left(get("i2")), (), 0)],
-                [(first[0], (), 0), (get("x0"), (0,), 0)],
+                [(first[0], (), 0), right_x(0)],
                 [(get("i0"), (), 0), (get("i1"), (), 0)],
                 [(get("a1"), (), zero), (x_left(get("a2")), (), 0)],
                 [(get("a0"), (), 0), (get("a1"), (), 0)],
@@ -528,9 +531,9 @@
         else:
             skip = zero // 2 if n == 1 else OUT_SIZES[n - 1]
             operands = [
-                [(left, (), 0), (get(f"x{n}"), (1,), 0)],
+                [(left, (), 0), left_x(n)],
                 both(get(f"i{n + 2}")),
-                [(later(n, 0), (), 0), (get(f"x{n}"), (0,), 0)],
+                [(later(n, 0), (), 0), right_x(n)],
                 both(get(f"i{n + 1}"), skip),
                 both(get(f"a{n + 2}")),
                 both(get(f"a{n + 1}"), skip),

time: 357 us -> 357 us (level)
  waiting for transfers between devices: 179 us -> 166 us
  starting transfers between devices: 94 us -> 106 us
  local copies, waits for them, and re-layouts: 12.4 us -> 6.84 us
  other arithmetic: 5.51 us -> 10.9 us
    ppermute x72 -> x73, waiting for transfers between devices: 179 us -> 166 us  [send(): self.add(name, operand, lambda array: lax.ppermute(array, axis, pairs))]
    ppermute x72 -> x73, starting transfers between devices: 94 us -> 106 us  [send(): self.add(name, operand, lambda array: lax.ppermute(array, axis, pairs))]
    unnamed x88 -> x68, local copies, waits for them, and re-layouts: 11 us -> 6.21 us
  transfers between devices with their start and end apart: 72 -> 73, of which waited for: 41 -> 32; matrix products, arithmetic and copies ran while one was open for 2% -> 3% of each run, Pallas kernels for 7% -> 7%
where the time goes in v9:
time: 357 us; the launch traced here: 355 us
  waiting for transfers between devices  166 us (46%)
  starting transfers between devices  106 us (30%)
  Pallas kernels  63.8 us (18%)
  other arithmetic  10.9 us (3%)
  local copies, waits for them, and re-layouts  6.84 us (2%)
    ppermute x73, waiting for transfers between devices, send(): self.add(name, operand, lambda array: lax.ppermute(array, axis, pairs))  166 us
    ppermute x73, starting transfers between devices, send(): self.add(name, operand, lambda array: lax.ppermute(array, axis, pairs))  106 us
    pallas_call x10, Pallas kernels, product_call(): pl.pallas_call(functools.partial(pieces_kernel, kernel, len(pieces)), gri...  25 us
    pallas_call x1, Pallas kernels, middle_call(): pl.pallas_call(functools.partial(middle_kernel, IN_SIZES, len(products)),...  17.9 us
    pallas_call x1, Pallas kernels, first_call(): pl.pallas_call(functools.partial(first_kernel, OUT_SIZES), grid=(pair.sha...  14.1 us
  transfers between devices with their start and end apart: 73, of which 32 were waited for; matrix products, arithmetic and copies ran while one was open for 3% of the time, Pallas kernels for 7%

profile of v9, /device:TPU:16, one launch (start us, length us, event | category | flops | bytes accessed | tf_op | source)
XLA Modules:
  0.0 354.9 jit_solution(11169925713608169124)
XLA Ops:
  3.8 14.1 %project.1 = (bf16[128,128,128]{2,1,0:T(8,128)(2,1)}, bf16[10,128,128]{2,1,0:T(8,128)(2,1)S(1)}, bf16[10,128,128]{2,1,0:T(8,128)(2,1)S(1)}, bf16[8,128,128]{2,1,...) custom-call(s32[4]{0:T(128)S(1)} %copy-done.27, ...), custom_call_target="tpu_custom_call" | custom-call | flops 100000000 | bytes 419430 | tf_op jit(solution)/shard_map/project/pallas_call | solution.py:346
  23.1 6.1 %collective-permute-done.refs_10_ = bf16[10,128,128]{2,1,0:T(8,128)(2,1)S(1)} collective-permute-done((bf16[10,128,128]{2,1,0:T(8,128)(2,1)S(1)}, bf16[10,128,128]{2,1,0:T(8,128)(2,1)S(1)}, u32[]{:S(2)}, u32[]{:S(2)}) %collective-permute-start) | collective-permute-done | bytes 327712 | tf_op jit(solution)/shard_map/ppermute | solution.py:434
  37.4 5.9 %collective-permute-done.1.refs_1_.refs_5_ = bf16[18,128,128]{2,1,0:T(8,128)(2,1)S(1)} collective-permute-done((bf16[18,128,128]{2,1,0:T(8,128)(2,1)S(1)}, bf16[18,128,128]{2,1,0:T(8,128)(2,1)S(1)}, u32[]{:S(2)}, u32[]{:S(2)}) %collective-permute-start.1) | collective-permute-done | bytes 589856 | tf_op jit(solution)/shard_map/ppermute | solution.py:434
  43.4 6.1 %collective-permute-done.4.refs_2_.refs_7_ = bf16[20,128,128]{2,1,0:T(8,128)(2,1)S(1)} collective-permute-done((bf16[20,128,128]{2,1,0:T(8,128)(2,1)S(1)}, bf16[20,128,128]{2,1,0:T(8,128)(2,1)S(1)}, u32[]{:S(2)}, u32[]{:S(2)}) %collective-permute-start.4) | collective-permute-done | bytes 655392 | tf_op jit(solution)/shard_map/ppermute | solution.py:434
  55.3 14.6 %collective-permute-done.5.refs_6_.refs_7_ = bf16[2,13,128,128]{3,2,1,0:T(8,128)(2,1)S(1)} collective-permute-done((bf16[2,13,128,128]{3,2,1,0:T(8,128)(2,1)S(1)}, bf16[2,13,128,128]{3,2,1,0:T(8,128)(2,1)S(1)}, u32[]{:S(2)}, u32[]{:S(2)}) %collective-permute-start.5) | collective-permute-done | bytes 852000 | tf_op jit(solution)/shard_map/ppermute | solution.py:434
  79.7 13.9 %collective-permute-done.11.refs_2_.refs_3_.refs_6_.refs_7_ = bf16[2,16,128,128]{3,2,1,0:T(8,128)(2,1)S(1)} collective-permute-done((bf16[2,16,128,128]{3,2,1,0:T(8,128)(2,1)S(1)}, bf16[2,16,128,128]{3,2,1,0:T(8,128)(2,1)S(1)}, u32[]{:S(2)}, u32[]{:S(2)}) %collective-permute-start.11) | collective-permute-done | bytes 1048608 | tf_op jit(solution)/shard_map/ppermute | solution.py:434
  103.8 5.6 %collective-permute-done.20.refs_1_.refs_5_ = bf16[6,128,128]{2,1,0:T(8,128)(2,1)S(1)} collective-permute-done((bf16[6,128,128]{2,1,0:T(8,128)(2,1)S(1)}, bf16[6,128,128]{2,1,0:T(8,128)(2,1)S(1)}, u32[]{:S(2)}, u32[]{:S(2)}) %collective-permute-start.20) | collective-permute-done | bytes 196640 | tf_op jit(solution)/shard_map/ppermute | solution.py:434
  113.0 4.4 %outgoing.7 = (bf16[8,128,128]{2,1,0:T(8,128)(2,1)S(1)}, bf16[8,128,128]{2,1,0:T(8,128)(2,1)S(1)}, bf16[2,8,128,128]{3,2,1,0:T(8,128)(2,1)S(1)}, bf16[2,2,8,128,128]{4,3,2,1,0:T(8,128)(2,1)}) custom-call(bf16[8,128,128]{2,1,0:T(8,128)(2,1)S(1)} %get-tuple-element.125.refs_0_, bf16[12,128,128]{2,1,0:T(8,128)(2,1)S(1)} %collective-permute-done.15.refs_1_.refs_5_, ...), custom_call_target="tpu_custom_call" | custom-call | flops 26843544 | bytes 262144 | tf_op jit(solution)/shard_map/outgoing/pallas_call | solution.py:403
  121.2 5.4 %collective-permute-start.14 = (bf16[2,8,128,128]{3,2,1,0:T(8,128)(2,1)}, bf16[2,8,128,128]{3,2,1,0:T(8,128)(2,1)}, u32[]{:S(2)}, u32[]{:S(2)}) collective-permute-start(bf16[2,8,128,128]{3,2,1,0:T(8,128)(2,1)} %fusion.11), channel_id=1, source_target_pairs={{4,0},{8,12},{5,1},{9,13},{6,2},{10,14},{7,3},{11,15},{20,16},{24,... | collective-permute-start | bytes 1572872 | tf_op jit(solution)/shard_map/ppermute | solution.py:434
  153.4 5.6 %collective-permute-done.19 = bf16[2,8,128,128]{3,2,1,0:T(8,128)(2,1)S(1)} collective-permute-done((bf16[2,8,128,128]{3,2,1,0:T(8,128)(2,1)S(1)}, bf16[2,8,128,128]{3,2,1,0:T(8,128)(2,1)S(1)}, u32[]{:S(2)}, u32[]{:S(2)}) %collective-permute-start.19) | collective-permute-done | bytes 524320 | tf_op jit(solution)/shard_map/ppermute | solution.py:434
  162.3 4.4 %collective-permute-start.30 = (bf16[2,2,128,128]{3,2,1,0:T(8,128)(2,1)S(1)}, bf16[2,2,128,128]{3,2,1,0:T(8,128)(2,1)S(1)}, u32[]{:S(2)}, u32[]{:S(2)}) collective-permute-start(bf16[2,2,128,128]{3,2,1,0:T(8,128)(2,1)S(1)} %fusion.59), channel_id=1, source_target_pairs={{4,0},{8,12},{5,1},{9,13},{6,2},{10,14},{7,3},{11,15},{20,16},{24,... | collective-permute-start | bytes 393224 | tf_op jit(solution)/shard_map/ppermute | solution.py:434
  174.3 17.9 %middle.1 = (bf16[128,128,128]{2,1,0:T(8,128)(2,1)S(1)}, bf16[128,128,128]{2,1,0:T(8,128)(2,1)S(1)}, bf16[2,8,128,128]{3,2,1,0:T(8,128)(2,1)S(1)}, bf16[2,8,128,...) custom-call(s32[4]{0:T(128)S(1)} %copy-done.28, ...), custom_call_target="tpu_custom_call" | custom-call | flops 150000000 | bytes 943718 | tf_op jit(solution)/shard_map/middle/pallas_call | solution.py:377
  194.6 12.5 %collective-permute-done.38.refs_4_.refs_10_ = bf16[2,8,128,128]{3,2,1,0:T(8,128)(2,1)S(1)} collective-permute-done((bf16[2,8,128,128]{3,2,1,0:T(8,128)(2,1)S(1)}, bf16[2,8,128,128]{3,2,1,0:T(8,128)(2,1)S(1)}, u32[]{:S(2)}, u32[]{:S(2)}) %collective-permute-start.38) | collective-permute-done | bytes 524320 | tf_op jit(solution)/shard_map/ppermute | solution.py:434
  210.2 9.3 %collective-permute-done.44 = bf16[2,8,128,128]{3,2,1,0:T(8,128)(2,1)S(1)} collective-permute-done((bf16[2,8,128,128]{3,2,1,0:T(8,128)(2,1)S(1)}, bf16[2,8,128,128]{3,2,1,0:T(8,128)(2,1)S(1)}, u32[]{:S(2)}, u32[]{:S(2)}) %collective-permute-start.44) | collective-permute-done | bytes 524320 | tf_op jit(solution)/shard_map/ppermute | solution.py:434
  231.3 7.0 %collective-permute-done.50 = bf16[2,8,128,128]{3,2,1,0:T(8,128)(2,1)S(1)} collective-permute-done((bf16[2,8,128,128]{3,2,1,0:T(8,128)(2,1)S(1)}, bf16[2,8,128,128]{3,2,1,0:T(8,128)(2,1)S(1)}, u32[]{:S(2)}, u32[]{:S(2)}) %collective-permute-start.50) | collective-permute-done | bytes 524320 | tf_op jit(solution)/shard_map/ppermute | solution.py:434
  239.8 7.8 %collective-permute-done.46.refs_4_.refs_5_.refs_10_.refs_11_ = bf16[2,2,8,128,128]{4,3,2,1,0:T(8,128)(2,1)S(1)} collective-permute-done((bf16[2,2,8,128,128]{4,3,2,1,0:T(8,128)(2,1)S(1)}, bf16[2,2,8,128,128]{4,3,2,1,0:T(8,128)(2,1)S(1)}, u32[]{:S(2)}, u32[]{:S(2)}) %collective-permute-start.46) | collective-permute-done | bytes 1048608 | tf_op jit(solution)/shard_map/ppermute | solution.py:434
  258.4 9.5 %collective-permute-done.52.refs_4_.refs_5_.refs_10_.refs_11_ = bf16[2,2,8,128,128]{4,3,2,1,0:T(8,128)(2,1)S(1)} collective-permute-done((bf16[2,2,8,128,128]{4,3,2,1,0:T(8,128)(2,1)S(1)}, bf16[2,2,8,128,128]{4,3,2,1,0:T(8,128)(2,1)S(1)}, u32[]{:S(2)}, u32[]{:S(2)}) %collective-permute-start.52) | collective-permute-done | bytes 1048608 | tf_op jit(solution)/shard_map/ppermute | solution.py:434
  270.3 6.4 %collective-permute-done.62 = bf16[2,4,128,128]{3,2,1,0:T(8,128)(2,1)S(1)} collective-permute-done((bf16[2,4,128,128]{3,2,1,0:T(8,128)(2,1)S(1)}, bf16[2,4,128,128]{3,2,1,0:T(8,128)(2,1)S(1)}, u32[]{:S(2)}, u32[]{:S(2)}) %collective-permute-start.62) | collective-permute-done | bytes 262176 | tf_op jit(solution)/shard_map/ppermute | solution.py:434
  286.3 4.6 %collective-permute-start.49 = (bf16[2,8,128,128]{3,2,1,0:T(8,128)(2,1)S(1)}, bf16[2,8,128,128]{3,2,1,0:T(8,128)(2,1)S(1)}, u32[]{:S(2)}, u32[]{:S(2)}) collective-permute-start(bf16[2,8,128,128]{3,2,1,0:T(8,128)(2,1)S(1)} %fusion.8), channel_id=1, source_target_pairs={{4,0},{8,12},{5,1},{9,13},{6,2},{10,14},{7,3},{11,15},{20,16},{24,... | collective-permute-start | bytes 1572872 | tf_op jit(solution)/shard_map/ppermute | solution.py:434
  292.7 7.6 %collective-permute-done.64.refs_4_.refs_5_.refs_10_.refs_11_ = bf16[2,2,4,128,128]{4,3,2,1,0:T(8,128)(2,1)S(1)} collective-permute-done((bf16[2,2,4,128,128]{4,3,2,1,0:T(8,128)(2,1)S(1)}, bf16[2,2,4,128,128]{4,3,2,1,0:T(8,128)(2,1)S(1)}, u32[]{:S(2)}, u32[]{:S(2)}) %collective-permute-start.64) | collective-permute-done | bytes 524320 | tf_op jit(solution)/shard_map/ppermute | solution.py:434
  300.4 6.8 %collective-permute-done.54 = bf16[2,2,8,128,128]{4,3,2,1,0:T(8,128)(2,1)S(1)} collective-permute-done((bf16[2,2,8,128,128]{4,3,2,1,0:T(8,128)(2,1)S(1)}, bf16[2,2,8,128,128]{4,3,2,1,0:T(8,128)(2,1)S(1)}, u32[]{:S(2)}, u32[]{:S(2)}) %collective-permute-start.54) | collective-permute-done | bytes 1048608 | tf_op jit(solution)/shard_map/ppermute | solution.py:434
  317.0 6.9 %collective-permute-done.60 = bf16[2,2,4,128,128]{4,3,2,1,0:T(8,128)(2,1)S(1)} collective-permute-done((bf16[2,2,4,128,128]{4,3,2,1,0:T(8,128)(2,1)S(1)}, bf16[2,2,4,128,128]{4,3,2,1,0:T(8,128)(2,1)S(1)}, u32[]{:S(2)}, u32[]{:S(2)}) %collective-permute-start.60) | collective-permute-done | bytes 524320 | tf_op jit(solution)/shard_map/ppermute | solution.py:434
  328.4 5.5 %collective-permute-done.66 = bf16[2,2,4,128,128]{4,3,2,1,0:T(8,128)(2,1)S(1)} collective-permute-done((bf16[2,2,4,128,128]{4,3,2,1,0:T(8,128)(2,1)S(1)}, bf16[2,2,4,128,128]{4,3,2,1,0:T(8,128)(2,1)S(1)}, u32[]{:S(2)}, u32[]{:S(2)}) %collective-permute-start.66) | collective-permute-done | bytes 524320 | tf_op jit(solution)/shard_map/ppermute | solution.py:434
  348.2 6.8 %finish.1 = bf16[128,128,128]{2,1,0:T(8,128)(2,1)} custom-call(bf16[128,128,128]{2,1,0:T(8,128)(2,1)S(1)} %get-tuple-element.157.pair_ref, bf16[128,128,128]{2,1,0:T(8,128)(2,1)S(1)} %get-tuple-element.158.gate_ref, bf16[2,64,128]{2,1,0:T(8,128)(2,1)S(1)} %copy-done.22, f32[64,1,128]{2,1,0:T(1,128)S(1)} %broadcast_in_dim.15.gain_ref, ...), custom_call_target="tpu_custom_call" | custom-call | flops 50000000 | bytes 734003 | tf_op jit(solution)/shard_map/finish/pallas_call | solution.py:361
  (269 shorter events, 158.6 us)
Async XLA Ops:
  49.7 20.2 %collective-permute-start.5 = (bf16[2,13,128,128]{3,2,1,0:T(8,128)(2,1)S(1)}, bf16[2,13,128,128]{3,2,1,0:T(8,128)(2,1)S(1)}, u32[]{:S(2)}, u32[]{:S(2)}) collective-permute-start(bf16[2,13,128,128]{3,2,1,0:T(8,128)(2,1)S(1)} %pad_maximum_fusion.4), channel_id=1, source_target_pairs={{0,4},{12,8},{1,5},{13,9},{2,6},{14,10},{3,7},{15,11},{16,20},{28,... | collective-permute-start | bytes 2555912 | tf_op jit(solution)/shard_map/ppermute | solution.py:434
  51.1 19.0 %collective-permute-start.10 = (bf16[16,128,128]{2,1,0:T(8,128)(2,1)S(1)}, bf16[16,128,128]{2,1,0:T(8,128)(2,1)S(1)}, u32[]{:S(2)}, u32[]{:S(2)}) collective-permute-start(bf16[16,128,128]{2,1,0:T(8,128)(2,1)S(1)} %get-tuple-element.118), channel_id=1, source_target_pairs={{0,2},{1,3},{2,0},{3,1},{4,6},{5,7},{6,4},{7,5},{8,10},{9,11},{10,... | collective-permute-start | bytes 1572872 | tf_op jit(solution)/shard_map/ppermute | solution.py:434
  51.8 20.4 %collective-permute-start.7 = (bf16[2,13,128,128]{3,2,1,0:T(8,128)(2,1)S(1)}, bf16[2,13,128,128]{3,2,1,0:T(8,128)(2,1)S(1)}, u32[]{:S(2)}, u32[]{:S(2)}) collective-permute-start(bf16[2,13,128,128]{3,2,1,0:T(8,128)(2,1)S(1)} %pad_maximum_fusion.5), channel_id=1, source_target_pairs={{4,8},{8,4},{5,9},{9,5},{6,10},{10,6},{7,11},{11,7},{20,24},{24,20... | collective-permute-start | bytes 2555912 | tf_op jit(solution)/shard_map/ppermute | solution.py:434
  70.1 23.5 %collective-permute-start.11 = (bf16[2,16,128,128]{3,2,1,0:T(8,128)(2,1)S(1)}, bf16[2,16,128,128]{3,2,1,0:T(8,128)(2,1)S(1)}, u32[]{:S(2)}, u32[]{:S(2)}) collective-permute-start(bf16[2,16,128,128]{3,2,1,0:T(8,128)(2,1)S(1)} %pad_maximum_fusion.2), channel_id=1, source_target_pairs={{0,4},{12,8},{1,5},{13,9},{2,6},{14,10},{3,7},{15,11},{16,20},{28,... | collective-permute-start | bytes 3145736 | tf_op jit(solution)/shard_map/ppermute | solution.py:434
  72.2 23.2 %collective-permute-start.12 = (bf16[2,16,128,128]{3,2,1,0:T(8,128)(2,1)S(1)}, bf16[2,16,128,128]{3,2,1,0:T(8,128)(2,1)S(1)}, u32[]{:S(2)}, u32[]{:S(2)}) collective-permute-start(bf16[2,16,128,128]{3,2,1,0:T(8,128)(2,1)S(1)} %pad_maximum_fusion.3), channel_id=1, source_target_pairs={{4,8},{8,4},{5,9},{9,5},{6,10},{10,6},{7,11},{11,7},{20,24},{24,20... | collective-permute-start | bytes 3145736 | tf_op jit(solution)/shard_map/ppermute | solution.py:434
  79.6 29.8 %collective-permute-start.8 = (bf16[2,2,10,128,128]{4,3,2,1,0:T(8,128)(2,1)S(1)}, bf16[2,2,10,128,128]{4,3,2,1,0:T(8,128)(2,1)S(1)}, u32[]{:S(2)}, u32[]{:S(2)}) collective-permute-start(bf16[2,2,10,128,128]{4,3,2,1,0:T(8,128)(2,1)S(1)} %get-tuple-element.114), channel_id=1, source_target_pairs={{0,1},{1,0},{2,3},{3,2},{4,5},{5,4},{6,7},{7,6},{8,9},{9,8},{10,11... | collective-permute-start | bytes 3932168 | tf_op jit(solution)/shard_map/ppermute | solution.py:434
  93.8 19.1 %collective-permute-start.16 = (bf16[2,12,128,128]{3,2,1,0:T(8,128)(2,1)S(1)}, bf16[2,12,128,128]{3,2,1,0:T(8,128)(2,1)S(1)}, u32[]{:S(2)}, u32[]{:S(2)}) collective-permute-start(bf16[2,12,128,128]{3,2,1,0:T(8,128)(2,1)S(1)} %pad_maximum_fusion.6), channel_id=1, source_target_pairs={{0,4},{12,8},{1,5},{13,9},{2,6},{14,10},{3,7},{15,11},{16,20},{28,... | collective-permute-start | bytes 2359304 | tf_op jit(solution)/shard_map/ppermute | solution.py:434
  95.5 17.5 %collective-permute-start.17 = (bf16[2,12,128,128]{3,2,1,0:T(8,128)(2,1)S(1)}, bf16[2,12,128,128]{3,2,1,0:T(8,128)(2,1)S(1)}, u32[]{:S(2)}, u32[]{:S(2)}) collective-permute-start(bf16[2,12,128,128]{3,2,1,0:T(8,128)(2,1)S(1)} %pad_maximum_fusion.7), channel_id=1, source_target_pairs={{4,8},{8,4},{5,9},{9,5},{6,10},{10,6},{7,11},{11,7},{20,24},{24,20... | collective-permute-start | bytes 2359304 | tf_op jit(solution)/shard_map/ppermute | solution.py:434
  102.0 18.2 %collective-permute-start.13 = (bf16[2,2,8,128,128]{4,3,2,1,0:T(8,128)(2,1)S(1)}, bf16[2,2,8,128,128]{4,3,2,1,0:T(8,128)(2,1)S(1)}, u32[]{:S(2)}, u32[]{:S(2)}) collective-permute-start(bf16[2,2,8,128,128]{4,3,2,1,0:T(8,128)(2,1)S(1)} %get-tuple-element.123), channel_id=1, source_target_pairs={{0,1},{1,0},{2,3},{3,2},{4,5},{5,4},{6,7},{7,6},{8,9},{9,8},{10,11... | collective-permute-start | bytes 3145736 | tf_op jit(solution)/shard_map/ppermute | solution.py:434
  110.4 20.5 %collective-permute-start.9 = (bf16[2,10,128,128]{3,2,1,0:T(8,128)(2,1)}, bf16[2,10,128,128]{3,2,1,0:T(8,128)(2,1)}, u32[]{:S(2)}, u32[]{:S(2)}) collective-permute-start(bf16[2,10,128,128]{3,2,1,0:T(8,128)(2,1)} %fusion), channel_id=1, source_target_pairs={{4,0},{8,12},{5,1},{9,13},{6,2},{10,14},{7,3},{11,15},{20,16},{24,... | collective-permute-start | bytes 1966088 | tf_op jit(solution)/shard_map/ppermute | solution.py:434
  117.4 26.0 %collective-permute-start.18 = (bf16[2,2,8,128,128]{4,3,2,1,0:T(8,128)(2,1)}, bf16[2,2,8,128,128]{4,3,2,1,0:T(8,128)(2,1)}, u32[]{:S(2)}, u32[]{:S(2)}) collective-permute-start(bf16[2,2,8,128,128]{4,3,2,1,0:T(8,128)(2,1)} %get-tuple-element.132), channel_id=1, source_target_pairs={{0,1},{1,0},{2,3},{3,2},{4,5},{5,4},{6,7},{7,6},{8,9},{9,8},{10,11... | collective-permute-start | bytes 3145736 | tf_op jit(solution)/shard_map/ppermute | solution.py:434
  151.4 19.3 %collective-permute-start.31 = (bf16[8,128,128]{2,1,0:T(8,128)(2,1)S(1)}, bf16[8,128,128]{2,1,0:T(8,128)(2,1)S(1)}, u32[]{:S(2)}, u32[]{:S(2)}) collective-permute-start(bf16[8,128,128]{2,1,0:T(8,128)(2,1)S(1)} %get-tuple-element.209), channel_id=1, source_target_pairs={{0,2},{1,3},{2,0},{3,1},{4,6},{5,7},{6,4},{7,5},{8,10},{9,11},{10,... | collective-permute-start | bytes 786440 | tf_op jit(solution)/shard_map/ppermute | solution.py:434
  219.7 28.0 %collective-permute-start.46 = (bf16[2,2,8,128,128]{4,3,2,1,0:T(8,128)(2,1)S(1)}, bf16[2,2,8,128,128]{4,3,2,1,0:T(8,128)(2,1)S(1)}, u32[]{:S(2)}, u32[]{:S(2)}) collective-permute-start(bf16[2,2,8,128,128]{4,3,2,1,0:T(8,128)(2,1)S(1)} %pad_maximum_fusion.refs_0_.refs_1_.refs_8_.refs_9_), channel_id=1, source_target_pairs={{0,4},{12,8},{1,5},{13,9},{2,6},{14,10},{3,7},{15,11},{16,20},{28,... | collective-permute-start | bytes 3145736 | tf_op jit(solution)/shard_map/ppermute | solution.py:434
  228.7 27.1 %collective-permute-start.42 = (bf16[2,2,8,128,128]{4,3,2,1,0:T(8,128)(2,1)S(1)}, bf16[2,2,8,128,128]{4,3,2,1,0:T(8,128)(2,1)S(1)}, u32[]{:S(2)}, u32[]{:S(2)}) collective-permute-start(bf16[2,2,8,128,128]{4,3,2,1,0:T(8,128)(2,1)S(1)} %get-tuple-element.163), channel_id=1, source_target_pairs={{4,8},{8,4},{5,9},{9,5},{6,10},{10,6},{7,11},{11,7},{20,24},{24,20... | collective-permute-start | bytes 3145736 | tf_op jit(solution)/shard_map/ppermute | solution.py:434
  238.4 29.5 %collective-permute-start.52 = (bf16[2,2,8,128,128]{4,3,2,1,0:T(8,128)(2,1)S(1)}, bf16[2,2,8,128,128]{4,3,2,1,0:T(8,128)(2,1)S(1)}, u32[]{:S(2)}, u32[]{:S(2)}) collective-permute-start(bf16[2,2,8,128,128]{4,3,2,1,0:T(8,128)(2,1)S(1)} %pad_maximum_fusion.1.refs_0_.refs_1_.refs_8_.refs_9_), channel_id=1, source_target_pairs={{0,4},{12,8},{1,5},{13,9},{2,6},{14,10},{3,7},{15,11},{16,20},{28,... | collective-permute-start | bytes 3145736 | tf_op jit(solution)/shard_map/ppermute | solution.py:434
  247.8 21.1 %collective-permute-start.56 = (bf16[2,4,128,128]{3,2,1,0:T(8,128)(2,1)S(1)}, bf16[2,4,128,128]{3,2,1,0:T(8,128)(2,1)S(1)}, u32[]{:S(2)}, u32[]{:S(2)}) collective-permute-start(bf16[2,4,128,128]{3,2,1,0:T(8,128)(2,1)S(1)} %get-tuple-element.180), channel_id=1, source_target_pairs={{0,2},{1,3},{2,0},{3,1},{4,6},{5,7},{6,4},{7,5},{8,10},{9,11},{10,... | collective-permute-start | bytes 786440 | tf_op jit(solution)/shard_map/ppermute | solution.py:434
  249.6 27.2 %collective-permute-start.51 = (bf16[2,8,128,128]{3,2,1,0:T(8,128)(2,1)S(1)}, bf16[2,8,128,128]{3,2,1,0:T(8,128)(2,1)S(1)}, u32[]{:S(2)}, u32[]{:S(2)}) collective-permute-start(bf16[2,8,128,128]{3,2,1,0:T(8,128)(2,1)S(1)} %fusion.4), channel_id=1, source_target_pairs={{0,1},{1,0},{2,3},{3,2},{4,5},{5,4},{6,7},{7,6},{8,9},{9,8},{10,11... | collective-permute-start | bytes 1572872 | tf_op jit(solution)/shard_map/ppermute | solution.py:434
  255.8 30.3 %collective-permute-start.48 = (bf16[2,2,8,128,128]{4,3,2,1,0:T(8,128)(2,1)S(1)}, bf16[2,2,8,128,128]{4,3,2,1,0:T(8,128)(2,1)S(1)}, u32[]{:S(2)}, u32[]{:S(2)}) collective-permute-start(bf16[2,2,8,128,128]{4,3,2,1,0:T(8,128)(2,1)S(1)} %get-tuple-element.170), channel_id=1, source_target_pairs={{4,8},{8,4},{5,9},{9,5},{6,10},{10,6},{7,11},{11,7},{20,24},{24,20... | collective-permute-start | bytes 3145736 | tf_op jit(solution)/shard_map/ppermute | solution.py:434
  279.7 27.5 %collective-permute-start.54 = (bf16[2,2,8,128,128]{4,3,2,1,0:T(8,128)(2,1)S(1)}, bf16[2,2,8,128,128]{4,3,2,1,0:T(8,128)(2,1)S(1)}, u32[]{:S(2)}, u32[]{:S(2)}) collective-permute-start(bf16[2,2,8,128,128]{4,3,2,1,0:T(8,128)(2,1)S(1)} %get-tuple-element.176), channel_id=1, source_target_pairs={{4,8},{8,4},{5,9},{9,5},{6,10},{10,6},{7,11},{11,7},{20,24},{24,20... | collective-permute-start | bytes 3145736 | tf_op jit(solution)/shard_map/ppermute | solution.py:434
  283.0 33.0 %collective-permute-start.43 = (bf16[2,8,128,128]{3,2,1,0:T(8,128)(2,1)S(1)}, bf16[2,8,128,128]{3,2,1,0:T(8,128)(2,1)S(1)}, u32[]{:S(2)}, u32[]{:S(2)}) collective-permute-start(bf16[2,8,128,128]{3,2,1,0:T(8,128)(2,1)S(1)} %fusion.9), channel_id=1, source_target_pairs={{4,0},{8,12},{5,1},{9,13},{6,2},{10,14},{7,3},{11,15},{20,16},{24,... | collective-permute-start | bytes 1572872 | tf_op jit(solution)/shard_map/ppermute | solution.py:434
  286.3 24.1 %collective-permute-start.49 = (bf16[2,8,128,128]{3,2,1,0:T(8,128)(2,1)S(1)}, bf16[2,8,128,128]{3,2,1,0:T(8,128)(2,1)S(1)}, u32[]{:S(2)}, u32[]{:S(2)}) collective-permute-start(bf16[2,8,128,128]{3,2,1,0:T(8,128)(2,1)S(1)} %fusion.8), channel_id=1, source_target_pairs={{4,0},{8,12},{5,1},{9,13},{6,2},{10,14},{7,3},{11,15},{20,16},{24,... | collective-permute-start | bytes 1572872 | tf_op jit(solution)/shard_map/ppermute | solution.py:434
  291.0 20.8 %collective-permute-start.63 = (bf16[2,4,128,128]{3,2,1,0:T(8,128)(2,1)S(1)}, bf16[2,4,128,128]{3,2,1,0:T(8,128)(2,1)S(1)}, u32[]{:S(2)}, u32[]{:S(2)}) collective-permute-start(bf16[2,4,128,128]{3,2,1,0:T(8,128)(2,1)S(1)} %fusion.21), channel_id=1, source_target_pairs={{0,1},{1,0},{2,3},{3,2},{4,5},{5,4},{6,7},{7,6},{8,9},{9,8},{10,11... | collective-permute-start | bytes 786440 | tf_op jit(solution)/shard_map/ppermute | solution.py:434
  313.3 20.6 %collective-permute-start.66 = (bf16[2,2,4,128,128]{4,3,2,1,0:T(8,128)(2,1)S(1)}, bf16[2,2,4,128,128]{4,3,2,1,0:T(8,128)(2,1)S(1)}, u32[]{:S(2)}, u32[]{:S(2)}) collective-permute-start(bf16[2,2,4,128,128]{4,3,2,1,0:T(8,128)(2,1)S(1)} %get-tuple-element.191), channel_id=1, source_target_pairs={{4,8},{8,4},{5,9},{9,5},{6,10},{10,6},{7,11},{11,7},{20,24},{24,20... | collective-permute-start | bytes 1572872 | tf_op jit(solution)/shard_map/ppermute | solution.py:434
  316.0 25.1 %collective-permute-start.68 = (bf16[8,128,128]{2,1,0:T(8,128)(2,1)S(1)}, bf16[8,128,128]{2,1,0:T(8,128)(2,1)S(1)}, u32[]{:S(2)}, u32[]{:S(2)}) collective-permute-start(bf16[8,128,128]{2,1,0:T(8,128)(2,1)S(1)} %get-tuple-element.205), channel_id=1, source_target_pairs={{0,2},{1,3},{2,0},{3,1},{4,6},{5,7},{6,4},{7,5},{8,10},{9,11},{10,... | collective-permute-start | bytes 786440 | tf_op jit(solution)/shard_map/ppermute | solution.py:434
  (83 other events, 1279.3 us)

commit v10 on v8

--- a/solution.py
+++ b/solution.py
@@ -14,7 +14,7 @@
 OUT_GROUPS = (1, 1, 1, 1, 1)
 IN_GROUPS = (1, 1, 1, 1, 1)
 OUT_ORDER = {'i1': ('i0',), 'i2': ('i1',), 'i3': ('i2',), 'i4': ('i3',), 'i5': ('i4',), 'i6': ('i5',), 'a1': ('a0',), 'a2': ('a1',), 'a3': ('a2',), 'a4': ('a3',), 'a5': ('a4', 'p1'), 'a6': ('a5',), 'x2': ('x1', 'a1'), 'x3': ('x2',), 'x4': ('x3',), 'o2': ('o1',), 'x1': ('a0',), 'p2': ('o0',), 'p3': ('o1',), 'p4': ('o2',)}
-IN_ORDER = {'i0x': ('i0',), 'i2': ('i1',), 'i3': ('i2',), 'i4': ('i3',), 'a1': ('a0', 'i1'), 'x1': ('x0', 'i0'), 'o2': ('o1',), 'o3': ('o2',), 'o4': ('o3',), 'x2': ('i0x',), 'b0': ('x3',)}
+IN_ORDER = {'i0x': ('i0',), 'i3': ('i2',), 'i4': ('i3',), 'a1': ('a0', 'i1'), 'a3': ('a2',), 'o2': ('o1',), 'o3': ('o2',), 'o4': ('o3',), 'x1': ('i0',), 'x2': ('i0x',), 'c4': ('c3',)}
 STEP = 16
 TOLD = 0.05
 VMEM = 28 * 1024 * 1024

time: 357 us -> 355 us (level)
  transfers between devices with their start and end apart: 72 -> 72, of which waited for: 41 -> 37; matrix products, arithmetic and copies ran while one was open for 2% -> 2% of each run, Pallas kernels for 7% -> 7%
where the time goes in v10:
time: 355 us; the launch traced here: 353 us
  waiting for transfers between devices  179 us (50%)
  starting transfers between devices  91.5 us (26%)
  Pallas kernels  62.4 us (18%)
  local copies, waits for them, and re-layouts  12.3 us (3%)
  other arithmetic  5.58 us (2%)
    ppermute x72, waiting for transfers between devices, send(): self.add(name, operand, lambda array: lax.ppermute(array, axis, pairs))  179 us
    ppermute x72, starting transfers between devices, send(): self.add(name, operand, lambda array: lax.ppermute(array, axis, pairs))  91.5 us
    pallas_call x10, Pallas kernels, product_call(): pl.pallas_call(functools.partial(pieces_kernel, kernel, len(pieces)), gri...  24.8 us
    pallas_call x1, Pallas kernels, middle_call(): pl.pallas_call(functools.partial(middle_kernel, IN_SIZES, len(products)),...  18 us
    pallas_call x1, Pallas kernels, first_call(): pl.pallas_call(functools.partial(first_kernel, OUT_SIZES), grid=(pair.sha...  12.8 us
    unnamed x88, local copies, waits for them, and re-layouts  11 us
  transfers between devices with their start and end apart: 72, of which 37 were waited for; matrix products, arithmetic and copies ran while one was open for 2% of the time, Pallas kernels for 7%

profile of v10, /device:TPU:16, one launch (start us, length us, event | category | flops | bytes accessed | tf_op | source)
XLA Modules:
  0.0 352.7 jit_solution(4326386441433868507)
XLA Ops:
  6.0 12.8 %project.1 = (bf16[128,128,128]{2,1,0:T(8,128)(2,1)S(1)}, bf16[8,128,128]{2,1,0:T(8,128)(2,1)S(1)}, bf16[8,128,128]{2,1,0:T(8,128)(2,1)S(1)}, bf16[8,128,128]{2,...) custom-call(s32[4]{0:T(128)S(1)} %copy-done.31, ...), custom_call_target="tpu_custom_call" | custom-call | flops 100000000 | bytes 419430 | tf_op jit(solution)/shard_map/project/pallas_call | solution.py:346
  24.0 6.0 %collective-permute-done.3.refs_10_ = bf16[8,128,128]{2,1,0:T(8,128)(2,1)S(1)} collective-permute-done((bf16[8,128,128]{2,1,0:T(8,128)(2,1)S(1)}, bf16[8,128,128]{2,1,0:T(8,128)(2,1)S(1)}, u32[]{:S(2)}, u32[]{:S(2)}) %collective-permute-start.3) | collective-permute-done | bytes 262176 | tf_op jit(solution)/shard_map/ppermute | solution.py:434
  37.5 6.3 %collective-permute-done.4.refs_1_.refs_5_ = bf16[2,8,128,128]{3,2,1,0:T(8,128)(2,1)S(1)} collective-permute-done((bf16[2,8,128,128]{3,2,1,0:T(8,128)(2,1)S(1)}, bf16[2,8,128,128]{3,2,1,0:T(8,128)(2,1)S(1)}, u32[]{:S(2)}, u32[]{:S(2)}) %collective-permute-start.4) | collective-permute-done | bytes 524320 | tf_op jit(solution)/shard_map/ppermute | solution.py:434
  52.9 6.8 %collective-permute-done.10.refs_1_.refs_5_ = bf16[2,8,128,128]{3,2,1,0:T(8,128)(2,1)S(1)} collective-permute-done((bf16[2,8,128,128]{3,2,1,0:T(8,128)(2,1)S(1)}, bf16[2,8,128,128]{3,2,1,0:T(8,128)(2,1)S(1)}, u32[]{:S(2)}, u32[]{:S(2)}) %collective-permute-start.10) | collective-permute-done | bytes 524320 | tf_op jit(solution)/shard_map/ppermute | solution.py:434
  59.7 6.1 %collective-permute-done.5.refs_6_.refs_7_ = bf16[2,12,128,128]{3,2,1,0:T(8,128)(2,1)S(1)} collective-permute-done((bf16[2,12,128,128]{3,2,1,0:T(8,128)(2,1)S(1)}, bf16[2,12,128,128]{3,2,1,0:T(8,128)(2,1)S(1)}, u32[]{:S(2)}, u32[]{:S(2)}) %collective-permute-start.5) | collective-permute-done | bytes 786464 | tf_op jit(solution)/shard_map/ppermute | solution.py:434
  75.3 13.9 %collective-permute-done.11.refs_2_.refs_3_.refs_6_.refs_7_ = bf16[2,16,128,128]{3,2,1,0:T(8,128)(2,1)S(1)} collective-permute-done((bf16[2,16,128,128]{3,2,1,0:T(8,128)(2,1)S(1)}, bf16[2,16,128,128]{3,2,1,0:T(8,128)(2,1)S(1)}, u32[]{:S(2)}, u32[]{:S(2)}) %collective-permute-start.11) | collective-permute-done | bytes 1048608 | tf_op jit(solution)/shard_map/ppermute | solution.py:434
  118.2 7.0 %collective-permute-done.14 = bf16[2,8,128,128]{3,2,1,0:T(8,128)(2,1)S(1)} collective-permute-done((bf16[2,8,128,128]{3,2,1,0:T(8,128)(2,1)S(1)}, bf16[2,8,128,128]{3,2,1,0:T(8,128)(2,1)S(1)}, u32[]{:S(2)}, u32[]{:S(2)}) %collective-permute-start.14) | collective-permute-done | bytes 524320 | tf_op jit(solution)/shard_map/ppermute | solution.py:434
  125.3 5.2 %collective-permute-start.19 = (bf16[2,8,128,128]{3,2,1,0:T(8,128)(2,1)}, bf16[2,8,128,128]{3,2,1,0:T(8,128)(2,1)}, u32[]{:S(2)}, u32[]{:S(2)}) collective-permute-start(bf16[2,8,128,128]{3,2,1,0:T(8,128)(2,1)} %fusion.11), channel_id=1, source_target_pairs={{4,0},{8,12},{5,1},{9,13},{6,2},{10,14},{7,3},{11,15},{20,16},{24,... | collective-permute-start | bytes 1572872 | tf_op jit(solution)/shard_map/ppermute | solution.py:434
  158.4 4.0 %collective-permute-done.28 = bf16[2,4,128,128]{3,2,1,0:T(8,128)(2,1)S(1)} collective-permute-done((bf16[2,4,128,128]{3,2,1,0:T(8,128)(2,1)S(1)}, bf16[2,4,128,128]{3,2,1,0:T(8,128)(2,1)S(1)}, u32[]{:S(2)}, u32[]{:S(2)}) %collective-permute-start.28) | collective-permute-done | bytes 262176 | tf_op jit(solution)/shard_map/ppermute | solution.py:434
  162.9 6.6 %collective-permute-done.32.rest_8_ = bf16[4,128,128]{2,1,0:T(8,128)(2,1)S(1)} collective-permute-done((bf16[4,128,128]{2,1,0:T(8,128)(2,1)S(1)}, bf16[4,128,128]{2,1,0:T(8,128)(2,1)S(1)}, u32[]{:S(2)}, u32[]{:S(2)}) %collective-permute-start.32) | collective-permute-done | bytes 131104 | tf_op jit(solution)/shard_map/ppermute | solution.py:434
  172.1 18.0 %middle.1 = (bf16[128,128,128]{2,1,0:T(8,128)(2,1)S(1)}, bf16[128,128,128]{2,1,0:T(8,128)(2,1)S(1)}, bf16[2,8,128,128]{3,2,1,0:T(8,128)(2,1)S(1)}, bf16[2,8,128,...) custom-call(s32[4]{0:T(128)S(1)} %copy-done.32, ...), custom_call_target="tpu_custom_call" | custom-call | flops 150000000 | bytes 943718 | tf_op jit(solution)/shard_map/middle/pallas_call | solution.py:377
  192.2 13.4 %collective-permute-done.37.refs_4_.refs_10_ = bf16[2,8,128,128]{3,2,1,0:T(8,128)(2,1)S(1)} collective-permute-done((bf16[2,8,128,128]{3,2,1,0:T(8,128)(2,1)S(1)}, bf16[2,8,128,128]{3,2,1,0:T(8,128)(2,1)S(1)}, u32[]{:S(2)}, u32[]{:S(2)}) %collective-permute-start.37) | collective-permute-done | bytes 524320 | tf_op jit(solution)/shard_map/ppermute | solution.py:434
  207.4 10.8 %collective-permute-done.43 = bf16[2,8,128,128]{3,2,1,0:T(8,128)(2,1)S(1)} collective-permute-done((bf16[2,8,128,128]{3,2,1,0:T(8,128)(2,1)S(1)}, bf16[2,8,128,128]{3,2,1,0:T(8,128)(2,1)S(1)}, u32[]{:S(2)}, u32[]{:S(2)}) %collective-permute-start.43) | collective-permute-done | bytes 524320 | tf_op jit(solution)/shard_map/ppermute | solution.py:434
  228.2 6.9 %collective-permute-done.49 = bf16[2,8,128,128]{3,2,1,0:T(8,128)(2,1)S(1)} collective-permute-done((bf16[2,8,128,128]{3,2,1,0:T(8,128)(2,1)S(1)}, bf16[2,8,128,128]{3,2,1,0:T(8,128)(2,1)S(1)}, u32[]{:S(2)}, u32[]{:S(2)}) %collective-permute-start.49) | collective-permute-done | bytes 524320 | tf_op jit(solution)/shard_map/ppermute | solution.py:434
  236.6 9.7 %collective-permute-done.45.refs_4_.refs_5_.refs_10_.refs_11_ = bf16[2,2,8,128,128]{4,3,2,1,0:T(8,128)(2,1)S(1)} collective-permute-done((bf16[2,2,8,128,128]{4,3,2,1,0:T(8,128)(2,1)S(1)}, bf16[2,2,8,128,128]{4,3,2,1,0:T(8,128)(2,1)S(1)}, u32[]{:S(2)}, u32[]{:S(2)}) %collective-permute-start.45) | collective-permute-done | bytes 1048608 | tf_op jit(solution)/shard_map/ppermute | solution.py:434
  255.3 10.3 %collective-permute-done.51.refs_4_.refs_5_.refs_10_.refs_11_ = bf16[2,2,8,128,128]{4,3,2,1,0:T(8,128)(2,1)S(1)} collective-permute-done((bf16[2,2,8,128,128]{4,3,2,1,0:T(8,128)(2,1)S(1)}, bf16[2,2,8,128,128]{4,3,2,1,0:T(8,128)(2,1)S(1)}, u32[]{:S(2)}, u32[]{:S(2)}) %collective-permute-start.51) | collective-permute-done | bytes 1048608 | tf_op jit(solution)/shard_map/ppermute | solution.py:434
  268.4 6.1 %collective-permute-done.61 = bf16[2,4,128,128]{3,2,1,0:T(8,128)(2,1)S(1)} collective-permute-done((bf16[2,4,128,128]{3,2,1,0:T(8,128)(2,1)S(1)}, bf16[2,4,128,128]{3,2,1,0:T(8,128)(2,1)S(1)}, u32[]{:S(2)}, u32[]{:S(2)}) %collective-permute-start.61) | collective-permute-done | bytes 262176 | tf_op jit(solution)/shard_map/ppermute | solution.py:434
  284.4 4.6 %collective-permute-start.48 = (bf16[2,8,128,128]{3,2,1,0:T(8,128)(2,1)S(1)}, bf16[2,8,128,128]{3,2,1,0:T(8,128)(2,1)S(1)}, u32[]{:S(2)}, u32[]{:S(2)}) collective-permute-start(bf16[2,8,128,128]{3,2,1,0:T(8,128)(2,1)S(1)} %fusion.9), channel_id=1, source_target_pairs={{4,0},{8,12},{5,1},{9,13},{6,2},{10,14},{7,3},{11,15},{20,16},{24,... | collective-permute-start | bytes 1572872 | tf_op jit(solution)/shard_map/ppermute | solution.py:434
  290.8 7.2 %collective-permute-done.63.refs_4_.refs_5_.refs_10_.refs_11_ = bf16[2,2,4,128,128]{4,3,2,1,0:T(8,128)(2,1)S(1)} collective-permute-done((bf16[2,2,4,128,128]{4,3,2,1,0:T(8,128)(2,1)S(1)}, bf16[2,2,4,128,128]{4,3,2,1,0:T(8,128)(2,1)S(1)}, u32[]{:S(2)}, u32[]{:S(2)}) %collective-permute-start.63) | collective-permute-done | bytes 524320 | tf_op jit(solution)/shard_map/ppermute | solution.py:434
  298.1 6.8 %collective-permute-done.53 = bf16[2,2,8,128,128]{4,3,2,1,0:T(8,128)(2,1)S(1)} collective-permute-done((bf16[2,2,8,128,128]{4,3,2,1,0:T(8,128)(2,1)S(1)}, bf16[2,2,8,128,128]{4,3,2,1,0:T(8,128)(2,1)S(1)}, u32[]{:S(2)}, u32[]{:S(2)}) %collective-permute-start.53) | collective-permute-done | bytes 1048608 | tf_op jit(solution)/shard_map/ppermute | solution.py:434
  310.1 3.6 %collective-permute-start.65 = (bf16[2,2,4,128,128]{4,3,2,1,0:T(8,128)(2,1)S(1)}, bf16[2,2,4,128,128]{4,3,2,1,0:T(8,128)(2,1)S(1)}, u32[]{:S(2)}, u32[]{:S(2)}) collective-permute-start(bf16[2,2,4,128,128]{4,3,2,1,0:T(8,128)(2,1)S(1)} %get-tuple-element.193), channel_id=1, source_target_pairs={{4,8},{8,4},{5,9},{9,5},{6,10},{10,6},{7,11},{11,7},{20,24},{24,20... | collective-permute-start | bytes 1572872 | tf_op jit(solution)/shard_map/ppermute | solution.py:434
  315.0 6.6 %collective-permute-done.59 = bf16[2,2,4,128,128]{4,3,2,1,0:T(8,128)(2,1)S(1)} collective-permute-done((bf16[2,2,4,128,128]{4,3,2,1,0:T(8,128)(2,1)S(1)}, bf16[2,2,4,128,128]{4,3,2,1,0:T(8,128)(2,1)S(1)}, u32[]{:S(2)}, u32[]{:S(2)}) %collective-permute-start.59) | collective-permute-done | bytes 524320 | tf_op jit(solution)/shard_map/ppermute | solution.py:434
  325.3 6.3 %collective-permute-done.65 = bf16[2,2,4,128,128]{4,3,2,1,0:T(8,128)(2,1)S(1)} collective-permute-done((bf16[2,2,4,128,128]{4,3,2,1,0:T(8,128)(2,1)S(1)}, bf16[2,2,4,128,128]{4,3,2,1,0:T(8,128)(2,1)S(1)}, u32[]{:S(2)}, u32[]{:S(2)}) %collective-permute-start.65) | collective-permute-done | bytes 524320 | tf_op jit(solution)/shard_map/ppermute | solution.py:434
  345.9 6.8 %finish.1 = bf16[128,128,128]{2,1,0:T(8,128)(2,1)} custom-call(bf16[128,128,128]{2,1,0:T(8,128)(2,1)S(1)} %get-tuple-element.159.pair_ref, bf16[128,128,128]{2,1,0:T(8,128)(2,1)S(1)} %get-tuple-element.160.gate_ref, bf16[2,64,128]{2,1,0:T(8,128)(2,1)S(1)} %copy-done.26, f32[64,1,128]{2,1,0:T(1,128)S(1)} %broadcast_in_dim.15.gain_ref, ...), custom_call_target="tpu_custom_call" | custom-call | flops 50000000 | bytes 734003 | tf_op jit(solution)/shard_map/finish/pallas_call | solution.py:361
  (287 shorter events, 159.5 us)
Async XLA Ops:
  47.6 18.2 %collective-permute-start.5 = (bf16[2,12,128,128]{3,2,1,0:T(8,128)(2,1)S(1)}, bf16[2,12,128,128]{3,2,1,0:T(8,128)(2,1)S(1)}, u32[]{:S(2)}, u32[]{:S(2)}) collective-permute-start(bf16[2,12,128,128]{3,2,1,0:T(8,128)(2,1)S(1)} %pad_maximum_fusion.4), channel_id=1, source_target_pairs={{0,4},{12,8},{1,5},{13,9},{2,6},{14,10},{3,7},{15,11},{16,20},{28,... | collective-permute-start | bytes 2359304 | tf_op jit(solution)/shard_map/ppermute | solution.py:434
  50.5 18.6 %collective-permute-start.7 = (bf16[2,12,128,128]{3,2,1,0:T(8,128)(2,1)S(1)}, bf16[2,12,128,128]{3,2,1,0:T(8,128)(2,1)S(1)}, u32[]{:S(2)}, u32[]{:S(2)}) collective-permute-start(bf16[2,12,128,128]{3,2,1,0:T(8,128)(2,1)S(1)} %pad_maximum_fusion.5), channel_id=1, source_target_pairs={{4,8},{8,4},{5,9},{9,5},{6,10},{10,6},{7,11},{11,7},{20,24},{24,20... | collective-permute-start | bytes 2359304 | tf_op jit(solution)/shard_map/ppermute | solution.py:434
  66.1 23.0 %collective-permute-start.11 = (bf16[2,16,128,128]{3,2,1,0:T(8,128)(2,1)S(1)}, bf16[2,16,128,128]{3,2,1,0:T(8,128)(2,1)S(1)}, u32[]{:S(2)}, u32[]{:S(2)}) collective-permute-start(bf16[2,16,128,128]{3,2,1,0:T(8,128)(2,1)S(1)} %pad_maximum_fusion.2), channel_id=1, source_target_pairs={{0,4},{12,8},{1,5},{13,9},{2,6},{14,10},{3,7},{15,11},{16,20},{28,... | collective-permute-start | bytes 3145736 | tf_op jit(solution)/shard_map/ppermute | solution.py:434
  69.1 23.3 %collective-permute-start.12 = (bf16[2,16,128,128]{3,2,1,0:T(8,128)(2,1)S(1)}, bf16[2,16,128,128]{3,2,1,0:T(8,128)(2,1)S(1)}, u32[]{:S(2)}, u32[]{:S(2)}) collective-permute-start(bf16[2,16,128,128]{3,2,1,0:T(8,128)(2,1)S(1)} %pad_maximum_fusion.3), channel_id=1, source_target_pairs={{4,8},{8,4},{5,9},{9,5},{6,10},{10,6},{7,11},{11,7},{20,24},{24,20... | collective-permute-start | bytes 3145736 | tf_op jit(solution)/shard_map/ppermute | solution.py:434
  75.2 19.5 %collective-permute-start.8 = (bf16[2,2,8,128,128]{4,3,2,1,0:T(8,128)(2,1)S(1)}, bf16[2,2,8,128,128]{4,3,2,1,0:T(8,128)(2,1)S(1)}, u32[]{:S(2)}, u32[]{:S(2)}) collective-permute-start(bf16[2,2,8,128,128]{4,3,2,1,0:T(8,128)(2,1)S(1)} %get-tuple-element.115), channel_id=1, source_target_pairs={{0,1},{1,0},{2,3},{3,2},{4,5},{5,4},{6,7},{7,6},{8,9},{9,8},{10,11... | collective-permute-start | bytes 3145736 | tf_op jit(solution)/shard_map/ppermute | solution.py:434
  89.5 16.5 %collective-permute-start.16 = (bf16[2,12,128,128]{3,2,1,0:T(8,128)(2,1)S(1)}, bf16[2,12,128,128]{3,2,1,0:T(8,128)(2,1)S(1)}, u32[]{:S(2)}, u32[]{:S(2)}) collective-permute-start(bf16[2,12,128,128]{3,2,1,0:T(8,128)(2,1)S(1)} %pad_maximum_fusion.6), channel_id=1, source_target_pairs={{0,4},{12,8},{1,5},{13,9},{2,6},{14,10},{3,7},{15,11},{16,20},{28,... | collective-permute-start | bytes 2359304 | tf_op jit(solution)/shard_map/ppermute | solution.py:434
  92.4 16.2 %collective-permute-start.17 = (bf16[2,12,128,128]{3,2,1,0:T(8,128)(2,1)S(1)}, bf16[2,12,128,128]{3,2,1,0:T(8,128)(2,1)S(1)}, u32[]{:S(2)}, u32[]{:S(2)}) collective-permute-start(bf16[2,12,128,128]{3,2,1,0:T(8,128)(2,1)S(1)} %pad_maximum_fusion.7), channel_id=1, source_target_pairs={{4,8},{8,4},{5,9},{9,5},{6,10},{10,6},{7,11},{11,7},{20,24},{24,20... | collective-permute-start | bytes 2359304 | tf_op jit(solution)/shard_map/ppermute | solution.py:434
  113.3 17.9 %collective-permute-start.21 = (bf16[2,8,128,128]{3,2,1,0:T(8,128)(2,1)S(1)}, bf16[2,8,128,128]{3,2,1,0:T(8,128)(2,1)S(1)}, u32[]{:S(2)}, u32[]{:S(2)}) collective-permute-start(bf16[2,8,128,128]{3,2,1,0:T(8,128)(2,1)S(1)} %pad_maximum_fusion.16), channel_id=1, source_target_pairs={{0,4},{12,8},{1,5},{13,9},{2,6},{14,10},{3,7},{15,11},{16,20},{28,... | collective-permute-start | bytes 1572872 | tf_op jit(solution)/shard_map/ppermute | solution.py:434
  114.7 18.6 %collective-permute-start.22 = (bf16[2,8,128,128]{3,2,1,0:T(8,128)(2,1)S(1)}, bf16[2,8,128,128]{3,2,1,0:T(8,128)(2,1)S(1)}, u32[]{:S(2)}, u32[]{:S(2)}) collective-permute-start(bf16[2,8,128,128]{3,2,1,0:T(8,128)(2,1)S(1)} %pad_maximum_fusion.17), channel_id=1, source_target_pairs={{4,8},{8,4},{5,9},{9,5},{6,10},{10,6},{7,11},{11,7},{20,24},{24,20... | collective-permute-start | bytes 1572872 | tf_op jit(solution)/shard_map/ppermute | solution.py:434
  146.3 16.6 %collective-permute-start.29 = (bf16[8,128,128]{2,1,0:T(8,128)(2,1)S(1)}, bf16[8,128,128]{2,1,0:T(8,128)(2,1)S(1)}, u32[]{:S(2)}, u32[]{:S(2)}) collective-permute-start(bf16[8,128,128]{2,1,0:T(8,128)(2,1)S(1)} %get-tuple-element.211), channel_id=1, source_target_pairs={{0,2},{1,3},{2,0},{3,1},{4,6},{5,7},{6,4},{7,5},{8,10},{9,11},{10,... | collective-permute-start | bytes 786440 | tf_op jit(solution)/shard_map/ppermute | solution.py:434
  147.0 16.0 %collective-permute-start.30 = (bf16[8,128,128]{2,1,0:T(8,128)(2,1)S(1)}, bf16[8,128,128]{2,1,0:T(8,128)(2,1)S(1)}, u32[]{:S(2)}, u32[]{:S(2)}) collective-permute-start(bf16[8,128,128]{2,1,0:T(8,128)(2,1)S(1)} %get-tuple-element.209), channel_id=1, source_target_pairs={{0,2},{1,3},{2,0},{3,1},{4,6},{5,7},{6,4},{7,5},{8,10},{9,11},{10,... | collective-permute-start | bytes 786440 | tf_op jit(solution)/shard_map/ppermute | solution.py:434
  218.3 28.0 %collective-permute-start.45 = (bf16[2,2,8,128,128]{4,3,2,1,0:T(8,128)(2,1)S(1)}, bf16[2,2,8,128,128]{4,3,2,1,0:T(8,128)(2,1)S(1)}, u32[]{:S(2)}, u32[]{:S(2)}) collective-permute-start(bf16[2,2,8,128,128]{4,3,2,1,0:T(8,128)(2,1)S(1)} %pad_maximum_fusion.refs_0_.refs_1_.refs_8_.refs_9_), channel_id=1, source_target_pairs={{0,4},{12,8},{1,5},{13,9},{2,6},{14,10},{3,7},{15,11},{16,20},{28,... | collective-permute-start | bytes 3145736 | tf_op jit(solution)/shard_map/ppermute | solution.py:434
  226.0 27.1 %collective-permute-start.41 = (bf16[2,2,8,128,128]{4,3,2,1,0:T(8,128)(2,1)S(1)}, bf16[2,2,8,128,128]{4,3,2,1,0:T(8,128)(2,1)S(1)}, u32[]{:S(2)}, u32[]{:S(2)}) collective-permute-start(bf16[2,2,8,128,128]{4,3,2,1,0:T(8,128)(2,1)S(1)} %get-tuple-element.165), channel_id=1, source_target_pairs={{4,8},{8,4},{5,9},{9,5},{6,10},{10,6},{7,11},{11,7},{20,24},{24,20... | collective-permute-start | bytes 3145736 | tf_op jit(solution)/shard_map/ppermute | solution.py:434
  235.2 30.4 %collective-permute-start.51 = (bf16[2,2,8,128,128]{4,3,2,1,0:T(8,128)(2,1)S(1)}, bf16[2,2,8,128,128]{4,3,2,1,0:T(8,128)(2,1)S(1)}, u32[]{:S(2)}, u32[]{:S(2)}) collective-permute-start(bf16[2,2,8,128,128]{4,3,2,1,0:T(8,128)(2,1)S(1)} %pad_maximum_fusion.1.refs_0_.refs_1_.refs_8_.refs_9_), channel_id=1, source_target_pairs={{0,4},{12,8},{1,5},{13,9},{2,6},{14,10},{3,7},{15,11},{16,20},{28,... | collective-permute-start | bytes 3145736 | tf_op jit(solution)/shard_map/ppermute | solution.py:434
  246.4 20.6 %collective-permute-start.55 = (bf16[2,4,128,128]{3,2,1,0:T(8,128)(2,1)S(1)}, bf16[2,4,128,128]{3,2,1,0:T(8,128)(2,1)S(1)}, u32[]{:S(2)}, u32[]{:S(2)}) collective-permute-start(bf16[2,4,128,128]{3,2,1,0:T(8,128)(2,1)S(1)} %get-tuple-element.182), channel_id=1, source_target_pairs={{0,2},{1,3},{2,0},{3,1},{4,6},{5,7},{6,4},{7,5},{8,10},{9,11},{10,... | collective-permute-start | bytes 786440 | tf_op jit(solution)/shard_map/ppermute | solution.py:434
  247.0 27.5 %collective-permute-start.50 = (bf16[2,8,128,128]{3,2,1,0:T(8,128)(2,1)S(1)}, bf16[2,8,128,128]{3,2,1,0:T(8,128)(2,1)S(1)}, u32[]{:S(2)}, u32[]{:S(2)}) collective-permute-start(bf16[2,8,128,128]{3,2,1,0:T(8,128)(2,1)S(1)} %fusion.5), channel_id=1, source_target_pairs={{0,1},{1,0},{2,3},{3,2},{4,5},{5,4},{6,7},{7,6},{8,9},{9,8},{10,11... | collective-permute-start | bytes 1572872 | tf_op jit(solution)/shard_map/ppermute | solution.py:434
  253.1 31.2 %collective-permute-start.47 = (bf16[2,2,8,128,128]{4,3,2,1,0:T(8,128)(2,1)S(1)}, bf16[2,2,8,128,128]{4,3,2,1,0:T(8,128)(2,1)S(1)}, u32[]{:S(2)}, u32[]{:S(2)}) collective-permute-start(bf16[2,2,8,128,128]{4,3,2,1,0:T(8,128)(2,1)S(1)} %get-tuple-element.172), channel_id=1, source_target_pairs={{4,8},{8,4},{5,9},{9,5},{6,10},{10,6},{7,11},{11,7},{20,24},{24,20... | collective-permute-start | bytes 3145736 | tf_op jit(solution)/shard_map/ppermute | solution.py:434
  277.5 27.5 %collective-permute-start.53 = (bf16[2,2,8,128,128]{4,3,2,1,0:T(8,128)(2,1)S(1)}, bf16[2,2,8,128,128]{4,3,2,1,0:T(8,128)(2,1)S(1)}, u32[]{:S(2)}, u32[]{:S(2)}) collective-permute-start(bf16[2,2,8,128,128]{4,3,2,1,0:T(8,128)(2,1)S(1)} %get-tuple-element.178), channel_id=1, source_target_pairs={{4,8},{8,4},{5,9},{9,5},{6,10},{10,6},{7,11},{11,7},{20,24},{24,20... | collective-permute-start | bytes 3145736 | tf_op jit(solution)/shard_map/ppermute | solution.py:434
  279.8 33.9 %collective-permute-start.42 = (bf16[2,8,128,128]{3,2,1,0:T(8,128)(2,1)S(1)}, bf16[2,8,128,128]{3,2,1,0:T(8,128)(2,1)S(1)}, u32[]{:S(2)}, u32[]{:S(2)}) collective-permute-start(bf16[2,8,128,128]{3,2,1,0:T(8,128)(2,1)S(1)} %fusion.10), channel_id=1, source_target_pairs={{4,0},{8,12},{5,1},{9,13},{6,2},{10,14},{7,3},{11,15},{20,16},{24,... | collective-permute-start | bytes 1572872 | tf_op jit(solution)/shard_map/ppermute | solution.py:434
  284.4 22.8 %collective-permute-start.48 = (bf16[2,8,128,128]{3,2,1,0:T(8,128)(2,1)S(1)}, bf16[2,8,128,128]{3,2,1,0:T(8,128)(2,1)S(1)}, u32[]{:S(2)}, u32[]{:S(2)}) collective-permute-start(bf16[2,8,128,128]{3,2,1,0:T(8,128)(2,1)S(1)} %fusion.9), channel_id=1, source_target_pairs={{4,0},{8,12},{5,1},{9,13},{6,2},{10,14},{7,3},{11,15},{20,16},{24,... | collective-permute-start | bytes 1572872 | tf_op jit(solution)/shard_map/ppermute | solution.py:434
  289.1 19.5 %collective-permute-start.62 = (bf16[2,4,128,128]{3,2,1,0:T(8,128)(2,1)S(1)}, bf16[2,4,128,128]{3,2,1,0:T(8,128)(2,1)S(1)}, u32[]{:S(2)}, u32[]{:S(2)}) collective-permute-start(bf16[2,4,128,128]{3,2,1,0:T(8,128)(2,1)S(1)} %fusion.27), channel_id=1, source_target_pairs={{0,1},{1,0},{2,3},{3,2},{4,5},{5,4},{6,7},{7,6},{8,9},{9,8},{10,11... | collective-permute-start | bytes 786440 | tf_op jit(solution)/shard_map/ppermute | solution.py:434
  304.9 16.7 %collective-permute-start.59 = (bf16[2,2,4,128,128]{4,3,2,1,0:T(8,128)(2,1)S(1)}, bf16[2,2,4,128,128]{4,3,2,1,0:T(8,128)(2,1)S(1)}, u32[]{:S(2)}, u32[]{:S(2)}) collective-permute-start(bf16[2,2,4,128,128]{4,3,2,1,0:T(8,128)(2,1)S(1)} %get-tuple-element.186), channel_id=1, source_target_pairs={{4,8},{8,4},{5,9},{9,5},{6,10},{10,6},{7,11},{11,7},{20,24},{24,20... | collective-permute-start | bytes 1572872 | tf_op jit(solution)/shard_map/ppermute | solution.py:434
  310.1 21.5 %collective-permute-start.65 = (bf16[2,2,4,128,128]{4,3,2,1,0:T(8,128)(2,1)S(1)}, bf16[2,2,4,128,128]{4,3,2,1,0:T(8,128)(2,1)S(1)}, u32[]{:S(2)}, u32[]{:S(2)}) collective-permute-start(bf16[2,2,4,128,128]{4,3,2,1,0:T(8,128)(2,1)S(1)} %get-tuple-element.193), channel_id=1, source_target_pairs={{4,8},{8,4},{5,9},{9,5},{6,10},{10,6},{7,11},{11,7},{20,24},{24,20... | collective-permute-start | bytes 1572872 | tf_op jit(solution)/shard_map/ppermute | solution.py:434
  313.8 25.3 %collective-permute-start.67 = (bf16[8,128,128]{2,1,0:T(8,128)(2,1)S(1)}, bf16[8,128,128]{2,1,0:T(8,128)(2,1)S(1)}, u32[]{:S(2)}, u32[]{:S(2)}) collective-permute-start(bf16[8,128,128]{2,1,0:T(8,128)(2,1)S(1)} %get-tuple-element.205), channel_id=1, source_target_pairs={{0,2},{1,3},{2,0},{3,1},{4,6},{5,7},{6,4},{7,5},{8,10},{9,11},{10,... | collective-permute-start | bytes 786440 | tf_op jit(solution)/shard_map/ppermute | solution.py:434
  (92 other events, 1260.0 us)

commit v11 on v10

--- a/solution.py
+++ b/solution.py
@@ -110,12 +110,9 @@
     place = lax.broadcasted_iota(jnp.int32, (channels, channels), 0)
     same = place == lax.broadcasted_iota(jnp.int32, (channels, channels), 1)
     centre = jnp.where(same, 1.0 - 1.0 / channels, -1.0 / channels).astype(jnp.bfloat16)
-    mean_of = jnp.full((2 * channels, channels), 1.0 / channels, jnp.bfloat16)
+    mean_of = jnp.full((channels, channels), 1.0 / channels, jnp.bfloat16)
     centred = dot(rows, centre)
-    square = centred * centred
-    high = square.astype(jnp.bfloat16)
-    low = (square - high.astype(jnp.float32)).astype(jnp.bfloat16)
-    spread = dot(jnp.concatenate([high, low], 1), mean_of)
+    spread = dot((centred * centred).astype(jnp.bfloat16), mean_of)
     return (centred * lax.rsqrt(spread + EPS) * gain).astype(jnp.bfloat16)
 
 

time: 355 us -> 352 us (level)
  transfers between devices with their start and end apart: 72 -> 72, of which waited for: 37 -> 36; matrix products, arithmetic and copies ran while one was open for 2% -> 2% of each run, Pallas kernels for 7% -> 7%
where the time goes in v11:
time: 352 us; the launch traced here: 350 us
  waiting for transfers between devices  180 us (51%)
  starting transfers between devices  91.4 us (26%)
  Pallas kernels  59.8 us (17%)
  local copies, waits for them, and re-layouts  12.3 us (3%)
  other arithmetic  5.58 us (2%)
    ppermute x72, waiting for transfers between devices, send(): self.add(name, operand, lambda array: lax.ppermute(array, axis, pairs))  180 us
    ppermute x72, starting transfers between devices, send(): self.add(name, operand, lambda array: lax.ppermute(array, axis, pairs))  91.4 us
    pallas_call x10, Pallas kernels, product_call(): pl.pallas_call(functools.partial(pieces_kernel, kernel, len(pieces)), gri...  24.8 us
    pallas_call x1, Pallas kernels, middle_call(): pl.pallas_call(functools.partial(middle_kernel, IN_SIZES, len(products)),...  16.8 us
    pallas_call x1, Pallas kernels, first_call(): pl.pallas_call(functools.partial(first_kernel, OUT_SIZES), grid=(pair.sha...  11.5 us
    unnamed x88, local copies, waits for them, and re-layouts  11 us
  transfers between devices with their start and end apart: 72, of which 36 were waited for; matrix products, arithmetic and copies ran while one was open for 2% of the time, Pallas kernels for 7%

profile of v11, /device:TPU:16, one launch (start us, length us, event | category | flops | bytes accessed | tf_op | source)
XLA Modules:
  0.0 350.2 jit_solution(9520210283742876462)
XLA Ops:
  6.0 11.5 %project.1 = (bf16[128,128,128]{2,1,0:T(8,128)(2,1)S(1)}, bf16[8,128,128]{2,1,0:T(8,128)(2,1)S(1)}, bf16[8,128,128]{2,1,0:T(8,128)(2,1)S(1)}, bf16[8,128,128]{2,...) custom-call(s32[4]{0:T(128)S(1)} %copy-done.31, ...), custom_call_target="tpu_custom_call" | custom-call | flops 100000000 | bytes 419430 | tf_op jit(solution)/shard_map/project/pallas_call | solution.py:343
  22.7 6.0 %collective-permute-done.3.refs_10_ = bf16[8,128,128]{2,1,0:T(8,128)(2,1)S(1)} collective-permute-done((bf16[8,128,128]{2,1,0:T(8,128)(2,1)S(1)}, bf16[8,128,128]{2,1,0:T(8,128)(2,1)S(1)}, u32[]{:S(2)}, u32[]{:S(2)}) %collective-permute-start.3) | collective-permute-done | bytes 262176 | tf_op jit(solution)/shard_map/ppermute | solution.py:431
  36.2 6.3 %collective-permute-done.4.refs_1_.refs_5_ = bf16[2,8,128,128]{3,2,1,0:T(8,128)(2,1)S(1)} collective-permute-done((bf16[2,8,128,128]{3,2,1,0:T(8,128)(2,1)S(1)}, bf16[2,8,128,128]{3,2,1,0:T(8,128)(2,1)S(1)}, u32[]{:S(2)}, u32[]{:S(2)}) %collective-permute-start.4) | collective-permute-done | bytes 524320 | tf_op jit(solution)/shard_map/ppermute | solution.py:431
  51.6 6.8 %collective-permute-done.10.refs_1_.refs_5_ = bf16[2,8,128,128]{3,2,1,0:T(8,128)(2,1)S(1)} collective-permute-done((bf16[2,8,128,128]{3,2,1,0:T(8,128)(2,1)S(1)}, bf16[2,8,128,128]{3,2,1,0:T(8,128)(2,1)S(1)}, u32[]{:S(2)}, u32[]{:S(2)}) %collective-permute-start.10) | collective-permute-done | bytes 524320 | tf_op jit(solution)/shard_map/ppermute | solution.py:431
  58.4 6.1 %collective-permute-done.5.refs_6_.refs_7_ = bf16[2,12,128,128]{3,2,1,0:T(8,128)(2,1)S(1)} collective-permute-done((bf16[2,12,128,128]{3,2,1,0:T(8,128)(2,1)S(1)}, bf16[2,12,128,128]{3,2,1,0:T(8,128)(2,1)S(1)}, u32[]{:S(2)}, u32[]{:S(2)}) %collective-permute-start.5) | collective-permute-done | bytes 786464 | tf_op jit(solution)/shard_map/ppermute | solution.py:431
  74.0 13.9 %collective-permute-done.11.refs_2_.refs_3_.refs_6_.refs_7_ = bf16[2,16,128,128]{3,2,1,0:T(8,128)(2,1)S(1)} collective-permute-done((bf16[2,16,128,128]{3,2,1,0:T(8,128)(2,1)S(1)}, bf16[2,16,128,128]{3,2,1,0:T(8,128)(2,1)S(1)}, u32[]{:S(2)}, u32[]{:S(2)}) %collective-permute-start.11) | collective-permute-done | bytes 1048608 | tf_op jit(solution)/shard_map/ppermute | solution.py:431
  116.9 7.1 %collective-permute-done.14 = bf16[2,8,128,128]{3,2,1,0:T(8,128)(2,1)S(1)} collective-permute-done((bf16[2,8,128,128]{3,2,1,0:T(8,128)(2,1)S(1)}, bf16[2,8,128,128]{3,2,1,0:T(8,128)(2,1)S(1)}, u32[]{:S(2)}, u32[]{:S(2)}) %collective-permute-start.14) | collective-permute-done | bytes 524320 | tf_op jit(solution)/shard_map/ppermute | solution.py:431
  124.0 5.2 %collective-permute-start.19 = (bf16[2,8,128,128]{3,2,1,0:T(8,128)(2,1)}, bf16[2,8,128,128]{3,2,1,0:T(8,128)(2,1)}, u32[]{:S(2)}, u32[]{:S(2)}) collective-permute-start(bf16[2,8,128,128]{3,2,1,0:T(8,128)(2,1)} %fusion.11), channel_id=1, source_target_pairs={{4,0},{8,12},{5,1},{9,13},{6,2},{10,14},{7,3},{11,15},{20,16},{24,... | collective-permute-start | bytes 1572872 | tf_op jit(solution)/shard_map/ppermute | solution.py:431
  152.8 3.7 %collective-permute-done.24 = bf16[2,4,128,128]{3,2,1,0:T(8,128)(2,1)S(1)} collective-permute-done((bf16[2,4,128,128]{3,2,1,0:T(8,128)(2,1)S(1)}, bf16[2,4,128,128]{3,2,1,0:T(8,128)(2,1)S(1)}, u32[]{:S(2)}, u32[]{:S(2)}) %collective-permute-start.24) | collective-permute-done | bytes 262176 | tf_op jit(solution)/shard_map/ppermute | solution.py:431
  157.0 4.0 %collective-permute-done.28 = bf16[2,4,128,128]{3,2,1,0:T(8,128)(2,1)S(1)} collective-permute-done((bf16[2,4,128,128]{3,2,1,0:T(8,128)(2,1)S(1)}, bf16[2,4,128,128]{3,2,1,0:T(8,128)(2,1)S(1)}, u32[]{:S(2)}, u32[]{:S(2)}) %collective-permute-start.28) | collective-permute-done | bytes 262176 | tf_op jit(solution)/shard_map/ppermute | solution.py:431
  161.6 6.7 %collective-permute-done.32.rest_8_ = bf16[4,128,128]{2,1,0:T(8,128)(2,1)S(1)} collective-permute-done((bf16[4,128,128]{2,1,0:T(8,128)(2,1)S(1)}, bf16[4,128,128]{2,1,0:T(8,128)(2,1)S(1)}, u32[]{:S(2)}, u32[]{:S(2)}) %collective-permute-start.32) | collective-permute-done | bytes 131104 | tf_op jit(solution)/shard_map/ppermute | solution.py:431
  170.9 16.8 %middle.1 = (bf16[128,128,128]{2,1,0:T(8,128)(2,1)S(1)}, bf16[128,128,128]{2,1,0:T(8,128)(2,1)S(1)}, bf16[2,8,128,128]{3,2,1,0:T(8,128)(2,1)S(1)}, bf16[2,8,128,...) custom-call(s32[4]{0:T(128)S(1)} %copy-done.32, ...), custom_call_target="tpu_custom_call" | custom-call | flops 150000000 | bytes 943718 | tf_op jit(solution)/shard_map/middle/pallas_call | solution.py:374
  189.4 13.6 %collective-permute-done.37.refs_4_.refs_10_ = bf16[2,8,128,128]{3,2,1,0:T(8,128)(2,1)S(1)} collective-permute-done((bf16[2,8,128,128]{3,2,1,0:T(8,128)(2,1)S(1)}, bf16[2,8,128,128]{3,2,1,0:T(8,128)(2,1)S(1)}, u32[]{:S(2)}, u32[]{:S(2)}) %collective-permute-start.37) | collective-permute-done | bytes 524320 | tf_op jit(solution)/shard_map/ppermute | solution.py:431
  205.0 10.7 %collective-permute-done.43 = bf16[2,8,128,128]{3,2,1,0:T(8,128)(2,1)S(1)} collective-permute-done((bf16[2,8,128,128]{3,2,1,0:T(8,128)(2,1)S(1)}, bf16[2,8,128,128]{3,2,1,0:T(8,128)(2,1)S(1)}, u32[]{:S(2)}, u32[]{:S(2)}) %collective-permute-start.43) | collective-permute-done | bytes 524320 | tf_op jit(solution)/shard_map/ppermute | solution.py:431
  225.7 6.9 %collective-permute-done.49 = bf16[2,8,128,128]{3,2,1,0:T(8,128)(2,1)S(1)} collective-permute-done((bf16[2,8,128,128]{3,2,1,0:T(8,128)(2,1)S(1)}, bf16[2,8,128,128]{3,2,1,0:T(8,128)(2,1)S(1)}, u32[]{:S(2)}, u32[]{:S(2)}) %collective-permute-start.49) | collective-permute-done | bytes 524320 | tf_op jit(solution)/shard_map/ppermute | solution.py:431
  234.2 9.6 %collective-permute-done.45.refs_4_.refs_5_.refs_10_.refs_11_ = bf16[2,2,8,128,128]{4,3,2,1,0:T(8,128)(2,1)S(1)} collective-permute-done((bf16[2,2,8,128,128]{4,3,2,1,0:T(8,128)(2,1)S(1)}, bf16[2,2,8,128,128]{4,3,2,1,0:T(8,128)(2,1)S(1)}, u32[]{:S(2)}, u32[]{:S(2)}) %collective-permute-start.45) | collective-permute-done | bytes 1048608 | tf_op jit(solution)/shard_map/ppermute | solution.py:431
  252.8 10.3 %collective-permute-done.51.refs_4_.refs_5_.refs_10_.refs_11_ = bf16[2,2,8,128,128]{4,3,2,1,0:T(8,128)(2,1)S(1)} collective-permute-done((bf16[2,2,8,128,128]{4,3,2,1,0:T(8,128)(2,1)S(1)}, bf16[2,2,8,128,128]{4,3,2,1,0:T(8,128)(2,1)S(1)}, u32[]{:S(2)}, u32[]{:S(2)}) %collective-permute-start.51) | collective-permute-done | bytes 1048608 | tf_op jit(solution)/shard_map/ppermute | solution.py:431
  265.8 6.1 %collective-permute-done.61 = bf16[2,4,128,128]{3,2,1,0:T(8,128)(2,1)S(1)} collective-permute-done((bf16[2,4,128,128]{3,2,1,0:T(8,128)(2,1)S(1)}, bf16[2,4,128,128]{3,2,1,0:T(8,128)(2,1)S(1)}, u32[]{:S(2)}, u32[]{:S(2)}) %collective-permute-start.61) | collective-permute-done | bytes 262176 | tf_op jit(solution)/shard_map/ppermute | solution.py:431
  281.9 4.6 %collective-permute-start.48 = (bf16[2,8,128,128]{3,2,1,0:T(8,128)(2,1)S(1)}, bf16[2,8,128,128]{3,2,1,0:T(8,128)(2,1)S(1)}, u32[]{:S(2)}, u32[]{:S(2)}) collective-permute-start(bf16[2,8,128,128]{3,2,1,0:T(8,128)(2,1)S(1)} %fusion.9), channel_id=1, source_target_pairs={{4,0},{8,12},{5,1},{9,13},{6,2},{10,14},{7,3},{11,15},{20,16},{24,... | collective-permute-start | bytes 1572872 | tf_op jit(solution)/shard_map/ppermute | solution.py:431
  288.2 7.2 %collective-permute-done.63.refs_4_.refs_5_.refs_10_.refs_11_ = bf16[2,2,4,128,128]{4,3,2,1,0:T(8,128)(2,1)S(1)} collective-permute-done((bf16[2,2,4,128,128]{4,3,2,1,0:T(8,128)(2,1)S(1)}, bf16[2,2,4,128,128]{4,3,2,1,0:T(8,128)(2,1)S(1)}, u32[]{:S(2)}, u32[]{:S(2)}) %collective-permute-start.63) | collective-permute-done | bytes 524320 | tf_op jit(solution)/shard_map/ppermute | solution.py:431
  295.5 6.8 %collective-permute-done.53 = bf16[2,2,8,128,128]{4,3,2,1,0:T(8,128)(2,1)S(1)} collective-permute-done((bf16[2,2,8,128,128]{4,3,2,1,0:T(8,128)(2,1)S(1)}, bf16[2,2,8,128,128]{4,3,2,1,0:T(8,128)(2,1)S(1)}, u32[]{:S(2)}, u32[]{:S(2)}) %collective-permute-start.53) | collective-permute-done | bytes 1048608 | tf_op jit(solution)/shard_map/ppermute | solution.py:431
  312.5 6.6 %collective-permute-done.59 = bf16[2,2,4,128,128]{4,3,2,1,0:T(8,128)(2,1)S(1)} collective-permute-done((bf16[2,2,4,128,128]{4,3,2,1,0:T(8,128)(2,1)S(1)}, bf16[2,2,4,128,128]{4,3,2,1,0:T(8,128)(2,1)S(1)}, u32[]{:S(2)}, u32[]{:S(2)}) %collective-permute-start.59) | collective-permute-done | bytes 524320 | tf_op jit(solution)/shard_map/ppermute | solution.py:431
  322.8 6.2 %collective-permute-done.65 = bf16[2,2,4,128,128]{4,3,2,1,0:T(8,128)(2,1)S(1)} collective-permute-done((bf16[2,2,4,128,128]{4,3,2,1,0:T(8,128)(2,1)S(1)}, bf16[2,2,4,128,128]{4,3,2,1,0:T(8,128)(2,1)S(1)}, u32[]{:S(2)}, u32[]{:S(2)}) %collective-permute-start.65) | collective-permute-done | bytes 524320 | tf_op jit(solution)/shard_map/ppermute | solution.py:431
  343.4 6.8 %finish.1 = bf16[128,128,128]{2,1,0:T(8,128)(2,1)} custom-call(bf16[128,128,128]{2,1,0:T(8,128)(2,1)S(1)} %get-tuple-element.159.pair_ref, bf16[128,128,128]{2,1,0:T(8,128)(2,1)S(1)} %get-tuple-element.160.gate_ref, bf16[2,64,128]{2,1,0:T(8,128)(2,1)S(1)} %copy-done.26, f32[64,1,128]{2,1,0:T(1,128)S(1)} %broadcast_in_dim.15.gain_ref, ...), custom_call_target="tpu_custom_call" | custom-call | flops 50000000 | bytes 734003 | tf_op jit(solution)/shard_map/finish/pallas_call | solution.py:358
  (287 shorter events, 159.2 us)
Async XLA Ops:
  46.2 18.2 %collective-permute-start.5 = (bf16[2,12,128,128]{3,2,1,0:T(8,128)(2,1)S(1)}, bf16[2,12,128,128]{3,2,1,0:T(8,128)(2,1)S(1)}, u32[]{:S(2)}, u32[]{:S(2)}) collective-permute-start(bf16[2,12,128,128]{3,2,1,0:T(8,128)(2,1)S(1)} %pad_maximum_fusion.4), channel_id=1, source_target_pairs={{0,4},{12,8},{1,5},{13,9},{2,6},{14,10},{3,7},{15,11},{16,20},{28,... | collective-permute-start | bytes 2359304 | tf_op jit(solution)/shard_map/ppermute | solution.py:431
  49.2 18.6 %collective-permute-start.7 = (bf16[2,12,128,128]{3,2,1,0:T(8,128)(2,1)S(1)}, bf16[2,12,128,128]{3,2,1,0:T(8,128)(2,1)S(1)}, u32[]{:S(2)}, u32[]{:S(2)}) collective-permute-start(bf16[2,12,128,128]{3,2,1,0:T(8,128)(2,1)S(1)} %pad_maximum_fusion.5), channel_id=1, source_target_pairs={{4,8},{8,4},{5,9},{9,5},{6,10},{10,6},{7,11},{11,7},{20,24},{24,20... | collective-permute-start | bytes 2359304 | tf_op jit(solution)/shard_map/ppermute | solution.py:431
  64.8 23.0 %collective-permute-start.11 = (bf16[2,16,128,128]{3,2,1,0:T(8,128)(2,1)S(1)}, bf16[2,16,128,128]{3,2,1,0:T(8,128)(2,1)S(1)}, u32[]{:S(2)}, u32[]{:S(2)}) collective-permute-start(bf16[2,16,128,128]{3,2,1,0:T(8,128)(2,1)S(1)} %pad_maximum_fusion.2), channel_id=1, source_target_pairs={{0,4},{12,8},{1,5},{13,9},{2,6},{14,10},{3,7},{15,11},{16,20},{28,... | collective-permute-start | bytes 3145736 | tf_op jit(solution)/shard_map/ppermute | solution.py:431
  67.8 23.3 %collective-permute-start.12 = (bf16[2,16,128,128]{3,2,1,0:T(8,128)(2,1)S(1)}, bf16[2,16,128,128]{3,2,1,0:T(8,128)(2,1)S(1)}, u32[]{:S(2)}, u32[]{:S(2)}) collective-permute-start(bf16[2,16,128,128]{3,2,1,0:T(8,128)(2,1)S(1)} %pad_maximum_fusion.3), channel_id=1, source_target_pairs={{4,8},{8,4},{5,9},{9,5},{6,10},{10,6},{7,11},{11,7},{20,24},{24,20... | collective-permute-start | bytes 3145736 | tf_op jit(solution)/shard_map/ppermute | solution.py:431
  73.9 19.5 %collective-permute-start.8 = (bf16[2,2,8,128,128]{4,3,2,1,0:T(8,128)(2,1)S(1)}, bf16[2,2,8,128,128]{4,3,2,1,0:T(8,128)(2,1)S(1)}, u32[]{:S(2)}, u32[]{:S(2)}) collective-permute-start(bf16[2,2,8,128,128]{4,3,2,1,0:T(8,128)(2,1)S(1)} %get-tuple-element.115), channel_id=1, source_target_pairs={{0,1},{1,0},{2,3},{3,2},{4,5},{5,4},{6,7},{7,6},{8,9},{9,8},{10,11... | collective-permute-start | bytes 3145736 | tf_op jit(solution)/shard_map/ppermute | solution.py:431
  88.1 16.5 %collective-permute-start.16 = (bf16[2,12,128,128]{3,2,1,0:T(8,128)(2,1)S(1)}, bf16[2,12,128,128]{3,2,1,0:T(8,128)(2,1)S(1)}, u32[]{:S(2)}, u32[]{:S(2)}) collective-permute-start(bf16[2,12,128,128]{3,2,1,0:T(8,128)(2,1)S(1)} %pad_maximum_fusion.6), channel_id=1, source_target_pairs={{0,4},{12,8},{1,5},{13,9},{2,6},{14,10},{3,7},{15,11},{16,20},{28,... | collective-permute-start | bytes 2359304 | tf_op jit(solution)/shard_map/ppermute | solution.py:431
  91.1 16.2 %collective-permute-start.17 = (bf16[2,12,128,128]{3,2,1,0:T(8,128)(2,1)S(1)}, bf16[2,12,128,128]{3,2,1,0:T(8,128)(2,1)S(1)}, u32[]{:S(2)}, u32[]{:S(2)}) collective-permute-start(bf16[2,12,128,128]{3,2,1,0:T(8,128)(2,1)S(1)} %pad_maximum_fusion.7), channel_id=1, source_target_pairs={{4,8},{8,4},{5,9},{9,5},{6,10},{10,6},{7,11},{11,7},{20,24},{24,20... | collective-permute-start | bytes 2359304 | tf_op jit(solution)/shard_map/ppermute | solution.py:431
  112.0 17.9 %collective-permute-start.21 = (bf16[2,8,128,128]{3,2,1,0:T(8,128)(2,1)S(1)}, bf16[2,8,128,128]{3,2,1,0:T(8,128)(2,1)S(1)}, u32[]{:S(2)}, u32[]{:S(2)}) collective-permute-start(bf16[2,8,128,128]{3,2,1,0:T(8,128)(2,1)S(1)} %pad_maximum_fusion.16), channel_id=1, source_target_pairs={{0,4},{12,8},{1,5},{13,9},{2,6},{14,10},{3,7},{15,11},{16,20},{28,... | collective-permute-start | bytes 1572872 | tf_op jit(solution)/shard_map/ppermute | solution.py:431
  113.4 18.6 %collective-permute-start.22 = (bf16[2,8,128,128]{3,2,1,0:T(8,128)(2,1)S(1)}, bf16[2,8,128,128]{3,2,1,0:T(8,128)(2,1)S(1)}, u32[]{:S(2)}, u32[]{:S(2)}) collective-permute-start(bf16[2,8,128,128]{3,2,1,0:T(8,128)(2,1)S(1)} %pad_maximum_fusion.17), channel_id=1, source_target_pairs={{4,8},{8,4},{5,9},{9,5},{6,10},{10,6},{7,11},{11,7},{20,24},{24,20... | collective-permute-start | bytes 1572872 | tf_op jit(solution)/shard_map/ppermute | solution.py:431
  145.1 16.5 %collective-permute-start.29 = (bf16[8,128,128]{2,1,0:T(8,128)(2,1)S(1)}, bf16[8,128,128]{2,1,0:T(8,128)(2,1)S(1)}, u32[]{:S(2)}, u32[]{:S(2)}) collective-permute-start(bf16[8,128,128]{2,1,0:T(8,128)(2,1)S(1)} %get-tuple-element.211), channel_id=1, source_target_pairs={{0,2},{1,3},{2,0},{3,1},{4,6},{5,7},{6,4},{7,5},{8,10},{9,11},{10,... | collective-permute-start | bytes 786440 | tf_op jit(solution)/shard_map/ppermute | solution.py:431
  145.6 16.0 %collective-permute-start.30 = (bf16[8,128,128]{2,1,0:T(8,128)(2,1)S(1)}, bf16[8,128,128]{2,1,0:T(8,128)(2,1)S(1)}, u32[]{:S(2)}, u32[]{:S(2)}) collective-permute-start(bf16[8,128,128]{2,1,0:T(8,128)(2,1)S(1)} %get-tuple-element.209), channel_id=1, source_target_pairs={{0,2},{1,3},{2,0},{3,1},{4,6},{5,7},{6,4},{7,5},{8,10},{9,11},{10,... | collective-permute-start | bytes 786440 | tf_op jit(solution)/shard_map/ppermute | solution.py:431
  215.8 28.0 %collective-permute-start.45 = (bf16[2,2,8,128,128]{4,3,2,1,0:T(8,128)(2,1)S(1)}, bf16[2,2,8,128,128]{4,3,2,1,0:T(8,128)(2,1)S(1)}, u32[]{:S(2)}, u32[]{:S(2)}) collective-permute-start(bf16[2,2,8,128,128]{4,3,2,1,0:T(8,128)(2,1)S(1)} %pad_maximum_fusion.refs_0_.refs_1_.refs_8_.refs_9_), channel_id=1, source_target_pairs={{0,4},{12,8},{1,5},{13,9},{2,6},{14,10},{3,7},{15,11},{16,20},{28,... | collective-permute-start | bytes 3145736 | tf_op jit(solution)/shard_map/ppermute | solution.py:431
  223.4 27.1 %collective-permute-start.41 = (bf16[2,2,8,128,128]{4,3,2,1,0:T(8,128)(2,1)S(1)}, bf16[2,2,8,128,128]{4,3,2,1,0:T(8,128)(2,1)S(1)}, u32[]{:S(2)}, u32[]{:S(2)}) collective-permute-start(bf16[2,2,8,128,128]{4,3,2,1,0:T(8,128)(2,1)S(1)} %get-tuple-element.165), channel_id=1, source_target_pairs={{4,8},{8,4},{5,9},{9,5},{6,10},{10,6},{7,11},{11,7},{20,24},{24,20... | collective-permute-start | bytes 3145736 | tf_op jit(solution)/shard_map/ppermute | solution.py:431
  232.7 30.4 %collective-permute-start.51 = (bf16[2,2,8,128,128]{4,3,2,1,0:T(8,128)(2,1)S(1)}, bf16[2,2,8,128,128]{4,3,2,1,0:T(8,128)(2,1)S(1)}, u32[]{:S(2)}, u32[]{:S(2)}) collective-permute-start(bf16[2,2,8,128,128]{4,3,2,1,0:T(8,128)(2,1)S(1)} %pad_maximum_fusion.1.refs_0_.refs_1_.refs_8_.refs_9_), channel_id=1, source_target_pairs={{0,4},{12,8},{1,5},{13,9},{2,6},{14,10},{3,7},{15,11},{16,20},{28,... | collective-permute-start | bytes 3145736 | tf_op jit(solution)/shard_map/ppermute | solution.py:431
  243.9 20.6 %collective-permute-start.55 = (bf16[2,4,128,128]{3,2,1,0:T(8,128)(2,1)S(1)}, bf16[2,4,128,128]{3,2,1,0:T(8,128)(2,1)S(1)}, u32[]{:S(2)}, u32[]{:S(2)}) collective-permute-start(bf16[2,4,128,128]{3,2,1,0:T(8,128)(2,1)S(1)} %get-tuple-element.182), channel_id=1, source_target_pairs={{0,2},{1,3},{2,0},{3,1},{4,6},{5,7},{6,4},{7,5},{8,10},{9,11},{10,... | collective-permute-start | bytes 786440 | tf_op jit(solution)/shard_map/ppermute | solution.py:431
  244.4 27.6 %collective-permute-start.50 = (bf16[2,8,128,128]{3,2,1,0:T(8,128)(2,1)S(1)}, bf16[2,8,128,128]{3,2,1,0:T(8,128)(2,1)S(1)}, u32[]{:S(2)}, u32[]{:S(2)}) collective-permute-start(bf16[2,8,128,128]{3,2,1,0:T(8,128)(2,1)S(1)} %fusion.5), channel_id=1, source_target_pairs={{0,1},{1,0},{2,3},{3,2},{4,5},{5,4},{6,7},{7,6},{8,9},{9,8},{10,11... | collective-permute-start | bytes 1572872 | tf_op jit(solution)/shard_map/ppermute | solution.py:431
  250.5 31.2 %collective-permute-start.47 = (bf16[2,2,8,128,128]{4,3,2,1,0:T(8,128)(2,1)S(1)}, bf16[2,2,8,128,128]{4,3,2,1,0:T(8,128)(2,1)S(1)}, u32[]{:S(2)}, u32[]{:S(2)}) collective-permute-start(bf16[2,2,8,128,128]{4,3,2,1,0:T(8,128)(2,1)S(1)} %get-tuple-element.172), channel_id=1, source_target_pairs={{4,8},{8,4},{5,9},{9,5},{6,10},{10,6},{7,11},{11,7},{20,24},{24,20... | collective-permute-start | bytes 3145736 | tf_op jit(solution)/shard_map/ppermute | solution.py:431
  274.9 27.5 %collective-permute-start.53 = (bf16[2,2,8,128,128]{4,3,2,1,0:T(8,128)(2,1)S(1)}, bf16[2,2,8,128,128]{4,3,2,1,0:T(8,128)(2,1)S(1)}, u32[]{:S(2)}, u32[]{:S(2)}) collective-permute-start(bf16[2,2,8,128,128]{4,3,2,1,0:T(8,128)(2,1)S(1)} %get-tuple-element.178), channel_id=1, source_target_pairs={{4,8},{8,4},{5,9},{9,5},{6,10},{10,6},{7,11},{11,7},{20,24},{24,20... | collective-permute-start | bytes 3145736 | tf_op jit(solution)/shard_map/ppermute | solution.py:431
  277.2 33.9 %collective-permute-start.42 = (bf16[2,8,128,128]{3,2,1,0:T(8,128)(2,1)S(1)}, bf16[2,8,128,128]{3,2,1,0:T(8,128)(2,1)S(1)}, u32[]{:S(2)}, u32[]{:S(2)}) collective-permute-start(bf16[2,8,128,128]{3,2,1,0:T(8,128)(2,1)S(1)} %fusion.10), channel_id=1, source_target_pairs={{4,0},{8,12},{5,1},{9,13},{6,2},{10,14},{7,3},{11,15},{20,16},{24,... | collective-permute-start | bytes 1572872 | tf_op jit(solution)/shard_map/ppermute | solution.py:431
  281.9 22.8 %collective-permute-start.48 = (bf16[2,8,128,128]{3,2,1,0:T(8,128)(2,1)S(1)}, bf16[2,8,128,128]{3,2,1,0:T(8,128)(2,1)S(1)}, u32[]{:S(2)}, u32[]{:S(2)}) collective-permute-start(bf16[2,8,128,128]{3,2,1,0:T(8,128)(2,1)S(1)} %fusion.9), channel_id=1, source_target_pairs={{4,0},{8,12},{5,1},{9,13},{6,2},{10,14},{7,3},{11,15},{20,16},{24,... | collective-permute-start | bytes 1572872 | tf_op jit(solution)/shard_map/ppermute | solution.py:431
  286.5 19.5 %collective-permute-start.62 = (bf16[2,4,128,128]{3,2,1,0:T(8,128)(2,1)S(1)}, bf16[2,4,128,128]{3,2,1,0:T(8,128)(2,1)S(1)}, u32[]{:S(2)}, u32[]{:S(2)}) collective-permute-start(bf16[2,4,128,128]{3,2,1,0:T(8,128)(2,1)S(1)} %fusion.27), channel_id=1, source_target_pairs={{0,1},{1,0},{2,3},{3,2},{4,5},{5,4},{6,7},{7,6},{8,9},{9,8},{10,11... | collective-permute-start | bytes 786440 | tf_op jit(solution)/shard_map/ppermute | solution.py:431
  302.4 16.7 %collective-permute-start.59 = (bf16[2,2,4,128,128]{4,3,2,1,0:T(8,128)(2,1)S(1)}, bf16[2,2,4,128,128]{4,3,2,1,0:T(8,128)(2,1)S(1)}, u32[]{:S(2)}, u32[]{:S(2)}) collective-permute-start(bf16[2,2,4,128,128]{4,3,2,1,0:T(8,128)(2,1)S(1)} %get-tuple-element.186), channel_id=1, source_target_pairs={{4,8},{8,4},{5,9},{9,5},{6,10},{10,6},{7,11},{11,7},{20,24},{24,20... | collective-permute-start | bytes 1572872 | tf_op jit(solution)/shard_map/ppermute | solution.py:431
  307.5 21.5 %collective-permute-start.65 = (bf16[2,2,4,128,128]{4,3,2,1,0:T(8,128)(2,1)S(1)}, bf16[2,2,4,128,128]{4,3,2,1,0:T(8,128)(2,1)S(1)}, u32[]{:S(2)}, u32[]{:S(2)}) collective-permute-start(bf16[2,2,4,128,128]{4,3,2,1,0:T(8,128)(2,1)S(1)} %get-tuple-element.193), channel_id=1, source_target_pairs={{4,8},{8,4},{5,9},{9,5},{6,10},{10,6},{7,11},{11,7},{20,24},{24,20... | collective-permute-start | bytes 1572872 | tf_op jit(solution)/shard_map/ppermute | solution.py:431
  311.2 25.3 %collective-permute-start.67 = (bf16[8,128,128]{2,1,0:T(8,128)(2,1)S(1)}, bf16[8,128,128]{2,1,0:T(8,128)(2,1)S(1)}, u32[]{:S(2)}, u32[]{:S(2)}) collective-permute-start(bf16[8,128,128]{2,1,0:T(8,128)(2,1)S(1)} %get-tuple-element.205), channel_id=1, source_target_pairs={{0,2},{1,3},{2,0},{3,1},{4,6},{5,7},{6,4},{7,5},{8,10},{9,11},{10,... | collective-permute-start | bytes 786440 | tf_op jit(solution)/shard_map/ppermute | solution.py:431
  (92 other events, 1259.9 us)

commit v12 on v11

--- a/solution.py
+++ b/solution.py
@@ -17,6 +17,7 @@
 IN_ORDER = {'i0x': ('i0',), 'i3': ('i2',), 'i4': ('i3',), 'a1': ('a0', 'i1'), 'a3': ('a2',), 'o2': ('o1',), 'o3': ('o2',), 'o4': ('o3',), 'x1': ('i0',), 'x2': ('i0x',), 'c4': ('c3',)}
 STEP = 16
 TOLD = 0.05
+FIRST_VMEM = 61 * 1024 * 1024
 VMEM = 28 * 1024 * 1024
 PRODUCT_VMEM = 10 * 1024 * 1024
 
@@ -347,7 +348,7 @@
         out_specs=[tile_spec(pair)] + specs,
         out_shape=[jax.ShapeDtypeStruct(pair.shape, pair.dtype)] + outs,
         scratch_shapes=part_scratch(pair, w_in, OUT_SIZES),
-        compiler_params=params(),
+        compiler_params=params(FIRST_VMEM),
         cost_estimate=cost(2e9, 8 << 20, 4 << 20),
         name="project",
     )(chain, block_mask, pair, w_in, w_gate, gain_in)

time: 352 us -> 349 us (level)
  local copies, waits for them, and re-layouts: 12.3 us -> 4.08 us
    unnamed x88 -> x94, local copies, waits for them, and re-layouts: 11 us -> 2.69 us
  transfers between devices with their start and end apart: 72 -> 72, of which waited for: 36 -> 38; matrix products, arithmetic and copies ran while one was open for 2% -> 2% of each run, Pallas kernels for 7% -> 7%
where the time goes in v12:
time: 349 us; the launch traced here: 347 us
  waiting for transfers between devices  179 us (51%)
  starting transfers between devices  94.7 us (27%)
  Pallas kernels  61.4 us (18%)
  other arithmetic  6.54 us (2%)
  local copies, waits for them, and re-layouts  4.08 us (1%)
    ppermute x72, waiting for transfers between devices, send(): self.add(name, operand, lambda array: lax.ppermute(array, axis, pairs))  179 us
    ppermute x72, starting transfers between devices, send(): self.add(name, operand, lambda array: lax.ppermute(array, axis, pairs))  94.7 us
    pallas_call x10, Pallas kernels, product_call(): pl.pallas_call(functools.partial(pieces_kernel, kernel, len(pieces)), gri...  24.8 us
    pallas_call x1, Pallas kernels, middle_call(): pl.pallas_call(functools.partial(middle_kernel, IN_SIZES, len(products)),...  16.8 us
    pallas_call x1, Pallas kernels, first_call(): pl.pallas_call(functools.partial(first_kernel, OUT_SIZES), grid=(pair.sha...  13 us
  transfers between devices with their start and end apart: 72, of which 38 were waited for; matrix products, arithmetic and copies ran while one was open for 2% of the time, Pallas kernels for 7%

profile of v12, /device:TPU:16, one launch (start us, length us, event | category | flops | bytes accessed | tf_op | source)
XLA Modules:
  0.0 346.9 jit_solution(17554796177615431714)
XLA Ops:
  0.0 13.0 %project.1 = (bf16[128,128,128]{2,1,0:T(8,128)(2,1)}, bf16[8,128,128]{2,1,0:T(8,128)(2,1)}, bf16[8,128,128]{2,1,0:T(8,128)(2,1)}, bf16[8,128,128]{2,1,0:T(8,128)...) custom-call(s32[4]{0:T(128)} %chain_ref.3, ...), custom_call_target="tpu_custom_call" | custom-call | flops 100000000 | bytes 419430 | tf_op jit(solution)/shard_map/project/pallas_call | solution.py:344
  18.2 6.2 %collective-permute-done.3.refs_10_ = bf16[8,128,128]{2,1,0:T(8,128)(2,1)S(1)} collective-permute-done((bf16[8,128,128]{2,1,0:T(8,128)(2,1)}, bf16[8,128,128]{2,1,0:T(8,128)(2,1)S(1)}, u32[]{:S(2)}, u32[]{:S(2)}) %collective-permute-start.3) | collective-permute-done | bytes 262176 | tf_op jit(solution)/shard_map/ppermute | solution.py:432
  32.8 5.4 %collective-permute-done.4.refs_1_.refs_5_ = bf16[2,8,128,128]{3,2,1,0:T(8,128)(2,1)S(1)} collective-permute-done((bf16[2,8,128,128]{3,2,1,0:T(8,128)(2,1)}, bf16[2,8,128,128]{3,2,1,0:T(8,128)(2,1)S(1)}, u32[]{:S(2)}, u32[]{:S(2)}) %collective-permute-start.4) | collective-permute-done | bytes 524320 | tf_op jit(solution)/shard_map/ppermute | solution.py:432
  38.2 4.5 %collective-permute-done.2.refs_2_.refs_7_ = bf16[16,128,128]{2,1,0:T(8,128)(2,1)S(1)} collective-permute-done((bf16[16,128,128]{2,1,0:T(8,128)(2,1)S(1)}, bf16[16,128,128]{2,1,0:T(8,128)(2,1)S(1)}, u32[]{:S(2)}, u32[]{:S(2)}) %collective-permute-start.2) | collective-permute-done | bytes 524320 | tf_op jit(solution)/shard_map/ppermute | solution.py:432
  48.5 6.8 %collective-permute-done.10.refs_1_.refs_5_ = bf16[2,8,128,128]{3,2,1,0:T(8,128)(2,1)S(1)} collective-permute-done((bf16[2,8,128,128]{3,2,1,0:T(8,128)(2,1)S(1)}, bf16[2,8,128,128]{3,2,1,0:T(8,128)(2,1)S(1)}, u32[]{:S(2)}, u32[]{:S(2)}) %collective-permute-start.10) | collective-permute-done | bytes 524320 | tf_op jit(solution)/shard_map/ppermute | solution.py:432
  55.3 6.1 %collective-permute-done.5.refs_6_.refs_7_ = bf16[2,12,128,128]{3,2,1,0:T(8,128)(2,1)S(1)} collective-permute-done((bf16[2,12,128,128]{3,2,1,0:T(8,128)(2,1)S(1)}, bf16[2,12,128,128]{3,2,1,0:T(8,128)(2,1)S(1)}, u32[]{:S(2)}, u32[]{:S(2)}) %collective-permute-start.5) | collective-permute-done | bytes 786464 | tf_op jit(solution)/shard_map/ppermute | solution.py:432
  70.8 14.0 %collective-permute-done.11.refs_2_.refs_3_.refs_6_.refs_7_ = bf16[2,16,128,128]{3,2,1,0:T(8,128)(2,1)S(1)} collective-permute-done((bf16[2,16,128,128]{3,2,1,0:T(8,128)(2,1)S(1)}, bf16[2,16,128,128]{3,2,1,0:T(8,128)(2,1)S(1)}, u32[]{:S(2)}, u32[]{:S(2)}) %collective-permute-start.11) | collective-permute-done | bytes 1048608 | tf_op jit(solution)/shard_map/ppermute | solution.py:432
  113.5 7.1 %collective-permute-done.14 = bf16[2,8,128,128]{3,2,1,0:T(8,128)(2,1)S(1)} collective-permute-done((bf16[2,8,128,128]{3,2,1,0:T(8,128)(2,1)S(1)}, bf16[2,8,128,128]{3,2,1,0:T(8,128)(2,1)S(1)}, u32[]{:S(2)}, u32[]{:S(2)}) %collective-permute-start.14) | collective-permute-done | bytes 524320 | tf_op jit(solution)/shard_map/ppermute | solution.py:432
  120.6 5.2 %collective-permute-start.19 = (bf16[2,8,128,128]{3,2,1,0:T(8,128)(2,1)}, bf16[2,8,128,128]{3,2,1,0:T(8,128)(2,1)}, u32[]{:S(2)}, u32[]{:S(2)}) collective-permute-start(bf16[2,8,128,128]{3,2,1,0:T(8,128)(2,1)} %fusion.11), channel_id=1, source_target_pairs={{4,0},{8,12},{5,1},{9,13},{6,2},{10,14},{7,3},{11,15},{20,16},{24,... | collective-permute-start | bytes 1572872 | tf_op jit(solution)/shard_map/ppermute | solution.py:432
  158.7 6.1 %collective-permute-done.32.rest_8_ = bf16[4,128,128]{2,1,0:T(8,128)(2,1)S(1)} collective-permute-done((bf16[4,128,128]{2,1,0:T(8,128)(2,1)S(1)}, bf16[4,128,128]{2,1,0:T(8,128)(2,1)S(1)}, u32[]{:S(2)}, u32[]{:S(2)}) %collective-permute-start.32) | collective-permute-done | bytes 131104 | tf_op jit(solution)/shard_map/ppermute | solution.py:432
  167.5 16.8 %middle.1 = (bf16[128,128,128]{2,1,0:T(8,128)(2,1)S(1)}, bf16[128,128,128]{2,1,0:T(8,128)(2,1)S(1)}, bf16[2,8,128,128]{3,2,1,0:T(8,128)(2,1)S(1)}, bf16[2,8,128,...) custom-call(s32[4]{0:T(128)S(1)} %copy-done.32, ...), custom_call_target="tpu_custom_call" | custom-call | flops 150000000 | bytes 943718 | tf_op jit(solution)/shard_map/middle/pallas_call | solution.py:375
  186.6 13.1 %collective-permute-done.37.refs_4_.refs_10_ = bf16[2,8,128,128]{3,2,1,0:T(8,128)(2,1)S(1)} collective-permute-done((bf16[2,8,128,128]{3,2,1,0:T(8,128)(2,1)S(1)}, bf16[2,8,128,128]{3,2,1,0:T(8,128)(2,1)S(1)}, u32[]{:S(2)}, u32[]{:S(2)}) %collective-permute-start.37) | collective-permute-done | bytes 524320 | tf_op jit(solution)/shard_map/ppermute | solution.py:432
  202.2 10.1 %collective-permute-done.43 = bf16[2,8,128,128]{3,2,1,0:T(8,128)(2,1)S(1)} collective-permute-done((bf16[2,8,128,128]{3,2,1,0:T(8,128)(2,1)S(1)}, bf16[2,8,128,128]{3,2,1,0:T(8,128)(2,1)S(1)}, u32[]{:S(2)}, u32[]{:S(2)}) %collective-permute-start.43) | collective-permute-done | bytes 524320 | tf_op jit(solution)/shard_map/ppermute | solution.py:432
  222.6 6.6 %collective-permute-done.49 = bf16[2,8,128,128]{3,2,1,0:T(8,128)(2,1)S(1)} collective-permute-done((bf16[2,8,128,128]{3,2,1,0:T(8,128)(2,1)S(1)}, bf16[2,8,128,128]{3,2,1,0:T(8,128)(2,1)S(1)}, u32[]{:S(2)}, u32[]{:S(2)}) %collective-permute-start.49) | collective-permute-done | bytes 524320 | tf_op jit(solution)/shard_map/ppermute | solution.py:432
  230.7 9.6 %collective-permute-done.45.refs_4_.refs_5_.refs_10_.refs_11_ = bf16[2,2,8,128,128]{4,3,2,1,0:T(8,128)(2,1)S(1)} collective-permute-done((bf16[2,2,8,128,128]{4,3,2,1,0:T(8,128)(2,1)S(1)}, bf16[2,2,8,128,128]{4,3,2,1,0:T(8,128)(2,1)S(1)}, u32[]{:S(2)}, u32[]{:S(2)}) %collective-permute-start.45) | collective-permute-done | bytes 1048608 | tf_op jit(solution)/shard_map/ppermute | solution.py:432
  249.6 10.1 %collective-permute-done.51.refs_4_.refs_5_.refs_10_.refs_11_ = bf16[2,2,8,128,128]{4,3,2,1,0:T(8,128)(2,1)S(1)} collective-permute-done((bf16[2,2,8,128,128]{4,3,2,1,0:T(8,128)(2,1)S(1)}, bf16[2,2,8,128,128]{4,3,2,1,0:T(8,128)(2,1)S(1)}, u32[]{:S(2)}, u32[]{:S(2)}) %collective-permute-start.51) | collective-permute-done | bytes 1048608 | tf_op jit(solution)/shard_map/ppermute | solution.py:432
  262.4 6.2 %collective-permute-done.61 = bf16[2,4,128,128]{3,2,1,0:T(8,128)(2,1)S(1)} collective-permute-done((bf16[2,4,128,128]{3,2,1,0:T(8,128)(2,1)S(1)}, bf16[2,4,128,128]{3,2,1,0:T(8,128)(2,1)S(1)}, u32[]{:S(2)}, u32[]{:S(2)}) %collective-permute-start.61) | collective-permute-done | bytes 262176 | tf_op jit(solution)/shard_map/ppermute | solution.py:432
  278.5 4.6 %collective-permute-start.48 = (bf16[2,8,128,128]{3,2,1,0:T(8,128)(2,1)S(1)}, bf16[2,8,128,128]{3,2,1,0:T(8,128)(2,1)S(1)}, u32[]{:S(2)}, u32[]{:S(2)}) collective-permute-start(bf16[2,8,128,128]{3,2,1,0:T(8,128)(2,1)S(1)} %fusion.9), channel_id=1, source_target_pairs={{4,0},{8,12},{5,1},{9,13},{6,2},{10,14},{7,3},{11,15},{20,16},{24,... | collective-permute-start | bytes 1572872 | tf_op jit(solution)/shard_map/ppermute | solution.py:432
  284.8 7.2 %collective-permute-done.63.refs_4_.refs_5_.refs_10_.refs_11_ = bf16[2,2,4,128,128]{4,3,2,1,0:T(8,128)(2,1)S(1)} collective-permute-done((bf16[2,2,4,128,128]{4,3,2,1,0:T(8,128)(2,1)S(1)}, bf16[2,2,4,128,128]{4,3,2,1,0:T(8,128)(2,1)S(1)}, u32[]{:S(2)}, u32[]{:S(2)}) %collective-permute-start.63) | collective-permute-done | bytes 524320 | tf_op jit(solution)/shard_map/ppermute | solution.py:432
  292.1 7.0 %collective-permute-done.53 = bf16[2,2,8,128,128]{4,3,2,1,0:T(8,128)(2,1)S(1)} collective-permute-done((bf16[2,2,8,128,128]{4,3,2,1,0:T(8,128)(2,1)S(1)}, bf16[2,2,8,128,128]{4,3,2,1,0:T(8,128)(2,1)S(1)}, u32[]{:S(2)}, u32[]{:S(2)}) %collective-permute-start.53) | collective-permute-done | bytes 1048608 | tf_op jit(solution)/shard_map/ppermute | solution.py:432
  309.1 6.7 %collective-permute-done.59 = bf16[2,2,4,128,128]{4,3,2,1,0:T(8,128)(2,1)S(1)} collective-permute-done((bf16[2,2,4,128,128]{4,3,2,1,0:T(8,128)(2,1)S(1)}, bf16[2,2,4,128,128]{4,3,2,1,0:T(8,128)(2,1)S(1)}, u32[]{:S(2)}, u32[]{:S(2)}) %collective-permute-start.59) | collective-permute-done | bytes 524320 | tf_op jit(solution)/shard_map/ppermute | solution.py:432
  319.7 6.1 %collective-permute-done.65 = bf16[2,2,4,128,128]{4,3,2,1,0:T(8,128)(2,1)S(1)} collective-permute-done((bf16[2,2,4,128,128]{4,3,2,1,0:T(8,128)(2,1)S(1)}, bf16[2,2,4,128,128]{4,3,2,1,0:T(8,128)(2,1)S(1)}, u32[]{:S(2)}, u32[]{:S(2)}) %collective-permute-start.65) | collective-permute-done | bytes 524320 | tf_op jit(solution)/shard_map/ppermute | solution.py:432
  333.1 3.5 %collective-permute-done.69.rest_7_ = bf16[8,128,128]{2,1,0:T(8,128)(2,1)S(1)} collective-permute-done((bf16[8,128,128]{2,1,0:T(8,128)(2,1)S(1)}, bf16[8,128,128]{2,1,0:T(8,128)(2,1)S(1)}, u32[]{:S(2)}, u32[]{:S(2)}) %collective-permute-start.69) | collective-permute-done | bytes 262176 | tf_op jit(solution)/shard_map/ppermute | solution.py:432
  340.1 6.8 %finish.1 = bf16[128,128,128]{2,1,0:T(8,128)(2,1)} custom-call(bf16[128,128,128]{2,1,0:T(8,128)(2,1)S(1)} %get-tuple-element.159.pair_ref, bf16[128,128,128]{2,1,0:T(8,128)(2,1)S(1)} %get-tuple-element.160.gate_ref, bf16[2,64,128]{2,1,0:T(8,128)(2,1)S(1)} %copy-done.29, f32[64,1,128]{2,1,0:T(1,128)S(1)} %broadcast_in_dim.15.gain_ref, ...), custom_call_target="tpu_custom_call" | custom-call | flops 50000000 | bytes 734003 | tf_op jit(solution)/shard_map/finish/pallas_call | solution.py:359
  (293 shorter events, 156.5 us)
Async XLA Ops:
  43.0 18.3 %collective-permute-start.5 = (bf16[2,12,128,128]{3,2,1,0:T(8,128)(2,1)S(1)}, bf16[2,12,128,128]{3,2,1,0:T(8,128)(2,1)S(1)}, u32[]{:S(2)}, u32[]{:S(2)}) collective-permute-start(bf16[2,12,128,128]{3,2,1,0:T(8,128)(2,1)S(1)} %pad_maximum_fusion.4), channel_id=1, source_target_pairs={{0,4},{12,8},{1,5},{13,9},{2,6},{14,10},{3,7},{15,11},{16,20},{28,... | collective-permute-start | bytes 2359304 | tf_op jit(solution)/shard_map/ppermute | solution.py:432
  45.9 18.5 %collective-permute-start.7 = (bf16[2,12,128,128]{3,2,1,0:T(8,128)(2,1)S(1)}, bf16[2,12,128,128]{3,2,1,0:T(8,128)(2,1)S(1)}, u32[]{:S(2)}, u32[]{:S(2)}) collective-permute-start(bf16[2,12,128,128]{3,2,1,0:T(8,128)(2,1)S(1)} %pad_maximum_fusion.5), channel_id=1, source_target_pairs={{4,8},{8,4},{5,9},{9,5},{6,10},{10,6},{7,11},{11,7},{20,24},{24,20... | collective-permute-start | bytes 2359304 | tf_op jit(solution)/shard_map/ppermute | solution.py:432
  61.7 23.0 %collective-permute-start.11 = (bf16[2,16,128,128]{3,2,1,0:T(8,128)(2,1)S(1)}, bf16[2,16,128,128]{3,2,1,0:T(8,128)(2,1)S(1)}, u32[]{:S(2)}, u32[]{:S(2)}) collective-permute-start(bf16[2,16,128,128]{3,2,1,0:T(8,128)(2,1)S(1)} %pad_maximum_fusion.2), channel_id=1, source_target_pairs={{0,4},{12,8},{1,5},{13,9},{2,6},{14,10},{3,7},{15,11},{16,20},{28,... | collective-permute-start | bytes 3145736 | tf_op jit(solution)/shard_map/ppermute | solution.py:432
  64.5 23.3 %collective-permute-start.12 = (bf16[2,16,128,128]{3,2,1,0:T(8,128)(2,1)S(1)}, bf16[2,16,128,128]{3,2,1,0:T(8,128)(2,1)S(1)}, u32[]{:S(2)}, u32[]{:S(2)}) collective-permute-start(bf16[2,16,128,128]{3,2,1,0:T(8,128)(2,1)S(1)} %pad_maximum_fusion.3), channel_id=1, source_target_pairs={{4,8},{8,4},{5,9},{9,5},{6,10},{10,6},{7,11},{11,7},{20,24},{24,20... | collective-permute-start | bytes 3145736 | tf_op jit(solution)/shard_map/ppermute | solution.py:432
  70.7 19.5 %collective-permute-start.8 = (bf16[2,2,8,128,128]{4,3,2,1,0:T(8,128)(2,1)S(1)}, bf16[2,2,8,128,128]{4,3,2,1,0:T(8,128)(2,1)S(1)}, u32[]{:S(2)}, u32[]{:S(2)}) collective-permute-start(bf16[2,2,8,128,128]{4,3,2,1,0:T(8,128)(2,1)S(1)} %get-tuple-element.115), channel_id=1, source_target_pairs={{0,1},{1,0},{2,3},{3,2},{4,5},{5,4},{6,7},{7,6},{8,9},{9,8},{10,11... | collective-permute-start | bytes 3145736 | tf_op jit(solution)/shard_map/ppermute | solution.py:432
  85.0 16.6 %collective-permute-start.16 = (bf16[2,12,128,128]{3,2,1,0:T(8,128)(2,1)S(1)}, bf16[2,12,128,128]{3,2,1,0:T(8,128)(2,1)S(1)}, u32[]{:S(2)}, u32[]{:S(2)}) collective-permute-start(bf16[2,12,128,128]{3,2,1,0:T(8,128)(2,1)S(1)} %pad_maximum_fusion.6), channel_id=1, source_target_pairs={{0,4},{12,8},{1,5},{13,9},{2,6},{14,10},{3,7},{15,11},{16,20},{28,... | collective-permute-start | bytes 2359304 | tf_op jit(solution)/shard_map/ppermute | solution.py:432
  87.8 16.1 %collective-permute-start.17 = (bf16[2,12,128,128]{3,2,1,0:T(8,128)(2,1)S(1)}, bf16[2,12,128,128]{3,2,1,0:T(8,128)(2,1)S(1)}, u32[]{:S(2)}, u32[]{:S(2)}) collective-permute-start(bf16[2,12,128,128]{3,2,1,0:T(8,128)(2,1)S(1)} %pad_maximum_fusion.7), channel_id=1, source_target_pairs={{4,8},{8,4},{5,9},{9,5},{6,10},{10,6},{7,11},{11,7},{20,24},{24,20... | collective-permute-start | bytes 2359304 | tf_op jit(solution)/shard_map/ppermute | solution.py:432
  108.7 17.9 %collective-permute-start.21 = (bf16[2,8,128,128]{3,2,1,0:T(8,128)(2,1)S(1)}, bf16[2,8,128,128]{3,2,1,0:T(8,128)(2,1)S(1)}, u32[]{:S(2)}, u32[]{:S(2)}) collective-permute-start(bf16[2,8,128,128]{3,2,1,0:T(8,128)(2,1)S(1)} %pad_maximum_fusion.16), channel_id=1, source_target_pairs={{0,4},{12,8},{1,5},{13,9},{2,6},{14,10},{3,7},{15,11},{16,20},{28,... | collective-permute-start | bytes 1572872 | tf_op jit(solution)/shard_map/ppermute | solution.py:432
  110.0 18.6 %collective-permute-start.22 = (bf16[2,8,128,128]{3,2,1,0:T(8,128)(2,1)S(1)}, bf16[2,8,128,128]{3,2,1,0:T(8,128)(2,1)S(1)}, u32[]{:S(2)}, u32[]{:S(2)}) collective-permute-start(bf16[2,8,128,128]{3,2,1,0:T(8,128)(2,1)S(1)} %pad_maximum_fusion.17), channel_id=1, source_target_pairs={{4,8},{8,4},{5,9},{9,5},{6,10},{10,6},{7,11},{11,7},{20,24},{24,20... | collective-permute-start | bytes 1572872 | tf_op jit(solution)/shard_map/ppermute | solution.py:432
  141.7 17.1 %collective-permute-start.29 = (bf16[8,128,128]{2,1,0:T(8,128)(2,1)S(1)}, bf16[8,128,128]{2,1,0:T(8,128)(2,1)S(1)}, u32[]{:S(2)}, u32[]{:S(2)}) collective-permute-start(bf16[8,128,128]{2,1,0:T(8,128)(2,1)S(1)} %get-tuple-element.211), channel_id=1, source_target_pairs={{0,2},{1,3},{2,0},{3,1},{4,6},{5,7},{6,4},{7,5},{8,10},{9,11},{10,... | collective-permute-start | bytes 786440 | tf_op jit(solution)/shard_map/ppermute | solution.py:432
  142.8 16.0 %collective-permute-start.30 = (bf16[8,128,128]{2,1,0:T(8,128)(2,1)S(1)}, bf16[8,128,128]{2,1,0:T(8,128)(2,1)S(1)}, u32[]{:S(2)}, u32[]{:S(2)}) collective-permute-start(bf16[8,128,128]{2,1,0:T(8,128)(2,1)S(1)} %get-tuple-element.209), channel_id=1, source_target_pairs={{0,2},{1,3},{2,0},{3,1},{4,6},{5,7},{6,4},{7,5},{8,10},{9,11},{10,... | collective-permute-start | bytes 786440 | tf_op jit(solution)/shard_map/ppermute | solution.py:432
  212.4 28.0 %collective-permute-start.45 = (bf16[2,2,8,128,128]{4,3,2,1,0:T(8,128)(2,1)S(1)}, bf16[2,2,8,128,128]{4,3,2,1,0:T(8,128)(2,1)S(1)}, u32[]{:S(2)}, u32[]{:S(2)}) collective-permute-start(bf16[2,2,8,128,128]{4,3,2,1,0:T(8,128)(2,1)S(1)} %pad_maximum_fusion.refs_0_.refs_1_.refs_8_.refs_9_), channel_id=1, source_target_pairs={{0,4},{12,8},{1,5},{13,9},{2,6},{14,10},{3,7},{15,11},{16,20},{28,... | collective-permute-start | bytes 3145736 | tf_op jit(solution)/shard_map/ppermute | solution.py:432
  220.0 27.1 %collective-permute-start.41 = (bf16[2,2,8,128,128]{4,3,2,1,0:T(8,128)(2,1)S(1)}, bf16[2,2,8,128,128]{4,3,2,1,0:T(8,128)(2,1)S(1)}, u32[]{:S(2)}, u32[]{:S(2)}) collective-permute-start(bf16[2,2,8,128,128]{4,3,2,1,0:T(8,128)(2,1)S(1)} %get-tuple-element.165), channel_id=1, source_target_pairs={{4,8},{8,4},{5,9},{9,5},{6,10},{10,6},{7,11},{11,7},{20,24},{24,20... | collective-permute-start | bytes 3145736 | tf_op jit(solution)/shard_map/ppermute | solution.py:432
  229.3 30.5 %collective-permute-start.51 = (bf16[2,2,8,128,128]{4,3,2,1,0:T(8,128)(2,1)S(1)}, bf16[2,2,8,128,128]{4,3,2,1,0:T(8,128)(2,1)S(1)}, u32[]{:S(2)}, u32[]{:S(2)}) collective-permute-start(bf16[2,2,8,128,128]{4,3,2,1,0:T(8,128)(2,1)S(1)} %pad_maximum_fusion.1.refs_0_.refs_1_.refs_8_.refs_9_), channel_id=1, source_target_pairs={{0,4},{12,8},{1,5},{13,9},{2,6},{14,10},{3,7},{15,11},{16,20},{28,... | collective-permute-start | bytes 3145736 | tf_op jit(solution)/shard_map/ppermute | solution.py:432
  240.5 20.5 %collective-permute-start.55 = (bf16[2,4,128,128]{3,2,1,0:T(8,128)(2,1)S(1)}, bf16[2,4,128,128]{3,2,1,0:T(8,128)(2,1)S(1)}, u32[]{:S(2)}, u32[]{:S(2)}) collective-permute-start(bf16[2,4,128,128]{3,2,1,0:T(8,128)(2,1)S(1)} %get-tuple-element.182), channel_id=1, source_target_pairs={{0,2},{1,3},{2,0},{3,1},{4,6},{5,7},{6,4},{7,5},{8,10},{9,11},{10,... | collective-permute-start | bytes 786440 | tf_op jit(solution)/shard_map/ppermute | solution.py:432
  241.6 27.1 %collective-permute-start.50 = (bf16[2,8,128,128]{3,2,1,0:T(8,128)(2,1)S(1)}, bf16[2,8,128,128]{3,2,1,0:T(8,128)(2,1)S(1)}, u32[]{:S(2)}, u32[]{:S(2)}) collective-permute-start(bf16[2,8,128,128]{3,2,1,0:T(8,128)(2,1)S(1)} %fusion.5), channel_id=1, source_target_pairs={{0,1},{1,0},{2,3},{3,2},{4,5},{5,4},{6,7},{7,6},{8,9},{9,8},{10,11... | collective-permute-start | bytes 1572872 | tf_op jit(solution)/shard_map/ppermute | solution.py:432
  247.1 31.2 %collective-permute-start.47 = (bf16[2,2,8,128,128]{4,3,2,1,0:T(8,128)(2,1)S(1)}, bf16[2,2,8,128,128]{4,3,2,1,0:T(8,128)(2,1)S(1)}, u32[]{:S(2)}, u32[]{:S(2)}) collective-permute-start(bf16[2,2,8,128,128]{4,3,2,1,0:T(8,128)(2,1)S(1)} %get-tuple-element.172), channel_id=1, source_target_pairs={{4,8},{8,4},{5,9},{9,5},{6,10},{10,6},{7,11},{11,7},{20,24},{24,20... | collective-permute-start | bytes 3145736 | tf_op jit(solution)/shard_map/ppermute | solution.py:432
  271.6 27.5 %collective-permute-start.53 = (bf16[2,2,8,128,128]{4,3,2,1,0:T(8,128)(2,1)S(1)}, bf16[2,2,8,128,128]{4,3,2,1,0:T(8,128)(2,1)S(1)}, u32[]{:S(2)}, u32[]{:S(2)}) collective-permute-start(bf16[2,2,8,128,128]{4,3,2,1,0:T(8,128)(2,1)S(1)} %get-tuple-element.178), channel_id=1, source_target_pairs={{4,8},{8,4},{5,9},{9,5},{6,10},{10,6},{7,11},{11,7},{20,24},{24,20... | collective-permute-start | bytes 3145736 | tf_op jit(solution)/shard_map/ppermute | solution.py:432
  274.1 33.7 %collective-permute-start.42 = (bf16[2,8,128,128]{3,2,1,0:T(8,128)(2,1)S(1)}, bf16[2,8,128,128]{3,2,1,0:T(8,128)(2,1)S(1)}, u32[]{:S(2)}, u32[]{:S(2)}) collective-permute-start(bf16[2,8,128,128]{3,2,1,0:T(8,128)(2,1)S(1)} %fusion.10), channel_id=1, source_target_pairs={{4,0},{8,12},{5,1},{9,13},{6,2},{10,14},{7,3},{11,15},{20,16},{24,... | collective-permute-start | bytes 1572872 | tf_op jit(solution)/shard_map/ppermute | solution.py:432
  278.5 23.1 %collective-permute-start.48 = (bf16[2,8,128,128]{3,2,1,0:T(8,128)(2,1)S(1)}, bf16[2,8,128,128]{3,2,1,0:T(8,128)(2,1)S(1)}, u32[]{:S(2)}, u32[]{:S(2)}) collective-permute-start(bf16[2,8,128,128]{3,2,1,0:T(8,128)(2,1)S(1)} %fusion.9), channel_id=1, source_target_pairs={{4,0},{8,12},{5,1},{9,13},{6,2},{10,14},{7,3},{11,15},{20,16},{24,... | collective-permute-start | bytes 1572872 | tf_op jit(solution)/shard_map/ppermute | solution.py:432
  283.1 19.8 %collective-permute-start.62 = (bf16[2,4,128,128]{3,2,1,0:T(8,128)(2,1)S(1)}, bf16[2,4,128,128]{3,2,1,0:T(8,128)(2,1)S(1)}, u32[]{:S(2)}, u32[]{:S(2)}) collective-permute-start(bf16[2,4,128,128]{3,2,1,0:T(8,128)(2,1)S(1)} %fusion.27), channel_id=1, source_target_pairs={{0,1},{1,0},{2,3},{3,2},{4,5},{5,4},{6,7},{7,6},{8,9},{9,8},{10,11... | collective-permute-start | bytes 786440 | tf_op jit(solution)/shard_map/ppermute | solution.py:432
  299.1 16.7 %collective-permute-start.59 = (bf16[2,2,4,128,128]{4,3,2,1,0:T(8,128)(2,1)S(1)}, bf16[2,2,4,128,128]{4,3,2,1,0:T(8,128)(2,1)S(1)}, u32[]{:S(2)}, u32[]{:S(2)}) collective-permute-start(bf16[2,2,4,128,128]{4,3,2,1,0:T(8,128)(2,1)S(1)} %get-tuple-element.186), channel_id=1, source_target_pairs={{4,8},{8,4},{5,9},{9,5},{6,10},{10,6},{7,11},{11,7},{20,24},{24,20... | collective-permute-start | bytes 1572872 | tf_op jit(solution)/shard_map/ppermute | solution.py:432
  304.4 21.3 %collective-permute-start.65 = (bf16[2,2,4,128,128]{4,3,2,1,0:T(8,128)(2,1)S(1)}, bf16[2,2,4,128,128]{4,3,2,1,0:T(8,128)(2,1)S(1)}, u32[]{:S(2)}, u32[]{:S(2)}) collective-permute-start(bf16[2,2,4,128,128]{4,3,2,1,0:T(8,128)(2,1)S(1)} %get-tuple-element.193), channel_id=1, source_target_pairs={{4,8},{8,4},{5,9},{9,5},{6,10},{10,6},{7,11},{11,7},{20,24},{24,20... | collective-permute-start | bytes 1572872 | tf_op jit(solution)/shard_map/ppermute | solution.py:432
  307.9 25.2 %collective-permute-start.67 = (bf16[8,128,128]{2,1,0:T(8,128)(2,1)S(1)}, bf16[8,128,128]{2,1,0:T(8,128)(2,1)S(1)}, u32[]{:S(2)}, u32[]{:S(2)}) collective-permute-start(bf16[8,128,128]{2,1,0:T(8,128)(2,1)S(1)} %get-tuple-element.205), channel_id=1, source_target_pairs={{0,2},{1,3},{2,0},{3,1},{4,6},{5,7},{6,4},{7,5},{8,10},{9,11},{10,... | collective-permute-start | bytes 786440 | tf_op jit(solution)/shard_map/ppermute | solution.py:432
  (95 other events, 1182.6 us)

commit v13 on v12

--- a/solution.py
+++ b/solution.py
@@ -17,6 +17,7 @@
 IN_ORDER = {'i0x': ('i0',), 'i3': ('i2',), 'i4': ('i3',), 'a1': ('a0', 'i1'), 'a3': ('a2',), 'o2': ('o1',), 'o3': ('o2',), 'o4': ('o3',), 'x1': ('i0',), 'x2': ('i0x',), 'c4': ('c3',)}
 STEP = 16
 TOLD = 0.05
+TOGETHER = 2
 FIRST_VMEM = 61 * 1024 * 1024
 VMEM = 28 * 1024 * 1024
 PRODUCT_VMEM = 10 * 1024 * 1024
@@ -281,8 +282,10 @@
 
 
 def pieces_kernel(kernel, count, *refs):
-    blocks = [ref[(0,) * (len(ref.shape) - 2)] for ref in refs[:count]]
-    kernel(*[blocks[k : k + 2] for k in range(0, count, 2)], refs[count:-1], refs[-1])
+    for channel in range(TOGETHER):
+        blocks = [ref[(0,) * (len(ref.shape) - 3) + (channel,)] for ref in refs[:count]]
+        outs = [ref.at[(slice(None),) * (len(ref.shape) - 3) + (pl.ds(channel, 1),)] for ref in refs[count:-1]]
+        kernel(*[blocks[k : k + 2] for k in range(0, count, 2)], outs, refs[-1])
 
 
 def params(limit=VMEM):
@@ -393,14 +396,16 @@
     size = pieces[0][0].shape[-1]
 
     def piece_spec(array, lead, first):
-        return pl.BlockSpec((1,) * (len(lead) + 1) + (size, size), lambda c: lead + (first + c, 0, 0))
+        return pl.BlockSpec(
+            (1,) * len(lead) + (TOGETHER, size, size), lambda c: lead + (first // TOGETHER + c, 0, 0)
+        )
 
     def out_spec(lead):
-        return pl.BlockSpec(lead + (1, size, size), lambda c: (0,) * len(lead) + (c, 0, 0))
+        return pl.BlockSpec(lead + (TOGETHER, size, size), lambda c: (0,) * len(lead) + (c, 0, 0))
 
     return pl.pallas_call(
         functools.partial(pieces_kernel, kernel, len(pieces)),
-        grid=(channels,),
+        grid=(channels // TOGETHER,),
         in_specs=[piece_spec(*piece) for piece in pieces],
         out_specs=[out_spec(lead) for lead in leads],
         out_shape=[jax.ShapeDtypeStruct(lead + (channels, size, size), jnp.bfloat16) for lead in leads],

time: 349 us -> 346 us (level)
  Pallas kernels: 61.4 us -> 54.6 us
  waiting for transfers between devices: 179 us -> 183 us
    pallas_call x10, Pallas kernels: 24.8 us -> 18 us  [product_call(): pl.pallas_call(functools.partial(pieces_kernel, kernel, len(pieces)), gri...]
    ppermute x72, waiting for transfers between devices: 179 us -> 183 us  [send(): self.add(name, operand, lambda array: lax.ppermute(array, axis, pairs))]
  transfers between devices with their start and end apart: 72 -> 72, of which waited for: 38 -> 38; matrix products, arithmetic and copies ran while one was open for 2% -> 2% of each run, Pallas kernels for 7% -> 5%
where the time goes in v13:
time: 346 us; the launch traced here: 344 us
  waiting for transfers between devices  183 us (53%)
  starting transfers between devices  94.8 us (27%)
  Pallas kernels  54.6 us (16%)
  other arithmetic  6.54 us (2%)
  local copies, waits for them, and re-layouts  4.08 us (1%)
    ppermute x72, waiting for transfers between devices, send(): self.add(name, operand, lambda array: lax.ppermute(array, axis, pairs))  183 us
    ppermute x72, starting transfers between devices, send(): self.add(name, operand, lambda array: lax.ppermute(array, axis, pairs))  94.8 us
    pallas_call x10, Pallas kernels, product_call(): pl.pallas_call(functools.partial(pieces_kernel, kernel, len(pieces)), gri...  18 us
    pallas_call x1, Pallas kernels, middle_call(): pl.pallas_call(functools.partial(middle_kernel, IN_SIZES, len(products)),...  16.8 us
    pallas_call x1, Pallas kernels, first_call(): pl.pallas_call(functools.partial(first_kernel, OUT_SIZES), grid=(pair.sha...  13 us
  transfers between devices with their start and end apart: 72, of which 38 were waited for; matrix products, arithmetic and copies ran while one was open for 2% of the time, Pallas kernels for 5%

profile of v13, /device:TPU:16, one launch (start us, length us, event | category | flops | bytes accessed | tf_op | source)
XLA Modules:
  0.0 344.5 jit_solution(9724765366516952960)
XLA Ops:
  0.0 13.0 %project.1 = (bf16[128,128,128]{2,1,0:T(8,128)(2,1)}, bf16[8,128,128]{2,1,0:T(8,128)(2,1)}, bf16[8,128,128]{2,1,0:T(8,128)(2,1)}, bf16[8,128,128]{2,1,0:T(8,128)...) custom-call(s32[4]{0:T(128)} %chain_ref.3, ...), custom_call_target="tpu_custom_call" | custom-call | flops 100000000 | bytes 419430 | tf_op jit(solution)/shard_map/project/pallas_call | solution.py:347
  18.2 6.2 %collective-permute-done.3.refs_10_ = bf16[8,128,128]{2,1,0:T(8,128)(2,1)S(1)} collective-permute-done((bf16[8,128,128]{2,1,0:T(8,128)(2,1)}, bf16[8,128,128]{2,1,0:T(8,128)(2,1)S(1)}, u32[]{:S(2)}, u32[]{:S(2)}) %collective-permute-start.3) | collective-permute-done | bytes 262176 | tf_op jit(solution)/shard_map/ppermute | solution.py:437
  32.8 5.4 %collective-permute-done.4.refs_1_.refs_5_ = bf16[2,8,128,128]{3,2,1,0:T(8,128)(2,1)S(1)} collective-permute-done((bf16[2,8,128,128]{3,2,1,0:T(8,128)(2,1)}, bf16[2,8,128,128]{3,2,1,0:T(8,128)(2,1)S(1)}, u32[]{:S(2)}, u32[]{:S(2)}) %collective-permute-start.4) | collective-permute-done | bytes 524320 | tf_op jit(solution)/shard_map/ppermute | solution.py:437
  38.2 4.5 %collective-permute-done.2.refs_2_.refs_7_ = bf16[16,128,128]{2,1,0:T(8,128)(2,1)S(1)} collective-permute-done((bf16[16,128,128]{2,1,0:T(8,128)(2,1)S(1)}, bf16[16,128,128]{2,1,0:T(8,128)(2,1)S(1)}, u32[]{:S(2)}, u32[]{:S(2)}) %collective-permute-start.2) | collective-permute-done | bytes 524320 | tf_op jit(solution)/shard_map/ppermute | solution.py:437
  48.5 6.8 %collective-permute-done.10.refs_1_.refs_5_ = bf16[2,8,128,128]{3,2,1,0:T(8,128)(2,1)S(1)} collective-permute-done((bf16[2,8,128,128]{3,2,1,0:T(8,128)(2,1)S(1)}, bf16[2,8,128,128]{3,2,1,0:T(8,128)(2,1)S(1)}, u32[]{:S(2)}, u32[]{:S(2)}) %collective-permute-start.10) | collective-permute-done | bytes 524320 | tf_op jit(solution)/shard_map/ppermute | solution.py:437
  55.3 6.1 %collective-permute-done.5.refs_6_.refs_7_ = bf16[2,12,128,128]{3,2,1,0:T(8,128)(2,1)S(1)} collective-permute-done((bf16[2,12,128,128]{3,2,1,0:T(8,128)(2,1)S(1)}, bf16[2,12,128,128]{3,2,1,0:T(8,128)(2,1)S(1)}, u32[]{:S(2)}, u32[]{:S(2)}) %collective-permute-start.5) | collective-permute-done | bytes 786464 | tf_op jit(solution)/shard_map/ppermute | solution.py:437
  69.9 14.8 %collective-permute-done.11.refs_2_.refs_3_.refs_6_.refs_7_ = bf16[2,16,128,128]{3,2,1,0:T(8,128)(2,1)S(1)} collective-permute-done((bf16[2,16,128,128]{3,2,1,0:T(8,128)(2,1)S(1)}, bf16[2,16,128,128]{3,2,1,0:T(8,128)(2,1)S(1)}, u32[]{:S(2)}, u32[]{:S(2)}) %collective-permute-start.11) | collective-permute-done | bytes 1048608 | tf_op jit(solution)/shard_map/ppermute | solution.py:437
  112.6 7.1 %collective-permute-done.14 = bf16[2,8,128,128]{3,2,1,0:T(8,128)(2,1)S(1)} collective-permute-done((bf16[2,8,128,128]{3,2,1,0:T(8,128)(2,1)S(1)}, bf16[2,8,128,128]{3,2,1,0:T(8,128)(2,1)S(1)}, u32[]{:S(2)}, u32[]{:S(2)}) %collective-permute-start.14) | collective-permute-done | bytes 524320 | tf_op jit(solution)/shard_map/ppermute | solution.py:437
  119.7 5.2 %collective-permute-start.19 = (bf16[2,8,128,128]{3,2,1,0:T(8,128)(2,1)}, bf16[2,8,128,128]{3,2,1,0:T(8,128)(2,1)}, u32[]{:S(2)}, u32[]{:S(2)}) collective-permute-start(bf16[2,8,128,128]{3,2,1,0:T(8,128)(2,1)} %fusion.11), channel_id=1, source_target_pairs={{4,0},{8,12},{5,1},{9,13},{6,2},{10,14},{7,3},{11,15},{20,16},{24,... | collective-permute-start | bytes 1572872 | tf_op jit(solution)/shard_map/ppermute | solution.py:437
  157.1 6.1 %collective-permute-done.32.rest_8_ = bf16[4,128,128]{2,1,0:T(8,128)(2,1)S(1)} collective-permute-done((bf16[4,128,128]{2,1,0:T(8,128)(2,1)S(1)}, bf16[4,128,128]{2,1,0:T(8,128)(2,1)S(1)}, u32[]{:S(2)}, u32[]{:S(2)}) %collective-permute-start.32) | collective-permute-done | bytes 131104 | tf_op jit(solution)/shard_map/ppermute | solution.py:437
  165.8 16.8 %middle.1 = (bf16[128,128,128]{2,1,0:T(8,128)(2,1)S(1)}, bf16[128,128,128]{2,1,0:T(8,128)(2,1)S(1)}, bf16[2,8,128,128]{3,2,1,0:T(8,128)(2,1)S(1)}, bf16[2,8,128,...) custom-call(s32[4]{0:T(128)S(1)} %copy-done.32, ...), custom_call_target="tpu_custom_call" | custom-call | flops 150000000 | bytes 943718 | tf_op jit(solution)/shard_map/middle/pallas_call | solution.py:378
  184.9 13.1 %collective-permute-done.37.refs_4_.refs_10_ = bf16[2,8,128,128]{3,2,1,0:T(8,128)(2,1)S(1)} collective-permute-done((bf16[2,8,128,128]{3,2,1,0:T(8,128)(2,1)S(1)}, bf16[2,8,128,128]{3,2,1,0:T(8,128)(2,1)S(1)}, u32[]{:S(2)}, u32[]{:S(2)}) %collective-permute-start.37) | collective-permute-done | bytes 524320 | tf_op jit(solution)/shard_map/ppermute | solution.py:437
  200.3 10.3 %collective-permute-done.43 = bf16[2,8,128,128]{3,2,1,0:T(8,128)(2,1)S(1)} collective-permute-done((bf16[2,8,128,128]{3,2,1,0:T(8,128)(2,1)S(1)}, bf16[2,8,128,128]{3,2,1,0:T(8,128)(2,1)S(1)}, u32[]{:S(2)}, u32[]{:S(2)}) %collective-permute-start.43) | collective-permute-done | bytes 524320 | tf_op jit(solution)/shard_map/ppermute | solution.py:437
  220.2 7.4 %collective-permute-done.49 = bf16[2,8,128,128]{3,2,1,0:T(8,128)(2,1)S(1)} collective-permute-done((bf16[2,8,128,128]{3,2,1,0:T(8,128)(2,1)S(1)}, bf16[2,8,128,128]{3,2,1,0:T(8,128)(2,1)S(1)}, u32[]{:S(2)}, u32[]{:S(2)}) %collective-permute-start.49) | collective-permute-done | bytes 524320 | tf_op jit(solution)/shard_map/ppermute | solution.py:437
  229.1 9.6 %collective-permute-done.45.refs_4_.refs_5_.refs_10_.refs_11_ = bf16[2,2,8,128,128]{4,3,2,1,0:T(8,128)(2,1)S(1)} collective-permute-done((bf16[2,2,8,128,128]{4,3,2,1,0:T(8,128)(2,1)S(1)}, bf16[2,2,8,128,128]{4,3,2,1,0:T(8,128)(2,1)S(1)}, u32[]{:S(2)}, u32[]{:S(2)}) %collective-permute-start.45) | collective-permute-done | bytes 1048608 | tf_op jit(solution)/shard_map/ppermute | solution.py:437
  247.3 10.9 %collective-permute-done.51.refs_4_.refs_5_.refs_10_.refs_11_ = bf16[2,2,8,128,128]{4,3,2,1,0:T(8,128)(2,1)S(1)} collective-permute-done((bf16[2,2,8,128,128]{4,3,2,1,0:T(8,128)(2,1)S(1)}, bf16[2,2,8,128,128]{4,3,2,1,0:T(8,128)(2,1)S(1)}, u32[]{:S(2)}, u32[]{:S(2)}) %collective-permute-start.51) | collective-permute-done | bytes 1048608 | tf_op jit(solution)/shard_map/ppermute | solution.py:437
  260.8 6.2 %collective-permute-done.61 = bf16[2,4,128,128]{3,2,1,0:T(8,128)(2,1)S(1)} collective-permute-done((bf16[2,4,128,128]{3,2,1,0:T(8,128)(2,1)S(1)}, bf16[2,4,128,128]{3,2,1,0:T(8,128)(2,1)S(1)}, u32[]{:S(2)}, u32[]{:S(2)}) %collective-permute-start.61) | collective-permute-done | bytes 262176 | tf_op jit(solution)/shard_map/ppermute | solution.py:437
  276.8 4.6 %collective-permute-start.48 = (bf16[2,8,128,128]{3,2,1,0:T(8,128)(2,1)S(1)}, bf16[2,8,128,128]{3,2,1,0:T(8,128)(2,1)S(1)}, u32[]{:S(2)}, u32[]{:S(2)}) collective-permute-start(bf16[2,8,128,128]{3,2,1,0:T(8,128)(2,1)S(1)} %fusion.9), channel_id=1, source_target_pairs={{4,0},{8,12},{5,1},{9,13},{6,2},{10,14},{7,3},{11,15},{20,16},{24,... | collective-permute-start | bytes 1572872 | tf_op jit(solution)/shard_map/ppermute | solution.py:437
  282.8 7.6 %collective-permute-done.63.refs_4_.refs_5_.refs_10_.refs_11_ = bf16[2,2,4,128,128]{4,3,2,1,0:T(8,128)(2,1)S(1)} collective-permute-done((bf16[2,2,4,128,128]{4,3,2,1,0:T(8,128)(2,1)S(1)}, bf16[2,2,4,128,128]{4,3,2,1,0:T(8,128)(2,1)S(1)}, u32[]{:S(2)}, u32[]{:S(2)}) %collective-permute-start.63) | collective-permute-done | bytes 524320 | tf_op jit(solution)/shard_map/ppermute | solution.py:437
  290.5 6.2 %collective-permute-done.53 = bf16[2,2,8,128,128]{4,3,2,1,0:T(8,128)(2,1)S(1)} collective-permute-done((bf16[2,2,8,128,128]{4,3,2,1,0:T(8,128)(2,1)S(1)}, bf16[2,2,8,128,128]{4,3,2,1,0:T(8,128)(2,1)S(1)}, u32[]{:S(2)}, u32[]{:S(2)}) %collective-permute-start.53) | collective-permute-done | bytes 1048608 | tf_op jit(solution)/shard_map/ppermute | solution.py:437
  306.3 7.1 %collective-permute-done.59 = bf16[2,2,4,128,128]{4,3,2,1,0:T(8,128)(2,1)S(1)} collective-permute-done((bf16[2,2,4,128,128]{4,3,2,1,0:T(8,128)(2,1)S(1)}, bf16[2,2,4,128,128]{4,3,2,1,0:T(8,128)(2,1)S(1)}, u32[]{:S(2)}, u32[]{:S(2)}) %collective-permute-start.59) | collective-permute-done | bytes 524320 | tf_op jit(solution)/shard_map/ppermute | solution.py:437
  317.3 6.0 %collective-permute-done.65 = bf16[2,2,4,128,128]{4,3,2,1,0:T(8,128)(2,1)S(1)} collective-permute-done((bf16[2,2,4,128,128]{4,3,2,1,0:T(8,128)(2,1)S(1)}, bf16[2,2,4,128,128]{4,3,2,1,0:T(8,128)(2,1)S(1)}, u32[]{:S(2)}, u32[]{:S(2)}) %collective-permute-start.65) | collective-permute-done | bytes 524320 | tf_op jit(solution)/shard_map/ppermute | solution.py:437
  330.7 3.5 %collective-permute-done.69.rest_7_ = bf16[8,128,128]{2,1,0:T(8,128)(2,1)S(1)} collective-permute-done((bf16[8,128,128]{2,1,0:T(8,128)(2,1)S(1)}, bf16[8,128,128]{2,1,0:T(8,128)(2,1)S(1)}, u32[]{:S(2)}, u32[]{:S(2)}) %collective-permute-start.69) | collective-permute-done | bytes 262176 | tf_op jit(solution)/shard_map/ppermute | solution.py:437
  337.7 6.8 %finish.1 = bf16[128,128,128]{2,1,0:T(8,128)(2,1)} custom-call(bf16[128,128,128]{2,1,0:T(8,128)(2,1)S(1)} %get-tuple-element.159.pair_ref, bf16[128,128,128]{2,1,0:T(8,128)(2,1)S(1)} %get-tuple-element.160.gate_ref, bf16[2,64,128]{2,1,0:T(8,128)(2,1)S(1)} %copy-done.29, f32[64,1,128]{2,1,0:T(1,128)S(1)} %broadcast_in_dim.15.gain_ref, ...), custom_call_target="tpu_custom_call" | custom-call | flops 50000000 | bytes 734003 | tf_op jit(solution)/shard_map/finish/pallas_call | solution.py:362
  (293 shorter events, 151.6 us)
Async XLA Ops:
  43.0 18.3 %collective-permute-start.5 = (bf16[2,12,128,128]{3,2,1,0:T(8,128)(2,1)S(1)}, bf16[2,12,128,128]{3,2,1,0:T(8,128)(2,1)S(1)}, u32[]{:S(2)}, u32[]{:S(2)}) collective-permute-start(bf16[2,12,128,128]{3,2,1,0:T(8,128)(2,1)S(1)} %pad_maximum_fusion.4), channel_id=1, source_target_pairs={{0,4},{12,8},{1,5},{13,9},{2,6},{14,10},{3,7},{15,11},{16,20},{28,... | collective-permute-start | bytes 2359304 | tf_op jit(solution)/shard_map/ppermute | solution.py:437
  45.9 18.5 %collective-permute-start.7 = (bf16[2,12,128,128]{3,2,1,0:T(8,128)(2,1)S(1)}, bf16[2,12,128,128]{3,2,1,0:T(8,128)(2,1)S(1)}, u32[]{:S(2)}, u32[]{:S(2)}) collective-permute-start(bf16[2,12,128,128]{3,2,1,0:T(8,128)(2,1)S(1)} %pad_maximum_fusion.5), channel_id=1, source_target_pairs={{4,8},{8,4},{5,9},{9,5},{6,10},{10,6},{7,11},{11,7},{20,24},{24,20... | collective-permute-start | bytes 2359304 | tf_op jit(solution)/shard_map/ppermute | solution.py:437
  61.7 23.0 %collective-permute-start.11 = (bf16[2,16,128,128]{3,2,1,0:T(8,128)(2,1)S(1)}, bf16[2,16,128,128]{3,2,1,0:T(8,128)(2,1)S(1)}, u32[]{:S(2)}, u32[]{:S(2)}) collective-permute-start(bf16[2,16,128,128]{3,2,1,0:T(8,128)(2,1)S(1)} %pad_maximum_fusion.2), channel_id=1, source_target_pairs={{0,4},{12,8},{1,5},{13,9},{2,6},{14,10},{3,7},{15,11},{16,20},{28,... | collective-permute-start | bytes 3145736 | tf_op jit(solution)/shard_map/ppermute | solution.py:437
  64.5 23.3 %collective-permute-start.12 = (bf16[2,16,128,128]{3,2,1,0:T(8,128)(2,1)S(1)}, bf16[2,16,128,128]{3,2,1,0:T(8,128)(2,1)S(1)}, u32[]{:S(2)}, u32[]{:S(2)}) collective-permute-start(bf16[2,16,128,128]{3,2,1,0:T(8,128)(2,1)S(1)} %pad_maximum_fusion.3), channel_id=1, source_target_pairs={{4,8},{8,4},{5,9},{9,5},{6,10},{10,6},{7,11},{11,7},{20,24},{24,20... | collective-permute-start | bytes 3145736 | tf_op jit(solution)/shard_map/ppermute | solution.py:437
  69.9 20.4 %collective-permute-start.8 = (bf16[2,2,8,128,128]{4,3,2,1,0:T(8,128)(2,1)S(1)}, bf16[2,2,8,128,128]{4,3,2,1,0:T(8,128)(2,1)S(1)}, u32[]{:S(2)}, u32[]{:S(2)}) collective-permute-start(bf16[2,2,8,128,128]{4,3,2,1,0:T(8,128)(2,1)S(1)} %get-tuple-element.115), channel_id=1, source_target_pairs={{0,1},{1,0},{2,3},{3,2},{4,5},{5,4},{6,7},{7,6},{8,9},{9,8},{10,11... | collective-permute-start | bytes 3145736 | tf_op jit(solution)/shard_map/ppermute | solution.py:437
  85.0 16.6 %collective-permute-start.16 = (bf16[2,12,128,128]{3,2,1,0:T(8,128)(2,1)S(1)}, bf16[2,12,128,128]{3,2,1,0:T(8,128)(2,1)S(1)}, u32[]{:S(2)}, u32[]{:S(2)}) collective-permute-start(bf16[2,12,128,128]{3,2,1,0:T(8,128)(2,1)S(1)} %pad_maximum_fusion.6), channel_id=1, source_target_pairs={{0,4},{12,8},{1,5},{13,9},{2,6},{14,10},{3,7},{15,11},{16,20},{28,... | collective-permute-start | bytes 2359304 | tf_op jit(solution)/shard_map/ppermute | solution.py:437
  87.8 16.1 %collective-permute-start.17 = (bf16[2,12,128,128]{3,2,1,0:T(8,128)(2,1)S(1)}, bf16[2,12,128,128]{3,2,1,0:T(8,128)(2,1)S(1)}, u32[]{:S(2)}, u32[]{:S(2)}) collective-permute-start(bf16[2,12,128,128]{3,2,1,0:T(8,128)(2,1)S(1)} %pad_maximum_fusion.7), channel_id=1, source_target_pairs={{4,8},{8,4},{5,9},{9,5},{6,10},{10,6},{7,11},{11,7},{20,24},{24,20... | collective-permute-start | bytes 2359304 | tf_op jit(solution)/shard_map/ppermute | solution.py:437
  107.8 17.9 %collective-permute-start.21 = (bf16[2,8,128,128]{3,2,1,0:T(8,128)(2,1)S(1)}, bf16[2,8,128,128]{3,2,1,0:T(8,128)(2,1)S(1)}, u32[]{:S(2)}, u32[]{:S(2)}) collective-permute-start(bf16[2,8,128,128]{3,2,1,0:T(8,128)(2,1)S(1)} %pad_maximum_fusion.16), channel_id=1, source_target_pairs={{0,4},{12,8},{1,5},{13,9},{2,6},{14,10},{3,7},{15,11},{16,20},{28,... | collective-permute-start | bytes 1572872 | tf_op jit(solution)/shard_map/ppermute | solution.py:437
  109.1 18.6 %collective-permute-start.22 = (bf16[2,8,128,128]{3,2,1,0:T(8,128)(2,1)S(1)}, bf16[2,8,128,128]{3,2,1,0:T(8,128)(2,1)S(1)}, u32[]{:S(2)}, u32[]{:S(2)}) collective-permute-start(bf16[2,8,128,128]{3,2,1,0:T(8,128)(2,1)S(1)} %pad_maximum_fusion.17), channel_id=1, source_target_pairs={{4,8},{8,4},{5,9},{9,5},{6,10},{10,6},{7,11},{11,7},{20,24},{24,20... | collective-permute-start | bytes 1572872 | tf_op jit(solution)/shard_map/ppermute | solution.py:437
  140.0 17.1 %collective-permute-start.29 = (bf16[8,128,128]{2,1,0:T(8,128)(2,1)S(1)}, bf16[8,128,128]{2,1,0:T(8,128)(2,1)S(1)}, u32[]{:S(2)}, u32[]{:S(2)}) collective-permute-start(bf16[8,128,128]{2,1,0:T(8,128)(2,1)S(1)} %get-tuple-element.211), channel_id=1, source_target_pairs={{0,2},{1,3},{2,0},{3,1},{4,6},{5,7},{6,4},{7,5},{8,10},{9,11},{10,... | collective-permute-start | bytes 786440 | tf_op jit(solution)/shard_map/ppermute | solution.py:437
  141.1 16.0 %collective-permute-start.30 = (bf16[8,128,128]{2,1,0:T(8,128)(2,1)S(1)}, bf16[8,128,128]{2,1,0:T(8,128)(2,1)S(1)}, u32[]{:S(2)}, u32[]{:S(2)}) collective-permute-start(bf16[8,128,128]{2,1,0:T(8,128)(2,1)S(1)} %get-tuple-element.209), channel_id=1, source_target_pairs={{0,2},{1,3},{2,0},{3,1},{4,6},{5,7},{6,4},{7,5},{8,10},{9,11},{10,... | collective-permute-start | bytes 786440 | tf_op jit(solution)/shard_map/ppermute | solution.py:437
  210.7 28.0 %collective-permute-start.45 = (bf16[2,2,8,128,128]{4,3,2,1,0:T(8,128)(2,1)S(1)}, bf16[2,2,8,128,128]{4,3,2,1,0:T(8,128)(2,1)S(1)}, u32[]{:S(2)}, u32[]{:S(2)}) collective-permute-start(bf16[2,2,8,128,128]{4,3,2,1,0:T(8,128)(2,1)S(1)} %pad_maximum_fusion.refs_0_.refs_1_.refs_8_.refs_9_), channel_id=1, source_target_pairs={{0,4},{12,8},{1,5},{13,9},{2,6},{14,10},{3,7},{15,11},{16,20},{28,... | collective-permute-start | bytes 3145736 | tf_op jit(solution)/shard_map/ppermute | solution.py:437
  217.7 27.1 %collective-permute-start.41 = (bf16[2,2,8,128,128]{4,3,2,1,0:T(8,128)(2,1)S(1)}, bf16[2,2,8,128,128]{4,3,2,1,0:T(8,128)(2,1)S(1)}, u32[]{:S(2)}, u32[]{:S(2)}) collective-permute-start(bf16[2,2,8,128,128]{4,3,2,1,0:T(8,128)(2,1)S(1)} %get-tuple-element.165), channel_id=1, source_target_pairs={{4,8},{8,4},{5,9},{9,5},{6,10},{10,6},{7,11},{11,7},{20,24},{24,20... | collective-permute-start | bytes 3145736 | tf_op jit(solution)/shard_map/ppermute | solution.py:437
  227.7 30.5 %collective-permute-start.51 = (bf16[2,2,8,128,128]{4,3,2,1,0:T(8,128)(2,1)S(1)}, bf16[2,2,8,128,128]{4,3,2,1,0:T(8,128)(2,1)S(1)}, u32[]{:S(2)}, u32[]{:S(2)}) collective-permute-start(bf16[2,2,8,128,128]{4,3,2,1,0:T(8,128)(2,1)S(1)} %pad_maximum_fusion.1.refs_0_.refs_1_.refs_8_.refs_9_), channel_id=1, source_target_pairs={{0,4},{12,8},{1,5},{13,9},{2,6},{14,10},{3,7},{15,11},{16,20},{28,... | collective-permute-start | bytes 3145736 | tf_op jit(solution)/shard_map/ppermute | solution.py:437
  238.9 20.6 %collective-permute-start.55 = (bf16[2,4,128,128]{3,2,1,0:T(8,128)(2,1)S(1)}, bf16[2,4,128,128]{3,2,1,0:T(8,128)(2,1)S(1)}, u32[]{:S(2)}, u32[]{:S(2)}) collective-permute-start(bf16[2,4,128,128]{3,2,1,0:T(8,128)(2,1)S(1)} %get-tuple-element.182), channel_id=1, source_target_pairs={{0,2},{1,3},{2,0},{3,1},{4,6},{5,7},{6,4},{7,5},{8,10},{9,11},{10,... | collective-permute-start | bytes 786440 | tf_op jit(solution)/shard_map/ppermute | solution.py:437
  239.9 27.1 %collective-permute-start.50 = (bf16[2,8,128,128]{3,2,1,0:T(8,128)(2,1)S(1)}, bf16[2,8,128,128]{3,2,1,0:T(8,128)(2,1)S(1)}, u32[]{:S(2)}, u32[]{:S(2)}) collective-permute-start(bf16[2,8,128,128]{3,2,1,0:T(8,128)(2,1)S(1)} %fusion.5), channel_id=1, source_target_pairs={{0,1},{1,0},{2,3},{3,2},{4,5},{5,4},{6,7},{7,6},{8,9},{9,8},{10,11... | collective-permute-start | bytes 1572872 | tf_op jit(solution)/shard_map/ppermute | solution.py:437
  244.8 31.9 %collective-permute-start.47 = (bf16[2,2,8,128,128]{4,3,2,1,0:T(8,128)(2,1)S(1)}, bf16[2,2,8,128,128]{4,3,2,1,0:T(8,128)(2,1)S(1)}, u32[]{:S(2)}, u32[]{:S(2)}) collective-permute-start(bf16[2,2,8,128,128]{4,3,2,1,0:T(8,128)(2,1)S(1)} %get-tuple-element.172), channel_id=1, source_target_pairs={{4,8},{8,4},{5,9},{9,5},{6,10},{10,6},{7,11},{11,7},{20,24},{24,20... | collective-permute-start | bytes 3145736 | tf_op jit(solution)/shard_map/ppermute | solution.py:437
  269.2 27.5 %collective-permute-start.53 = (bf16[2,2,8,128,128]{4,3,2,1,0:T(8,128)(2,1)S(1)}, bf16[2,2,8,128,128]{4,3,2,1,0:T(8,128)(2,1)S(1)}, u32[]{:S(2)}, u32[]{:S(2)}) collective-permute-start(bf16[2,2,8,128,128]{4,3,2,1,0:T(8,128)(2,1)S(1)} %get-tuple-element.178), channel_id=1, source_target_pairs={{4,8},{8,4},{5,9},{9,5},{6,10},{10,6},{7,11},{11,7},{20,24},{24,20... | collective-permute-start | bytes 3145736 | tf_op jit(solution)/shard_map/ppermute | solution.py:437
  271.7 33.3 %collective-permute-start.42 = (bf16[2,8,128,128]{3,2,1,0:T(8,128)(2,1)S(1)}, bf16[2,8,128,128]{3,2,1,0:T(8,128)(2,1)S(1)}, u32[]{:S(2)}, u32[]{:S(2)}) collective-permute-start(bf16[2,8,128,128]{3,2,1,0:T(8,128)(2,1)S(1)} %fusion.10), channel_id=1, source_target_pairs={{4,0},{8,12},{5,1},{9,13},{6,2},{10,14},{7,3},{11,15},{20,16},{24,... | collective-permute-start | bytes 1572872 | tf_op jit(solution)/shard_map/ppermute | solution.py:437
  276.8 22.4 %collective-permute-start.48 = (bf16[2,8,128,128]{3,2,1,0:T(8,128)(2,1)S(1)}, bf16[2,8,128,128]{3,2,1,0:T(8,128)(2,1)S(1)}, u32[]{:S(2)}, u32[]{:S(2)}) collective-permute-start(bf16[2,8,128,128]{3,2,1,0:T(8,128)(2,1)S(1)} %fusion.9), channel_id=1, source_target_pairs={{4,0},{8,12},{5,1},{9,13},{6,2},{10,14},{7,3},{11,15},{20,16},{24,... | collective-permute-start | bytes 1572872 | tf_op jit(solution)/shard_map/ppermute | solution.py:437
  281.5 19.0 %collective-permute-start.62 = (bf16[2,4,128,128]{3,2,1,0:T(8,128)(2,1)S(1)}, bf16[2,4,128,128]{3,2,1,0:T(8,128)(2,1)S(1)}, u32[]{:S(2)}, u32[]{:S(2)}) collective-permute-start(bf16[2,4,128,128]{3,2,1,0:T(8,128)(2,1)S(1)} %fusion.27), channel_id=1, source_target_pairs={{0,1},{1,0},{2,3},{3,2},{4,5},{5,4},{6,7},{7,6},{8,9},{9,8},{10,11... | collective-permute-start | bytes 786440 | tf_op jit(solution)/shard_map/ppermute | solution.py:437
  296.7 16.7 %collective-permute-start.59 = (bf16[2,2,4,128,128]{4,3,2,1,0:T(8,128)(2,1)S(1)}, bf16[2,2,4,128,128]{4,3,2,1,0:T(8,128)(2,1)S(1)}, u32[]{:S(2)}, u32[]{:S(2)}) collective-permute-start(bf16[2,2,4,128,128]{4,3,2,1,0:T(8,128)(2,1)S(1)} %get-tuple-element.186), channel_id=1, source_target_pairs={{4,8},{8,4},{5,9},{9,5},{6,10},{10,6},{7,11},{11,7},{20,24},{24,20... | collective-permute-start | bytes 1572872 | tf_op jit(solution)/shard_map/ppermute | solution.py:437
  301.7 21.7 %collective-permute-start.65 = (bf16[2,2,4,128,128]{4,3,2,1,0:T(8,128)(2,1)S(1)}, bf16[2,2,4,128,128]{4,3,2,1,0:T(8,128)(2,1)S(1)}, u32[]{:S(2)}, u32[]{:S(2)}) collective-permute-start(bf16[2,2,4,128,128]{4,3,2,1,0:T(8,128)(2,1)S(1)} %get-tuple-element.193), channel_id=1, source_target_pairs={{4,8},{8,4},{5,9},{9,5},{6,10},{10,6},{7,11},{11,7},{20,24},{24,20... | collective-permute-start | bytes 1572872 | tf_op jit(solution)/shard_map/ppermute | solution.py:437
  305.2 25.6 %collective-permute-start.67 = (bf16[8,128,128]{2,1,0:T(8,128)(2,1)S(1)}, bf16[8,128,128]{2,1,0:T(8,128)(2,1)S(1)}, u32[]{:S(2)}, u32[]{:S(2)}) collective-permute-start(bf16[8,128,128]{2,1,0:T(8,128)(2,1)S(1)} %get-tuple-element.205), channel_id=1, source_target_pairs={{0,2},{1,3},{2,0},{3,1},{4,6},{5,7},{6,4},{7,5},{8,10},{9,11},{10,... | collective-permute-start | bytes 786440 | tf_op jit(solution)/shard_map/ppermute | solution.py:437
  (95 other events, 1174.1 us)

commit v14 on v13

--- a/solution.py
+++ b/solution.py
@@ -17,7 +17,7 @@
 IN_ORDER = {'i0x': ('i0',), 'i3': ('i2',), 'i4': ('i3',), 'a1': ('a0', 'i1'), 'a3': ('a2',), 'o2': ('o1',), 'o3': ('o2',), 'o4': ('o3',), 'x1': ('i0',), 'x2': ('i0x',), 'c4': ('c3',)}
 STEP = 16
 TOLD = 0.05
-TOGETHER = 2
+TOGETHER = 4
 FIRST_VMEM = 61 * 1024 * 1024
 VMEM = 28 * 1024 * 1024
 PRODUCT_VMEM = 10 * 1024 * 1024

time: 346 us -> 345 us (level)
  Pallas kernels: 54.6 us -> 50.9 us
    pallas_call x10, Pallas kernels: 18 us -> 14.4 us  [product_call(): pl.pallas_call(functools.partial(pieces_kernel, kernel, len(pieces)), gri...]
  transfers between devices with their start and end apart: 72 -> 72, of which waited for: 38 -> 39; matrix products, arithmetic and copies ran while one was open for 2% -> 2% of each run, Pallas kernels for 5% -> 4%
where the time goes in v14:
time: 345 us; the launch traced here: 343 us
  waiting for transfers between devices  186 us (54%)
  starting transfers between devices  94.6 us (27%)
  Pallas kernels  50.9 us (15%)
  other arithmetic  6.54 us (2%)
  local copies, waits for them, and re-layouts  4.08 us (1%)
    ppermute x72, waiting for transfers between devices, send(): self.add(name, operand, lambda array: lax.ppermute(array, axis, pairs))  186 us
    ppermute x72, starting transfers between devices, send(): self.add(name, operand, lambda array: lax.ppermute(array, axis, pairs))  94.6 us
    pallas_call x1, Pallas kernels, middle_call(): pl.pallas_call(functools.partial(middle_kernel, IN_SIZES, len(products)),...  16.8 us
    pallas_call x10, Pallas kernels, product_call(): pl.pallas_call(functools.partial(pieces_kernel, kernel, len(pieces)), gri...  14.4 us
    pallas_call x1, Pallas kernels, first_call(): pl.pallas_call(functools.partial(first_kernel, OUT_SIZES), grid=(pair.sha...  13 us
  transfers between devices with their start and end apart: 72, of which 39 were waited for; matrix products, arithmetic and copies ran while one was open for 2% of the time, Pallas kernels for 4%

profile of v14, /device:TPU:16, one launch (start us, length us, event | category | flops | bytes accessed | tf_op | source)
XLA Modules:
  0.0 343.4 jit_solution(623607961268059888)
XLA Ops:
  0.0 13.0 %project.1 = (bf16[128,128,128]{2,1,0:T(8,128)(2,1)}, bf16[8,128,128]{2,1,0:T(8,128)(2,1)}, bf16[8,128,128]{2,1,0:T(8,128)(2,1)}, bf16[8,128,128]{2,1,0:T(8,128)...) custom-call(s32[4]{0:T(128)} %chain_ref.3, ...), custom_call_target="tpu_custom_call" | custom-call | flops 100000000 | bytes 419430 | tf_op jit(solution)/shard_map/project/pallas_call | solution.py:347
  18.2 6.2 %collective-permute-done.3.refs_10_ = bf16[8,128,128]{2,1,0:T(8,128)(2,1)S(1)} collective-permute-done((bf16[8,128,128]{2,1,0:T(8,128)(2,1)}, bf16[8,128,128]{2,1,0:T(8,128)(2,1)S(1)}, u32[]{:S(2)}, u32[]{:S(2)}) %collective-permute-start.3) | collective-permute-done | bytes 262176 | tf_op jit(solution)/shard_map/ppermute | solution.py:437
  32.8 5.4 %collective-permute-done.4.refs_1_.refs_5_ = bf16[2,8,128,128]{3,2,1,0:T(8,128)(2,1)S(1)} collective-permute-done((bf16[2,8,128,128]{3,2,1,0:T(8,128)(2,1)}, bf16[2,8,128,128]{3,2,1,0:T(8,128)(2,1)S(1)}, u32[]{:S(2)}, u32[]{:S(2)}) %collective-permute-start.4) | collective-permute-done | bytes 524320 | tf_op jit(solution)/shard_map/ppermute | solution.py:437
  38.2 4.5 %collective-permute-done.2.refs_2_.refs_7_ = bf16[16,128,128]{2,1,0:T(8,128)(2,1)S(1)} collective-permute-done((bf16[16,128,128]{2,1,0:T(8,128)(2,1)S(1)}, bf16[16,128,128]{2,1,0:T(8,128)(2,1)S(1)}, u32[]{:S(2)}, u32[]{:S(2)}) %collective-permute-start.2) | collective-permute-done | bytes 524320 | tf_op jit(solution)/shard_map/ppermute | solution.py:437
  48.5 6.8 %collective-permute-done.10.refs_1_.refs_5_ = bf16[2,8,128,128]{3,2,1,0:T(8,128)(2,1)S(1)} collective-permute-done((bf16[2,8,128,128]{3,2,1,0:T(8,128)(2,1)S(1)}, bf16[2,8,128,128]{3,2,1,0:T(8,128)(2,1)S(1)}, u32[]{:S(2)}, u32[]{:S(2)}) %collective-permute-start.10) | collective-permute-done | bytes 524320 | tf_op jit(solution)/shard_map/ppermute | solution.py:437
  55.3 6.1 %collective-permute-done.5.refs_6_.refs_7_ = bf16[2,12,128,128]{3,2,1,0:T(8,128)(2,1)S(1)} collective-permute-done((bf16[2,12,128,128]{3,2,1,0:T(8,128)(2,1)S(1)}, bf16[2,12,128,128]{3,2,1,0:T(8,128)(2,1)S(1)}, u32[]{:S(2)}, u32[]{:S(2)}) %collective-permute-start.5) | collective-permute-done | bytes 786464 | tf_op jit(solution)/shard_map/ppermute | solution.py:437
  69.5 15.3 %collective-permute-done.11.refs_2_.refs_3_.refs_6_.refs_7_ = bf16[2,16,128,128]{3,2,1,0:T(8,128)(2,1)S(1)} collective-permute-done((bf16[2,16,128,128]{3,2,1,0:T(8,128)(2,1)S(1)}, bf16[2,16,128,128]{3,2,1,0:T(8,128)(2,1)S(1)}, u32[]{:S(2)}, u32[]{:S(2)}) %collective-permute-start.11) | collective-permute-done | bytes 1048608 | tf_op jit(solution)/shard_map/ppermute | solution.py:437
  112.1 7.1 %collective-permute-done.14 = bf16[2,8,128,128]{3,2,1,0:T(8,128)(2,1)S(1)} collective-permute-done((bf16[2,8,128,128]{3,2,1,0:T(8,128)(2,1)S(1)}, bf16[2,8,128,128]{3,2,1,0:T(8,128)(2,1)S(1)}, u32[]{:S(2)}, u32[]{:S(2)}) %collective-permute-start.14) | collective-permute-done | bytes 524320 | tf_op jit(solution)/shard_map/ppermute | solution.py:437
  119.2 5.2 %collective-permute-start.19 = (bf16[2,8,128,128]{3,2,1,0:T(8,128)(2,1)}, bf16[2,8,128,128]{3,2,1,0:T(8,128)(2,1)}, u32[]{:S(2)}, u32[]{:S(2)}) collective-permute-start(bf16[2,8,128,128]{3,2,1,0:T(8,128)(2,1)} %fusion.11), channel_id=1, source_target_pairs={{4,0},{8,12},{5,1},{9,13},{6,2},{10,14},{7,3},{11,15},{20,16},{24,... | collective-permute-start | bytes 1572872 | tf_op jit(solution)/shard_map/ppermute | solution.py:437
  156.4 6.1 %collective-permute-done.32.rest_8_ = bf16[4,128,128]{2,1,0:T(8,128)(2,1)S(1)} collective-permute-done((bf16[4,128,128]{2,1,0:T(8,128)(2,1)S(1)}, bf16[4,128,128]{2,1,0:T(8,128)(2,1)S(1)}, u32[]{:S(2)}, u32[]{:S(2)}) %collective-permute-start.32) | collective-permute-done | bytes 131104 | tf_op jit(solution)/shard_map/ppermute | solution.py:437
  165.1 16.8 %middle.1 = (bf16[128,128,128]{2,1,0:T(8,128)(2,1)S(1)}, bf16[128,128,128]{2,1,0:T(8,128)(2,1)S(1)}, bf16[2,8,128,128]{3,2,1,0:T(8,128)(2,1)S(1)}, bf16[2,8,128,...) custom-call(s32[4]{0:T(128)S(1)} %copy-done.32, ...), custom_call_target="tpu_custom_call" | custom-call | flops 150000000 | bytes 943718 | tf_op jit(solution)/shard_map/middle/pallas_call | solution.py:378
  184.2 13.1 %collective-permute-done.37.refs_4_.refs_10_ = bf16[2,8,128,128]{3,2,1,0:T(8,128)(2,1)S(1)} collective-permute-done((bf16[2,8,128,128]{3,2,1,0:T(8,128)(2,1)S(1)}, bf16[2,8,128,128]{3,2,1,0:T(8,128)(2,1)S(1)}, u32[]{:S(2)}, u32[]{:S(2)}) %collective-permute-start.37) | collective-permute-done | bytes 524320 | tf_op jit(solution)/shard_map/ppermute | solution.py:437
  199.7 10.3 %collective-permute-done.43 = bf16[2,8,128,128]{3,2,1,0:T(8,128)(2,1)S(1)} collective-permute-done((bf16[2,8,128,128]{3,2,1,0:T(8,128)(2,1)S(1)}, bf16[2,8,128,128]{3,2,1,0:T(8,128)(2,1)S(1)}, u32[]{:S(2)}, u32[]{:S(2)}) %collective-permute-start.43) | collective-permute-done | bytes 524320 | tf_op jit(solution)/shard_map/ppermute | solution.py:437
  219.1 7.8 %collective-permute-done.49 = bf16[2,8,128,128]{3,2,1,0:T(8,128)(2,1)S(1)} collective-permute-done((bf16[2,8,128,128]{3,2,1,0:T(8,128)(2,1)S(1)}, bf16[2,8,128,128]{3,2,1,0:T(8,128)(2,1)S(1)}, u32[]{:S(2)}, u32[]{:S(2)}) %collective-permute-start.49) | collective-permute-done | bytes 524320 | tf_op jit(solution)/shard_map/ppermute | solution.py:437
  228.4 9.6 %collective-permute-done.45.refs_4_.refs_5_.refs_10_.refs_11_ = bf16[2,2,8,128,128]{4,3,2,1,0:T(8,128)(2,1)S(1)} collective-permute-done((bf16[2,2,8,128,128]{4,3,2,1,0:T(8,128)(2,1)S(1)}, bf16[2,2,8,128,128]{4,3,2,1,0:T(8,128)(2,1)S(1)}, u32[]{:S(2)}, u32[]{:S(2)}) %collective-permute-start.45) | collective-permute-done | bytes 1048608 | tf_op jit(solution)/shard_map/ppermute | solution.py:437
  246.2 11.2 %collective-permute-done.51.refs_4_.refs_5_.refs_10_.refs_11_ = bf16[2,2,8,128,128]{4,3,2,1,0:T(8,128)(2,1)S(1)} collective-permute-done((bf16[2,2,8,128,128]{4,3,2,1,0:T(8,128)(2,1)S(1)}, bf16[2,2,8,128,128]{4,3,2,1,0:T(8,128)(2,1)S(1)}, u32[]{:S(2)}, u32[]{:S(2)}) %collective-permute-start.51) | collective-permute-done | bytes 1048608 | tf_op jit(solution)/shard_map/ppermute | solution.py:437
  260.1 6.2 %collective-permute-done.61 = bf16[2,4,128,128]{3,2,1,0:T(8,128)(2,1)S(1)} collective-permute-done((bf16[2,4,128,128]{3,2,1,0:T(8,128)(2,1)S(1)}, bf16[2,4,128,128]{3,2,1,0:T(8,128)(2,1)S(1)}, u32[]{:S(2)}, u32[]{:S(2)}) %collective-permute-start.61) | collective-permute-done | bytes 262176 | tf_op jit(solution)/shard_map/ppermute | solution.py:437
  276.1 4.6 %collective-permute-start.48 = (bf16[2,8,128,128]{3,2,1,0:T(8,128)(2,1)S(1)}, bf16[2,8,128,128]{3,2,1,0:T(8,128)(2,1)S(1)}, u32[]{:S(2)}, u32[]{:S(2)}) collective-permute-start(bf16[2,8,128,128]{3,2,1,0:T(8,128)(2,1)S(1)} %fusion.9), channel_id=1, source_target_pairs={{4,0},{8,12},{5,1},{9,13},{6,2},{10,14},{7,3},{11,15},{20,16},{24,... | collective-permute-start | bytes 1572872 | tf_op jit(solution)/shard_map/ppermute | solution.py:437
  281.9 7.8 %collective-permute-done.63.refs_4_.refs_5_.refs_10_.refs_11_ = bf16[2,2,4,128,128]{4,3,2,1,0:T(8,128)(2,1)S(1)} collective-permute-done((bf16[2,2,4,128,128]{4,3,2,1,0:T(8,128)(2,1)S(1)}, bf16[2,2,4,128,128]{4,3,2,1,0:T(8,128)(2,1)S(1)}, u32[]{:S(2)}, u32[]{:S(2)}) %collective-permute-start.63) | collective-permute-done | bytes 524320 | tf_op jit(solution)/shard_map/ppermute | solution.py:437
  289.8 5.8 %collective-permute-done.53 = bf16[2,2,8,128,128]{4,3,2,1,0:T(8,128)(2,1)S(1)} collective-permute-done((bf16[2,2,8,128,128]{4,3,2,1,0:T(8,128)(2,1)S(1)}, bf16[2,2,8,128,128]{4,3,2,1,0:T(8,128)(2,1)S(1)}, u32[]{:S(2)}, u32[]{:S(2)}) %collective-permute-start.53) | collective-permute-done | bytes 1048608 | tf_op jit(solution)/shard_map/ppermute | solution.py:437
  305.0 7.4 %collective-permute-done.59 = bf16[2,2,4,128,128]{4,3,2,1,0:T(8,128)(2,1)S(1)} collective-permute-done((bf16[2,2,4,128,128]{4,3,2,1,0:T(8,128)(2,1)S(1)}, bf16[2,2,4,128,128]{4,3,2,1,0:T(8,128)(2,1)S(1)}, u32[]{:S(2)}, u32[]{:S(2)}) %collective-permute-start.59) | collective-permute-done | bytes 524320 | tf_op jit(solution)/shard_map/ppermute | solution.py:437
  316.2 6.1 %collective-permute-done.65 = bf16[2,2,4,128,128]{4,3,2,1,0:T(8,128)(2,1)S(1)} collective-permute-done((bf16[2,2,4,128,128]{4,3,2,1,0:T(8,128)(2,1)S(1)}, bf16[2,2,4,128,128]{4,3,2,1,0:T(8,128)(2,1)S(1)}, u32[]{:S(2)}, u32[]{:S(2)}) %collective-permute-start.65) | collective-permute-done | bytes 524320 | tf_op jit(solution)/shard_map/ppermute | solution.py:437
  329.7 3.5 %collective-permute-done.69.rest_7_ = bf16[8,128,128]{2,1,0:T(8,128)(2,1)S(1)} collective-permute-done((bf16[8,128,128]{2,1,0:T(8,128)(2,1)S(1)}, bf16[8,128,128]{2,1,0:T(8,128)(2,1)S(1)}, u32[]{:S(2)}, u32[]{:S(2)}) %collective-permute-start.69) | collective-permute-done | bytes 262176 | tf_op jit(solution)/shard_map/ppermute | solution.py:437
  336.6 6.8 %finish.1 = bf16[128,128,128]{2,1,0:T(8,128)(2,1)} custom-call(bf16[128,128,128]{2,1,0:T(8,128)(2,1)S(1)} %get-tuple-element.159.pair_ref, bf16[128,128,128]{2,1,0:T(8,128)(2,1)S(1)} %get-tuple-element.160.gate_ref, bf16[2,64,128]{2,1,0:T(8,128)(2,1)S(1)} %copy-done.29, f32[64,1,128]{2,1,0:T(1,128)S(1)} %broadcast_in_dim.15.gain_ref, ...), custom_call_target="tpu_custom_call" | custom-call | flops 50000000 | bytes 734003 | tf_op jit(solution)/shard_map/finish/pallas_call | solution.py:362
  (293 shorter events, 149.2 us)
Async XLA Ops:
  43.0 18.3 %collective-permute-start.5 = (bf16[2,12,128,128]{3,2,1,0:T(8,128)(2,1)S(1)}, bf16[2,12,128,128]{3,2,1,0:T(8,128)(2,1)S(1)}, u32[]{:S(2)}, u32[]{:S(2)}) collective-permute-start(bf16[2,12,128,128]{3,2,1,0:T(8,128)(2,1)S(1)} %pad_maximum_fusion.4), channel_id=1, source_target_pairs={{0,4},{12,8},{1,5},{13,9},{2,6},{14,10},{3,7},{15,11},{16,20},{28,... | collective-permute-start | bytes 2359304 | tf_op jit(solution)/shard_map/ppermute | solution.py:437
  45.9 18.5 %collective-permute-start.7 = (bf16[2,12,128,128]{3,2,1,0:T(8,128)(2,1)S(1)}, bf16[2,12,128,128]{3,2,1,0:T(8,128)(2,1)S(1)}, u32[]{:S(2)}, u32[]{:S(2)}) collective-permute-start(bf16[2,12,128,128]{3,2,1,0:T(8,128)(2,1)S(1)} %pad_maximum_fusion.5), channel_id=1, source_target_pairs={{4,8},{8,4},{5,9},{9,5},{6,10},{10,6},{7,11},{11,7},{20,24},{24,20... | collective-permute-start | bytes 2359304 | tf_op jit(solution)/shard_map/ppermute | solution.py:437
  61.7 23.0 %collective-permute-start.11 = (bf16[2,16,128,128]{3,2,1,0:T(8,128)(2,1)S(1)}, bf16[2,16,128,128]{3,2,1,0:T(8,128)(2,1)S(1)}, u32[]{:S(2)}, u32[]{:S(2)}) collective-permute-start(bf16[2,16,128,128]{3,2,1,0:T(8,128)(2,1)S(1)} %pad_maximum_fusion.2), channel_id=1, source_target_pairs={{0,4},{12,8},{1,5},{13,9},{2,6},{14,10},{3,7},{15,11},{16,20},{28,... | collective-permute-start | bytes 3145736 | tf_op jit(solution)/shard_map/ppermute | solution.py:437
  64.5 23.3 %collective-permute-start.12 = (bf16[2,16,128,128]{3,2,1,0:T(8,128)(2,1)S(1)}, bf16[2,16,128,128]{3,2,1,0:T(8,128)(2,1)S(1)}, u32[]{:S(2)}, u32[]{:S(2)}) collective-permute-start(bf16[2,16,128,128]{3,2,1,0:T(8,128)(2,1)S(1)} %pad_maximum_fusion.3), channel_id=1, source_target_pairs={{4,8},{8,4},{5,9},{9,5},{6,10},{10,6},{7,11},{11,7},{20,24},{24,20... | collective-permute-start | bytes 3145736 | tf_op jit(solution)/shard_map/ppermute | solution.py:437
  69.4 20.9 %collective-permute-start.8 = (bf16[2,2,8,128,128]{4,3,2,1,0:T(8,128)(2,1)S(1)}, bf16[2,2,8,128,128]{4,3,2,1,0:T(8,128)(2,1)S(1)}, u32[]{:S(2)}, u32[]{:S(2)}) collective-permute-start(bf16[2,2,8,128,128]{4,3,2,1,0:T(8,128)(2,1)S(1)} %get-tuple-element.115), channel_id=1, source_target_pairs={{0,1},{1,0},{2,3},{3,2},{4,5},{5,4},{6,7},{7,6},{8,9},{9,8},{10,11... | collective-permute-start | bytes 3145736 | tf_op jit(solution)/shard_map/ppermute | solution.py:437
  85.0 16.6 %collective-permute-start.16 = (bf16[2,12,128,128]{3,2,1,0:T(8,128)(2,1)S(1)}, bf16[2,12,128,128]{3,2,1,0:T(8,128)(2,1)S(1)}, u32[]{:S(2)}, u32[]{:S(2)}) collective-permute-start(bf16[2,12,128,128]{3,2,1,0:T(8,128)(2,1)S(1)} %pad_maximum_fusion.6), channel_id=1, source_target_pairs={{0,4},{12,8},{1,5},{13,9},{2,6},{14,10},{3,7},{15,11},{16,20},{28,... | collective-permute-start | bytes 2359304 | tf_op jit(solution)/shard_map/ppermute | solution.py:437
  87.8 16.1 %collective-permute-start.17 = (bf16[2,12,128,128]{3,2,1,0:T(8,128)(2,1)S(1)}, bf16[2,12,128,128]{3,2,1,0:T(8,128)(2,1)S(1)}, u32[]{:S(2)}, u32[]{:S(2)}) collective-permute-start(bf16[2,12,128,128]{3,2,1,0:T(8,128)(2,1)S(1)} %pad_maximum_fusion.7), channel_id=1, source_target_pairs={{4,8},{8,4},{5,9},{9,5},{6,10},{10,6},{7,11},{11,7},{20,24},{24,20... | collective-permute-start | bytes 2359304 | tf_op jit(solution)/shard_map/ppermute | solution.py:437
  107.3 17.9 %collective-permute-start.21 = (bf16[2,8,128,128]{3,2,1,0:T(8,128)(2,1)S(1)}, bf16[2,8,128,128]{3,2,1,0:T(8,128)(2,1)S(1)}, u32[]{:S(2)}, u32[]{:S(2)}) collective-permute-start(bf16[2,8,128,128]{3,2,1,0:T(8,128)(2,1)S(1)} %pad_maximum_fusion.16), channel_id=1, source_target_pairs={{0,4},{12,8},{1,5},{13,9},{2,6},{14,10},{3,7},{15,11},{16,20},{28,... | collective-permute-start | bytes 1572872 | tf_op jit(solution)/shard_map/ppermute | solution.py:437
  108.7 18.6 %collective-permute-start.22 = (bf16[2,8,128,128]{3,2,1,0:T(8,128)(2,1)S(1)}, bf16[2,8,128,128]{3,2,1,0:T(8,128)(2,1)S(1)}, u32[]{:S(2)}, u32[]{:S(2)}) collective-permute-start(bf16[2,8,128,128]{3,2,1,0:T(8,128)(2,1)S(1)} %pad_maximum_fusion.17), channel_id=1, source_target_pairs={{4,8},{8,4},{5,9},{9,5},{6,10},{10,6},{7,11},{11,7},{20,24},{24,20... | collective-permute-start | bytes 1572872 | tf_op jit(solution)/shard_map/ppermute | solution.py:437
  139.3 17.1 %collective-permute-start.29 = (bf16[8,128,128]{2,1,0:T(8,128)(2,1)S(1)}, bf16[8,128,128]{2,1,0:T(8,128)(2,1)S(1)}, u32[]{:S(2)}, u32[]{:S(2)}) collective-permute-start(bf16[8,128,128]{2,1,0:T(8,128)(2,1)S(1)} %get-tuple-element.211), channel_id=1, source_target_pairs={{0,2},{1,3},{2,0},{3,1},{4,6},{5,7},{6,4},{7,5},{8,10},{9,11},{10,... | collective-permute-start | bytes 786440 | tf_op jit(solution)/shard_map/ppermute | solution.py:437
  140.5 15.9 %collective-permute-start.30 = (bf16[8,128,128]{2,1,0:T(8,128)(2,1)S(1)}, bf16[8,128,128]{2,1,0:T(8,128)(2,1)S(1)}, u32[]{:S(2)}, u32[]{:S(2)}) collective-permute-start(bf16[8,128,128]{2,1,0:T(8,128)(2,1)S(1)} %get-tuple-element.209), channel_id=1, source_target_pairs={{0,2},{1,3},{2,0},{3,1},{4,6},{5,7},{6,4},{7,5},{8,10},{9,11},{10,... | collective-permute-start | bytes 786440 | tf_op jit(solution)/shard_map/ppermute | solution.py:437
  210.0 28.0 %collective-permute-start.45 = (bf16[2,2,8,128,128]{4,3,2,1,0:T(8,128)(2,1)S(1)}, bf16[2,2,8,128,128]{4,3,2,1,0:T(8,128)(2,1)S(1)}, u32[]{:S(2)}, u32[]{:S(2)}) collective-permute-start(bf16[2,2,8,128,128]{4,3,2,1,0:T(8,128)(2,1)S(1)} %pad_maximum_fusion.refs_0_.refs_1_.refs_8_.refs_9_), channel_id=1, source_target_pairs={{0,4},{12,8},{1,5},{13,9},{2,6},{14,10},{3,7},{15,11},{16,20},{28,... | collective-permute-start | bytes 3145736 | tf_op jit(solution)/shard_map/ppermute | solution.py:437
  216.6 27.1 %collective-permute-start.41 = (bf16[2,2,8,128,128]{4,3,2,1,0:T(8,128)(2,1)S(1)}, bf16[2,2,8,128,128]{4,3,2,1,0:T(8,128)(2,1)S(1)}, u32[]{:S(2)}, u32[]{:S(2)}) collective-permute-start(bf16[2,2,8,128,128]{4,3,2,1,0:T(8,128)(2,1)S(1)} %get-tuple-element.165), channel_id=1, source_target_pairs={{4,8},{8,4},{5,9},{9,5},{6,10},{10,6},{7,11},{11,7},{20,24},{24,20... | collective-permute-start | bytes 3145736 | tf_op jit(solution)/shard_map/ppermute | solution.py:437
  227.0 30.4 %collective-permute-start.51 = (bf16[2,2,8,128,128]{4,3,2,1,0:T(8,128)(2,1)S(1)}, bf16[2,2,8,128,128]{4,3,2,1,0:T(8,128)(2,1)S(1)}, u32[]{:S(2)}, u32[]{:S(2)}) collective-permute-start(bf16[2,2,8,128,128]{4,3,2,1,0:T(8,128)(2,1)S(1)} %pad_maximum_fusion.1.refs_0_.refs_1_.refs_8_.refs_9_), channel_id=1, source_target_pairs={{0,4},{12,8},{1,5},{13,9},{2,6},{14,10},{3,7},{15,11},{16,20},{28,... | collective-permute-start | bytes 3145736 | tf_op jit(solution)/shard_map/ppermute | solution.py:437
  238.1 20.6 %collective-permute-start.55 = (bf16[2,4,128,128]{3,2,1,0:T(8,128)(2,1)S(1)}, bf16[2,4,128,128]{3,2,1,0:T(8,128)(2,1)S(1)}, u32[]{:S(2)}, u32[]{:S(2)}) collective-permute-start(bf16[2,4,128,128]{3,2,1,0:T(8,128)(2,1)S(1)} %get-tuple-element.182), channel_id=1, source_target_pairs={{0,2},{1,3},{2,0},{3,1},{4,6},{5,7},{6,4},{7,5},{8,10},{9,11},{10,... | collective-permute-start | bytes 786440 | tf_op jit(solution)/shard_map/ppermute | solution.py:437
  239.2 27.1 %collective-permute-start.50 = (bf16[2,8,128,128]{3,2,1,0:T(8,128)(2,1)S(1)}, bf16[2,8,128,128]{3,2,1,0:T(8,128)(2,1)S(1)}, u32[]{:S(2)}, u32[]{:S(2)}) collective-permute-start(bf16[2,8,128,128]{3,2,1,0:T(8,128)(2,1)S(1)} %fusion.5), channel_id=1, source_target_pairs={{0,1},{1,0},{2,3},{3,2},{4,5},{5,4},{6,7},{7,6},{8,9},{9,8},{10,11... | collective-permute-start | bytes 1572872 | tf_op jit(solution)/shard_map/ppermute | solution.py:437
  243.7 32.3 %collective-permute-start.47 = (bf16[2,2,8,128,128]{4,3,2,1,0:T(8,128)(2,1)S(1)}, bf16[2,2,8,128,128]{4,3,2,1,0:T(8,128)(2,1)S(1)}, u32[]{:S(2)}, u32[]{:S(2)}) collective-permute-start(bf16[2,2,8,128,128]{4,3,2,1,0:T(8,128)(2,1)S(1)} %get-tuple-element.172), channel_id=1, source_target_pairs={{4,8},{8,4},{5,9},{9,5},{6,10},{10,6},{7,11},{11,7},{20,24},{24,20... | collective-permute-start | bytes 3145736 | tf_op jit(solution)/shard_map/ppermute | solution.py:437
  268.2 27.5 %collective-permute-start.53 = (bf16[2,2,8,128,128]{4,3,2,1,0:T(8,128)(2,1)S(1)}, bf16[2,2,8,128,128]{4,3,2,1,0:T(8,128)(2,1)S(1)}, u32[]{:S(2)}, u32[]{:S(2)}) collective-permute-start(bf16[2,2,8,128,128]{4,3,2,1,0:T(8,128)(2,1)S(1)} %get-tuple-element.178), channel_id=1, source_target_pairs={{4,8},{8,4},{5,9},{9,5},{6,10},{10,6},{7,11},{11,7},{20,24},{24,20... | collective-permute-start | bytes 3145736 | tf_op jit(solution)/shard_map/ppermute | solution.py:437
  270.6 33.1 %collective-permute-start.42 = (bf16[2,8,128,128]{3,2,1,0:T(8,128)(2,1)S(1)}, bf16[2,8,128,128]{3,2,1,0:T(8,128)(2,1)S(1)}, u32[]{:S(2)}, u32[]{:S(2)}) collective-permute-start(bf16[2,8,128,128]{3,2,1,0:T(8,128)(2,1)S(1)} %fusion.10), channel_id=1, source_target_pairs={{4,0},{8,12},{5,1},{9,13},{6,2},{10,14},{7,3},{11,15},{20,16},{24,... | collective-permute-start | bytes 1572872 | tf_op jit(solution)/shard_map/ppermute | solution.py:437
  276.1 22.0 %collective-permute-start.48 = (bf16[2,8,128,128]{3,2,1,0:T(8,128)(2,1)S(1)}, bf16[2,8,128,128]{3,2,1,0:T(8,128)(2,1)S(1)}, u32[]{:S(2)}, u32[]{:S(2)}) collective-permute-start(bf16[2,8,128,128]{3,2,1,0:T(8,128)(2,1)S(1)} %fusion.9), channel_id=1, source_target_pairs={{4,0},{8,12},{5,1},{9,13},{6,2},{10,14},{7,3},{11,15},{20,16},{24,... | collective-permute-start | bytes 1572872 | tf_op jit(solution)/shard_map/ppermute | solution.py:437
  280.8 18.7 %collective-permute-start.62 = (bf16[2,4,128,128]{3,2,1,0:T(8,128)(2,1)S(1)}, bf16[2,4,128,128]{3,2,1,0:T(8,128)(2,1)S(1)}, u32[]{:S(2)}, u32[]{:S(2)}) collective-permute-start(bf16[2,4,128,128]{3,2,1,0:T(8,128)(2,1)S(1)} %fusion.27), channel_id=1, source_target_pairs={{0,1},{1,0},{2,3},{3,2},{4,5},{5,4},{6,7},{7,6},{8,9},{9,8},{10,11... | collective-permute-start | bytes 786440 | tf_op jit(solution)/shard_map/ppermute | solution.py:437
  295.6 16.7 %collective-permute-start.59 = (bf16[2,2,4,128,128]{4,3,2,1,0:T(8,128)(2,1)S(1)}, bf16[2,2,4,128,128]{4,3,2,1,0:T(8,128)(2,1)S(1)}, u32[]{:S(2)}, u32[]{:S(2)}) collective-permute-start(bf16[2,2,4,128,128]{4,3,2,1,0:T(8,128)(2,1)S(1)} %get-tuple-element.186), channel_id=1, source_target_pairs={{4,8},{8,4},{5,9},{9,5},{6,10},{10,6},{7,11},{11,7},{20,24},{24,20... | collective-permute-start | bytes 1572872 | tf_op jit(solution)/shard_map/ppermute | solution.py:437
  300.3 22.0 %collective-permute-start.65 = (bf16[2,2,4,128,128]{4,3,2,1,0:T(8,128)(2,1)S(1)}, bf16[2,2,4,128,128]{4,3,2,1,0:T(8,128)(2,1)S(1)}, u32[]{:S(2)}, u32[]{:S(2)}) collective-permute-start(bf16[2,2,4,128,128]{4,3,2,1,0:T(8,128)(2,1)S(1)} %get-tuple-element.193), channel_id=1, source_target_pairs={{4,8},{8,4},{5,9},{9,5},{6,10},{10,6},{7,11},{11,7},{20,24},{24,20... | collective-permute-start | bytes 1572872 | tf_op jit(solution)/shard_map/ppermute | solution.py:437
  303.8 25.8 %collective-permute-start.67 = (bf16[8,128,128]{2,1,0:T(8,128)(2,1)S(1)}, bf16[8,128,128]{2,1,0:T(8,128)(2,1)S(1)}, u32[]{:S(2)}, u32[]{:S(2)}) collective-permute-start(bf16[8,128,128]{2,1,0:T(8,128)(2,1)S(1)} %get-tuple-element.205), channel_id=1, source_target_pairs={{0,2},{1,3},{2,0},{3,1},{4,6},{5,7},{6,4},{7,5},{8,10},{9,11},{10,... | collective-permute-start | bytes 786440 | tf_op jit(solution)/shard_map/ppermute | solution.py:437
  (95 other events, 1172.4 us)
